TPU v7x, 32 devices: a whole 2x2x4 slice. The times are simulated.
32 devices in a mesh: dp: 8 (over z, y), fsdp: 4 (over x, core).
Axes of the slice: x: 2, y: 2, z: 4, core: 2. Of those that a mesh axis runs over, the one named last changes fastest.
Arguments:
- inputs: bfloat16 [32768, 512], P(('dp', 'fsdp')), may hold values from -8.5 to 8.5
- embedding: bfloat16 [32768, 512], P(('dp', 'fsdp')), may hold values from -6 to 6
- segments: int32 [32, 1024], P(('dp', 'fsdp')), may hold values from 0 to 5, never falling along the last dimension, each value on 1 to 512 neighbouring positions
- routes_first: int32 [32768, 1], P(('dp', 'fsdp')), may hold values from 0 to 3; in each aligned block of 1024 rows (0 to 1023, 1024 to 2047, ...) at most 512 rows name the same one
- routes_second: int32 [32768, 1], P(('dp', 'fsdp')), may hold values from 0 to 3; in each aligned block of 1024 rows (0 to 1023, 1024 to 2047, ...) at most 512 rows name the same one
- cotangent: bfloat16 [32768, 512], P(('dp', 'fsdp')), may hold values from -8.5 to 8.5
- first_gain: bfloat16 [512], P(('dp', 'fsdp')), may hold values from 0.5 to 1.5
- first_bias: bfloat16 [512], P(('dp', 'fsdp')), may hold values from -1.75 to 1.75
- first_router: bfloat16 [1024, 4], P(('dp', 'fsdp')), may hold values from -0.09375 to 0.09375
- first_up: bfloat16 [4, 512, 2048], P(None, ('dp', 'fsdp')), may hold values from -0.25 to 0.25
- first_down: bfloat16 [4, 2048, 512], P(None, ('dp', 'fsdp')), may hold values from -1.5 to 1.5
- attend_gain: bfloat16 [512], P(('dp', 'fsdp')), may hold values from 0.5 to 1.5
- attend_bias: bfloat16 [512], P(('dp', 'fsdp')), may hold values from -1.75 to 1.75
- project_in: bfloat16 [512, 1536], P(('dp', 'fsdp')), may hold values from -0.25 to 0.25
- relative_weight: bfloat16 [512, 512], P(('dp', 'fsdp')), may hold values from -0.25 to 0.25
- content_bias: bfloat16 [512], P(('dp', 'fsdp')), may hold values from -3 to 3
- position_bias: bfloat16 [512], P(('dp', 'fsdp')), may hold values from -3 to 3
- attend_out: bfloat16 [512, 512], P(('dp', 'fsdp')), may hold values from -1.5 to 1.5
- depth_gain: bfloat16 [512], P(('dp', 'fsdp')), may hold values from 0.5 to 1.5
- depth_bias: bfloat16 [512], P(('dp', 'fsdp')), may hold values from -1.75 to 1.75
- gated_in: bfloat16 [512, 1024], P(('dp', 'fsdp')), may hold values from -0.25 to 0.25
- depth_kernel: bfloat16 [15, 512], P(None, ('dp', 'fsdp')), may hold values from -1.5 to 1.5
- batch_gain: bfloat16 [512], P(('dp', 'fsdp')), may hold values from 0.5 to 1.5
- batch_bias: bfloat16 [512], P(('dp', 'fsdp')), may hold values from -1.75 to 1.75
- point_out: bfloat16 [512, 512], P(('dp', 'fsdp')), may hold values from -0.25 to 0.25
- second_gain: bfloat16 [512], P(('dp', 'fsdp')), may hold values from 0.5 to 1.5
- second_bias: bfloat16 [512], P(('dp', 'fsdp')), may hold values from -1.75 to 1.75
- second_router: bfloat16 [1024, 4], P(('dp', 'fsdp')), may hold values from -0.09375 to 0.09375
- second_up: bfloat16 [4, 512, 2048], P(None, ('dp', 'fsdp')), may hold values from -0.25 to 0.25
- second_down: bfloat16 [4, 2048, 512], P(None, ('dp', 'fsdp')), may hold values from -1.5 to 1.5
- final_gain: bfloat16 [512], P(('dp', 'fsdp')), may hold values from 0.5 to 1.5
- final_bias: bfloat16 [512], P(('dp', 'fsdp')), may hold values from -1.75 to 1.75
Outputs:
- result: bfloat16 [32768, 512], P(('dp', 'fsdp'))
- input_gradient: float32 [32768, 512], P(('dp', 'fsdp'))
- first_gain_gradient: float32 [512], P(('dp', 'fsdp'))
- first_bias_gradient: float32 [512], P(('dp', 'fsdp'))
- first_router_gradient: float32 [1024, 4], P(('dp', 'fsdp'))
- first_up_gradient: float32 [4, 512, 2048], P(None, ('dp', 'fsdp'))
- first_down_gradient: float32 [4, 2048, 512], P(None, ('dp', 'fsdp'))
- attend_gain_gradient: float32 [512], P(('dp', 'fsdp'))
- attend_bias_gradient: float32 [512], P(('dp', 'fsdp'))
- project_in_gradient: float32 [512, 1536], P(('dp', 'fsdp'))
- relative_weight_gradient: float32 [512, 512], P(('dp', 'fsdp'))
- content_bias_gradient: float32 [512], P(('dp', 'fsdp'))
- position_bias_gradient: float32 [512], P(('dp', 'fsdp'))
- attend_out_gradient: float32 [512, 512], P(('dp', 'fsdp'))
- depth_gain_gradient: float32 [512], P(('dp', 'fsdp'))
- depth_bias_gradient: float32 [512], P(('dp', 'fsdp'))
- gated_in_gradient: float32 [512, 1024], P(('dp', 'fsdp'))
- depth_kernel_gradient: float32 [15, 512], P(None, ('dp', 'fsdp'))
- batch_gain_gradient: float32 [512], P(('dp', 'fsdp'))
- batch_bias_gradient: float32 [512], P(('dp', 'fsdp'))
- point_out_gradient: float32 [512, 512], P(('dp', 'fsdp'))
- second_gain_gradient: float32 [512], P(('dp', 'fsdp'))
- second_bias_gradient: float32 [512], P(('dp', 'fsdp'))
- second_router_gradient: float32 [1024, 4], P(('dp', 'fsdp'))
- second_up_gradient: float32 [4, 512, 2048], P(None, ('dp', 'fsdp'))
- second_down_gradient: float32 [4, 2048, 512], P(None, ('dp', 'fsdp'))
- final_gain_gradient: float32 [512], P(('dp', 'fsdp'))
- final_bias_gradient: float32 [512], P(('dp', 'fsdp'))
Inputs may be any that keep to these rules, and one draw needn't show every extreme that they name: `segments`: in each row the numbers never fall and each utterance holds 1 to 512 frames. `routes_first`: at most 512 of one device's frames name the same expert, and this bound is reached. `routes_second`: at most 512 of one device's frames name the same expert, and this bound is reached.
All inputs are finite; a program needn't handle non-finite values.
Results may differ from a plain program's by a relative error of at most 0.039.
Values may be sent and summed in bfloat16 or wider, within the bound.
No kernel may reach another device: no remote copies, remote signals or barrier semaphores. Data moves between devices by JAX's collectives and lax.ppermute only.
A program may use at most 384 MiB of HBM per device.

v0:
```python
import jax
import jax.numpy as jnp
from jax import lax
from jax.sharding import PartitionSpec as P

HEADS = 8
EXPERTS = 4
KERNEL = 15
HEAD_DIM = 64
CAPACITY = 512


eps = 1e-05
blocked = -1000000000.0
highest = lax.Precision.HIGHEST


def layer_norm(value, gain, bias):
    average = jnp.mean(value, -1, keepdims=True)
    centered = value - average
    spread = jnp.mean(centered * centered, -1, keepdims=True)
    return centered * lax.rsqrt(spread + eps) * gain + bias


def swish(value):
    return value * jax.nn.sigmoid(value)


def swish_slope(value):
    sigma = jax.nn.sigmoid(value)
    return sigma * (1.0 + value * (1.0 - sigma))


def product(left, right):
    return jnp.dot(left, right, preferred_element_type=jnp.float32)


def across(left, right):
    return jnp.einsum("td,te->de", left, right, preferred_element_type=jnp.float32)


def against(left, right):
    return jnp.einsum("te,de->td", left, right, preferred_element_type=jnp.float32)


def position_table(length, width):
    steps = jnp.arange(2 * length - 1).astype(jnp.float32)
    distance = length - 1 - steps
    freqs = jnp.exp(jnp.arange(0, width, 2).astype(jnp.float32) * (-jnp.log(10000.0) / width))
    angle = distance[:, None] * freqs[None, :]
    return jnp.stack([jnp.sin(angle), jnp.cos(angle)], -1).reshape(2 * length - 1, width)


def shift_rows(wide, count, keys):
    heads = wide.shape[0]
    span = wide.shape[2]
    flat = wide.reshape(heads, count * span)
    flat = lax.slice_in_dim(flat, count - 1, count - 1 + count * (span - 1), axis=1)
    return flat.reshape(heads, count, span - 1)[:, :, :keys]


def unshift_rows(slope, span):
    heads, count, keys = slope.shape
    padded = jnp.pad(slope, ((0, 0), (0, 0), (0, span - 1 - keys)))
    flat = padded.reshape(heads, count * (span - 1))
    flat = jnp.pad(flat, ((0, 0), (count - 1, 1)))
    return flat.reshape(heads, count, span)


def depthwise(glu, segment, kernel):
    half = KERNEL // 2
    length = glu.shape[0]
    padded = jnp.pad(glu, ((half, half), (0, 0)))
    padded_seg = jnp.pad(segment, (half, half), constant_values=-1)
    total = jnp.zeros_like(glu)
    for index_tap in range(KERNEL):
        same = padded_seg[index_tap : index_tap + length] == segment
        total = total + kernel[index_tap] * jnp.where(
            same[:, None], padded[index_tap : index_tap + length], 0.0
        )
    return total


def gated_depth(joined, segment, kernel):
    width = joined.shape[1] // 2
    glu = joined[:, :width] * jax.nn.sigmoid(joined[:, width:])
    return depthwise(glu, segment, kernel)


def dispatch(route, capacity):
    length = route.shape[0]
    experts = jnp.arange(EXPERTS, dtype=jnp.int32)
    onehot = (route[:, None] == experts[None, :]).astype(jnp.int32)
    counts = jnp.sum(onehot, 0)
    starts = jnp.cumsum(counts) - counts
    order = jnp.argsort(route, stable=True)
    place = jnp.argsort(order, stable=True)
    slots = jnp.arange(capacity, dtype=jnp.int32)
    picked = jnp.minimum(starts[:, None] + slots[None, :], length - 1)
    sources = order[picked]
    valid = slots[None, :] < counts[:, None]
    own_start = jnp.sum(onehot * starts[None, :], 1)
    target = route * capacity + place - own_start
    return (onehot, sources, valid, target)


def expert_forward(resid, embedding, route, small, large):
    gain, bias, router = small
    width = resid.shape[1]
    normed = layer_norm(resid, gain.astype(jnp.float32), bias.astype(jnp.float32))
    low_normed = normed.astype(jnp.bfloat16)
    joined = jnp.concatenate([low_normed, embedding], 1)
    chances = jax.nn.softmax(product(joined, router), -1)
    onehot, sources, valid, target = dispatch(route, CAPACITY)
    chosen = onehot.astype(jnp.float32)
    gate = jnp.sum(chances * chosen, 1)
    buffer = low_normed[sources]
    up_full, down_full = (
        lax.all_gather(large[0], ("dp", "fsdp"), axis=1, tiled=True),
        lax.all_gather(large[1], ("dp", "fsdp"), axis=1, tiled=True),
    )
    inner = jnp.einsum("ecd,edf->ecf", buffer, up_full, preferred_element_type=jnp.float32)
    active = swish(inner).astype(jnp.bfloat16)
    outgoing = jnp.einsum("ecf,efd->ecd", active, down_full, preferred_element_type=jnp.float32)
    branch = outgoing.reshape(-1, width)[target]
    owned = (up_full, down_full)
    kept = (
        joined,
        chances,
        chosen,
        gate,
        sources,
        valid,
        target,
        buffer,
        inner,
        active,
        branch,
        owned,
    )
    return (resid + 0.5 * gate[:, None] * branch, kept)


def expert_backward(resid, slope, small, kept):
    gain, bias, router = small
    joined, chances, chosen, gate, sources, valid, target, held, inner, active, branch, owned = kept
    width = resid.shape[1]
    low_slope = (0.5 * gate[:, None] * slope).astype(jnp.bfloat16)
    gate_slope = 0.5 * jnp.sum(slope * branch, 1)
    logit_slope = chances * (chosen - gate[:, None]) * gate_slope[:, None]
    slot_slope = jnp.where(valid[:, :, None], low_slope[sources], jnp.zeros((), jnp.bfloat16))
    up_full, down_full = owned
    down_grad = jnp.einsum("ecf,ecd->efd", active, slot_slope, preferred_element_type=jnp.float32)
    active_slope = jnp.einsum(
        "ecd,efd->ecf", slot_slope, down_full, preferred_element_type=jnp.float32
    )
    inner_slope = (active_slope * swish_slope(inner)).astype(jnp.bfloat16)
    up_grad = jnp.einsum("ecd,ecf->edf", held, inner_slope, preferred_element_type=jnp.float32)
    slot_normed = jnp.einsum(
        "ecf,edf->ecd", inner_slope, up_full, preferred_element_type=jnp.float32
    )
    large_grads = (
        lax.psum_scatter(up_grad, ("dp", "fsdp"), scatter_dimension=1, tiled=True),
        lax.psum_scatter(down_grad, ("dp", "fsdp"), scatter_dimension=1, tiled=True),
    )
    router_float = router.astype(jnp.float32)
    normed_slope = slot_normed.reshape(-1, width)[target]
    normed_slope = normed_slope + jnp.dot(logit_slope, router_float[:width].T, precision=highest)
    router_grad = jnp.dot(joined.astype(jnp.float32).T, logit_slope, precision=highest)
    unused, norm_back = jax.vjp(
        layer_norm, resid, gain.astype(jnp.float32), bias.astype(jnp.float32)
    )
    resid_slope, gain_grad, bias_grad = norm_back(normed_slope)
    return (slope + resid_slope, (gain_grad, bias_grad, router_grad), large_grads)


def attention_inputs(resid, weights):
    gain, bias, project_in, relative_weight, content_bias, position_bias, attend_out = weights
    length, width = resid.shape
    normed = layer_norm(resid, gain.astype(jnp.float32), bias.astype(jnp.float32))
    low_normed = normed.astype(jnp.bfloat16)
    mixed = product(low_normed, project_in)
    query = mixed[:, :width].reshape(length, HEADS, HEAD_DIM)
    keys = mixed[:, width : 2 * width].reshape(length, HEADS, HEAD_DIM).astype(jnp.bfloat16)
    values = mixed[:, 2 * width :].reshape(length, HEADS, HEAD_DIM).astype(jnp.bfloat16)
    query_u = (query + content_bias.astype(jnp.float32).reshape(HEADS, HEAD_DIM)).astype(
        jnp.bfloat16
    )
    query_v = (query + position_bias.astype(jnp.float32).reshape(HEADS, HEAD_DIM)).astype(
        jnp.bfloat16
    )
    table = position_table(length, width).astype(jnp.bfloat16)
    relpos = (
        product(table, relative_weight)
        .astype(jnp.bfloat16)
        .reshape(2 * length - 1, HEADS, HEAD_DIM)
    )
    return (low_normed, query_u, query_v, keys, values, table, relpos)


def block_scores(offset, count, query_u, query_v, keys, relpos, segment):
    length = keys.shape[0]
    span = count + length - 1
    part_u = lax.slice_in_dim(query_u, offset, offset + count, axis=0)
    part_v = lax.slice_in_dim(query_v, offset, offset + count, axis=0)
    near = lax.slice_in_dim(relpos, length - count - offset, length - count - offset + span, axis=0)
    content = jnp.einsum("ihe,jhe->hij", part_u, keys, preferred_element_type=jnp.float32)
    wide = jnp.einsum("ihe,mhe->him", part_v, near, preferred_element_type=jnp.float32)
    scores = (content + shift_rows(wide, count, length)) * HEAD_DIM ** (-0.5)
    same = lax.slice_in_dim(segment, offset, offset + count, axis=0)[:, None] == segment[None, :]
    return (jnp.where(same[None], scores, blocked), part_u, part_v, near)


def attention_forward(resid, segment, weights):
    low_normed, query_u, query_v, keys, values, table, relpos = attention_inputs(resid, weights)
    length = resid.shape[0]
    count = min(512, length)
    contexts = []
    totals = []
    for offset in range(0, length, count):
        scores, part_u, part_v, near = block_scores(
            offset, count, query_u, query_v, keys, relpos, segment
        )
        peak = jnp.max(scores, -1, keepdims=True)
        raised = jnp.exp(scores - peak)
        summed = jnp.sum(raised, -1, keepdims=True)
        chances = (raised / summed).astype(jnp.bfloat16)
        block_context = jnp.einsum(
            "hij,jhe->ihe", chances, values, preferred_element_type=jnp.float32
        )
        contexts.append(block_context.reshape(count, -1))
        totals.append((peak + jnp.log(summed))[:, :, 0])
    context = jnp.concatenate(contexts, 0).astype(jnp.bfloat16)
    log_total = jnp.concatenate(totals, 1)
    return (resid + product(context, weights[6]), log_total, context)


def attention_backward(resid, segment, slope, weights, log_total, context):
    gain, bias, project_in, relative_weight, content_bias, position_bias, attend_out = weights
    low_normed, query_u, query_v, keys, values, table, relpos = attention_inputs(resid, weights)
    length, width = resid.shape
    count = min(512, length)
    scale = HEAD_DIM ** (-0.5)
    low_slope = slope.astype(jnp.bfloat16)
    out_grad = across(context, low_slope)
    context_slope = (
        against(low_slope, attend_out).astype(jnp.bfloat16).reshape(length, HEADS, HEAD_DIM)
    )
    keys_slope = jnp.zeros((length, HEADS, HEAD_DIM), jnp.float32)
    values_slope = jnp.zeros((length, HEADS, HEAD_DIM), jnp.float32)
    rel_slope = jnp.zeros((2 * length - 1, HEADS, HEAD_DIM), jnp.float32)
    pieces_u = []
    pieces_v = []
    for offset in range(0, length, count):
        scores, part_u, part_v, near = block_scores(
            offset, count, query_u, query_v, keys, relpos, segment
        )
        chances = jnp.exp(scores - log_total[:, offset : offset + count, None])
        part_slope = lax.slice_in_dim(context_slope, offset, offset + count, axis=0)
        chance_slope = jnp.einsum(
            "ihe,jhe->hij", part_slope, values, preferred_element_type=jnp.float32
        )
        values_slope = values_slope + jnp.einsum(
            "hij,ihe->jhe",
            chances.astype(jnp.bfloat16),
            part_slope,
            preferred_element_type=jnp.float32,
        )
        inner_sum = jnp.sum(chances * chance_slope, -1, keepdims=True)
        score_slope = (chances * (chance_slope - inner_sum) * scale).astype(jnp.bfloat16)
        pieces_u.append(
            jnp.einsum("hij,jhe->ihe", score_slope, keys, preferred_element_type=jnp.float32)
        )
        keys_slope = keys_slope + jnp.einsum(
            "hij,ihe->jhe", score_slope, part_u, preferred_element_type=jnp.float32
        )
        wide_slope = unshift_rows(score_slope, count + length - 1)
        pieces_v.append(
            jnp.einsum("him,mhe->ihe", wide_slope, near, preferred_element_type=jnp.float32)
        )
        start_row = length - count - offset
        rel_slope = rel_slope.at[start_row : start_row + count + length - 1].add(
            jnp.einsum("him,ihe->mhe", wide_slope, part_v, preferred_element_type=jnp.float32)
        )
    slope_u = jnp.concatenate(pieces_u, 0)
    slope_v = jnp.concatenate(pieces_v, 0)
    mixed_slope = jnp.concatenate(
        [
            (slope_u + slope_v).reshape(length, width),
            keys_slope.reshape(length, width),
            values_slope.reshape(length, width),
        ],
        1,
    ).astype(jnp.bfloat16)
    project_grad = across(low_normed, mixed_slope)
    normed_slope = against(mixed_slope, project_in)
    relative_grad = across(table, rel_slope.reshape(2 * length - 1, width).astype(jnp.bfloat16))
    unused, norm_back = jax.vjp(
        layer_norm, resid, gain.astype(jnp.float32), bias.astype(jnp.float32)
    )
    resid_slope, gain_grad, bias_grad = norm_back(normed_slope)
    grads = (
        gain_grad,
        bias_grad,
        project_grad,
        relative_grad,
        jnp.sum(slope_u, 0).reshape(width),
        jnp.sum(slope_v, 0).reshape(width),
        out_grad,
    )
    return (slope + resid_slope, grads)


def conv_front(resid, segment, weights):
    normed = layer_norm(resid, weights[0].astype(jnp.float32), weights[1].astype(jnp.float32))
    low_normed = normed.astype(jnp.bfloat16)
    joined = product(low_normed, weights[2])
    return (low_normed, joined, gated_depth(joined, segment, weights[3].astype(jnp.float32)))


def conv_backward(resid, segment, slope, weights, average, spread, frames):
    point_out = weights[6]
    batch_gain = weights[4].astype(jnp.float32)
    batch_bias = weights[5].astype(jnp.float32)
    low_normed, joined, depth = conv_front(resid, segment, weights)
    inverse = lax.rsqrt(spread + eps)
    centered = (depth - average) * inverse
    shifted = centered * batch_gain + batch_bias
    tail = swish(shifted).astype(jnp.bfloat16)
    low_slope = slope.astype(jnp.bfloat16)
    out_grad = across(tail, low_slope)
    shift_slope = against(low_slope, point_out) * swish_slope(shifted)
    bgain_grad = jnp.sum(shift_slope * centered, 0)
    bbias_grad = jnp.sum(shift_slope, 0)
    cent_slope = shift_slope * batch_gain
    first_sum, second_sum = lax.psum(
        (jnp.sum(cent_slope, 0), jnp.sum(cent_slope * centered, 0)), ("dp", "fsdp")
    )
    depth_slope = inverse * (cent_slope - first_sum / frames - centered * second_sum / frames)

    def local_depth(joined_in, kernel_in):
        return gated_depth(joined_in, segment, kernel_in)

    unused, depth_back = jax.vjp(local_depth, joined, weights[3].astype(jnp.float32))
    joined_slope, kernel_grad = depth_back(depth_slope)
    low_joined = joined_slope.astype(jnp.bfloat16)
    in_grad = across(low_normed, low_joined)
    normed_slope = against(low_joined, weights[2])
    unused_norm, norm_back = jax.vjp(
        layer_norm, resid, weights[0].astype(jnp.float32), weights[1].astype(jnp.float32)
    )
    resid_slope, gain_grad, bias_grad = norm_back(normed_slope)
    return (
        slope + resid_slope,
        (gain_grad, bias_grad, in_grad, kernel_grad, bgain_grad, bbias_grad, out_grad),
    )


def on_device(
    inputs,
    embedding,
    segments,
    routes_first,
    routes_second,
    cotangent,
    first_gain,
    first_bias,
    first_router,
    first_up,
    first_down,
    attend_gain,
    attend_bias,
    project_in,
    relative_weight,
    content_bias,
    position_bias,
    attend_out,
    depth_gain,
    depth_bias,
    gated_in,
    depth_kernel,
    batch_gain,
    batch_bias,
    point_out,
    second_gain,
    second_bias,
    second_router,
    second_up,
    second_down,
    final_gain,
    final_bias,
):
    segment = segments[0]
    first_route = routes_first[:, 0]
    second_route = routes_second[:, 0]
    frames = inputs.shape[0] * lax.axis_size(("dp", "fsdp"))
    smalls = (
        lax.all_gather(first_gain, ("dp", "fsdp"), axis=0, tiled=True),
        lax.all_gather(first_bias, ("dp", "fsdp"), axis=0, tiled=True),
        lax.all_gather(first_router, ("dp", "fsdp"), axis=0, tiled=True),
        lax.all_gather(second_gain, ("dp", "fsdp"), axis=0, tiled=True),
        lax.all_gather(second_bias, ("dp", "fsdp"), axis=0, tiled=True),
        lax.all_gather(second_router, ("dp", "fsdp"), axis=0, tiled=True),
    )
    first_small = (smalls[0], smalls[1], smalls[2])
    second_small = (smalls[3], smalls[4], smalls[5])
    attend_full = (
        lax.all_gather(attend_gain, ("dp", "fsdp"), axis=0, tiled=True),
        lax.all_gather(attend_bias, ("dp", "fsdp"), axis=0, tiled=True),
        lax.all_gather(project_in, ("dp", "fsdp"), axis=0, tiled=True),
        lax.all_gather(relative_weight, ("dp", "fsdp"), axis=0, tiled=True),
        lax.all_gather(content_bias, ("dp", "fsdp"), axis=0, tiled=True),
        lax.all_gather(position_bias, ("dp", "fsdp"), axis=0, tiled=True),
        lax.all_gather(attend_out, ("dp", "fsdp"), axis=0, tiled=True),
    )
    conv_full = (
        lax.all_gather(depth_gain, ("dp", "fsdp"), axis=0, tiled=True),
        lax.all_gather(depth_bias, ("dp", "fsdp"), axis=0, tiled=True),
        lax.all_gather(gated_in, ("dp", "fsdp"), axis=0, tiled=True),
        lax.all_gather(depth_kernel, ("dp", "fsdp"), axis=1, tiled=True),
        lax.all_gather(batch_gain, ("dp", "fsdp"), axis=0, tiled=True),
        lax.all_gather(batch_bias, ("dp", "fsdp"), axis=0, tiled=True),
        lax.all_gather(point_out, ("dp", "fsdp"), axis=0, tiled=True),
        lax.all_gather(final_gain, ("dp", "fsdp"), axis=0, tiled=True),
        lax.all_gather(final_bias, ("dp", "fsdp"), axis=0, tiled=True),
    )
    start_resid = inputs.astype(jnp.float32)
    first_resid, first_kept = expert_forward(
        start_resid, embedding, first_route, first_small, (first_up, first_down)
    )
    attend_resid, log_total, context = attention_forward(first_resid, segment, attend_full)
    low_normed, joined, depth = conv_front(attend_resid, segment, conv_full)
    first_sum, second_sum = lax.psum((jnp.sum(depth, 0), jnp.sum(depth * depth, 0)), ("dp", "fsdp"))
    average = first_sum / frames
    spread = second_sum / frames - average * average
    shifted = (depth - average) * lax.rsqrt(spread + eps) * conv_full[4].astype(
        jnp.float32
    ) + conv_full[5].astype(jnp.float32)
    tail = swish(shifted).astype(jnp.bfloat16)
    conv_resid = attend_resid + product(tail, conv_full[6])
    second_resid, second_kept = expert_forward(
        conv_resid, embedding, second_route, second_small, (second_up, second_down)
    )
    result, final_back = jax.vjp(
        layer_norm, second_resid, conv_full[7].astype(jnp.float32), conv_full[8].astype(jnp.float32)
    )
    slope, final_gain_grad, final_bias_grad = final_back(cotangent.astype(jnp.float32))
    slope, second_grads, second_large = expert_backward(
        conv_resid, slope, second_small, second_kept
    )
    slope, conv_grads = conv_backward(
        attend_resid, segment, slope, conv_full, average, spread, frames
    )
    slope, attend_grads = attention_backward(
        first_resid, segment, slope, attend_full, log_total, context
    )
    slope, first_grads, first_large = expert_backward(start_resid, slope, first_small, first_kept)
    shards = (
        lax.psum_scatter(attend_grads[0], ("dp", "fsdp"), scatter_dimension=0, tiled=True),
        lax.psum_scatter(attend_grads[1], ("dp", "fsdp"), scatter_dimension=0, tiled=True),
        lax.psum_scatter(attend_grads[2], ("dp", "fsdp"), scatter_dimension=0, tiled=True),
        lax.psum_scatter(attend_grads[3], ("dp", "fsdp"), scatter_dimension=0, tiled=True),
        lax.psum_scatter(attend_grads[4], ("dp", "fsdp"), scatter_dimension=0, tiled=True),
        lax.psum_scatter(attend_grads[5], ("dp", "fsdp"), scatter_dimension=0, tiled=True),
        lax.psum_scatter(attend_grads[6], ("dp", "fsdp"), scatter_dimension=0, tiled=True),
        lax.psum_scatter(conv_grads[0], ("dp", "fsdp"), scatter_dimension=0, tiled=True),
        lax.psum_scatter(conv_grads[1], ("dp", "fsdp"), scatter_dimension=0, tiled=True),
        lax.psum_scatter(conv_grads[2], ("dp", "fsdp"), scatter_dimension=0, tiled=True),
        lax.psum_scatter(conv_grads[3], ("dp", "fsdp"), scatter_dimension=1, tiled=True),
        lax.psum_scatter(conv_grads[4], ("dp", "fsdp"), scatter_dimension=0, tiled=True),
        lax.psum_scatter(conv_grads[5], ("dp", "fsdp"), scatter_dimension=0, tiled=True),
        lax.psum_scatter(conv_grads[6], ("dp", "fsdp"), scatter_dimension=0, tiled=True),
        lax.psum_scatter(final_gain_grad, ("dp", "fsdp"), scatter_dimension=0, tiled=True),
        lax.psum_scatter(final_bias_grad, ("dp", "fsdp"), scatter_dimension=0, tiled=True),
        lax.psum_scatter(first_grads[0], ("dp", "fsdp"), scatter_dimension=0, tiled=True),
        lax.psum_scatter(first_grads[1], ("dp", "fsdp"), scatter_dimension=0, tiled=True),
        lax.psum_scatter(first_grads[2], ("dp", "fsdp"), scatter_dimension=0, tiled=True),
        lax.psum_scatter(second_grads[0], ("dp", "fsdp"), scatter_dimension=0, tiled=True),
        lax.psum_scatter(second_grads[1], ("dp", "fsdp"), scatter_dimension=0, tiled=True),
        lax.psum_scatter(second_grads[2], ("dp", "fsdp"), scatter_dimension=0, tiled=True),
    )
    return (
        result.astype(jnp.bfloat16),
        slope,
        shards[16],
        shards[17],
        shards[18],
        first_large[0],
        first_large[1],
        shards[0],
        shards[1],
        shards[2],
        shards[3],
        shards[4],
        shards[5],
        shards[6],
        shards[7],
        shards[8],
        shards[9],
        shards[10],
        shards[11],
        shards[12],
        shards[13],
        shards[19],
        shards[20],
        shards[21],
        second_large[0],
        second_large[1],
        shards[14],
        shards[15],
    )


def solution(mesh):
    placed = (
        P(("dp", "fsdp"), None),
        P(("dp", "fsdp"), None),
        P(("dp", "fsdp"), None),
        P(("dp", "fsdp"), None),
        P(("dp", "fsdp"), None),
        P(("dp", "fsdp"), None),
        P(("dp", "fsdp")),
        P(("dp", "fsdp")),
        P(("dp", "fsdp"), None),
        P(None, ("dp", "fsdp"), None),
        P(None, ("dp", "fsdp"), None),
        P(("dp", "fsdp")),
        P(("dp", "fsdp")),
        P(("dp", "fsdp"), None),
        P(("dp", "fsdp"), None),
        P(("dp", "fsdp")),
        P(("dp", "fsdp")),
        P(("dp", "fsdp"), None),
        P(("dp", "fsdp")),
        P(("dp", "fsdp")),
        P(("dp", "fsdp"), None),
        P(None, ("dp", "fsdp")),
        P(("dp", "fsdp")),
        P(("dp", "fsdp")),
        P(("dp", "fsdp"), None),
        P(("dp", "fsdp")),
        P(("dp", "fsdp")),
        P(("dp", "fsdp"), None),
        P(None, ("dp", "fsdp"), None),
        P(None, ("dp", "fsdp"), None),
        P(("dp", "fsdp")),
        P(("dp", "fsdp")),
    )
    return jax.shard_map(
        on_device,
        mesh=mesh,
        in_specs=placed,
        out_specs=(
            P(("dp", "fsdp"), None),
            P(("dp", "fsdp"), None),
            P(("dp", "fsdp")),
            P(("dp", "fsdp")),
            P(("dp", "fsdp"), None),
            P(None, ("dp", "fsdp"), None),
            P(None, ("dp", "fsdp"), None),
            P(("dp", "fsdp")),
            P(("dp", "fsdp")),
            P(("dp", "fsdp"), None),
            P(("dp", "fsdp"), None),
            P(("dp", "fsdp")),
            P(("dp", "fsdp")),
            P(("dp", "fsdp"), None),
            P(("dp", "fsdp")),
            P(("dp", "fsdp")),
            P(("dp", "fsdp"), None),
            P(None, ("dp", "fsdp")),
            P(("dp", "fsdp")),
            P(("dp", "fsdp")),
            P(("dp", "fsdp"), None),
            P(("dp", "fsdp")),
            P(("dp", "fsdp")),
            P(("dp", "fsdp"), None),
            P(None, ("dp", "fsdp"), None),
            P(None, ("dp", "fsdp"), None),
            P(("dp", "fsdp")),
            P(("dp", "fsdp")),
        ),
        check_vma=False,
    )
```

profile of v0, /device:TPU:0, one launch (start us, length us, event | category | flops | bytes accessed | tf_op | source)
XLA Modules:
  0.0 3072.8 jit_solution(14626800628061342555)
XLA Ops:
  15.6 43.6 %all-gather.1 = bf16[32,32,4]{1,2,0:T(4,128)(2,1)S(1)} all-gather(bf16[1,32,4]{1,2,0:T(4,128)(2,1)} %bitcast.263), channel_id=1, replica_groups=mesh['dp'=8,'fsdp'=4] {'dp','fsdp'}, dimensions={0}, use_global_device_ids=true | all-gather | bytes 8448 | tf_op jit(solution)/shard_map/all_gather | solution.py:403
  71.2 37.6 %all-reduce.70 = (bf16[512]{0:T(512)(128)(2,1)S(1)}, bf16[512]{0:T(512)(128)(2,1)S(1)}, bf16[512]{0:T(512)(128)(2,1)S(1)}, bf16[512]{0:T(512)(128)(2,1)S(1)}, bf...) all-reduce(bf16[512]{0:T(512)(128)(2,1)S(1)} %dynamic-update-slice., ...), channel_id=1, replica_groups=mesh['dp'=8,'fsdp'=4] {'dp','fsdp'}, use_global_device_ids=true, to_apply=%add.43 | all-reduce | flops 7168 | bytes 28672
  152.7 40.1 %all-gather = bf16[32,32,4]{1,2,0:T(4,128)(2,1)S(1)} all-gather(bf16[1,32,4]{1,2,0:T(4,128)(2,1)S(1)} %bitcast.264), channel_id=1, replica_groups=mesh['dp'=8,'fsdp'=4] {'dp','fsdp'}, dimensions={0}, use_global_device_ids=true | all-gather | bytes 8448 | tf_op jit(solution)/shard_map/all_gather | solution.py:400
  194.9 37.0 %all_gather.90 = bf16[15,512]{0,1:T(8,128)(2,1)S(1)} all-gather(bf16[15,16]{0,1:T(8,128)(2,1)S(1)} %copy.156), channel_id=1, replica_groups=mesh['dp'=8,'fsdp'=4] {'dp','fsdp'}, dimensions={1}, use_global_device_ids=true | all-gather | bytes 15840 | tf_op jit(solution)/shard_map/all_gather | solution.py:420
  234.6 42.6 %all_gather.89 = bf16[512,512]{1,0:T(8,128)(2,1)} all-gather(bf16[16,512]{1,0:T(8,128)(2,1)S(1)} %copy-done.141), channel_id=1, replica_groups=mesh['dp'=8,'fsdp'=4] {'dp','fsdp'}, dimensions={0}, use_global_device_ids=true | all-gather | bytes 540672 | tf_op jit(solution)/shard_map/all_gather | solution.py:414
  277.2 41.1 %all_gather.96 = bf16[512,512]{1,0:T(8,128)(2,1)} all-gather(bf16[16,512]{1,0:T(8,128)(2,1)S(1)} %copy-done.142), channel_id=1, replica_groups=mesh['dp'=8,'fsdp'=4] {'dp','fsdp'}, dimensions={0}, use_global_device_ids=true | all-gather | bytes 540672 | tf_op jit(solution)/shard_map/all_gather | solution.py:423
  318.4 43.7 %all_gather.88 = bf16[512,512]{1,0:T(8,128)(2,1)} all-gather(bf16[16,512]{1,0:T(8,128)(2,1)S(1)} %copy-done.143), channel_id=1, replica_groups=mesh['dp'=8,'fsdp'=4] {'dp','fsdp'}, dimensions={0}, use_global_device_ids=true | all-gather | bytes 540672 | tf_op jit(solution)/shard_map/all_gather | solution.py:411
  370.3 60.3 %multiply_sine_fusion = (bf16[2047,256,1]{0,2,1:T(2,128)(2,1)S(1)}, bf16[2047,256,1]{0,2,1:T(2,128)(2,1)S(1)}) fusion(f32[2047]{0:T(1024)S(1)} %convert_subtract_fusion.1, f32[256]{0:T(256)S(1)} %multiply_exponential_fusion), kind=kLoop, calls=%fused_computation.78 | loop fusion | flops 1572096 | bytes 2105340 | tf_op jit(solution)/shard_map/sin | solution.py:51
  457.0 14.7 multiply_convert_fusion.5
  520.3 37.9 %reshape.1071 = f32[6287360]{0:T(1024)} reshape(f32[8,512,1535]{2,1,0:T(8,128)} %fusion.69) | data formatting | bytes 50298880
  558.2 23.8 reshape.893
  582.0 19.4 slice.467
  601.4 20.1 reshape.1073
  621.5 24.2 reshape.894
  674.2 38.1 %reshape.1075 = f32[6287360]{0:T(1024)} reshape(f32[8,512,1535]{2,1,0:T(8,128)} %fusion.74) | data formatting | bytes 50298880
  712.4 23.8 reshape.890
  736.2 19.3 slice.462
  755.5 20.1 reshape.1077
  775.6 24.2 reshape.891
  799.9 13.8 fusion.179
  849.0 36.8 %all-reduce.69 = (f32[512]{0:T(512)S(1)}, f32[512]{0:T(512)S(1)}) all-reduce(f32[512]{0:T(512)S(1)} %get-tuple-element.211, f32[512]{0:T(512)S(1)} %get-tuple-element.210), channel_id=1, replica_groups=mesh['dp'=8,'fsdp'=4] {'dp','fsdp'}, use_global_device_ids=true, to_apply=%region_21.22 | all-reduce | flops 1024 | bytes 8192 | tf_op jit(solution)/shard_map/psum | solution.py:433
  904.6 14.3 multiply_convert_fusion.4
  963.3 15.9 multiply_convert_fusion.3
  1013.9 41.6 %all-reduce.68 = (f32[512]{0:T(512)S(1)}, f32[512]{0:T(512)S(1)}) all-reduce(f32[512]{0:T(512)S(1)} %get-tuple-element.177, f32[512]{0:T(512)S(1)} %get-tuple-element.201), channel_id=1, replica_groups=mesh['dp'=8,'fsdp'=4] {'dp','fsdp'}, use_global_device_ids=true, to_apply=%region_42.43 | all-reduce | flops 1024 | bytes 8192 | tf_op jit(solution)/shard_map/psum | solution.py:336
  1092.5 20.1 multiply_convert_fusion.1
  1112.6 19.7 multiply_convert_fusion.2
  1172.9 21.5 reshape.1079
  1194.4 14.4 reshape.902
  1220.7 28.1 reshape.1081
  1248.8 24.1 reshape.903
  1291.0 21.6 reshape.1083
  1312.6 14.3 reshape.900
  1338.7 28.1 reshape.1085
  1366.8 24.1 reshape.901
  1437.9 18.2 scatter-add.9
  1524.4 17.9 multiply_convert_fusion
  1542.2 14.3 fusion.187
  1584.0 39.9 %all-reduce.67 = (f32[512]{0:T(512)S(1)}, f32[512]{0:T(512)S(1)}, f32[512]{0:T(512)S(1)}, f32[512]{0:T(512)S(1)}, f32[512]{0:T(512)S(1)}, /*index=5*/f32[512]{0:...) all-reduce(f32[512]{0:T(512)S(1)} %get-tuple-element.197, ...), channel_id=2, replica_groups=mesh['dp'=8,'fsdp'=4] {'dp','fsdp'}, use_global_device_ids=true, to_apply=%region_53.54.clone | all-reduce | flops 7168 | bytes 57344
  1641.2 36.8 %reduce-scatter.39.cloned.1.call-done = f32[16,15]{1,0:T(8,128)} async-done(((f32[512,15]{1,0:T(8,128)}), f32[16,15]{1,0:T(8,128)}) %reduce-scatter.39.cloned.1.call-update) | async-done | bytes 976
  1679.4 132.1 %reduce-scatter.31.cloned.1.call-done = f32[16,512]{1,0:T(8,128)} async-done(((f32[512,512]{1,0:T(8,128)}), f32[16,512]{1,0:T(8,128)}) %reduce-scatter.31.cloned.1.call-update) | async-done | bytes 32784 | tf_op jit(solution)/shard_map/reduce_scatter | solution.py:472
  1811.5 133.6 %reduce-scatter.27.cloned.1.call-done = f32[16,512]{1,0:T(8,128)} async-done(((f32[512,512]{1,0:T(8,128)}), f32[16,512]{1,0:T(8,128)}) %reduce-scatter.27.cloned.1.call-update) | async-done | bytes 32784 | tf_op jit(solution)/shard_map/reduce_scatter | solution.py:465
  1945.1 133.5 %reduce-scatter.25.cloned.1.call-done = f32[16,512]{1,0:T(8,128)} async-done(((f32[512,512]{1,0:T(8,128)}), f32[16,512]{1,0:T(8,128)}) %reduce-scatter.25.cloned.1.call-update) | async-done | bytes 32784 | tf_op jit(solution)/shard_map/reduce_scatter | solution.py:462
  2078.6 135.5 %reduce-scatter.29.cloned.1.call-done = f32[16,1024]{1,0:T(8,128)} async-done(((f32[512,1024]{1,0:T(8,128)}), f32[16,1024]{1,0:T(8,128)}) %reduce-scatter.29.cloned.1.call-update) | async-done | bytes 65552 | tf_op jit(solution)/shard_map/reduce_scatter | solution.py:468
  2214.1 104.2 %reduce-scatter.23.cloned.1.call-done = f32[16,1536]{1,0:T(8,128)} async-done(((f32[512,1536]{1,0:T(8,128)}), f32[16,1536]{1,0:T(8,128)}) %reduce-scatter.23.cloned.1.call-update) | async-done | bytes 98320 | tf_op jit(solution)/shard_map/reduce_scatter | solution.py:461
  2318.4 184.6 %reduce-scatter.35.cloned.1.call-done = f32[4,64,512]{2,1,0:T(8,128)} async-done(((f32[4,2048,512]{2,1,0:T(8,128)}), f32[4,64,512]{2,1,0:T(8,128)}) %reduce-scatter.35.cloned.1.call-update) | async-done | bytes 524304 | tf_op jit(solution)/shard_map/reduce_scatter | solution.py:164
  2503.0 187.4 %reduce-scatter.33.cloned.1.call-done = f32[4,16,2048]{2,1,0:T(8,128)} async-done(((f32[4,512,2048]{2,1,0:T(8,128)}), f32[4,16,2048]{2,1,0:T(8,128)}) %reduce-scatter.33.cloned.1.call-update) | async-done | bytes 524304 | tf_op jit(solution)/shard_map/reduce_scatter | solution.py:163
  2690.4 188.0 %reduce-scatter.21.cloned.1.call-done = f32[4,64,512]{2,1,0:T(8,128)} async-done(((f32[4,2048,512]{2,1,0:T(8,128)}), f32[4,64,512]{2,1,0:T(8,128)}) %reduce-scatter.21.cloned.1.call-update) | async-done | bytes 524304 | tf_op jit(solution)/shard_map/reduce_scatter | solution.py:164
  2878.4 187.3 %reduce-scatter.19.cloned.1.call-done = f32[4,16,2048]{2,1,0:T(8,128)} async-done(((f32[4,512,2048]{2,1,0:T(8,128)}), f32[4,16,2048]{2,1,0:T(8,128)}) %reduce-scatter.19.cloned.1.call-update) | async-done | bytes 524304 | tf_op jit(solution)/shard_map/reduce_scatter | solution.py:163
  (740 shorter events, 591.8 us)
Async XLA Ops:
  7.2 449.8 %all-gather.9.cloned.1.call-start = ((), (), s32[]{:S(2)}) async-start(), calls=%async_computation.12 | async-start | bytes 8650752 | tf_op jit(solution)/shard_map/all_gather | solution.py:119
  7.9 463.8 %all-gather.11.cloned.1.call-start = ((), (), s32[]{:S(2)}) async-start(), calls=%async_computation.13 | async-start | bytes 8650752 | tf_op jit(solution)/shard_map/all_gather | solution.py:120
  8.7 485.6 %all-gather.13.cloned.1.call-start = ((), (), s32[]{:S(2)}) async-start(), calls=%async_computation.14 | async-start | bytes 1622016 | tf_op jit(solution)/shard_map/all_gather | solution.py:410
  9.4 826.6 %all-gather.15.cloned.1.call-start = ((), (), s32[]{:S(2)}) async-start(), calls=%async_computation.15 | async-start | bytes 1081344 | tf_op jit(solution)/shard_map/all_gather | solution.py:419
  10.0 894.6 %all-gather.17.cloned.1.call-start = ((), (), s32[]{:S(2)}) async-start(), calls=%async_computation.16 | async-start | bytes 8650752 | tf_op jit(solution)/shard_map/all_gather | solution.py:119
  10.6 908.3 %all-gather.19.cloned.1.call-start = ((), (), s32[]{:S(2)}) async-start(), calls=%async_computation.17 | async-start | bytes 8650752 | tf_op jit(solution)/shard_map/all_gather | solution.py:120
  11.2 1627.3 %reduce-scatter.41.cloned.1.call-start = ((), (), s32[]{:S(2)}) async-start(), calls=%async_computation.29 | async-start | bytes 540672
  14.5 100.6 %copy-start.197 = (s32[4]{0:T(128)}, s32[4]{0:T(128)S(1)}, u32[]{:S(2)}) copy-start(s32[4]{0:T(128)S(1)} %convert_reduce_fusion.3) | copy-start | bytes 52
  59.2 79.0 %copy-start.71 = (bf16[32,32,4]{1,2,0:T(4,128)(2,1)}, bf16[32,32,4]{1,2,0:T(4,128)(2,1)S(1)}, u32[]{:S(2)}) copy-start(bf16[32,32,4]{1,2,0:T(4,128)(2,1)S(1)} %all-gather.1) | copy-start | bytes 24580
  108.8 385.5 %copy-start.92 = (f32[512]{0:T(512)}, f32[512]{0:T(512)S(1)}, u32[]{:S(2)}) copy-start(f32[512]{0:T(512)S(1)} %convert_element_type.228) | copy-start | bytes 6148
  108.8 255.8 %copy-start.95 = (f32[512]{0:T(512)}, f32[512]{0:T(512)S(1)}, u32[]{:S(2)}) copy-start(f32[512]{0:T(512)S(1)} %convert_element_type.222) | copy-start | bytes 6148
  111.7 382.6 %copy-start.136 = (f32[512]{0:T(512)}, f32[512]{0:T(512)S(1)}, u32[]{:S(2)}) copy-start(f32[512]{0:T(512)S(1)} %convert_element_type.229) | copy-start | bytes 6148
  143.3 51.0 %slice-start.11 = ((bf16[32,32,4]{1,2,0:T(4,128)(2,1)}), bf16[16,32,4]{1,2,0:T(4,128)(2,1)S(1)}, s32[]{:S(2)}) async-start(bf16[32,32,4]{1,2,0:T(4,128)(2,1)} %copy-done.71), calls=%async_computation.41 | async-start | bytes 32768 | tf_op jit(solution)/shard_map/slice | solution.py:168
  151.9 295.9 %copy-start.85 = (s32[2048]{0:T(1024)}, s32[2048]{0:T(1024)S(1)}, u32[]{:S(2)}) copy-start(s32[2048]{0:T(1024)S(1)} %broadcast_clamp_fusion.3) | copy-start | bytes 24580
  231.9 45.3 %copy-start.142 = (bf16[16,512]{1,0:T(8,128)(2,1)S(1)}, bf16[16,512]{1,0:T(8,128)(2,1)}, u32[]{:S(2)}) copy-start(bf16[16,512]{1,0:T(8,128)(2,1)} %param.60) | copy-start | bytes 49156
  231.9 86.5 %copy-start.143 = (bf16[16,512]{1,0:T(8,128)(2,1)S(1)}, bf16[16,512]{1,0:T(8,128)(2,1)}, u32[]{:S(2)}) copy-start(bf16[16,512]{1,0:T(8,128)(2,1)} %param.50) | copy-start | bytes 49156
  231.9 130.1 %copy-start.56 = (bf16[1024,512]{1,0:T(8,128)(2,1)S(1)}, bf16[1024,512]{1,0:T(8,128)(2,1)}, u32[]{:S(2)}) copy-start(bf16[1024,512]{1,0:T(8,128)(2,1)} %param.36) | copy-start | bytes 3145732
  362.6 129.4 %copy-start.5 = (bf16[1024,512]{0,1:T(8,128)(2,1)}, bf16[1024,512]{0,1:T(8,128)(2,1)S(1)}, u32[]{:S(2)}) copy-start(bf16[1024,512]{0,1:T(8,128)(2,1)S(1)} %copy.148) | copy-start | bytes 3145732
  368.0 62.7 %copy-start.119 = (f32[1024]{0:T(1024)}, f32[1024]{0:T(1024)S(1)}, u32[]{:S(2)}) copy-start(f32[1024]{0:T(1024)S(1)} %fusion.93) | copy-start | bytes 12292
  368.0 62.6 %copy-start.115 = (f32[1024]{0:T(1024)}, f32[1024]{0:T(1024)S(1)}, u32[]{:S(2)}) copy-start(f32[1024]{0:T(1024)S(1)} %fusion.86) | copy-start | bytes 12292
  368.0 123.9 %copy-start.100 = (f32[1024]{0:T(1024)}, f32[1024]{0:T(1024)S(1)}, u32[]{:S(2)}) copy-start(f32[1024]{0:T(1024)S(1)} %broadcast_multiply_fusion.4) | copy-start | bytes 12292
  445.6 38.3 %copy-start.102 = (s32[1024]{0:T(1024)}, s32[1024]{0:T(1024)S(1)}, u32[]{:S(2)}) copy-start(s32[1024]{0:T(1024)S(1)} %fusion.116) | copy-start | bytes 12292
  502.6 297.3 %copy-start.11 = (bf16[1024,512]{0,1:T(8,128)(2,1)}, bf16[1024,512]{0,1:T(8,128)(2,1)S(1)}, u32[]{:S(2)}) copy-start(bf16[1024,512]{0,1:T(8,128)(2,1)S(1)} %copy.155) | copy-start | bytes 3145732
  621.5 24.2 copy-start.17
  775.6 24.2 copy-start.34
  775.6 24.2 copy-start.47
  799.8 22.6 slice-start
  799.9 22.6 slice-start.1
  841.3 44.5 %copy-start.65 = (bf16[512,512]{1,0:T(8,128)(2,1)S(1)}, bf16[512,512]{1,0:T(8,128)(2,1)}, u32[]{:S(2)}) copy-start(bf16[512,512]{1,0:T(8,128)(2,1)} %all_gather.96) | copy-start | bytes 1572868
  841.3 44.5 %copy-start.184 = (f32[512]{0:T(512)S(1)}, f32[512]{0:T(512)}, u32[]{:S(2)}) copy-start(f32[512]{0:T(512)} %convert_element_type.246) | copy-start | bytes 6148
  841.3 44.5 %copy-start.201 = (f32[512]{0:T(512)S(1)}, f32[512]{0:T(512)}, u32[]{:S(2)}) copy-start(f32[512]{0:T(512)} %convert_element_type.247) | copy-start | bytes 6148
  885.8 169.7 %copy-start.187 = (f32[512]{0:T(512)}, f32[512]{0:T(512)S(1)}, u32[]{:S(2)}) copy-start(f32[512]{0:T(512)S(1)} %get-tuple-element.320) | copy-start | bytes 6148
  885.8 169.7 %copy-start.189 = (f32[512]{0:T(512)}, f32[512]{0:T(512)S(1)}, u32[]{:S(2)}) copy-start(f32[512]{0:T(512)S(1)} %get-tuple-element.321) | copy-start | bytes 6148
  1010.0 45.5 %copy-start.10 = (f32[1024,512]{1,0:T(8,128)S(1)}, f32[1024,512]{1,0:T(8,128)}, u32[]{:S(2)}) copy-start(f32[1024,512]{1,0:T(8,128)} %copy-done.9) | copy-start | bytes 6291460
  1087.8 24.8 copy-start.51
  1141.7 498.1 %reduce-scatter.37.cloned.1.call-start = ((), (), s32[]{:S(2)}) async-start(), calls=%async_computation.27 | async-start | bytes 540672
  1248.8 24.1 copy-start.20
  1366.8 24.1 copy-start.18
  1412.3 265.8 %reduce-scatter.39.cloned.1.call-start = ((), (), s32[]{:S(2)}) async-start(), calls=%async_computation.28 | async-start | bytes 270336
  1413.4 398.1 %reduce-scatter.31.cloned.1.call-start = ((), (), s32[]{:S(2)}) async-start(), calls=%async_computation.24 | async-start | bytes 1081344 | tf_op jit(solution)/shard_map/reduce_scatter | solution.py:472
  1417.7 527.3 %reduce-scatter.27.cloned.1.call-start = ((), (), s32[]{:S(2)}) async-start(), calls=%async_computation.22 | async-start | bytes 1081344 | tf_op jit(solution)/shard_map/reduce_scatter | solution.py:465
  1421.2 657.4 %reduce-scatter.25.cloned.1.call-start = ((), (), s32[]{:S(2)}) async-start(), calls=%async_computation.21 | async-start | bytes 1081344 | tf_op jit(solution)/shard_map/reduce_scatter | solution.py:462
  1460.6 753.5 %reduce-scatter.29.cloned.1.call-start = ((), (), s32[]{:S(2)}) async-start(), calls=%async_computation.23 | async-start | bytes 2162688 | tf_op jit(solution)/shard_map/reduce_scatter | solution.py:468
  1466.2 852.1 %reduce-scatter.23.cloned.1.call-start = ((), (), s32[]{:S(2)}) async-start(), calls=%async_computation.20 | async-start | bytes 3244032 | tf_op jit(solution)/shard_map/reduce_scatter | solution.py:461
  1472.6 1030.4 %reduce-scatter.35.cloned.1.call-start = ((), (), s32[]{:S(2)}) async-start(), calls=%async_computation.26 | async-start | bytes 17301504 | tf_op jit(solution)/shard_map/reduce_scatter | solution.py:164
  1487.6 1202.8 %reduce-scatter.33.cloned.1.call-start = ((), (), s32[]{:S(2)}) async-start(), calls=%async_computation.25 | async-start | bytes 17301504 | tf_op jit(solution)/shard_map/reduce_scatter | solution.py:163
  1500.8 1377.6 %reduce-scatter.21.cloned.1.call-start = ((), (), s32[]{:S(2)}) async-start(), calls=%async_computation.19 | async-start | bytes 17301504 | tf_op jit(solution)/shard_map/reduce_scatter | solution.py:164
  1524.1 1541.6 %reduce-scatter.19.cloned.1.call-start = ((), (), s32[]{:S(2)}) async-start(), calls=%async_computation.18 | async-start | bytes 17301504 | tf_op jit(solution)/shard_map/reduce_scatter | solution.py:163
  (187 other events, 686.8 us)
Sparse Core Ops, SparseCore 0:
  10.9 81.0 all-gather.8
  95.0 78.7 all-gather.10
  176.6 53.7 all-gather.12
  233.1 53.4 all-gather.14
  289.3 78.1 all-gather.16
  370.2 77.0 all-gather.18
  1141.8 133.7 reduce-scatter.40
  1412.4 133.8 reduce-scatter.36
  1548.5 129.4 reduce-scatter.38
  1680.8 130.6 reduce-scatter.30
  1814.3 130.7 reduce-scatter.26
  1947.8 130.7 reduce-scatter.24
  2081.4 132.6 reduce-scatter.28
  2220.9 97.4 reduce-scatter.22
  2321.2 181.7 reduce-scatter.34
  2505.8 184.4 reduce-scatter.32
  2693.2 185.1 reduce-scatter.20
  2881.2 184.4 reduce-scatter.18
where the time goes:
time: 3090 us; the launch traced here: 3070 us
  waiting for transfers between devices  1430 us (46%)
  local copies, waits for them, and re-layouts  657 us (21%)
  blocking collectives  404 us (13%)
  matrix products  394 us (13%)
  other arithmetic  172 us (6%)
    reduce_scatter x2, waiting for transfers between devices, expert_backward(): lax.psum_scatter(up_grad, ('dp', 'fsdp'), scatter_dimension=1, tiled=True)  375 us
    reduce_scatter x2, waiting for transfers between devices, expert_backward(): lax.psum_scatter(down_grad, ('dp', 'fsdp'), scatter_dimension=1, tiled=True)  373 us
    unnamed x496, local copies, waits for them, and re-layouts  272 us
    reduce_scatter x1, waiting for transfers between devices, on_device(): lax.psum_scatter(conv_grads[2], ('dp', 'fsdp'), scatter_dimension=0, tile...  136 us
    reduce_scatter x1, waiting for transfers between devices, on_device(): lax.psum_scatter(attend_grads[6], ('dp', 'fsdp'), scatter_dimension=0, ti...  134 us
    reduce_scatter x1, waiting for transfers between devices, on_device(): lax.psum_scatter(attend_grads[3], ('dp', 'fsdp'), scatter_dimension=0, ti...  134 us
    reduce_scatter x1, waiting for transfers between devices, on_device(): lax.psum_scatter(conv_grads[6], ('dp', 'fsdp'), scatter_dimension=0, tile...  132 us
    reduce_scatter x1, waiting for transfers between devices, on_device(): lax.psum_scatter(attend_grads[2], ('dp', 'fsdp'), scatter_dimension=0, ti...  104 us
  transfers between devices with their start and end apart: 18, of which 10 were waited for; matrix products, arithmetic and copies ran while one was open for 33% of the time, Pallas kernels for 0%

commit v1 on v0

v1 whole, which is shorter than its diff:
```python
import functools

import jax
import jax.numpy as jnp
from jax import lax
from jax.experimental import pallas as pl
from jax.experimental.pallas import tpu as pltpu
from jax.sharding import PartitionSpec as P

HEADS = 8
EXPERTS = 4
KERNEL = 15
HEAD_DIM = 64
CAPACITY = 512
AXES = ("dp", "fsdp")

eps = 1e-05
blocked = -1000000000.0


def product(left, right):
    return jnp.dot(left, right, preferred_element_type=jnp.float32)


NN = (((1,), (0,)), ((), ()))
NT = (((1,), (1,)), ((), ()))
TN = (((0,), (0,)), ((), ()))


def mul(left, right, dims=NN):
    return lax.dot_general(left, right, dims, preferred_element_type=jnp.float32)


def norm_parts(value):
    average = jnp.mean(value, -1, keepdims=True)
    centered = value - average
    spread = jnp.mean(centered * centered, -1, keepdims=True)
    inverse = lax.rsqrt(spread + eps)
    return centered * inverse, inverse


def norm_slope(unit, inverse, slope, gain):
    scaled = slope * gain
    first = jnp.mean(scaled, -1, keepdims=True)
    second = jnp.mean(scaled * unit, -1, keepdims=True)
    return (scaled - first - unit * second) * inverse


def head_mask(rows, head):
    lane = lax.broadcasted_iota(jnp.int32, (rows, 2 * HEAD_DIM), 1)
    return (lane >= head * HEAD_DIM) & (lane < (head + 1) * HEAD_DIM)


def angles(length, width):
    freqs = jnp.exp(jnp.arange(0, width, 2).astype(jnp.float32) * (-jnp.log(10000.0) / width))
    coarse = (jnp.arange(length // 32) * 32).astype(jnp.float32)[:, None] * freqs[None, :]
    fine = jnp.arange(32).astype(jnp.float32)[:, None] * freqs[None, :]
    cos_a, sin_a = jnp.cos(coarse)[:, None], jnp.sin(coarse)[:, None]
    cos_b, sin_b = jnp.cos(fine)[None], jnp.sin(fine)[None]
    cosine = (cos_a * cos_b - sin_a * sin_b).reshape(length, width // 2)
    sine = (sin_a * cos_b + cos_a * sin_b).reshape(length, width // 2)
    return cosine, sine


def attend_forward_kernel(
    resid_ref,
    gain_ref,
    bias_ref,
    pq_ref,
    pk_ref,
    pv_ref,
    rel_ref,
    cb_ref,
    pb_ref,
    segr_ref,
    segc_ref,
    tab_ref,
    cos_ref,
    sin_ref,
    ha_ref,
    qu_ref,
    qv_ref,
    k_ref,
    v_ref,
    p_ref,
    ctx_ref,
    kt_ref,
):
    length = resid_ref.shape[0]
    half = cos_ref.shape[1]
    pair = 2 * HEAD_DIM
    rows = 256

    @pl.when(pl.program_id(0) == 0)
    def first():
        unit, inverse = norm_parts(resid_ref[...])
        ha_ref[...] = (unit * gain_ref[...] + bias_ref[...]).astype(jnp.bfloat16)
        kt_ref[:, pair:] = tab_ref[...]

    normed = ha_ref[...]
    query = mul(normed, pq_ref[...])
    keys = mul(normed, pk_ref[...]).astype(jnp.bfloat16)
    k_ref[...] = keys
    kt_ref[:, :pair] = keys
    v_ref[...] = mul(normed, pv_ref[...]).astype(jnp.bfloat16)
    qu_ref[...] = (query + cb_ref[...]).astype(jnp.bfloat16)
    qv_ref[...] = (query + pb_ref[...]).astype(jnp.bfloat16)

    def block(index, carry):
        at = pl.ds(pl.multiple_of(index * rows, rows), rows)
        same = segc_ref[at, :] == segr_ref[...]
        cosine, sine = cos_ref[at, :], sin_ref[at, :]
        contexts = []
        for head in range(2):
            own = head_mask(rows, head)
            part_u = jnp.where(own, qu_ref[at, :], 0) * 0.125
            part_v = jnp.where(own, qv_ref[at, :], 0)
            coef = mul(part_v, rel_ref[...], NT) * 0.125
            left, right = coef[:, :half], coef[:, half:]
            turned_a = (left * sine + right * cosine).astype(jnp.bfloat16)
            turned_b = (right * sine - left * cosine).astype(jnp.bfloat16)
            scores = mul(
                jnp.concatenate([part_u.astype(jnp.bfloat16), turned_a, turned_b], 1), kt_ref[...], NT
            )
            scores = jnp.where(same, scores, blocked)
            peak = jnp.max(scores, -1, keepdims=True)
            raised = jnp.exp(scores - peak)
            summed = jnp.sum(raised, -1, keepdims=True)
            chances = (raised * (1.0 / summed)).astype(jnp.bfloat16)
            p_ref[head, at, :] = chances
            contexts.append(mul(chances, v_ref[...]))
        ctx_ref[at, :] = jnp.where(head_mask(rows, 0), contexts[0], contexts[1]).astype(jnp.bfloat16)
        return carry

    lax.fori_loop(0, length // rows, block, 0)


def attend_backward_kernel(
    p_ref,
    tab_ref,
    cos_ref,
    sin_ref,
    resid_ref,
    slope_ref,
    ha_ref,
    qu_ref,
    qv_ref,
    k_ref,
    v_ref,
    ctx_ref,
    ao_ref,
    pq_ref,
    pk_ref,
    pv_ref,
    rel_ref,
    gain_ref,
    g1_ref,
    dao_ref,
    dpq_ref,
    dpk_ref,
    dpv_ref,
    drel_ref,
    dcb_ref,
    dpb_ref,
    dgain_ref,
    dbias_ref,
    kt_ref,
    dout_ref,
    dctx_ref,
    dn_ref,
    dq_ref,
    dkt_ref,
    dvt_ref,
    drt_ref,
):
    length = resid_ref.shape[0]
    half = cos_ref.shape[1]
    pair = 2 * HEAD_DIM
    rows = 256
    step = pl.program_id(0)

    @pl.when(step == 0)
    def first():
        dout_ref[...] = slope_ref[...].astype(jnp.bfloat16)
        kt_ref[:, pair:] = tab_ref[...]
        dn_ref[...] = jnp.zeros_like(dn_ref)

    kt_ref[:, :pair] = k_ref[...]
    dao_ref[...] = mul(ctx_ref[...], dout_ref[...], TN)
    dctx_ref[...] = mul(dout_ref[...], ao_ref[...], NT).astype(jnp.bfloat16)
    dkt_ref[...] = jnp.zeros_like(dkt_ref)
    dvt_ref[...] = jnp.zeros_like(dvt_ref)
    drt_ref[...] = jnp.zeros_like(drt_ref)
    dcb_ref[...] = jnp.zeros_like(dcb_ref)
    dpb_ref[...] = jnp.zeros_like(dpb_ref)

    def block(index, carry):
        at = pl.ds(pl.multiple_of(index * rows, rows), rows)
        cosine, sine = cos_ref[at, :], sin_ref[at, :]
        total = jnp.zeros((rows, pair), jnp.float32)
        sum_u = jnp.zeros((1, pair), jnp.float32)
        sum_v = jnp.zeros((1, pair), jnp.float32)
        for head in range(2):
            own = head_mask(rows, head)
            part = jnp.where(own, dctx_ref[at, :], 0)
            low = p_ref[head, at, :]
            chances = low.astype(jnp.float32)
            raw = mul(part, v_ref[...], NT)
            weighted = chances * raw
            delta = jnp.sum(weighted, -1, keepdims=True)
            slope = ((weighted - chances * delta) * 0.125).astype(jnp.bfloat16)
            dvt_ref[...] += mul(part, low, TN)
            dkt_ref[...] += mul(jnp.where(own, qu_ref[at, :], 0), slope, TN)
            wide = mul(slope, kt_ref[...])
            slope_u = jnp.where(own, wide[:, :pair], 0.0)
            first, second = wide[:, pair : pair + half], wide[:, pair + half :]
            coef = jnp.concatenate(
                [
                    (first * sine - second * cosine).astype(jnp.bfloat16),
                    (first * cosine + second * sine).astype(jnp.bfloat16),
                ],
                1,
            )
            slope_v = jnp.where(own, mul(coef, rel_ref[...]), 0.0)
            drt_ref[...] += mul(jnp.where(own, qv_ref[at, :], 0), coef, TN)
            total = total + slope_u + slope_v
            sum_u = sum_u + jnp.sum(slope_u, 0, keepdims=True)
            sum_v = sum_v + jnp.sum(slope_v, 0, keepdims=True)
        dq_ref[at, :] = total
        dcb_ref[...] += sum_u
        dpb_ref[...] += sum_v
        return carry

    lax.fori_loop(0, length // rows, block, 0)
    low_q = dq_ref[...].astype(jnp.bfloat16)
    low_k = dkt_ref[...].T.astype(jnp.bfloat16)
    low_v = dvt_ref[...].T.astype(jnp.bfloat16)
    drel_ref[...] = drt_ref[...].T
    normed = ha_ref[...]
    dpq_ref[...] = mul(normed, low_q, TN)
    dpk_ref[...] = mul(normed, low_k, TN)
    dpv_ref[...] = mul(normed, low_v, TN)
    dn_ref[...] += (
        mul(low_q, pq_ref[...], NT) + mul(low_k, pk_ref[...], NT) + mul(low_v, pv_ref[...], NT)
    )

    @pl.when(step == pl.num_programs(0) - 1)
    def last():
        unit, inverse = norm_parts(resid_ref[...])
        slope = dn_ref[...]
        dgain_ref[...] = jnp.sum(slope * unit, 0, keepdims=True)
        dbias_ref[...] = jnp.sum(slope, 0, keepdims=True)
        g1_ref[...] = slope_ref[...] + norm_slope(unit, inverse, slope, gain_ref[...])


def whole(shape):
    return pl.BlockSpec(shape, lambda p: (0,) * len(shape))


def columns(rows, width, shift=0):
    return pl.BlockSpec((rows, width), lambda p: (0, p + shift))


def attention_forward(resid, segments, weights, tables):
    gain, bias, project_in, relative, content_bias, position_bias, attend_out = weights
    table, cosine, sine = tables
    length, width = resid.shape
    pair = 2 * HEAD_DIM
    pairs = HEADS // 2
    low = jnp.bfloat16
    shape = jax.ShapeDtypeStruct
    return pl.pallas_call(
        attend_forward_kernel,
        grid=(pairs,),
        in_specs=[
            whole((length, width)),
            whole((1, width)),
            whole((1, width)),
            columns(width, pair),
            columns(width, pair, pairs),
            columns(width, pair, 2 * pairs),
            columns(width, pair),
            columns(1, pair),
            columns(1, pair),
            whole((1, length)),
            whole((length, 1)),
            whole((length, width)),
            whole((length, width // 2)),
            whole((length, width // 2)),
        ],
        out_specs=[whole((length, width))]
        + [columns(length, pair)] * 4
        + [pl.BlockSpec((2, length, length), lambda p: (p, 0, 0)), columns(length, pair)],
        out_shape=[shape((length, width), low)] * 5
        + [shape((HEADS, length, length), low), shape((length, width), low)],
        scratch_shapes=[pltpu.VMEM((length, pair + width), low)],
        compiler_params=pltpu.CompilerParams(vmem_limit_bytes=56 * 1024 * 1024),
        cost_estimate=pl.CostEstimate(flops=24 * 10**9, bytes_accessed=30 * 10**6, transcendentals=8 * 10**6),
        name="attend_forward",
    )(
        resid,
        gain,
        bias,
        project_in,
        project_in,
        project_in,
        relative,
        content_bias,
        position_bias,
        segments,
        segments.reshape(length, 1),
        table,
        cosine,
        sine,
    )


def attention_backward(resid, slope, weights, tables, kept):
    gain, bias, project_in, relative, content_bias, position_bias, attend_out = weights
    table, cosine, sine = tables
    normed, query_u, query_v, keys, values, chances, context = kept
    length, width = resid.shape
    pair = 2 * HEAD_DIM
    pairs = HEADS // 2
    low, full = jnp.bfloat16, jnp.float32
    shape = jax.ShapeDtypeStruct
    return pl.pallas_call(
        attend_backward_kernel,
        grid=(pairs,),
        in_specs=[
            pl.BlockSpec((2, length, length), lambda p: (p, 0, 0)),
            whole((length, width)),
            whole((length, width // 2)),
            whole((length, width // 2)),
            whole((length, width)),
            whole((length, width)),
            whole((length, width)),
        ]
        + [columns(length, pair)] * 5
        + [
            pl.BlockSpec((pair, width), lambda p: (p, 0)),
            columns(width, pair),
            columns(width, pair, pairs),
            columns(width, pair, 2 * pairs),
            columns(width, pair),
            whole((1, width)),
        ],
        out_specs=[
            whole((length, width)),
            pl.BlockSpec((pair, width), lambda p: (p, 0)),
            columns(width, pair),
            columns(width, pair),
            columns(width, pair),
            columns(width, pair),
            columns(1, pair),
            columns(1, pair),
            whole((1, width)),
            whole((1, width)),
        ],
        out_shape=[shape((length, width), full)]
        + [shape((width, width), full)] * 5
        + [shape((1, width), full)] * 4,
        scratch_shapes=[
            pltpu.VMEM((length, pair + width), low),
            pltpu.VMEM((length, width), low),
            pltpu.VMEM((length, pair), low),
            pltpu.VMEM((length, width), full),
            pltpu.VMEM((length, pair), full),
            pltpu.VMEM((pair, length), full),
            pltpu.VMEM((pair, length), full),
            pltpu.VMEM((pair, width), full),
        ],
        compiler_params=pltpu.CompilerParams(vmem_limit_bytes=60 * 1024 * 1024),
        cost_estimate=pl.CostEstimate(flops=40 * 10**9, bytes_accessed=40 * 10**6, transcendentals=0),
        name="attend_backward",
    )(
        chances,
        table,
        cosine,
        sine,
        resid,
        slope,
        normed,
        query_u,
        query_v,
        keys,
        values,
        context,
        attend_out,
        project_in,
        project_in,
        project_in,
        relative,
        gain,
    )


TILE = 256


def one_hot_rows(pos_row, base):
    slot = lax.broadcasted_iota(jnp.int32, (TILE, pos_row.shape[1]), 0) + base
    return (slot == pos_row).astype(jnp.float32).astype(jnp.bfloat16)


def one_hot_columns(pos_col, base):
    slot = lax.broadcasted_iota(jnp.int32, (pos_col.shape[0], TILE), 1) + base
    return (slot == pos_col).astype(jnp.float32).astype(jnp.bfloat16)


def routed(route_col):
    lane = lax.broadcasted_iota(jnp.int32, (route_col.shape[0], 128), 1)
    return (lane == route_col).astype(jnp.float32)


def sigmoid(value):
    return 1.0 / (1.0 + jnp.exp(-value))


def split_mul(wide, narrow, dims):
    high = wide.astype(jnp.bfloat16)
    rest = (wide - high.astype(jnp.float32)).astype(jnp.bfloat16)
    return mul(high, narrow, dims) + mul(rest, narrow, dims)


def route_probs(normed, embed, router_ref):
    width = normed.shape[1]
    logits = mul(normed, router_ref[:width, :]) + mul(embed, router_ref[width:, :])
    lane = lax.broadcasted_iota(jnp.int32, logits.shape, 1)
    logits = jnp.where(lane < EXPERTS, logits, -jnp.inf)
    raised = jnp.exp(logits - jnp.max(logits, -1, keepdims=True))
    return raised / jnp.sum(raised, -1, keepdims=True)


def expert_tile(index, normed, pos_row, up, down):
    base = index * TILE
    picked = mul(one_hot_rows(pos_row, base), normed).astype(jnp.bfloat16)
    total = None
    chunk = 512
    for start in range(0, up.shape[1], chunk):
        inner = mul(picked, up[:, start : start + chunk])
        active = (inner * sigmoid(inner)).astype(jnp.bfloat16)
        part = mul(active, down[start : start + chunk, :])
        total = part if total is None else total + part
    return total.astype(jnp.bfloat16)


def expert_forward_steps(counts_ref, normed_ref, posr_ref, posc_ref, up_ref, down_ref, branch_ref):
    expert = pl.program_id(0)
    width = normed_ref.shape[1]
    up = up_ref[...].reshape(width, -1)
    down = down_ref[...].reshape(-1, width)

    @pl.when(expert == 0)
    def clear():
        branch_ref[...] = jnp.zeros_like(branch_ref)

    for part in range(CAPACITY // TILE):

        @pl.when(counts_ref[expert] > part * TILE)
        def run():
            index = expert * (CAPACITY // TILE) + part
            outgoing = expert_tile(index, normed_ref[...], posr_ref[...], up, down)
            branch_ref[...] += mul(one_hot_columns(posc_ref[...], index * TILE), outgoing)


def first_forward_kernel(
    counts_ref, normed_ref, posr_ref, posc_ref, up_ref, down_ref, resid_ref, probs_ref, route_ref,
    out_ref, branch_ref,
):
    expert_forward_steps(counts_ref, normed_ref, posr_ref, posc_ref, up_ref, down_ref, branch_ref)

    @pl.when(pl.program_id(0) == pl.num_programs(0) - 1)
    def last():
        gate = jnp.sum(probs_ref[...] * routed(route_ref[...]), -1, keepdims=True)
        out_ref[...] = resid_ref[...].astype(jnp.float32) + 0.5 * gate * branch_ref[...]


def second_forward_kernel(
    counts_ref, normed_ref, posr_ref, posc_ref, up_ref, down_ref, resid_ref, probs_ref, route_ref,
    cot_ref, gain_ref, bias_ref,
    result_ref, g4_ref, dgain_ref, dbias_ref, branch_ref,
):
    expert_forward_steps(counts_ref, normed_ref, posr_ref, posc_ref, up_ref, down_ref, branch_ref)

    @pl.when(pl.program_id(0) == pl.num_programs(0) - 1)
    def last():
        gate = jnp.sum(probs_ref[...] * routed(route_ref[...]), -1, keepdims=True)
        unit, inverse = norm_parts(resid_ref[...] + 0.5 * gate * branch_ref[...])
        gain = gain_ref[...]
        cot = cot_ref[...].astype(jnp.float32)
        result_ref[...] = (unit * gain + bias_ref[...]).astype(jnp.bfloat16)
        dgain_ref[...] = jnp.sum(cot * unit, 0, keepdims=True)
        dbias_ref[...] = jnp.sum(cot, 0, keepdims=True)
        g4_ref[...] = norm_slope(unit, inverse, cot, gain)


def expert_backward_kernel(
    counts_ref, normed_ref, posr_ref, posc_ref, up_ref, down_ref, resid_ref, probs_ref, route_ref,
    branch_ref, slope_ref, embed_ref, router_ref, gain_ref,
    dup_ref, ddown_ref, out_ref, dgain_ref, dbias_ref, drouter_ref,
    low_ref, dlogits_ref, dnorm_ref, picked_ref, dpicked_ref, active_ref, dinner_ref,
):
    expert = pl.program_id(0)
    width = normed_ref.shape[1]
    up = up_ref[...].reshape(width, -1)
    down = down_ref[...].reshape(-1, width)
    hidden = up.shape[1]
    chunk = 512

    @pl.when(expert == 0)
    def first():
        chosen = routed(route_ref[...])
        probs = probs_ref[...]
        gate = jnp.sum(probs * chosen, -1, keepdims=True)
        slope = slope_ref[...]
        low_ref[...] = (0.5 * gate * slope).astype(jnp.bfloat16)
        dgate = 0.5 * jnp.sum(slope * branch_ref[...], -1, keepdims=True)
        dlogits = probs * (chosen - gate) * dgate
        dlogits_ref[...] = dlogits
        dnorm_ref[...] = split_mul(dlogits, router_ref[:width, :], NT)

    def tile(part):
        index = expert * (CAPACITY // TILE) + part
        at = slice(part * TILE, (part + 1) * TILE)
        hot = one_hot_rows(posr_ref[...], index * TILE)
        picked = mul(hot, normed_ref[...]).astype(jnp.bfloat16)
        dpicked = mul(hot, low_ref[...]).astype(jnp.bfloat16)
        picked_ref[at, :] = picked
        dpicked_ref[at, :] = dpicked
        total = None
        for start in range(0, hidden, chunk):
            span = slice(start, start + chunk)
            inner = mul(picked, up[:, span])
            sigma = sigmoid(inner)
            active_ref[at, span] = (inner * sigma).astype(jnp.bfloat16)
            dactive = mul(dpicked, down[span, :], NT)
            dinner = (dactive * (sigma * (1.0 + inner * (1.0 - sigma)))).astype(jnp.bfloat16)
            dinner_ref[at, span] = dinner
            part_sum = mul(dinner, up[:, span], NT)
            total = part_sum if total is None else total + part_sum
        dnorm_ref[...] += mul(one_hot_columns(posc_ref[...], index * TILE), total.astype(jnp.bfloat16))

    def weight_grads(rows):
        for start in range(0, hidden, chunk):
            span = slice(start, start + chunk)
            dup_ref[..., span] = (
                mul(picked_ref[:rows, :], dinner_ref[:rows, span], TN)
                .astype(jnp.bfloat16)
                .reshape(dup_ref.shape[:-1] + (chunk,))
            )
            grads = mul(active_ref[:rows, span], dpicked_ref[:rows, :], TN).astype(jnp.bfloat16)
            owned = ddown_ref.shape[2]
            if owned > chunk:
                ddown_ref[0, 0, span, :] = grads
            else:
                groups = slice(start // owned, (start + chunk) // owned)
                ddown_ref[groups] = grads.reshape((chunk // owned,) + ddown_ref.shape[1:])

    tile(0)
    count = counts_ref[expert]

    @pl.when(count <= TILE)
    def small():
        weight_grads(TILE)

    @pl.when(count > TILE)
    def large():
        tile(1)
        weight_grads(2 * TILE)

    @pl.when(expert == pl.num_programs(0) - 1)
    def last():
        unit, inverse = norm_parts(resid_ref[...].astype(jnp.float32))
        slope = dnorm_ref[...]
        dgain_ref[...] = jnp.sum(slope * unit, 0, keepdims=True)
        dbias_ref[...] = jnp.sum(slope, 0, keepdims=True)
        out_ref[...] = slope_ref[...] + norm_slope(unit, inverse, slope, gain_ref[...])
        dlogits = dlogits_ref[...]
        drouter_ref[:, :width] = split_mul(dlogits, normed_ref[...], TN)
        drouter_ref[:, width:] = split_mul(dlogits, embed_ref[...], TN)


def fixed(shape):
    return pl.BlockSpec(shape, lambda e, counts: (0,) * len(shape))


def expert_specs(length, width, up, down):
    return [
        fixed((length, width)),
        fixed((1, length)),
        fixed((length, 1)),
        pl.BlockSpec((up.shape[0], 1) + up.shape[2:], lambda e, counts: (0, e, 0, 0)),
        pl.BlockSpec((down.shape[0], 1) + down.shape[2:], lambda e, counts: (0, e, 0, 0)),
        fixed((length, width)),
        fixed((length, 128)),
        fixed((length, 1)),
    ]


def expert_call(kernel, name, extra_specs, out_specs, out_shape, scratch, flops, args):
    counts, normed, pos_row, pos_col, up, down = args[:6]
    length, width = normed.shape
    return pl.pallas_call(
        kernel,
        grid_spec=pltpu.PrefetchScalarGridSpec(
            num_scalar_prefetch=1,
            grid=(EXPERTS,),
            in_specs=expert_specs(length, width, up, down) + extra_specs,
            out_specs=out_specs,
            scratch_shapes=scratch,
        ),
        out_shape=out_shape,
        compiler_params=pltpu.CompilerParams(vmem_limit_bytes=60 * 1024 * 1024),
        cost_estimate=pl.CostEstimate(flops=flops, bytes_accessed=30 * 10**6, transcendentals=4 * 10**6),
        name=name,
    )(*args)


def first_forward(args):
    length, width = args[1].shape
    full = jnp.float32
    out = jax.ShapeDtypeStruct((length, width), full)
    return expert_call(
        first_forward_kernel,
        "first_forward",
        [],
        [fixed((length, width))] * 2,
        [out, out],
        [],
        10 * 10**9,
        args,
    )


def second_forward(args):
    length, width = args[1].shape
    full = jnp.float32
    wide = jax.ShapeDtypeStruct((length, width), full)
    thin = jax.ShapeDtypeStruct((1, width), full)
    return expert_call(
        second_forward_kernel,
        "second_forward",
        [fixed((length, width)), fixed((1, width)), fixed((1, width))],
        [fixed((length, width))] * 2 + [fixed((1, width))] * 2 + [fixed((length, width))],
        [jax.ShapeDtypeStruct((length, width), jnp.bfloat16), wide, thin, thin, wide],
        [],
        10 * 10**9,
        args,
    )


def expert_backward(args):
    length, width = args[1].shape
    up, down = args[4:6]
    hidden = up.shape[3]
    low, full = jnp.bfloat16, jnp.float32
    shape = jax.ShapeDtypeStruct
    thin = shape((1, width), full)
    return expert_call(
        expert_backward_kernel,
        "expert_backward",
        [
            fixed((length, width)),
            fixed((length, width)),
            fixed((length, width)),
            fixed((2 * width, 128)),
            fixed((1, width)),
        ],
        [
            pl.BlockSpec((up.shape[0], 1) + up.shape[2:], lambda e, counts: (0, e, 0, 0)),
            pl.BlockSpec((down.shape[0], 1) + down.shape[2:], lambda e, counts: (0, e, 0, 0)),
            fixed((length, width)),
            fixed((1, width)),
            fixed((1, width)),
            fixed((128, 2 * width)),
        ],
        [
            shape(up.shape, low),
            shape(down.shape, low),
            shape((length, width), full),
            thin,
            thin,
            shape((128, 2 * width), full),
        ],
        [
            pltpu.VMEM((length, width), low),
            pltpu.VMEM((length, 128), full),
            pltpu.VMEM((length, width), full),
            pltpu.VMEM((CAPACITY, width), low),
            pltpu.VMEM((CAPACITY, width), low),
            pltpu.VMEM((CAPACITY, hidden), low),
            pltpu.VMEM((CAPACITY, hidden), low),
        ],
        28 * 10**9,
        args,
    )


def enter_kernel(resid_ref, embed_ref, router_ref, gain_ref, bias_ref, normed_ref, probs_ref):
    unit, inverse = norm_parts(resid_ref[...].astype(jnp.float32))
    normed = (unit * gain_ref[...] + bias_ref[...]).astype(jnp.bfloat16)
    normed_ref[...] = normed
    probs_ref[...] = route_probs(normed, embed_ref[...], router_ref)


def expert_enter(resid, embedding, router, gain, bias):
    length, width = resid.shape
    return pl.pallas_call(
        enter_kernel,
        out_shape=[
            jax.ShapeDtypeStruct((length, width), jnp.bfloat16),
            jax.ShapeDtypeStruct((length, 128), jnp.float32),
        ],
        compiler_params=pltpu.CompilerParams(vmem_limit_bytes=40 * 1024 * 1024),
        name="expert_enter",
    )(resid, embedding, router, gain, bias)


def places(routes):
    length = routes.shape[0]
    chosen = (routes == jnp.arange(EXPERTS, dtype=jnp.int32)[None, :]).astype(jnp.float32)
    row = lax.broadcasted_iota(jnp.int32, (length, length), 0)
    before = (lax.broadcasted_iota(jnp.int32, (length, length), 1) < row).astype(jnp.bfloat16)
    earlier = product(before, chosen.astype(jnp.bfloat16))
    slot = jnp.sum(earlier * chosen, 1).astype(jnp.int32) + routes[:, 0] * CAPACITY
    counts = jnp.sum(chosen, 0).astype(jnp.int32)
    return counts, slot[None, :], slot[:, None]


CHUNK = 64
EDGE = 8


def tap_masks(segments):
    half = KERNEL // 2
    segment = segments[0]
    length = segment.shape[0]
    padded = jnp.pad(segment, (half, half), constant_values=-1)
    same = [padded[k : k + length] == segment for k in range(KERNEL)]
    masks = jnp.stack(same, 1).astype(jnp.float32)
    return jnp.pad(masks, ((0, 0), (0, 128 - KERNEL)))


def conv_front_kernel(
    resid_ref, ctx_ref, ao_ref, gain_ref, bias_ref, gated_ref, taps_ref, mask_ref,
    out_ref, normed_ref, joined_ref, depth_ref, sums_ref,
    pad_ref,
):
    length, width = resid_ref.shape
    resid = resid_ref[...] + mul(ctx_ref[...], ao_ref[...])
    out_ref[...] = resid
    unit, inverse = norm_parts(resid)
    normed = (unit * gain_ref[...] + bias_ref[...]).astype(jnp.bfloat16)
    normed_ref[...] = normed
    joined = mul(normed, gated_ref[...])
    joined_ref[...] = joined
    pad_ref[:EDGE, :] = jnp.zeros((EDGE, width), jnp.float32)
    pad_ref[EDGE + length :, :] = jnp.zeros((EDGE, width), jnp.float32)
    pad_ref[EDGE : EDGE + length, :] = joined[:, :width] * sigmoid(joined[:, width:])
    sums_ref[...] = jnp.zeros_like(sums_ref)

    def chunk(index, carry):
        at = pl.ds(pl.multiple_of(index * CHUNK, CHUNK), CHUNK)
        window = pad_ref[pl.ds(pl.multiple_of(index * CHUNK, CHUNK), CHUNK + 2 * EDGE), :]
        masks = mask_ref[at, :]
        total = jnp.zeros((CHUNK, width), jnp.float32)
        for k in range(KERNEL):
            total = total + window[k + 1 : k + 1 + CHUNK] * masks[:, k : k + 1] * taps_ref[k : k + 1, :]
        depth_ref[at, :] = total
        sums_ref[0:1, :] += jnp.sum(total, 0, keepdims=True)
        sums_ref[1:2, :] += jnp.sum(total * total, 0, keepdims=True)
        return carry

    lax.fori_loop(0, length // CHUNK, chunk, 0)


def conv_front(resid, context, attend_out, gain, bias, gated_in, taps, masks):
    length, width = resid.shape
    low, full = jnp.bfloat16, jnp.float32
    shape = jax.ShapeDtypeStruct
    return pl.pallas_call(
        conv_front_kernel,
        out_shape=[
            shape((length, width), full),
            shape((length, width), low),
            shape((length, 2 * width), full),
            shape((length, width), full),
            shape((2, width), full),
        ],
        scratch_shapes=[pltpu.VMEM((length + 2 * EDGE, width), full)],
        compiler_params=pltpu.CompilerParams(vmem_limit_bytes=56 * 1024 * 1024),
        cost_estimate=pl.CostEstimate(flops=4 * 10**9, bytes_accessed=16 * 10**6, transcendentals=10**6),
        name="conv_front",
    )(resid, context, attend_out, gain, bias, gated_in, taps, masks)


def batch_stats(stats, frames):
    average = stats[0:1, :] * (1.0 / frames)
    spread = stats[1:2, :] * (1.0 / frames) - average * average
    return average, lax.rsqrt(spread + eps)


def conv_tail_kernel(
    frames, depth_ref, stats_ref, bgain_ref, bbias_ref, point_ref, resid_ref,
    embed_ref, router_ref, gain_ref, bias_ref,
    out_ref, normed_ref, probs_ref,
):
    average, inverse = batch_stats(stats_ref[...], frames)
    shifted = (depth_ref[...] - average) * inverse * bgain_ref[...] + bbias_ref[...]
    tail = (shifted * sigmoid(shifted)).astype(jnp.bfloat16)
    resid = resid_ref[...] + mul(tail, point_ref[...])
    out_ref[...] = resid
    unit, spread = norm_parts(resid)
    normed = (unit * gain_ref[...] + bias_ref[...]).astype(jnp.bfloat16)
    normed_ref[...] = normed
    probs_ref[...] = route_probs(normed, embed_ref[...], router_ref)


def conv_tail(frames, depth, stats, bgain, bbias, point_out, resid, embedding, router, gain, bias):
    length, width = resid.shape
    shape = jax.ShapeDtypeStruct
    return pl.pallas_call(
        functools.partial(conv_tail_kernel, frames),
        out_shape=[
            shape((length, width), jnp.float32),
            shape((length, width), jnp.bfloat16),
            shape((length, 128), jnp.float32),
        ],
        compiler_params=pltpu.CompilerParams(vmem_limit_bytes=56 * 1024 * 1024),
        cost_estimate=pl.CostEstimate(flops=10**9, bytes_accessed=8 * 10**6, transcendentals=10**6),
        name="conv_tail",
    )(depth, stats, bgain, bbias, point_out, resid, embedding, router, gain, bias)


def conv_turn_kernel(
    frames, slope_ref, depth_ref, stats_ref, bgain_ref, bbias_ref, point_ref,
    dshift_ref, dpoint_ref, sums_ref,
):
    average, inverse = batch_stats(stats_ref[...], frames)
    centered = (depth_ref[...] - average) * inverse
    shifted = centered * bgain_ref[...] + bbias_ref[...]
    sigma = sigmoid(shifted)
    low = slope_ref[...].astype(jnp.bfloat16)
    dpoint_ref[...] = mul((shifted * sigma).astype(jnp.bfloat16), low, TN)
    dshift = mul(low, point_ref[...], NT) * (sigma * (1.0 + shifted * (1.0 - sigma)))
    dshift_ref[...] = dshift
    sums_ref[0:1, :] = jnp.sum(dshift * centered, 0, keepdims=True)
    sums_ref[1:2, :] = jnp.sum(dshift, 0, keepdims=True)


def conv_turn(frames, slope, depth, stats, bgain, bbias, point_out):
    length, width = slope.shape
    shape = jax.ShapeDtypeStruct
    return pl.pallas_call(
        functools.partial(conv_turn_kernel, frames),
        out_shape=[
            shape((length, width), jnp.float32),
            shape((width, width), jnp.float32),
            shape((2, width), jnp.float32),
        ],
        compiler_params=pltpu.CompilerParams(vmem_limit_bytes=56 * 1024 * 1024),
        cost_estimate=pl.CostEstimate(flops=10**9, bytes_accessed=8 * 10**6, transcendentals=10**6),
        name="conv_turn",
    )(slope, depth, stats, bgain, bbias, point_out)


def conv_back_kernel(
    frames, slope_ref, dshift_ref, depth_ref, stats_ref, sums_ref, bgain_ref, joined_ref, normed_ref,
    resid_ref, gain_ref, gated_ref, taps_ref, mask_ref,
    out_ref, dgated_ref, dtaps_ref, dgain_ref, dbias_ref,
    pad_ref, dpad_ref, dtap_ref, dglu_ref,
):
    length, width = resid_ref.shape
    average, inverse = batch_stats(stats_ref[...], frames)
    bgain = bgain_ref[...]
    sums = sums_ref[...] * (1.0 / frames) * bgain
    centered = (depth_ref[...] - average) * inverse
    edge = jnp.zeros((EDGE, width), jnp.float32)
    left = joined_ref[:, :width]
    sigma = sigmoid(joined_ref[:, width:])
    for ref, value in (
        (pad_ref, left * sigma),
        (dpad_ref, inverse * (dshift_ref[...] * bgain - sums[1:2, :] - centered * sums[0:1, :])),
    ):
        ref[:EDGE, :] = edge
        ref[EDGE + length :, :] = edge
        ref[EDGE : EDGE + length, :] = value
    dtap_ref[...] = jnp.zeros_like(dtap_ref)

    def chunk(index, carry):
        at = pl.ds(pl.multiple_of(index * CHUNK, CHUNK), CHUNK)
        around = pl.ds(pl.multiple_of(index * CHUNK, CHUNK), CHUNK + 2 * EDGE)
        window = pad_ref[around, :]
        dwindow = dpad_ref[around, :]
        masks = mask_ref[at, :]
        middle = dwindow[EDGE : EDGE + CHUNK]
        total = jnp.zeros((CHUNK, width), jnp.float32)
        for k in range(KERNEL):
            mask = masks[:, k : k + 1]
            back = KERNEL - 1 - k
            total = total + dwindow[k + 1 : k + 1 + CHUNK] * mask * taps_ref[back : back + 1, :]
            term = window[k + 1 : k + 1 + CHUNK] * mask * middle
            dtap_ref[8 * k : 8 * k + 8, :] += jnp.sum(term.reshape(CHUNK // 8, 8, width), 0)
        dglu_ref[at, :] = total
        return carry

    lax.fori_loop(0, length // CHUNK, chunk, 0)
    for k in range(KERNEL):
        dtaps_ref[k : k + 1, :] = jnp.sum(dtap_ref[8 * k : 8 * k + 8, :], 0, keepdims=True)
    dglu = dglu_ref[...]
    low = jnp.concatenate(
        [
            (dglu * sigma).astype(jnp.bfloat16),
            (dglu * left * sigma * (1.0 - sigma)).astype(jnp.bfloat16),
        ],
        1,
    )
    dgated_ref[...] = mul(normed_ref[...], low, TN)
    slope = mul(low, gated_ref[...], NT)
    unit, spread = norm_parts(resid_ref[...])
    dgain_ref[...] = jnp.sum(slope * unit, 0, keepdims=True)
    dbias_ref[...] = jnp.sum(slope, 0, keepdims=True)
    out_ref[...] = slope_ref[...] + norm_slope(unit, spread, slope, gain_ref[...])


def conv_back(
    frames, slope, dshift, depth, stats, sums, bgain, joined, normed, resid, gain, gated_in, taps, masks
):
    length, width = resid.shape
    full = jnp.float32
    shape = jax.ShapeDtypeStruct
    padded = pltpu.VMEM((length + 2 * EDGE, width), full)
    return pl.pallas_call(
        functools.partial(conv_back_kernel, frames),
        out_shape=[
            shape((length, width), full),
            shape((width, 2 * width), full),
            shape((KERNEL, width), full),
            shape((1, width), full),
            shape((1, width), full),
        ],
        scratch_shapes=[
            padded,
            padded,
            pltpu.VMEM((8 * KERNEL, width), full),
            pltpu.VMEM((length, width), full),
        ],
        compiler_params=pltpu.CompilerParams(vmem_limit_bytes=60 * 1024 * 1024),
        cost_estimate=pl.CostEstimate(flops=6 * 10**9, bytes_accessed=20 * 10**6, transcendentals=10**6),
        name="conv_back",
    )(slope, dshift, depth, stats, sums, bgain, joined, normed, resid, gain, gated_in, taps, masks)


def total_of(value):
    count = lax.axis_size(AXES)
    bit = 1
    while bit < count:
        value = value + lax.ppermute(value, AXES, [(d, d ^ bit) for d in range(count)])
        bit *= 2
    return value


def gather_experts(value):
    blocks = lax.all_gather(value, AXES, axis=0, tiled=False)
    if value.shape[1] % 16:
        blocks = blocks.transpose(1, 0, 2, 3).reshape((1, EXPERTS, -1, value.shape[2]))
    return blocks


def scatter_experts(value):
    devices = lax.axis_size(AXES)
    if value.shape[0] == 1:
        value = value.reshape((EXPERTS, devices, -1, value.shape[3])).transpose(1, 0, 2, 3)
    return lax.psum_scatter(value, AXES, scatter_dimension=0, tiled=False).astype(jnp.float32)


def gather_rows(value):
    return lax.all_gather(value, AXES, axis=0, tiled=True)


def scatter_rows(value):
    return lax.psum_scatter(value, AXES, scatter_dimension=0, tiled=True)


def router_columns(router):
    count = router.shape[0] // 2
    return router.reshape(2, count, EXPERTS).transpose(1, 0, 2).reshape(count, 2 * EXPERTS)


def router_rows(packed, devices):
    count = packed.shape[0] // devices
    return (
        packed.reshape(devices, count, 2, EXPERTS).transpose(0, 2, 1, 3).reshape(-1, EXPERTS)
    )


def on_device(
    inputs,
    embedding,
    segments,
    routes_first,
    routes_second,
    cotangent,
    first_gain,
    first_bias,
    first_router,
    first_up,
    first_down,
    attend_gain,
    attend_bias,
    project_in,
    relative_weight,
    content_bias,
    position_bias,
    attend_out,
    depth_gain,
    depth_bias,
    gated_in,
    depth_kernel,
    batch_gain,
    batch_bias,
    point_out,
    second_gain,
    second_bias,
    second_router,
    second_up,
    second_down,
    final_gain,
    final_bias,
):
    segment = segments[0]
    devices = lax.axis_size(AXES)
    length, width = inputs.shape
    frames = length * devices
    vectors = jnp.stack(
        [
            first_gain,
            first_bias,
            second_gain,
            second_bias,
            attend_gain,
            attend_bias,
            content_bias,
            position_bias,
            depth_gain,
            depth_bias,
            batch_gain,
            batch_bias,
            final_gain,
            final_bias,
        ],
        1,
    )
    n_vec = vectors.shape[1]
    small = jnp.concatenate(
        [
            vectors,
            depth_kernel.T,
            router_columns(first_router),
            router_columns(second_router),
        ],
        1,
    )
    n_small = small.shape[1]
    small = jnp.pad(small, ((0, 0), (0, 128 - n_small)))
    packed = gather_rows(
        jnp.concatenate(
            [small, project_in, relative_weight, attend_out, gated_in, point_out], 1
        )
    )
    small = packed[:, :n_small]
    rows = small[:, : n_vec + KERNEL].T
    col = n_vec + KERNEL
    first_router_full = router_rows(small[:, col : col + 2 * EXPERTS], devices)
    second_router_full = router_rows(small[:, col + 2 * EXPERTS : col + 4 * EXPERTS], devices)
    at = 128
    project_full = packed[:, at : at + 3 * width]
    at = at + 3 * width
    relative_full = packed[:, at : at + width]
    at = at + width
    attend_out_full = packed[:, at : at + width]
    at = at + width
    gated_full = packed[:, at : at + 2 * width]
    at = at + 2 * width
    point_full = packed[:, at : at + width]
    relative_full = relative_full.reshape(width // 2, 2, width).transpose(1, 0, 2).reshape(width, width)
    floats = rows.astype(jnp.float32)

    def vec(index):
        return floats[index : index + 1]

    def router_wide(router):
        return jnp.pad(router, ((0, 0), (0, 128 - EXPERTS)))

    first_router_full = router_wide(first_router_full)
    second_router_full = router_wide(second_router_full)
    taps = floats[n_vec : n_vec + KERNEL]
    masks = tap_masks(segments)
    first_places = places(routes_first)
    second_places = places(routes_second)
    first_ups, first_downs = gather_experts(first_up), gather_experts(first_down)
    second_ups, second_downs = gather_experts(second_up), gather_experts(second_down)
    attend_full = (
        vec(4),
        vec(5),
        project_full,
        relative_full,
        vec(6),
        vec(7),
        attend_out_full,
    )
    cosine, sine = angles(length, width)
    tables = (jnp.concatenate([cosine, sine], 1).astype(jnp.bfloat16), cosine, sine)

    first_normed, first_probs = expert_enter(inputs, embedding, first_router_full, vec(0), vec(1))
    first_common = (
        first_places[0],
        first_normed,
        first_places[1],
        first_places[2],
        first_ups,
        first_downs,
        inputs,
        first_probs,
        routes_first,
    )
    first_resid, first_branch = first_forward(first_common)
    attend_kept = attention_forward(first_resid, segments, attend_full, tables)
    attend_resid, conv_normed, joined, depth, stats = conv_front(
        first_resid, attend_kept[6], attend_out_full, vec(8), vec(9), gated_full, taps, masks
    )
    stats = total_of(stats)
    conv_resid, second_normed, second_probs = conv_tail(
        frames, depth, stats, vec(10), vec(11), point_full, attend_resid,
        embedding, second_router_full, vec(2), vec(3),
    )
    second_common = (
        second_places[0],
        second_normed,
        second_places[1],
        second_places[2],
        second_ups,
        second_downs,
        conv_resid,
        second_probs,
        routes_second,
    )
    result, slope, final_gain_grad, final_bias_grad, second_branch = second_forward(
        second_common + (cotangent, vec(12), vec(13))
    )
    second_dup, second_ddown, slope, dgain_second, dbias_second, drouter_second = expert_backward(
        second_common + (second_branch, slope, embedding, second_router_full, vec(2))
    )
    second_up_grad, second_down_grad = scatter_experts(second_dup), scatter_experts(second_ddown)
    dshift, dpoint, sums = conv_turn(frames, slope, depth, stats, vec(10), vec(11), point_full)
    sums = total_of(sums)
    slope, dgated, dtaps, dgain_depth, dbias_depth = conv_back(
        frames, slope, dshift, depth, stats, sums, vec(10), joined, conv_normed,
        attend_resid, vec(8), gated_full, taps, masks,
    )
    slope, dao, dpq, dpk, dpv, drel, dcb, dpb, dgain_attend, dbias_attend = attention_backward(
        first_resid, slope, attend_full, tables, attend_kept
    )
    drel = drel.reshape(2, width // 2, width).transpose(1, 0, 2).reshape(width, width)
    matrices = jnp.concatenate([dpq, dpk, dpv, drel, dao, dgated, dpoint], 1).astype(jnp.bfloat16)
    matrices = scatter_rows(matrices).astype(jnp.float32)
    first_dup, first_ddown, slope, dgain_first, dbias_first, drouter_first = expert_backward(
        first_common + (first_branch, slope, embedding, first_router_full, vec(0))
    )
    first_up_grad, first_down_grad = scatter_experts(first_dup), scatter_experts(first_ddown)

    def columns_of(grad):
        return (
            grad[:EXPERTS]
            .reshape(EXPERTS, devices, 2, -1)
            .transpose(1, 3, 2, 0)
            .reshape(width, 2 * EXPERTS)
        )

    small_grad = scatter_rows(
        jnp.concatenate(
            [
                jnp.concatenate(
                    [
                        dgain_first,
                        dbias_first,
                        dgain_second,
                        dbias_second,
                        dgain_attend,
                        dbias_attend,
                        dcb,
                        dpb,
                        dgain_depth,
                        dbias_depth,
                        final_gain_grad,
                        final_bias_grad,
                        dtaps,
                    ],
                    0,
                ).T,
                columns_of(drouter_first),
                columns_of(drouter_second),
            ],
            1,
        )
    )
    own = small_grad.shape[0]
    start = own * lax.axis_index(AXES)
    own_sums = lax.dynamic_slice_in_dim(sums, start, own, 1)

    def vector(index):
        return small_grad[:, index]

    def router_of(start):
        block = small_grad[:, start : start + 2 * EXPERTS]
        return block.reshape(own, 2, EXPERTS).transpose(1, 0, 2).reshape(2 * own, EXPERTS)

    return (
        result,
        slope,
        vector(0),
        vector(1),
        router_of(12 + KERNEL),
        first_up_grad,
        first_down_grad,
        vector(4),
        vector(5),
        matrices[:, : 3 * width],
        matrices[:, 3 * width : 4 * width],
        vector(6),
        vector(7),
        matrices[:, 4 * width : 5 * width],
        vector(8),
        vector(9),
        matrices[:, 5 * width : 7 * width],
        small_grad[:, 12 : 12 + KERNEL].T,
        own_sums[0],
        own_sums[1],
        matrices[:, 7 * width : 8 * width],
        vector(2),
        vector(3),
        router_of(12 + KERNEL + 2 * EXPERTS),
        second_up_grad,
        second_down_grad,
        vector(10),
        vector(11),
    )


def solution(mesh):
    placed = (
        P(("dp", "fsdp"), None),
        P(("dp", "fsdp"), None),
        P(("dp", "fsdp"), None),
        P(("dp", "fsdp"), None),
        P(("dp", "fsdp"), None),
        P(("dp", "fsdp"), None),
        P(("dp", "fsdp")),
        P(("dp", "fsdp")),
        P(("dp", "fsdp"), None),
        P(None, ("dp", "fsdp"), None),
        P(None, ("dp", "fsdp"), None),
        P(("dp", "fsdp")),
        P(("dp", "fsdp")),
        P(("dp", "fsdp"), None),
        P(("dp", "fsdp"), None),
        P(("dp", "fsdp")),
        P(("dp", "fsdp")),
        P(("dp", "fsdp"), None),
        P(("dp", "fsdp")),
        P(("dp", "fsdp")),
        P(("dp", "fsdp"), None),
        P(None, ("dp", "fsdp")),
        P(("dp", "fsdp")),
        P(("dp", "fsdp")),
        P(("dp", "fsdp"), None),
        P(("dp", "fsdp")),
        P(("dp", "fsdp")),
        P(("dp", "fsdp"), None),
        P(None, ("dp", "fsdp"), None),
        P(None, ("dp", "fsdp"), None),
        P(("dp", "fsdp")),
        P(("dp", "fsdp")),
    )
    return jax.shard_map(
        on_device,
        mesh=mesh,
        in_specs=placed,
        out_specs=(
            P(("dp", "fsdp"), None),
            P(("dp", "fsdp"), None),
            P(("dp", "fsdp")),
            P(("dp", "fsdp")),
            P(("dp", "fsdp"), None),
            P(None, ("dp", "fsdp"), None),
            P(None, ("dp", "fsdp"), None),
            P(("dp", "fsdp")),
            P(("dp", "fsdp")),
            P(("dp", "fsdp"), None),
            P(("dp", "fsdp"), None),
            P(("dp", "fsdp")),
            P(("dp", "fsdp")),
            P(("dp", "fsdp"), None),
            P(("dp", "fsdp")),
            P(("dp", "fsdp")),
            P(("dp", "fsdp"), None),
            P(None, ("dp", "fsdp")),
            P(("dp", "fsdp")),
            P(("dp", "fsdp")),
            P(("dp", "fsdp"), None),
            P(("dp", "fsdp")),
            P(("dp", "fsdp")),
            P(("dp", "fsdp"), None),
            P(None, ("dp", "fsdp"), None),
            P(None, ("dp", "fsdp"), None),
            P(("dp", "fsdp")),
            P(("dp", "fsdp")),
        ),
        check_vma=False,
    )
```

time: 3090 us -> 1510 us (0.49)
  local copies, waits for them, and re-layouts: 657 us -> 63.6 us
  blocking collectives: 404 us -> 0 us
  matrix products: 394 us -> 1.71 us
  waiting for transfers between devices: 1430 us -> 1090 us
  Pallas kernels: 0 us -> 295 us
  other arithmetic: 172 us -> 25.8 us
    reduce_scatter x9 -> x5, waiting for transfers between devices: 1390 us -> 706 us  [the longest x4 579 us: scatter_experts(): lax.psum_scatter(value, AXES, scatter_dimension=0, tiled=False)]
    dot_general x39 -> x0, matrix products: 329 us -> none  [the longest x2 33.8 us: expert_backward(): jnp.einsum('ecd,efd->ecf', slot_slope, down_full, preferred_element_type=...]
    pallas_call x0 -> x11, Pallas kernels: none -> 295 us  [the longest x4 134 us: expert_call(): pl.pallas_call(kernel, grid_spec=pltpu.PrefetchScalarGridSpec(num_scalar_...]
    unnamed x496 -> x88, local copies, waits for them, and re-layouts: 272 us -> 18.8 us
    all_gather x6 -> x0, blocking collectives: 248 us -> none  [the longest x1 43.7 us: on_device(): lax.all_gather(relative_weight, ('dp', 'fsdp'), axis=0, tiled=True)]
    all_gather x6 -> x5, waiting for transfers between devices: 0.05 us -> 235 us  [the longest x4 184 us: gather_experts(): blocks = lax.all_gather(value, AXES, axis=0, tiled=False)]
    reshape x8 -> x15, local copies, waits for them, and re-layouts: 173 us -> 7.08 us  [the longest x1 1.71 us: attention_forward(): segments.reshape(length, 1)]
    gather x16 -> x0, local copies, waits for them, and re-layouts: 89.9 us -> none  [the longest x4 18.8 us: expert_forward(): branch = outgoing.reshape(-1, width)[target]]
  transfers between devices with their start and end apart: 18 -> 21, of which waited for: 10 -> 20; matrix products, arithmetic and copies ran while one was open for 33% -> 4% of each run, Pallas kernels for 0% -> 6%
where the time goes in v1:
time: 1510 us; the launch traced here: 1500 us
  waiting for transfers between devices  1090 us (72%)
  Pallas kernels  295 us (20%)
  local copies, waits for them, and re-layouts  63.6 us (4%)
  other arithmetic  25.8 us (2%)
    reduce_scatter x4, waiting for transfers between devices, scatter_experts(): lax.psum_scatter(value, AXES, scatter_dimension=0, tiled=False)  579 us
    all_gather x4, waiting for transfers between devices, gather_experts(): blocks = lax.all_gather(value, AXES, axis=0, tiled=False)  184 us
    pallas_call x4, Pallas kernels, expert_call(): pl.pallas_call(kernel, grid_spec=pltpu.PrefetchScalarGridSpec(num_scalar_...  134 us
    unnamed x12, waiting for transfers between devices  127 us
    reduce_scatter x1, waiting for transfers between devices, scatter_rows(): return lax.psum_scatter(value, AXES, scatter_dimension=0, tiled=True)  127 us
    pallas_call x1, Pallas kernels, attention_backward(): pl.pallas_call(attend_backward_kernel, grid=(pairs,), in_specs=[pl.BlockS...  58.9 us
    all_gather x1, waiting for transfers between devices, gather_rows(): return lax.all_gather(value, AXES, axis=0, tiled=True)  51.3 us
    pallas_call x1, Pallas kernels, attention_forward(): pl.pallas_call(attend_forward_kernel, grid=(pairs,), in_specs=[whole((len...  46.6 us
  transfers between devices with their start and end apart: 21, of which 20 were waited for; matrix products, arithmetic and copies ran while one was open for 4% of the time, Pallas kernels for 6%

profile of v1, /device:TPU:0, one launch (start us, length us, event | category | flops | bytes accessed | tf_op | source)
XLA Modules:
  0.0 1499.6 jit_solution(7421060892612483813)
XLA Ops:
  31.2 1.7 copy.170.segc_ref
  38.8 51.3 %all-gather.10.cloned.1.call-done = bf16[512,4224]{1,0:T(8,128)(2,1)} async-done(((bf16[16,4224]{1,0:T(8,128)(2,1)}), bf16[512,4224]{1,0:T(8,128)(2,1)}) %all-gather.10.cloned.1.call-update) | async-done | bytes 4325392 | tf_op jit(solution)/shard_map/all_gather | solution.py:979
  90.1 1.8 fusion.22
  94.2 2.5 fusion.23
  100.3 1.3 expert_enter.1
  103.4 2.7 slice.261.pq_ref.pk_ref.pv_ref
  106.0 2.3 slice.268.gated_ref
  108.3 60.5 %all-gather.12.cloned.1.call-done = bf16[128,16,2048]{2,1,0:T(8,128)(2,1)} async-done(((bf16[4,16,2048]{2,1,0:T(8,128)(2,1)}), bf16[128,16,2048]{2,1,0:T(8,128)(2,1)}) %all-gather.12.cloned.1.call-update) | async-done | bytes 8388624 | tf_op jit(solution)/shard_map/all_gather | solution.py:965
  168.8 78.9 %all-gather.14.cloned.1.call-done = bf16[128,64,512]{2,1,0:T(8,128)(2,1)} async-done(((bf16[4,64,512]{2,1,0:T(8,128)(2,1)}), bf16[128,64,512]{2,1,0:T(8,128)(2,1)}) %all-gather.14.cloned.1.call-update) | async-done | bytes 8388624 | tf_op jit(solution)/shard_map/all_gather | solution.py:965
  247.7 23.2 %first_forward.1 = (f32[1024,512]{1,0:T(8,128)}, f32[1024,512]{1,0:T(8,128)}) custom-call(s32[4]{0:T(128)} %convert_element_type.163.counts_ref, bf16[1024,512]{1,0:T(8,128)(2,1)} %copy-done.4, s32[1,1024]{1,0:T(1,128)} %add.97.posr_ref, s32[1024,1]{1,0:T(8,128)} %get-tuple-element.143.posc_ref, bf16[32,4,16,2048]{3,2,1,0:T(8,128)(2,1)} %bitcast.168, ...), custom_call_target="tpu_custom_call" | custom-call | flops 10000000000 | bytes 30000000 | tf_op jit(solution)/shard_map/first_forward/pallas_call | solution.py:604
  270.9 46.6 %attend_forward.1 = (bf16[1024,512]{1,0:T(8,128)(2,1)}, bf16[1024,512]{1,0:T(8,128)(2,1)}, bf16[1024,512]{1,0:T(8,128)(2,1)}, bf16[1024,512]{1,0:T(8,128)(2,1)},...) custom-call(f32[1024,512]{1,0:T(8,128)} %get-tuple-element.84.resid_ref, ...), custom_call_target="tpu_custom_call" | custom-call | flops 24000000000 | bytes 30000000 | tf_op jit(solution)/shard_map/attend_forward/pallas_call | solution.py:272
  317.6 16.5 %conv_front.1 = (f32[1024,512]{1,0:T(8,128)}, bf16[1024,512]{1,0:T(8,128)(2,1)}, f32[1024,1024]{1,0:T(8,128)}, f32[1024,512]{1,0:T(8,128)}, f32[2,512]{1,0:T(2,128)}) custom-call(f32[1024,512]{1,0:T(8,128)} %get-tuple-element.84.resid_ref, bf16[1024,512]{1,0:T(8,128)(2,1)} %get-tuple-element.85.ctx_ref, bf16[512,512]{1,0:T(8,128)(2,1)} %get-tuple-element.139.ao_ref, ...), custom_call_target="tpu_custom_call" | custom-call | flops 4000000000 | bytes 16000000 | tf_op jit(solution)/shard_map/conv_front/pallas_call | solution.py:782
  334.1 1.4 collective-permute-done
  336.2 1.4 collective-permute-start.1
  337.6 2.2 collective-permute-done.1
  339.8 4.3 collective-permute-start.2
  345.7 2.1 collective-permute-start.3
  354.5 6.1 conv_tail.1
  360.6 44.6 %all-gather.18.cloned.1.call-done = bf16[128,64,512]{2,1,0:T(8,128)(2,1)} async-done(((bf16[4,64,512]{2,1,0:T(8,128)(2,1)}), bf16[128,64,512]{2,1,0:T(8,128)(2,1)}) %all-gather.18.cloned.1.call-update) | async-done | bytes 8388624 | tf_op jit(solution)/shard_map/all_gather | solution.py:965
  405.2 27.8 %second_forward.1 = (bf16[1024,512]{1,0:T(8,128)(2,1)}, f32[1024,512]{1,0:T(8,128)}, f32[1,512]{1,0:T(1,128)}, f32[1,512]{1,0:T(1,128)}, f32[1024,512]{1,0:T(8,128)}) custom-call(s32[4]{0:T(128)} %convert_element_type.161.counts_ref, bf16[1024,512]{1,0:T(8,128)(2,1)} %get-tuple-element.89.normed_ref, s32[1,1024]{1,0:T(1,128)} %add.106.posr_ref, ...), custom_call_target="tpu_custom_call" | custom-call | flops 10000000000 | bytes 30000000 | tf_op jit(solution)/shard_map/second_forward/pallas_call | solution.py:604
  433.0 43.8 %expert_backward.2 = (bf16[32,4,16,2048]{3,2,1,0:T(8,128)(2,1)}, bf16[32,4,64,512]{3,2,1,0:T(8,128)(2,1)}, f32[1024,512]{1,0:T(8,128)}, f32[1,512]{1,0:T(1,128)}, f32[1,512]{1,0:T(1,128)}, /*index=5*/f32[128,1024]{1,0:T(8,128)}) custom-call(s32[4]{0:T(128)} %convert_element_type.161.counts_ref, bf16[1024,512]{1,0:T(8,128)(2,1)} %get-tuple-element.89.normed_ref, ...), custom_call_target="tpu_custom_call" | custom-call | flops 28000000000 | bytes 30000000 | tf_op jit(solution)/shard_map/expert_backward/pallas_call | solution.py:604
  476.9 5.7 conv_turn.1
  482.5 1.4 collective-permute-done.5
  484.6 3.6 collective-permute-done.6
  488.2 1.5 collective-permute-start.7
  489.7 2.1 collective-permute-done.7
  491.8 1.4 collective-permute-start.8
  493.2 2.2 collective-permute-done.8
  495.4 1.9 collective-permute-start.9
  498.4 1.5 collective-permute-done.9
  500.5 25.7 %conv_back.1 = (f32[1024,512]{1,0:T(8,128)}, f32[512,1024]{1,0:T(8,128)}, f32[15,512]{1,0:T(8,128)}, f32[1,512]{1,0:T(1,128)}, f32[1,512]{1,0:T(1,128)}) custom-call(f32[1024,512]{1,0:T(8,128)} %get-tuple-element.97.slope_ref, f32[1024,512]{1,0:T(8,128)} %get-tuple-element.98.dshift_ref, f32[1024,512]{1,0:T(8,128)} %get-tuple-element.86.depth_ref, ...), custom_call_target="tpu_custom_call" | custom-call | flops 6000000000 | bytes 20000000 | tf_op jit(solution)/shard_map/conv_back/pallas_call | solution.py:934
  526.2 58.9 %attend_backward.1 = (f32[1024,512]{1,0:T(8,128)}, f32[512,512]{1,0:T(8,128)}, f32[512,512]{1,0:T(8,128)}, f32[512,512]{1,0:T(8,128)}, f32[512,512]{1,0:T(8,128)...) custom-call(bf16[8,1024,1024]{2,1,0:T(8,128)(2,1)} %get-tuple-element.9, ...), custom_call_target="tpu_custom_call" | custom-call | flops 40000000000 | bytes 40000000 | tf_op jit(solution)/shard_map/attend_backward/pallas_call | solution.py:327
  585.3 39.0 %expert_backward.3 = (bf16[32,4,16,2048]{3,2,1,0:T(8,128)(2,1)}, bf16[32,4,64,512]{3,2,1,0:T(8,128)(2,1)}, f32[1024,512]{1,0:T(8,128)}, f32[1,512]{1,0:T(1,128)}, f32[1,512]{1,0:T(1,128)}, /*index=5*/f32[128,1024]{1,0:T(8,128)}) custom-call(s32[4]{0:T(128)} %convert_element_type.163.counts_ref, bf16[1024,512]{1,0:T(8,128)(2,1)} %copy-done.4, ...), custom_call_target="tpu_custom_call" | custom-call | flops 28000000000 | bytes 30000000 | tf_op jit(solution)/shard_map/expert_backward/pallas_call | solution.py:604
  629.1 2.3 convert_dynamic-update-slice_fusion.4
  631.3 2.1 convert_dynamic-update-slice_fusion.3
  641.5 122.0 %reduce-scatter.19.cloned.1.call-done = f32[16,43]{1,0:T(8,128)} async-done(((f32[512,43]{1,0:T(8,128)}), f32[16,43]{1,0:T(8,128)}) %reduce-scatter.19.cloned.1.call-update) | async-done | bytes 2768
  775.4 127.0 %reduce-scatter.13.cloned.1.call-done = bf16[16,4096]{1,0:T(8,128)(2,1)} async-done(((bf16[512,4096]{1,0:T(8,128)(2,1)}), bf16[16,4096]{1,0:T(8,128)(2,1)}) %reduce-scatter.13.cloned.1.call-update) | async-done | bytes 131088 | tf_op jit(solution)/shard_map/reduce_scatter | solution.py:983
  902.5 1.4 slice.283
  903.9 1.4 slice.290
  905.3 1.4 fusion.24
  906.7 143.1 %reduce-scatter.17.cloned.1.call-done = bf16[1,4,64,512]{3,2,1,0:T(8,128)(2,1)} async-done(((bf16[32,4,64,512]{3,2,1,0:T(8,128)(2,1)}), bf16[1,4,64,512]{3,2,1,0:T(8,128)(2,1)}) %reduce-scatter.17.cloned.1.call-update) | async-done | bytes 262160 | tf_op jit(solution)/shard_map/reduce_scatter | solution.py:975
  1049.8 1.8 bitcast_convert_fusion
  1051.6 145.3 %reduce-scatter.15.cloned.1.call-done = bf16[1,4,16,2048]{3,2,1,0:T(8,128)(2,1)} async-done(((bf16[32,4,16,2048]{3,2,1,0:T(8,128)(2,1)}), bf16[1,4,16,2048]{3,2,1,0:T(8,128)(2,1)}) %reduce-scatter.15.cloned.1.call-update) | async-done | bytes 262160 | tf_op jit(solution)/shard_map/reduce_scatter | solution.py:975
  1197.0 1.8 bitcast_convert_fusion.1
  1198.7 145.2 %reduce-scatter.9.cloned.1.call-done = bf16[1,4,16,2048]{3,2,1,0:T(8,128)(2,1)} async-done(((bf16[32,4,16,2048]{3,2,1,0:T(8,128)(2,1)}), bf16[1,4,16,2048]{3,2,1,0:T(8,128)(2,1)}) %reduce-scatter.9.cloned.1.call-update) | async-done | bytes 262160 | tf_op jit(solution)/shard_map/reduce_scatter | solution.py:975
  1343.9 1.8 bitcast_convert_fusion.3
  1345.7 145.4 %reduce-scatter.11.cloned.1.call-done = bf16[1,4,64,512]{3,2,1,0:T(8,128)(2,1)} async-done(((bf16[32,4,64,512]{3,2,1,0:T(8,128)(2,1)}), bf16[1,4,64,512]{3,2,1,0:T(8,128)(2,1)}) %reduce-scatter.11.cloned.1.call-update) | async-done | bytes 262160 | tf_op jit(solution)/shard_map/reduce_scatter | solution.py:975
  1491.1 1.8 bitcast_convert_fusion.2
  (230 shorter events, 73.1 us)
Async XLA Ops:
  7.2 25.7 %copy-start.20 = (s32[1,1024]{1,0:T(1,128)S(1)}, s32[1,1024]{1,0:T(1,128)}, u32[]{:S(2)}) copy-start(s32[1,1024]{1,0:T(1,128)} %segr_ref.1) | copy-start | bytes 12292
  7.2 82.9 %all-gather.10.cloned.1.call-start = ((), (), s32[]{:S(2)}) async-start(), calls=%async_computation.6 | async-start | bytes 4460544 | tf_op jit(solution)/shard_map/all_gather | solution.py:979
  24.7 144.1 %all-gather.12.cloned.1.call-start = ((), (), s32[]{:S(2)}) async-start(), calls=%async_computation.12 | async-start | bytes 8650752 | tf_op jit(solution)/shard_map/all_gather | solution.py:965
  25.5 222.3 %all-gather.14.cloned.1.call-start = ((), (), s32[]{:S(2)}) async-start(), calls=%async_computation.13 | async-start | bytes 8650752 | tf_op jit(solution)/shard_map/all_gather | solution.py:965
  26.2 334.4 %all-gather.16.cloned.1.call-start = ((), (), s32[]{:S(2)}) async-start(), calls=%async_computation.14 | async-start | bytes 8650752 | tf_op jit(solution)/shard_map/all_gather | solution.py:965
  26.8 378.4 %all-gather.18.cloned.1.call-start = ((), (), s32[]{:S(2)}) async-start(), calls=%async_computation.15 | async-start | bytes 8650752 | tf_op jit(solution)/shard_map/all_gather | solution.py:965
  27.4 736.1 %reduce-scatter.19.cloned.1.call-start = ((), (), s32[]{:S(2)}) async-start(), calls=%async_computation.16 | async-start | bytes 270336
  28.3 9.4 copy-start.8
  36.6 60.1 %copy-start.6 = (f32[32,32,256]{2,1,0:T(8,128)}, f32[32,32,256]{2,1,0:T(8,128)S(1)}, u32[]{:S(2)}) copy-start(f32[32,32,256]{2,1,0:T(8,128)S(1)} %get-tuple-element.148) | copy-start | bytes 3145732
  38.8 61.5 %copy-start = (bf16[1024,512]{1,0:T(8,128)(2,1)S(1)}, bf16[1024,512]{1,0:T(8,128)(2,1)}, u32[]{:S(2)}) copy-start(bf16[1024,512]{1,0:T(8,128)(2,1)} %embed_ref.7) | copy-start | bytes 3145732
  38.8 61.5 %copy-start.2 = (bf16[1024,512]{1,0:T(8,128)(2,1)S(1)}, bf16[1024,512]{1,0:T(8,128)(2,1)}, u32[]{:S(2)}) copy-start(bf16[1024,512]{1,0:T(8,128)(2,1)} %resid_ref.5) | copy-start | bytes 3145732
  94.2 4.7 copy-start.17
  99.6 171.3 %copy-start.1 = (bf16[1024,128]{1,0:T(8,128)(2,1)}, bf16[1024,128]{1,0:T(8,128)(2,1)S(1)}, u32[]{:S(2)}) copy-start(bf16[1024,128]{1,0:T(8,128)(2,1)S(1)} %pad.22.router_ref) | copy-start | bytes 786436
  100.3 170.6 %copy-start.3 = (f32[1,512]{1,0:T(1,128)}, f32[1,512]{1,0:T(1,128)S(1)}, u32[]{:S(2)}) copy-start(f32[1,512]{1,0:T(1,128)S(1)} %get-tuple-element.163.gain_ref) | copy-start | bytes 6148
  317.6 26.6 %copy-start.19 = (s32[1024,1]{0,1:T(1,128)S(1)}, s32[1024,1]{0,1:T(1,128)}, u32[]{:S(2)}) copy-start(s32[1024,1]{0,1:T(1,128)} %param.36) | copy-start | bytes 12292
  317.6 33.7 %copy-start.15 = (bf16[512,8]{1,0:T(8,128)(2,1)S(1)}, bf16[512,8]{1,0:T(8,128)(2,1)}, u32[]{:S(2)}) copy-start(bf16[512,8]{1,0:T(8,128)(2,1)} %get-tuple-element.136) | copy-start | bytes 24580
  334.1 1.4 collective-permute-start
  336.2 3.6 collective-permute-start.1
  339.8 5.9 collective-permute-start.2
  344.9 15.7 %copy-start.9 = (s32[1024,1]{1,0:T(8,128)}, s32[1024,1]{1,0:T(8,128)S(1)}, u32[]{:S(2)}) copy-start(s32[1024,1]{1,0:T(8,128)S(1)} %copy.174.route_ref) | copy-start | bytes 12292
  345.7 3.7 collective-permute-start.3
  349.4 4.5 collective-permute-start.4
  482.5 1.4 collective-permute-start.5
  484.6 3.6 collective-permute-start.6
  488.2 3.6 collective-permute-start.7
  491.8 3.6 collective-permute-start.8
  495.4 4.5 collective-permute-start.9
  585.1 40.3 %copy-start.18 = (f32[15,512]{1,0:T(8,128)S(1)}, f32[15,512]{1,0:T(8,128)}, u32[]{:S(2)}) copy-start(f32[15,512]{1,0:T(8,128)} %get-tuple-element.122) | copy-start | bytes 92164
  585.1 40.3 %copy-start.21 = (f32[1,512]{1,0:T(1,128)S(1)}, f32[1,512]{1,0:T(1,128)}, u32[]{:S(2)}) copy-start(f32[1,512]{1,0:T(1,128)} %get-tuple-element.120) | copy-start | bytes 6148
  585.2 40.3 %copy-start.22 = (f32[1,512]{1,0:T(1,128)S(1)}, f32[1,512]{1,0:T(1,128)}, u32[]{:S(2)}) copy-start(f32[1,512]{1,0:T(1,128)} %get-tuple-element.121) | copy-start | bytes 6148
  585.2 40.3 %copy-start.23 = (f32[1,512]{1,0:T(1,128)S(1)}, f32[1,512]{1,0:T(1,128)}, u32[]{:S(2)}) copy-start(f32[1,512]{1,0:T(1,128)} %get-tuple-element.112) | copy-start | bytes 6148
  585.2 40.3 %copy-start.24 = (f32[1,512]{1,0:T(1,128)S(1)}, f32[1,512]{1,0:T(1,128)}, u32[]{:S(2)}) copy-start(f32[1,512]{1,0:T(1,128)} %get-tuple-element.113) | copy-start | bytes 6148
  585.2 40.3 %copy-start.25 = (f32[1,512]{1,0:T(1,128)S(1)}, f32[1,512]{1,0:T(1,128)}, u32[]{:S(2)}) copy-start(f32[1,512]{1,0:T(1,128)} %get-tuple-element.118) | copy-start | bytes 6148
  585.2 40.3 %copy-start.26 = (f32[1,512]{1,0:T(1,128)S(1)}, f32[1,512]{1,0:T(1,128)}, u32[]{:S(2)}) copy-start(f32[1,512]{1,0:T(1,128)} %get-tuple-element.119) | copy-start | bytes 6148
  585.2 40.3 %copy-start.27 = (f32[1,512]{1,0:T(1,128)S(1)}, f32[1,512]{1,0:T(1,128)}, u32[]{:S(2)}) copy-start(f32[1,512]{1,0:T(1,128)} %get-tuple-element.116) | copy-start | bytes 6148
  585.2 40.3 %copy-start.28 = (f32[1,512]{1,0:T(1,128)S(1)}, f32[1,512]{1,0:T(1,128)}, u32[]{:S(2)}) copy-start(f32[1,512]{1,0:T(1,128)} %get-tuple-element.117) | copy-start | bytes 6148
  585.2 40.3 %copy-start.29 = (f32[1,512]{1,0:T(1,128)S(1)}, f32[1,512]{1,0:T(1,128)}, u32[]{:S(2)}) copy-start(f32[1,512]{1,0:T(1,128)} %get-tuple-element.114) | copy-start | bytes 6148
  585.2 40.3 %copy-start.30 = (f32[1,512]{1,0:T(1,128)S(1)}, f32[1,512]{1,0:T(1,128)}, u32[]{:S(2)}) copy-start(f32[1,512]{1,0:T(1,128)} %get-tuple-element.115) | copy-start | bytes 6148
  585.3 42.1 %copy-start.14 = (f32[512,512]{1,0:T(8,128)S(1)}, f32[512,512]{1,0:T(8,128)}, u32[]{:S(2)}) copy-start(f32[512,512]{1,0:T(8,128)} %get-tuple-element.127) | copy-start | bytes 3145732
  585.3 43.0 %copy-start.13 = (f32[512,512]{1,0:T(8,128)S(1)}, f32[512,512]{1,0:T(8,128)}, u32[]{:S(2)}) copy-start(f32[512,512]{1,0:T(8,128)} %get-tuple-element.130) | copy-start | bytes 3145732
  627.3 275.2 %reduce-scatter.13.cloned.1.call-start = ((), (), s32[]{:S(2)}) async-start(), calls=%async_computation.9 | async-start | bytes 4325376 | tf_op jit(solution)/shard_map/reduce_scatter | solution.py:983
  628.3 7.0 copy-start.10
  629.1 5.3 copy-start.12
  629.1 7.4 copy-start.11
  637.4 412.5 %reduce-scatter.17.cloned.1.call-start = ((), (), s32[]{:S(2)}) async-start(), calls=%async_computation.11 | async-start | bytes 8650752 | tf_op jit(solution)/shard_map/reduce_scatter | solution.py:975
  638.1 558.8 %reduce-scatter.15.cloned.1.call-start = ((), (), s32[]{:S(2)}) async-start(), calls=%async_computation.10 | async-start | bytes 8650752 | tf_op jit(solution)/shard_map/reduce_scatter | solution.py:975
  638.8 705.1 %reduce-scatter.9.cloned.1.call-start = ((), (), s32[]{:S(2)}) async-start(), calls=%async_computation.7 | async-start | bytes 8650752 | tf_op jit(solution)/shard_map/reduce_scatter | solution.py:975
  639.4 851.7 %reduce-scatter.11.cloned.1.call-start = ((), (), s32[]{:S(2)}) async-start(), calls=%async_computation.8 | async-start | bytes 8650752 | tf_op jit(solution)/shard_map/reduce_scatter | solution.py:975
  (4 other events, 3.5 us)
Sparse Core Ops, SparseCore 0:
  24.8 65.2 all-gather.9
  93.0 75.7 all-gather.11
  171.7 76.0 all-gather.13
  250.5 75.9 all-gather.15
  329.1 76.0 all-gather.17
  627.4 136.0 reduce-scatter.18
  765.8 136.6 reduce-scatter.12
  904.9 144.8 reduce-scatter.16
  1052.2 144.6 reduce-scatter.14
  1199.2 144.6 reduce-scatter.8
  1346.3 144.7 reduce-scatter.10

commit v2 on v1

--- a/solution.py
+++ b/solution.py
@@ -395,16 +395,201 @@
     )
 
 
-TILE = 256
-
-
-def one_hot_rows(pos_row, base):
-    slot = lax.broadcasted_iota(jnp.int32, (TILE, pos_row.shape[1]), 0) + base
+def grid_of(count_dp, count_fsdp):
+    depth = 4 if count_dp % 4 == 0 else count_dp
+    cores = 2 if count_fsdp % 2 == 0 else 1
+    return {"z": depth, "y": count_dp // depth, "x": count_fsdp // cores, "c": cores}
+
+
+def sizes():
+    return grid_of(lax.axis_size("dp"), lax.axis_size("fsdp"))
+
+
+def place(grid, axis):
+    index = lax.axis_index(AXES)
+    for name in ("c", "x", "y", "z"):
+        if name == axis:
+            return index % grid[name]
+        index = index // grid[name]
+
+
+def number(grid, at):
+    return ((at["z"] * grid["y"] + at["y"]) * grid["x"] + at["x"]) * grid["c"] + at["c"]
+
+
+def move(value, grid, **steps):
+    pairs = []
+    for z in range(grid["z"]):
+        for y in range(grid["y"]):
+            for x in range(grid["x"]):
+                for c in range(grid["c"]):
+                    at = {"z": z, "y": y, "x": x, "c": c}
+                    to = {name: (at[name] + steps.get(name, 0)) % grid[name] for name in at}
+                    pairs.append((number(grid, at), number(grid, to)))
+    return lax.ppermute(value, AXES, pairs)
+
+
+def total_of(value):
+    count = lax.axis_size(AXES)
+    bit = 1
+    while bit < count:
+        value = value + lax.ppermute(value, AXES, [(d, d ^ bit) for d in range(count)])
+        bit *= 2
+    return value
+
+
+def gather_small(value):
+    count = lax.axis_size(AXES)
+    index = lax.axis_index(AXES)
+    value = value[None]
+    bit = 1
+    while bit < count:
+        other = lax.ppermute(value, AXES, [(d, d ^ bit) for d in range(count)])
+        upper = (index // bit) % 2 == 1
+        value = jnp.where(
+            upper, jnp.concatenate([other, value], 0), jnp.concatenate([value, other], 0)
+        )
+        bit *= 2
+    return value
+
+
+PLANE = ((0, 1), (1, 0), (1, 1))
+
+
+def joined(pieces):
+    return (
+        jnp.concatenate([value for value, _ in pieces], 0),
+        [offset for _, offsets in pieces for offset in offsets],
+    )
+
+
+def along_depth(piece, grid):
+    value, offsets = piece
+    steps = [piece]
+    for step in range(1, grid["z"]):
+        value = move(value, grid, z=1)
+        steps.append((value, [dict(o, z=(o["z"] - step) % grid["z"]) for o in offsets]))
+    return steps
+
+
+def over_plane(piece, grid):
+    value, offsets = piece
+    return [piece] + [
+        (move(value, grid, y=dy, x=dx), [dict(o, y=o["y"] ^ dy, x=o["x"] ^ dx) for o in offsets])
+        for dy, dx in PLANE
+    ]
+
+
+def over_cores(pieces, grid):
+    return pieces + [
+        (move(value, grid, c=1), [dict(o, c=1 - o["c"]) for o in offsets])
+        for value, offsets in pieces
+    ]
+
+
+def gather_pieces(block, grid, depth_first):
+    piece = (block[None], [{"z": 0, "y": 0, "x": 0, "c": 0}])
+    if depth_first:
+        pieces = over_plane(joined(along_depth(piece, grid)), grid)
+    else:
+        pieces = along_depth(joined(over_plane(piece, grid)), grid)
+    return over_cores(pieces, grid)
+
+
+def owners(pieces, grid):
+    own = {axis: place(grid, axis) for axis in grid}
+    found = []
+    for _, offsets in pieces:
+        for offset in offsets:
+            at = {axis: (own[axis] + offset[axis]) % grid[axis] for axis in grid}
+            found.append(number(grid, at))
+    return jnp.stack(found)
+
+
+FAST = {"z": 4, "y": 2, "x": 2, "c": 2}
+
+
+def gather_experts(value, depth_first):
+    grid = sizes()
+    if grid == FAST:
+        pieces = gather_pieces(value, grid, depth_first)
+        return [piece for piece, _ in pieces], owners(pieces, grid)
+    return gather_whole(value)
+
+
+def gather_whole(value):
+    grid = sizes()
+    if grid == FAST:
+        blocks = lax.all_gather(value, AXES, axis=0, tiled=False)
+        return [blocks], jnp.arange(blocks.shape[0], dtype=jnp.int32)
+    blocks = lax.all_gather(value, AXES, axis=1, tiled=True)
+    return [blocks[None]], jnp.zeros((1,), jnp.int32)
+
+
+def block_at(value, index, at):
+    return lax.dynamic_index_in_dim(value, index % value.shape[at], at, keepdims=False)
+
+
+def wide(value):
+    return value.astype(jnp.float32)
+
+
+def sum_cores(value, grid, at):
+    own = place(grid, "c")
+    other = move(block_at(value, own + 1, at), grid, c=1)
+    return (wide(block_at(value, own, at)) + wide(other)).astype(value.dtype)
+
+
+def sum_plane(value, grid, at, dtype):
+    y, x = place(grid, "y"), place(grid, "x")
+
+    def block(dy, dx):
+        return block_at(block_at(value, y + dy, at), x + dx, at)
+
+    total = wide(block(0, 0))
+    for dy, dx in PLANE:
+        total = total + wide(move(block(dy, dx), grid, y=dy, x=dx))
+    return total.astype(dtype)
+
+
+def sum_depth(value, grid, dtype):
+    length = grid["z"]
+    own = place(grid, "z")
+    part = block_at(value, own + length - 1, 0)
+    for step in range(1, length):
+        total = wide(block_at(value, own + 2 * length - 1 - step, 0)) + wide(move(part, grid, z=1))
+        part = total.astype(dtype if step == length - 1 else value.dtype)
+    return part
+
+
+def scatter_blocks(value, depth_first):
+    grid = sizes()
+    if grid != FAST:
+        return wide(lax.psum_scatter(value, AXES, scatter_dimension=0, tiled=False))
+    value = value.reshape((4, 2, 2, 2) + value.shape[1:])
+    value = sum_cores(value, grid, 3)
+    if depth_first:
+        return sum_plane(sum_depth(value, grid, value.dtype), grid, 0, jnp.float32)
+    return sum_depth(sum_plane(value, grid, 1, value.dtype), grid, jnp.float32)
+
+
+def by_devices(value):
+    if value.shape[0] > 1:
+        return value
+    devices = lax.axis_size(AXES)
+    return value.reshape((EXPERTS, devices, -1, value.shape[3])).transpose(1, 0, 2, 3)
+
+
+ROWS = (256, 384, 512)
+
+
+def one_hot_rows(pos_row, base, rows):
+    slot = lax.broadcasted_iota(jnp.int32, (rows, pos_row.shape[1]), 0) + base
     return (slot == pos_row).astype(jnp.float32).astype(jnp.bfloat16)
 
 
-def one_hot_columns(pos_col, base):
-    slot = lax.broadcasted_iota(jnp.int32, (pos_col.shape[0], TILE), 1) + base
+def one_hot_columns(pos_col, base, rows):
+    slot = lax.broadcasted_iota(jnp.int32, (pos_col.shape[0], rows), 1) + base
     return (slot == pos_col).astype(jnp.float32).astype(jnp.bfloat16)
 
 
@@ -432,58 +617,205 @@
     return raised / jnp.sum(raised, -1, keepdims=True)
 
 
-def expert_tile(index, normed, pos_row, up, down):
-    base = index * TILE
-    picked = mul(one_hot_rows(pos_row, base), normed).astype(jnp.bfloat16)
+def sized(count, body):
+    lower = -1
+    for rows in ROWS:
+        pl.when((count > lower) & (count <= rows))(functools.partial(body, rows))
+        lower = rows
+
+
+def assemble(refs, ids_ref, whole_ref):
+    at = 0
+    for ref in refs:
+        rows = ref.shape[2]
+        for block in range(ref.shape[0]):
+            start = pl.multiple_of(ids_ref[at] * rows, rows)
+            whole_ref[pl.ds(start, rows), :] = ref[block, 0]
+            at += 1
+
+
+class Weights:
+    def __init__(self, gathered):
+        self.arrays, self.ids = gathered
+        rows = sum(piece.shape[0] * piece.shape[2] for piece in self.arrays)
+        self.shape = (rows, self.arrays[0].shape[3])
+        self.rows = self.arrays[0].shape[2]
+
+    def specs(self):
+        return [by_owner(piece.shape) for piece in self.arrays]
+
+
+def fixed(shape):
+    return pl.BlockSpec(shape, lambda e, *_: (0,) * len(shape))
+
+
+def by_expert(shape):
+    return pl.BlockSpec((1,) + shape, lambda e, *_: (e,) + (0,) * len(shape))
+
+
+def by_owner(shape):
+    return pl.BlockSpec((shape[0], 1) + shape[2:], lambda e, *_: (0, e, 0, 0))
+
+
+def grads_shape(weights):
+    count = weights.shape[0] // weights.rows
+    return (count, EXPERTS, weights.rows, weights.shape[1])
+
+
+def expert_call(kernel, name, counts, weights, inputs, outputs, scratch, flops):
+    scalars = [counts] + [weight.ids for weight in weights]
+    arrays = [piece for weight in weights for piece in weight.arrays]
+    n_in, n_out = len(inputs), len(outputs)
+
+    def body(*refs):
+        count_ref, *ids = refs[: len(scalars)]
+        refs = refs[len(scalars) :]
+        pieces, refs = refs[: len(arrays)], refs[len(arrays) :]
+        operands, results, rest = refs[:n_in], refs[n_in : n_in + n_out], refs[n_in + n_out :]
+        expert = pl.program_id(0)
+        for at, weight in enumerate(weights):
+            own = pieces[: len(weight.arrays)]
+            pieces = pieces[len(weight.arrays) :]
+            assemble(own, ids[at], rest[at])
+        kernel(expert, count_ref[expert], *rest[: len(weights)], *operands, *results, *rest[len(weights) :])
+
+    return pl.pallas_call(
+        body,
+        grid_spec=pltpu.PrefetchScalarGridSpec(
+            num_scalar_prefetch=len(scalars),
+            grid=(EXPERTS,),
+            in_specs=[spec for weight in weights for spec in weight.specs()]
+            + [spec for _, spec in inputs],
+            out_specs=[spec for _, spec in outputs],
+            scratch_shapes=[pltpu.VMEM(weight.shape, jnp.bfloat16) for weight in weights] + scratch,
+        ),
+        out_shape=[shape for shape, _ in outputs],
+        compiler_params=pltpu.CompilerParams(vmem_limit_bytes=60 * 1024 * 1024),
+        cost_estimate=pl.CostEstimate(
+            flops=flops, bytes_accessed=20 * 10**6, transcendentals=4 * 10**6
+        ),
+        name=name,
+    )(*scalars, *arrays, *[value for value, _ in inputs])
+
+
+def struct(shape, dtype=jnp.float32):
+    return jax.ShapeDtypeStruct(shape, dtype)
+
+
+def whole_in(value):
+    return (value, fixed(value.shape))
+
+
+def whole_out(shape, dtype=jnp.float32):
+    return (struct(shape, dtype), fixed(shape))
+
+
+def expert_in(value):
+    return (value, by_expert(value.shape[1:]))
+
+
+def expert_out(shape, dtype=jnp.bfloat16):
+    return (struct((EXPERTS,) + shape, dtype), by_expert(shape))
+
+
+def spans(hidden):
+    chunk = 512
+    return [slice(start, start + chunk) for start in range(0, hidden, chunk)]
+
+
+def up_part(expert, rows, up_ref, normed_ref, posr_ref, picked_ref, inner_ref, then=None):
+    hot = one_hot_rows(posr_ref[...], expert * CAPACITY, rows)
+    picked = mul(hot, normed_ref[...]).astype(jnp.bfloat16)
+    picked_ref[0, :rows, :] = picked
     total = None
-    chunk = 512
-    for start in range(0, up.shape[1], chunk):
-        inner = mul(picked, up[:, start : start + chunk])
-        active = (inner * sigmoid(inner)).astype(jnp.bfloat16)
-        part = mul(active, down[start : start + chunk, :])
-        total = part if total is None else total + part
-    return total.astype(jnp.bfloat16)
-
-
-def expert_forward_steps(counts_ref, normed_ref, posr_ref, posc_ref, up_ref, down_ref, branch_ref):
-    expert = pl.program_id(0)
-    width = normed_ref.shape[1]
-    up = up_ref[...].reshape(width, -1)
-    down = down_ref[...].reshape(-1, width)
-
+    for span in spans(up_ref.shape[1]):
+        inner = mul(picked, up_ref[:, span])
+        inner_ref[0, :rows, span] = inner.astype(jnp.bfloat16)
+        if then is not None:
+            part = then(inner, span)
+            total = part if total is None else total + part
+    return total
+
+
+def first_up_kernel(expert, count, up_ref, normed_ref, posr_ref, picked_ref, inner_ref):
+    def run(rows):
+        up_part(expert, rows, up_ref, normed_ref, posr_ref, picked_ref, inner_ref)
+
+    sized(count, run)
+
+
+def first_up_call(counts, pos_row, normed, up):
+    length, width = normed.shape
+    return expert_call(
+        first_up_kernel,
+        "first_up",
+        counts,
+        [up],
+        [whole_in(normed), whole_in(pos_row)],
+        [expert_out((CAPACITY, width)), expert_out((CAPACITY, up.shape[1]))],
+        [],
+        5 * 10**9,
+    )
+
+
+def first_down_kernel(
+    expert, count, down_ref, inner_ref, posc_ref, resid_ref, probs_ref, route_ref, out_ref, branch_ref
+):
     @pl.when(expert == 0)
     def clear():
         branch_ref[...] = jnp.zeros_like(branch_ref)
 
-    for part in range(CAPACITY // TILE):
-
-        @pl.when(counts_ref[expert] > part * TILE)
-        def run():
-            index = expert * (CAPACITY // TILE) + part
-            outgoing = expert_tile(index, normed_ref[...], posr_ref[...], up, down)
-            branch_ref[...] += mul(one_hot_columns(posc_ref[...], index * TILE), outgoing)
-
-
-def first_forward_kernel(
-    counts_ref, normed_ref, posr_ref, posc_ref, up_ref, down_ref, resid_ref, probs_ref, route_ref,
-    out_ref, branch_ref,
-):
-    expert_forward_steps(counts_ref, normed_ref, posr_ref, posc_ref, up_ref, down_ref, branch_ref)
-
-    @pl.when(pl.program_id(0) == pl.num_programs(0) - 1)
+    def run(rows):
+        total = None
+        for span in spans(down_ref.shape[0]):
+            inner = inner_ref[0, :rows, span].astype(jnp.float32)
+            part = mul((inner * sigmoid(inner)).astype(jnp.bfloat16), down_ref[span, :])
+            total = part if total is None else total + part
+        hot = one_hot_columns(posc_ref[...], expert * CAPACITY, rows)
+        branch_ref[...] += mul(hot, total.astype(jnp.bfloat16))
+
+    sized(count, run)
+
+    @pl.when(expert == EXPERTS - 1)
     def last():
         gate = jnp.sum(probs_ref[...] * routed(route_ref[...]), -1, keepdims=True)
         out_ref[...] = resid_ref[...].astype(jnp.float32) + 0.5 * gate * branch_ref[...]
 
 
+def first_down_call(counts, pos_col, inner, resid, probs, routes, down):
+    shape = resid.shape
+    return expert_call(
+        first_down_kernel,
+        "first_down",
+        counts,
+        [down],
+        [expert_in(inner)] + [whole_in(v) for v in (pos_col, resid, probs, routes)],
+        [whole_out(shape), whole_out(shape)],
+        [],
+        5 * 10**9,
+    )
+
+
 def second_forward_kernel(
-    counts_ref, normed_ref, posr_ref, posc_ref, up_ref, down_ref, resid_ref, probs_ref, route_ref,
-    cot_ref, gain_ref, bias_ref,
-    result_ref, g4_ref, dgain_ref, dbias_ref, branch_ref,
+    expert, count, up_ref, down_ref,
+    normed_ref, posr_ref, posc_ref, resid_ref, probs_ref, route_ref, cot_ref, gain_ref, bias_ref,
+    picked_ref, inner_ref, branch_ref, result_ref, g4_ref, dgain_ref, dbias_ref,
 ):
-    expert_forward_steps(counts_ref, normed_ref, posr_ref, posc_ref, up_ref, down_ref, branch_ref)
-
-    @pl.when(pl.program_id(0) == pl.num_programs(0) - 1)
+    @pl.when(expert == 0)
+    def clear():
+        branch_ref[...] = jnp.zeros_like(branch_ref)
+
+    def run(rows):
+        def then(inner, span):
+            return mul((inner * sigmoid(inner)).astype(jnp.bfloat16), down_ref[span, :])
+
+        total = up_part(expert, rows, up_ref, normed_ref, posr_ref, picked_ref, inner_ref, then)
+        hot = one_hot_columns(posc_ref[...], expert * CAPACITY, rows)
+        branch_ref[...] += mul(hot, total.astype(jnp.bfloat16))
+
+    sized(count, run)
+
+    @pl.when(expert == EXPERTS - 1)
     def last():
         gate = jnp.sum(probs_ref[...] * routed(route_ref[...]), -1, keepdims=True)
         unit, inverse = norm_parts(resid_ref[...] + 0.5 * gate * branch_ref[...])
@@ -495,206 +827,296 @@
         g4_ref[...] = norm_slope(unit, inverse, cot, gain)
 
 
-def expert_backward_kernel(
-    counts_ref, normed_ref, posr_ref, posc_ref, up_ref, down_ref, resid_ref, probs_ref, route_ref,
-    branch_ref, slope_ref, embed_ref, router_ref, gain_ref,
-    dup_ref, ddown_ref, out_ref, dgain_ref, dbias_ref, drouter_ref,
-    low_ref, dlogits_ref, dnorm_ref, picked_ref, dpicked_ref, active_ref, dinner_ref,
-):
-    expert = pl.program_id(0)
-    width = normed_ref.shape[1]
-    up = up_ref[...].reshape(width, -1)
-    down = down_ref[...].reshape(-1, width)
-    hidden = up.shape[1]
-    chunk = 512
-
-    @pl.when(expert == 0)
-    def first():
-        chosen = routed(route_ref[...])
-        probs = probs_ref[...]
-        gate = jnp.sum(probs * chosen, -1, keepdims=True)
-        slope = slope_ref[...]
-        low_ref[...] = (0.5 * gate * slope).astype(jnp.bfloat16)
-        dgate = 0.5 * jnp.sum(slope * branch_ref[...], -1, keepdims=True)
-        dlogits = probs * (chosen - gate) * dgate
-        dlogits_ref[...] = dlogits
-        dnorm_ref[...] = split_mul(dlogits, router_ref[:width, :], NT)
-
-    def tile(part):
-        index = expert * (CAPACITY // TILE) + part
-        at = slice(part * TILE, (part + 1) * TILE)
-        hot = one_hot_rows(posr_ref[...], index * TILE)
-        picked = mul(hot, normed_ref[...]).astype(jnp.bfloat16)
-        dpicked = mul(hot, low_ref[...]).astype(jnp.bfloat16)
-        picked_ref[at, :] = picked
-        dpicked_ref[at, :] = dpicked
-        total = None
-        for start in range(0, hidden, chunk):
-            span = slice(start, start + chunk)
-            inner = mul(picked, up[:, span])
-            sigma = sigmoid(inner)
-            active_ref[at, span] = (inner * sigma).astype(jnp.bfloat16)
-            dactive = mul(dpicked, down[span, :], NT)
-            dinner = (dactive * (sigma * (1.0 + inner * (1.0 - sigma)))).astype(jnp.bfloat16)
-            dinner_ref[at, span] = dinner
-            part_sum = mul(dinner, up[:, span], NT)
-            total = part_sum if total is None else total + part_sum
-        dnorm_ref[...] += mul(one_hot_columns(posc_ref[...], index * TILE), total.astype(jnp.bfloat16))
-
-    def weight_grads(rows):
-        for start in range(0, hidden, chunk):
-            span = slice(start, start + chunk)
-            dup_ref[..., span] = (
-                mul(picked_ref[:rows, :], dinner_ref[:rows, span], TN)
-                .astype(jnp.bfloat16)
-                .reshape(dup_ref.shape[:-1] + (chunk,))
-            )
-            grads = mul(active_ref[:rows, span], dpicked_ref[:rows, :], TN).astype(jnp.bfloat16)
-            owned = ddown_ref.shape[2]
-            if owned > chunk:
-                ddown_ref[0, 0, span, :] = grads
-            else:
-                groups = slice(start // owned, (start + chunk) // owned)
-                ddown_ref[groups] = grads.reshape((chunk // owned,) + ddown_ref.shape[1:])
-
-    tile(0)
-    count = counts_ref[expert]
-
-    @pl.when(count <= TILE)
-    def small():
-        weight_grads(TILE)
-
-    @pl.when(count > TILE)
-    def large():
-        tile(1)
-        weight_grads(2 * TILE)
-
-    @pl.when(expert == pl.num_programs(0) - 1)
-    def last():
-        unit, inverse = norm_parts(resid_ref[...].astype(jnp.float32))
-        slope = dnorm_ref[...]
-        dgain_ref[...] = jnp.sum(slope * unit, 0, keepdims=True)
-        dbias_ref[...] = jnp.sum(slope, 0, keepdims=True)
-        out_ref[...] = slope_ref[...] + norm_slope(unit, inverse, slope, gain_ref[...])
-        dlogits = dlogits_ref[...]
-        drouter_ref[:, :width] = split_mul(dlogits, normed_ref[...], TN)
-        drouter_ref[:, width:] = split_mul(dlogits, embed_ref[...], TN)
-
-
-def fixed(shape):
-    return pl.BlockSpec(shape, lambda e, counts: (0,) * len(shape))
-
-
-def expert_specs(length, width, up, down):
-    return [
-        fixed((length, width)),
-        fixed((1, length)),
-        fixed((length, 1)),
-        pl.BlockSpec((up.shape[0], 1) + up.shape[2:], lambda e, counts: (0, e, 0, 0)),
-        pl.BlockSpec((down.shape[0], 1) + down.shape[2:], lambda e, counts: (0, e, 0, 0)),
-        fixed((length, width)),
-        fixed((length, 128)),
-        fixed((length, 1)),
-    ]
-
-
-def expert_call(kernel, name, extra_specs, out_specs, out_shape, scratch, flops, args):
-    counts, normed, pos_row, pos_col, up, down = args[:6]
+def second_forward_call(counts, pos_row, pos_col, normed, resid, probs, routes, cot, gain, bias, up, down):
     length, width = normed.shape
-    return pl.pallas_call(
-        kernel,
-        grid_spec=pltpu.PrefetchScalarGridSpec(
-            num_scalar_prefetch=1,
-            grid=(EXPERTS,),
-            in_specs=expert_specs(length, width, up, down) + extra_specs,
-            out_specs=out_specs,
-            scratch_shapes=scratch,
-        ),
-        out_shape=out_shape,
-        compiler_params=pltpu.CompilerParams(vmem_limit_bytes=60 * 1024 * 1024),
-        cost_estimate=pl.CostEstimate(flops=flops, bytes_accessed=30 * 10**6, transcendentals=4 * 10**6),
-        name=name,
-    )(*args)
-
-
-def first_forward(args):
-    length, width = args[1].shape
-    full = jnp.float32
-    out = jax.ShapeDtypeStruct((length, width), full)
-    return expert_call(
-        first_forward_kernel,
-        "first_forward",
-        [],
-        [fixed((length, width))] * 2,
-        [out, out],
-        [],
-        10 * 10**9,
-        args,
-    )
-
-
-def second_forward(args):
-    length, width = args[1].shape
-    full = jnp.float32
-    wide = jax.ShapeDtypeStruct((length, width), full)
-    thin = jax.ShapeDtypeStruct((1, width), full)
     return expert_call(
         second_forward_kernel,
         "second_forward",
-        [fixed((length, width)), fixed((1, width)), fixed((1, width))],
-        [fixed((length, width))] * 2 + [fixed((1, width))] * 2 + [fixed((length, width))],
-        [jax.ShapeDtypeStruct((length, width), jnp.bfloat16), wide, thin, thin, wide],
+        counts,
+        [up, down],
+        [whole_in(v) for v in (normed, pos_row, pos_col, resid, probs, routes, cot, gain, bias)],
+        [
+            expert_out((CAPACITY, width)),
+            expert_out((CAPACITY, up.shape[1])),
+            whole_out((length, width)),
+            whole_out((length, width), jnp.bfloat16),
+            whole_out((length, width)),
+            whole_out((1, width)),
+            whole_out((1, width)),
+        ],
         [],
         10 * 10**9,
-        args,
-    )
-
-
-def expert_backward(args):
-    length, width = args[1].shape
-    up, down = args[4:6]
-    hidden = up.shape[3]
-    low, full = jnp.bfloat16, jnp.float32
-    shape = jax.ShapeDtypeStruct
-    thin = shape((1, width), full)
+    )
+
+
+def enter_slope(slope_ref, probs_ref, route_ref, branch_ref, low_ref, dlogits_ref):
+    chosen = routed(route_ref[...])
+    probs = probs_ref[...]
+    gate = jnp.sum(probs * chosen, -1, keepdims=True)
+    slope = slope_ref[...]
+    low_ref[...] = (0.5 * gate * slope).astype(jnp.bfloat16)
+    dgate = 0.5 * jnp.sum(slope * branch_ref[...], -1, keepdims=True)
+    dlogits_ref[...] = probs * (chosen - gate) * dgate
+
+
+def leave_slope(
+    dnorm, dlogits, slope_ref, resid_ref, normed_ref, embed_ref, gain_ref,
+    out_ref, dgain_ref, dbias_ref, drouter_ref,
+):
+    width = resid_ref.shape[1]
+    unit, inverse = norm_parts(resid_ref[...].astype(jnp.float32))
+    dgain_ref[...] = jnp.sum(dnorm * unit, 0, keepdims=True)
+    dbias_ref[...] = jnp.sum(dnorm, 0, keepdims=True)
+    out_ref[...] = slope_ref[...] + norm_slope(unit, inverse, dnorm, gain_ref[...])
+    drouter_ref[:, :width] = split_mul(dlogits, normed_ref[...], TN)
+    drouter_ref[:, width:] = split_mul(dlogits, embed_ref[...], TN)
+
+
+def active_of(inner):
+    inner = inner.astype(jnp.float32)
+    return (inner * sigmoid(inner)).astype(jnp.bfloat16)
+
+
+def slope_of(inner):
+    inner = inner.astype(jnp.float32)
+    sigma = sigmoid(inner)
+    return sigma * (1.0 + inner * (1.0 - sigma))
+
+
+def store_rows(ref, span, value):
+    owned = ref.shape[2]
+    count = span.stop - span.start
+    if owned > count:
+        ref[0, 0, span, :] = value
+    else:
+        ref[span.start // owned : span.stop // owned] = value.reshape((count // owned,) + ref.shape[1:])
+
+
+def down_grads(rows, inner_ref, dpicked, ddown_ref):
+    for span in spans(inner_ref.shape[2]):
+        grads = mul(active_of(inner_ref[0, :rows, span]), dpicked, TN)
+        store_rows(ddown_ref, span, grads.astype(jnp.bfloat16))
+
+
+def up_grads(picked, dinner, span, dup_ref):
+    grads = mul(picked, dinner, TN).astype(jnp.bfloat16)
+    dup_ref[:, :, :, span] = grads.reshape(dup_ref.shape[:3] + (grads.shape[1],))
+
+
+def first_back_kernel(
+    expert, count, slope_ref, probs_ref, route_ref, branch_ref, posr_ref, inner_ref,
+    ddown_ref, dpicked_ref, dlogits_ref,
+    low_ref,
+):
+    @pl.when(expert == 0)
+    def first():
+        enter_slope(slope_ref, probs_ref, route_ref, branch_ref, low_ref, dlogits_ref)
+
+    def run(rows):
+        hot = one_hot_rows(posr_ref[...], expert * CAPACITY, rows)
+        dpicked = mul(hot, low_ref[...]).astype(jnp.bfloat16)
+        dpicked_ref[0, :rows, :] = dpicked
+        down_grads(rows, inner_ref, dpicked, ddown_ref)
+
+    sized(count, run)
+
+
+def first_back_call(counts, pos_row, slope, probs, routes, branch, inner, down):
+    length, width = slope.shape
+    shape = grads_shape(down)
     return expert_call(
-        expert_backward_kernel,
-        "expert_backward",
+        first_back_kernel,
+        "first_down_grads",
+        counts,
+        [],
+        [whole_in(v) for v in (slope, probs, routes, branch, pos_row)] + [expert_in(inner)],
         [
-            fixed((length, width)),
-            fixed((length, width)),
-            fixed((length, width)),
-            fixed((2 * width, 128)),
-            fixed((1, width)),
+            (struct(shape, jnp.bfloat16), by_owner(shape)),
+            expert_out((CAPACITY, width)),
+            whole_out((length, 128)),
+        ],
+        [pltpu.VMEM((length, width), jnp.bfloat16)],
+        5 * 10**9,
+    )
+
+
+def first_middle_kernel(expert, count, down_ref, dpicked_ref, picked_ref, inner_ref, dup_ref, dinner_ref):
+    def run(rows):
+        dpicked = dpicked_ref[0, :rows, :]
+        picked = picked_ref[0, :rows, :]
+        for span in spans(inner_ref.shape[2]):
+            dactive = mul(dpicked, down_ref[span, :], NT)
+            dinner = (dactive * slope_of(inner_ref[0, :rows, span])).astype(jnp.bfloat16)
+            dinner_ref[0, :rows, span] = dinner
+            up_grads(picked, dinner, span, dup_ref)
+
+    sized(count, run)
+
+
+def first_middle_call(counts, dpicked, picked, inner, up, down):
+    shape = grads_shape(up)
+    return expert_call(
+        first_middle_kernel,
+        "first_up_grads",
+        counts,
+        [down],
+        [expert_in(v) for v in (dpicked, picked, inner)],
+        [(struct(shape, jnp.bfloat16), by_owner(shape)), expert_out(inner.shape[1:])],
+        [],
+        9 * 10**9,
+    )
+
+
+def first_leave_kernel(
+    expert, count, up_ref, dinner_ref, posc_ref, dlogits_ref, router_ref, slope_ref, resid_ref, normed_ref,
+    embed_ref, gain_ref,
+    out_ref, dgain_ref, dbias_ref, drouter_ref,
+    dnorm_ref,
+):
+    width = up_ref.shape[0]
+
+    @pl.when(expert == 0)
+    def first():
+        dnorm_ref[...] = split_mul(dlogits_ref[...], router_ref[:width, :], NT)
+
+    def run(rows):
+        total = mul(dinner_ref[0, :rows, :], up_ref[...], NT).astype(jnp.bfloat16)
+        dnorm_ref[...] += mul(one_hot_columns(posc_ref[...], expert * CAPACITY, rows), total)
+
+    sized(count, run)
+
+    @pl.when(expert == EXPERTS - 1)
+    def last():
+        leave_slope(
+            dnorm_ref[...], dlogits_ref[...], slope_ref, resid_ref, normed_ref, embed_ref, gain_ref,
+            out_ref, dgain_ref, dbias_ref, drouter_ref,
+        )
+
+
+def first_leave_call(counts, pos_col, dinner, dlogits, router, slope, resid, normed, embedding, gain, up):
+    length, width = slope.shape
+    return expert_call(
+        first_leave_kernel,
+        "first_leave",
+        counts,
+        [up],
+        [expert_in(dinner)]
+        + [whole_in(v) for v in (pos_col, dlogits, router, slope, resid, normed, embedding, gain)],
+        [
+            whole_out((length, width)),
+            whole_out((1, width)),
+            whole_out((1, width)),
+            whole_out((128, 2 * width)),
+        ],
+        [pltpu.VMEM((length, width), jnp.float32)],
+        5 * 10**9,
+    )
+
+
+def second_back_kernel(
+    expert, count, up_ref, down_ref, slope_ref, probs_ref, route_ref, branch_ref, posr_ref, posc_ref, inner_ref,
+    router_ref, resid_ref, normed_ref, embed_ref, gain_ref,
+    out_ref, dgain_ref, dbias_ref, drouter_ref, dpicked_ref, dinner_ref,
+    low_ref, dlogits_ref, dnorm_ref,
+):
+    width = up_ref.shape[0]
+
+    @pl.when(expert == 0)
+    def first():
+        enter_slope(slope_ref, probs_ref, route_ref, branch_ref, low_ref, dlogits_ref)
+        dnorm_ref[...] = split_mul(dlogits_ref[...], router_ref[:width, :], NT)
+
+    def run(rows):
+        hot = one_hot_rows(posr_ref[...], expert * CAPACITY, rows)
+        dpicked = mul(hot, low_ref[...]).astype(jnp.bfloat16)
+        dpicked_ref[0, :rows, :] = dpicked
+        total = None
+        for span in spans(up_ref.shape[1]):
+            dactive = mul(dpicked, down_ref[span, :], NT)
+            dinner = (dactive * slope_of(inner_ref[0, :rows, span])).astype(jnp.bfloat16)
+            dinner_ref[0, :rows, span] = dinner
+            part = mul(dinner, up_ref[:, span], NT)
+            total = part if total is None else total + part
+        hot = one_hot_columns(posc_ref[...], expert * CAPACITY, rows)
+        dnorm_ref[...] += mul(hot, total.astype(jnp.bfloat16))
+
+    sized(count, run)
+
+    @pl.when(expert == EXPERTS - 1)
+    def last():
+        leave_slope(
+            dnorm_ref[...], dlogits_ref[...], slope_ref, resid_ref, normed_ref, embed_ref, gain_ref,
+            out_ref, dgain_ref, dbias_ref, drouter_ref,
+        )
+
+
+def second_back_call(
+    counts, pos_row, pos_col, slope, probs, routes, branch, inner, router, resid, normed, embedding, gain, up, down
+):
+    length, width = slope.shape
+    return expert_call(
+        second_back_kernel,
+        "second_back",
+        counts,
+        [up, down],
+        [whole_in(v) for v in (slope, probs, routes, branch, pos_row, pos_col)]
+        + [expert_in(inner)]
+        + [whole_in(v) for v in (router, resid, normed, embedding, gain)],
+        [
+            whole_out((length, width)),
+            whole_out((1, width)),
+            whole_out((1, width)),
+            whole_out((128, 2 * width)),
+            expert_out((CAPACITY, width)),
+            expert_out(inner.shape[1:]),
         ],
         [
-            pl.BlockSpec((up.shape[0], 1) + up.shape[2:], lambda e, counts: (0, e, 0, 0)),
-            pl.BlockSpec((down.shape[0], 1) + down.shape[2:], lambda e, counts: (0, e, 0, 0)),
-            fixed((length, width)),
-            fixed((1, width)),
-            fixed((1, width)),
-            fixed((128, 2 * width)),
+            pltpu.VMEM((length, width), jnp.bfloat16),
+            pltpu.VMEM((length, 128), jnp.float32),
+            pltpu.VMEM((length, width), jnp.float32),
         ],
-        [
-            shape(up.shape, low),
-            shape(down.shape, low),
-            shape((length, width), full),
-            thin,
-            thin,
-            shape((128, 2 * width), full),
-        ],
-        [
-            pltpu.VMEM((length, width), low),
-            pltpu.VMEM((length, 128), full),
-            pltpu.VMEM((length, width), full),
-            pltpu.VMEM((CAPACITY, width), low),
-            pltpu.VMEM((CAPACITY, width), low),
-            pltpu.VMEM((CAPACITY, hidden), low),
-            pltpu.VMEM((CAPACITY, hidden), low),
-        ],
-        28 * 10**9,
-        args,
-    )
+        10 * 10**9,
+    )
+
+
+def second_grads_kernel(expert, count, picked_ref, inner_ref, dpicked_ref, dinner_ref, out_ref):
+    def run(rows):
+        picked = picked_ref[0, :rows, :]
+        dpicked = dpicked_ref[0, :rows, :]
+        owned = out_ref.shape[2] // 2
+        width = dpicked.shape[1]
+        for span in spans(inner_ref.shape[2]):
+            chunk = span.stop - span.start
+            grads = mul(picked, dinner_ref[0, :rows, span], TN).astype(jnp.bfloat16)
+            out_ref[:, :, :owned, span] = grads.reshape((-1, 1, owned, chunk))
+            grads = mul(active_of(inner_ref[0, :rows, span]), dpicked, TN).astype(jnp.bfloat16)
+            across = inner_ref.shape[2] // width
+            if owned >= chunk:
+                at = span.start // owned * width
+                out_ref[0, 0, owned:, at : at + width] = grads
+                continue
+            first = span.start // (across * owned)
+            count = chunk // (across * owned)
+            grads = grads.reshape((count, 1, across, owned, width))
+            for at in range(across):
+                out_ref[first : first + count, :, owned:, at * width : (at + 1) * width] = grads[:, :, at]
+
+    sized(count, run)
+
+
+def second_grads_call(counts, picked, inner, dpicked, dinner, devices):
+    hidden, width = inner.shape[2], picked.shape[2]
+    shape = (devices, EXPERTS, 2 * width // devices, hidden)
+    return expert_call(
+        second_grads_kernel,
+        "second_grads",
+        counts,
+        [],
+        [expert_in(v) for v in (picked, inner, dpicked, dinner)],
+        [(struct(shape, jnp.bfloat16), by_owner(shape))],
+        [],
+        10 * 10**9,
+    )[0]
 
 
 def enter_kernel(resid_ref, embed_ref, router_ref, gain_ref, bias_ref, normed_ref, probs_ref):
@@ -713,6 +1135,7 @@
             jax.ShapeDtypeStruct((length, 128), jnp.float32),
         ],
         compiler_params=pltpu.CompilerParams(vmem_limit_bytes=40 * 1024 * 1024),
+        cost_estimate=pl.CostEstimate(flops=10**9, bytes_accessed=4 * 10**6, transcendentals=10**5),
         name="expert_enter",
     )(resid, embedding, router, gain, bias)
 
@@ -952,35 +1375,28 @@
     )(slope, dshift, depth, stats, sums, bgain, joined, normed, resid, gain, gated_in, taps, masks)
 
 
-def total_of(value):
-    count = lax.axis_size(AXES)
-    bit = 1
-    while bit < count:
-        value = value + lax.ppermute(value, AXES, [(d, d ^ bit) for d in range(count)])
-        bit *= 2
-    return value
-
-
-def gather_experts(value):
-    blocks = lax.all_gather(value, AXES, axis=0, tiled=False)
-    if value.shape[1] % 16:
-        blocks = blocks.transpose(1, 0, 2, 3).reshape((1, EXPERTS, -1, value.shape[2]))
-    return blocks
-
-
-def scatter_experts(value):
-    devices = lax.axis_size(AXES)
-    if value.shape[0] == 1:
-        value = value.reshape((EXPERTS, devices, -1, value.shape[3])).transpose(1, 0, 2, 3)
-    return lax.psum_scatter(value, AXES, scatter_dimension=0, tiled=False).astype(jnp.float32)
-
-
 def gather_rows(value):
     return lax.all_gather(value, AXES, axis=0, tiled=True)
 
 
-def scatter_rows(value):
-    return lax.psum_scatter(value, AXES, scatter_dimension=0, tiled=True)
+def scatter_small(value):
+    return scatter_blocks(value.reshape((lax.axis_size(AXES), -1) + value.shape[1:]), False)
+
+
+def gathered_count(devices):
+    return devices if sizes() == FAST else 1
+
+
+def scatter_second(value, devices, width):
+    if value.shape[0] == 1:
+        up = by_devices(value[:, :, :width])
+        down = value[0, :, width:].reshape(EXPERTS, width, -1, width).transpose(0, 2, 1, 3)
+        down = by_devices(down.reshape(1, EXPERTS, -1, width))
+        return [wide(lax.psum_scatter(part, AXES, scatter_dimension=0)) for part in (up, down)]
+    total = wide(lax.psum_scatter(value, AXES, scatter_dimension=0, tiled=False))
+    owned = width // devices
+    down = total[:, owned:].reshape(EXPERTS, owned, -1, width).transpose(0, 2, 1, 3)
+    return [total[:, :owned], down.reshape(EXPERTS, -1, width)]
 
 
 def router_columns(router):
@@ -1064,17 +1480,17 @@
     )
     n_small = small.shape[1]
     small = jnp.pad(small, ((0, 0), (0, 128 - n_small)))
+    first_ups = Weights(gather_experts(first_up, True))
+    first_downs = Weights(gather_experts(first_down, False))
+    small = gather_small(small).reshape(width, 128)[:, :n_small]
     packed = gather_rows(
-        jnp.concatenate(
-            [small, project_in, relative_weight, attend_out, gated_in, point_out], 1
-        )
-    )
-    small = packed[:, :n_small]
+        jnp.concatenate([project_in, relative_weight, attend_out, gated_in, point_out], 1)
+    )
     rows = small[:, : n_vec + KERNEL].T
     col = n_vec + KERNEL
     first_router_full = router_rows(small[:, col : col + 2 * EXPERTS], devices)
     second_router_full = router_rows(small[:, col + 2 * EXPERTS : col + 4 * EXPERTS], devices)
-    at = 128
+    at = 0
     project_full = packed[:, at : at + 3 * width]
     at = at + 3 * width
     relative_full = packed[:, at : at + width]
@@ -1099,8 +1515,8 @@
     masks = tap_masks(segments)
     first_places = places(routes_first)
     second_places = places(routes_second)
-    first_ups, first_downs = gather_experts(first_up), gather_experts(first_down)
-    second_ups, second_downs = gather_experts(second_up), gather_experts(second_down)
+    second_ups = Weights(gather_whole(second_up))
+    second_downs = Weights(gather_whole(second_down))
     attend_full = (
         vec(4),
         vec(5),
@@ -1114,18 +1530,11 @@
     tables = (jnp.concatenate([cosine, sine], 1).astype(jnp.bfloat16), cosine, sine)
 
     first_normed, first_probs = expert_enter(inputs, embedding, first_router_full, vec(0), vec(1))
-    first_common = (
-        first_places[0],
-        first_normed,
-        first_places[1],
-        first_places[2],
-        first_ups,
-        first_downs,
-        inputs,
-        first_probs,
-        routes_first,
-    )
-    first_resid, first_branch = first_forward(first_common)
+    counts, pos_row, pos_col = first_places
+    first_picked, first_inner = first_up_call(counts, pos_row, first_normed, first_ups)
+    first_resid, first_branch = first_down_call(
+        counts, pos_col, first_inner, inputs, first_probs, routes_first, first_downs
+    )
     attend_kept = attention_forward(first_resid, segments, attend_full, tables)
     attend_resid, conv_normed, joined, depth, stats = conv_front(
         first_resid, attend_kept[6], attend_out_full, vec(8), vec(9), gated_full, taps, masks
@@ -1135,25 +1544,31 @@
         frames, depth, stats, vec(10), vec(11), point_full, attend_resid,
         embedding, second_router_full, vec(2), vec(3),
     )
-    second_common = (
-        second_places[0],
-        second_normed,
-        second_places[1],
-        second_places[2],
-        second_ups,
-        second_downs,
-        conv_resid,
-        second_probs,
-        routes_second,
-    )
-    result, slope, final_gain_grad, final_bias_grad, second_branch = second_forward(
-        second_common + (cotangent, vec(12), vec(13))
-    )
-    second_dup, second_ddown, slope, dgain_second, dbias_second, drouter_second = expert_backward(
-        second_common + (second_branch, slope, embedding, second_router_full, vec(2))
-    )
-    second_up_grad, second_down_grad = scatter_experts(second_dup), scatter_experts(second_ddown)
+    (
+        second_picked,
+        second_inner,
+        second_branch,
+        result,
+        slope,
+        final_gain_grad,
+        final_bias_grad,
+    ) = second_forward_call(
+        *second_places, second_normed, conv_resid, second_probs, routes_second,
+        cotangent, vec(12), vec(13), second_ups, second_downs,
+    )
+    slope, dgain_second, dbias_second, drouter_second, dpicked, dinner = second_back_call(
+        *second_places, slope, second_probs, routes_second, second_branch, second_inner,
+        second_router_full, conv_resid, second_normed, embedding, vec(2), second_ups, second_downs,
+    )
     dshift, dpoint, sums = conv_turn(frames, slope, depth, stats, vec(10), vec(11), point_full)
+    sums, dpicked = lax.optimization_barrier((sums, dpicked))
+    second_large = scatter_second(
+        second_grads_call(
+            second_places[0], second_picked, second_inner, dpicked, dinner, gathered_count(devices)
+        ),
+        devices,
+        width,
+    )
     sums = total_of(sums)
     slope, dgated, dtaps, dgain_depth, dbias_depth = conv_back(
         frames, slope, dshift, depth, stats, sums, vec(10), joined, conv_normed,
@@ -1163,12 +1578,21 @@
         first_resid, slope, attend_full, tables, attend_kept
     )
     drel = drel.reshape(2, width // 2, width).transpose(1, 0, 2).reshape(width, width)
-    matrices = jnp.concatenate([dpq, dpk, dpv, drel, dao, dgated, dpoint], 1).astype(jnp.bfloat16)
-    matrices = scatter_rows(matrices).astype(jnp.float32)
-    first_dup, first_ddown, slope, dgain_first, dbias_first, drouter_first = expert_backward(
-        first_common + (first_branch, slope, embedding, first_router_full, vec(0))
-    )
-    first_up_grad, first_down_grad = scatter_experts(first_dup), scatter_experts(first_ddown)
+    matrices = scatter_small(
+        jnp.concatenate([dpq, dpk, dpv, drel, dao, dgated, dpoint], 1).astype(jnp.bfloat16)
+    )
+    first_ddown, dpicked, dlogits = first_back_call(
+        counts, pos_row, slope, first_probs, routes_first, first_branch, first_inner, first_downs
+    )
+    first_down_grad = scatter_blocks(by_devices(first_ddown), True)
+    first_dup, dinner = first_middle_call(
+        counts, dpicked, first_picked, first_inner, first_ups, first_downs
+    )
+    first_up_grad = scatter_blocks(by_devices(first_dup), False)
+    slope, dgain_first, dbias_first, drouter_first = first_leave_call(
+        counts, pos_col, dinner, dlogits, first_router_full, slope, inputs, first_normed, embedding,
+        vec(0), first_ups,
+    )
 
     def columns_of(grad):
         return (
@@ -1178,7 +1602,7 @@
             .reshape(width, 2 * EXPERTS)
         )
 
-    small_grad = scatter_rows(
+    small_grad = scatter_small(
         jnp.concatenate(
             [
                 jnp.concatenate(
@@ -1237,12 +1661,12 @@
         small_grad[:, 12 : 12 + KERNEL].T,
         own_sums[0],
         own_sums[1],
-        matrices[:, 7 * width : 8 * width],
+        matrices[:, 7 * width :],
         vector(2),
         vector(3),
         router_of(12 + KERNEL + 2 * EXPERTS),
-        second_up_grad,
-        second_down_grad,
+        second_large[0],
+        second_large[1],
         vector(10),
         vector(11),
     )

time: 1510 us -> 727 us (0.48)
  waiting for transfers between devices: 1090 us -> 213 us
  starting transfers between devices: 13.6 us -> 75.6 us
  other arithmetic: 25.8 us -> 42 us
    reduce_scatter x5 -> x1, waiting for transfers between devices: 706 us -> 0.01 us  [scatter_second(): lax.psum_scatter(value, AXES, scatter_dimension=0, tiled=False)]
    ppermute x0 -> x53, waiting for transfers between devices: none -> 190 us  [the longest x48 159 us: move(): return lax.ppermute(value, AXES, pairs)]
    all_gather x4 -> x2, waiting for transfers between devices: 184 us -> 3.51 us  [gather_whole(): blocks = lax.all_gather(value, AXES, axis=0, tiled=False)]
    unnamed x12 -> x4, waiting for transfers between devices: 127 us -> 1.41 us
    ppermute x0 -> x53, starting transfers between devices: none -> 63.4 us  [the longest x48 46.4 us: move(): return lax.ppermute(value, AXES, pairs)]
    all_gather x1, waiting for transfers between devices: 51.3 us -> 0.01 us  [gather_rows(): return lax.all_gather(value, AXES, axis=0, tiled=True)]
    pallas_call x4 -> x8, Pallas kernels: 134 us -> 144 us  [expert_call(): pl.pallas_call(body, grid_spec=pltpu.PrefetchScalarGridSpec(num_scalar_pr...]
  transfers between devices with their start and end apart: 21 -> 67, of which waited for: 20 -> 31; matrix products, arithmetic and copies ran while one was open for 4% -> 14% of each run, Pallas kernels for 6% -> 32%
where the time goes in v2:
time: 727 us; the launch traced here: 721 us
  Pallas kernels  306 us (42%)
  waiting for transfers between devices  213 us (29%)
  starting transfers between devices  75.6 us (10%)
  local copies, waits for them, and re-layouts  67.8 us (9%)
  other arithmetic  42 us (6%)
  between operations  15.5 us (2%)
    ppermute x48, waiting for transfers between devices, move(): return lax.ppermute(value, AXES, pairs)  159 us
    pallas_call x8, Pallas kernels, expert_call(): pl.pallas_call(body, grid_spec=pltpu.PrefetchScalarGridSpec(num_scalar_pr...  144 us
    pallas_call x1, Pallas kernels, attention_backward(): pl.pallas_call(attend_backward_kernel, grid=(pairs,), in_specs=[pl.BlockS...  59.1 us
    pallas_call x1, Pallas kernels, attention_forward(): pl.pallas_call(attend_forward_kernel, grid=(pairs,), in_specs=[whole((len...  46.8 us
    ppermute x48, starting transfers between devices, move(): return lax.ppermute(value, AXES, pairs)  46.4 us
    ppermute x5, waiting for transfers between devices, gather_small(): other = lax.ppermute(value, AXES, [(d, d ^ bit) for d in range(count)])  30.6 us
    pallas_call x1, Pallas kernels, conv_back(): pl.pallas_call(functools.partial(conv_back_kernel, frames), out_shape=[sh...  26.1 us
    ppermute x10, waiting for transfers between devices, total_of(): lax.ppermute(value, AXES, [(d, d ^ bit) for d in range(count)])  18.3 us
  transfers between devices with their start and end apart: 67, of which 31 were waited for; matrix products, arithmetic and copies ran while one was open for 14% of the time, Pallas kernels for 32%

profile of v2, /device:TPU:0, one launch (start us, length us, event | category | flops | bytes accessed | tf_op | source)
XLA Modules:
  0.0 721.0 jit_solution(950866898662311711)
XLA Ops:
  13.2 3.0 collective-permute-start
  37.6 27.9 %collective-permute-done.11 = bf16[1,4,16,2048]{3,2,1,0:T(8,128)(2,1)S(1)} collective-permute-done((bf16[1,4,16,2048]{3,2,1,0:T(8,128)(2,1)S(1)}, bf16[1,4,16,2048]{3,2,1,0:T(8,128)(2,1)S(1)}, u32[]{:S(2)}, u32[]{:S(2)}) %collective-permute-start.11) | collective-permute-done | bytes 262176 | tf_op jit(solution)/shard_map/ppermute | solution.py:429
  66.7 7.1 collective-permute-done.12
  78.8 26.8 %collective-permute-done.21 = bf16[2,16,128]{2,1,0:T(8,128)(2,1)S(1)} collective-permute-done((bf16[2,16,128]{2,1,0:T(8,128)(2,1)S(1)}, bf16[2,16,128]{2,1,0:T(8,128)(2,1)S(1)}, u32[]{:S(2)}, u32[]{:S(2)}) %collective-permute-start.21) | collective-permute-done | bytes 8224 | tf_op jit(solution)/shard_map/ppermute | solution.py:447
  109.3 12.4 %collective-permute-start.23 = (bf16[8,16,128]{2,1,0:T(8,128)(2,1)S(1)}, bf16[8,16,128]{2,1,0:T(8,128)(2,1)S(1)}, u32[]{:S(2)}, u32[]{:S(2)}) collective-permute-start(bf16[8,16,128]{2,1,0:T(8,128)(2,1)S(1)} %maximum_select_fusion.2), channel_id=1, source_target_pairs={{0,8},{1,9},{2,10},{3,11},{4,12},{5,13},{6,14},{7,15},{8,0},{9,1},... | collective-permute-start | bytes 98312 | tf_op jit(solution)/shard_map/ppermute | solution.py:447
  127.0 2.7 collective-permute-done.24
  135.5 4.2 collective-permute-done.15.refs_5_
  146.4 15.2 %collective-permute-done.5.refs_5_ = bf16[4,4,64,512]{3,2,1,0:T(8,128)(2,1)} collective-permute-done((bf16[4,4,64,512]{3,2,1,0:T(8,128)(2,1)}, bf16[4,4,64,512]{3,2,1,0:T(8,128)(2,1)}, u32[]{:S(2)}, u32[]{:S(2)}) %collective-permute-start.5) | collective-permute-done | bytes 1048608 | tf_op jit(solution)/shard_map/ppermute | solution.py:429
  167.0 11.8 %first_up.1 = (bf16[4,512,512]{2,1,0:T(8,128)(2,1)}, bf16[4,512,2048]{2,1,0:T(8,128)(2,1)}) custom-call(s32[4]{0:T(128)} %convert_element_type.332.refs_0_, s32[32]{0:T(128)} %stack.257.refs_1_, bf16[4,4,16,2048]{3,2,1,0:T(8,128)(2,1)} %pad_maximum_fusion.1.refs_2_, bf16[4,4,16,2048]{3,2,1,0:T(8,128)(2,1)} %collective-permute-done.13.refs_3_, ...), custom_call_target="tpu_custom_call" | custom-call | flops 5000000000 | bytes 20000000 | tf_op jit(solution)/shard_map/first_up/pallas_call | solution.py:682
  178.9 14.5 %first_down.1 = (f32[1024,512]{1,0:T(8,128)}, f32[1024,512]{1,0:T(8,128)}) custom-call(s32[4]{0:T(128)} %convert_element_type.332.refs_0_, s32[32]{0:T(128)} %stack.256.refs_1_, bf16[4,4,64,512]{3,2,1,0:T(8,128)(2,1)} %copy-done.8, bf16[4,4,64,512]{3,2,1,0:T(8,128)(2,1)} %collective-permute-done.3.refs_3_, ...), custom_call_target="tpu_custom_call" | custom-call | flops 5000000000 | bytes 20000000 | tf_op jit(solution)/shard_map/first_down/pallas_call | solution.py:682
  196.9 2.7 slice.269.pq_ref.pk_ref.pv_ref
  201.9 46.8 %attend_forward.1 = (bf16[1024,512]{1,0:T(8,128)(2,1)}, bf16[1024,512]{1,0:T(8,128)(2,1)}, bf16[1024,512]{1,0:T(8,128)(2,1)}, bf16[1024,512]{1,0:T(8,128)(2,1)},...) custom-call(f32[1024,512]{1,0:T(8,128)} %get-tuple-element.94.resid_ref, ...), custom_call_target="tpu_custom_call" | custom-call | flops 24000000000 | bytes 30000000 | tf_op jit(solution)/shard_map/attend_forward/pallas_call | solution.py:272
  248.7 16.7 %conv_front.1 = (f32[1024,512]{1,0:T(8,128)}, bf16[1024,512]{1,0:T(8,128)(2,1)}, f32[1024,1024]{1,0:T(8,128)}, f32[1024,512]{1,0:T(8,128)}, f32[2,512]{1,0:T(2,128)}) custom-call(f32[1024,512]{1,0:T(8,128)} %get-tuple-element.94.resid_ref, bf16[1024,512]{1,0:T(8,128)(2,1)} %get-tuple-element.95.ctx_ref, bf16[512,512]{1,0:T(8,128)(2,1)} %get-tuple-element.258.ao_ref, ...), custom_call_target="tpu_custom_call" | custom-call | flops 4000000000 | bytes 16000000 | tf_op jit(solution)/shard_map/conv_front/pallas_call | solution.py:1205
  269.0 3.6 collective-permute-done.26
  277.2 3.1 collective-permute-done.28
  285.4 6.1 conv_tail.1
  291.5 3.5 all-gather.10.cloned.1.call-done
  295.5 24.0 %second_forward.1 = (bf16[4,512,512]{2,1,0:T(8,128)(2,1)}, bf16[4,512,2048]{2,1,0:T(8,128)(2,1)}, f32[1024,512]{1,0:T(8,128)}, bf16[1024,512]{1,0:T(8,128)(2,1)}...) custom-call(s32[4]{0:T(128)} %convert_element_type.330.refs_0_, s32[32]{0:T(128)} %iota.78.refs_1_.refs_2_, ...), custom_call_target="tpu_custom_call" | custom-call | flops 10000000000 | bytes 20000000 | tf_op jit(solution)/shard_map/second_forward/pallas_call | solution.py:682
  320.1 27.4 %second_back.1 = (f32[1024,512]{1,0:T(8,128)}, f32[1,512]{1,0:T(1,128)}, f32[1,512]{1,0:T(1,128)}, f32[128,1024]{1,0:T(8,128)}, bf16[4,512,512]{2,1,0:T(8,128)(2,1)}, /*index=5*/bf16[4,512,2048]{2,1,0:T(8,128)(2,1)}) custom-call(s32[4]{0:T(128)} %convert_element_type.330.refs_0_, s32[32]{0:T(128)} %iota.84.refs_1_.refs_2_, s32[32]{0:T(128)} %iota.84.refs_1_.refs_2_, ...), custom_call_target="tpu_custom_call" | custom-call | flops 10000000000 | bytes 20000000 | tf_op jit(solution)/shard_map/second_back/pallas_call | solution.py:682
  347.5 5.7 conv_turn.1
  353.2 17.1 %second_grads.1 = bf16[32,4,32,2048]{3,2,1,0:T(8,128)(2,1)} custom-call(s32[4]{0:T(128)} %convert_element_type.330.refs_0_, bf16[4,512,512]{2,1,0:T(8,128)(2,1)} %get-tuple-element.151.refs_1_, bf16[4,512,2048]{2,1,0:T(8,128)(2,1)} %get-tuple-element.106.refs_11_.refs_2_, bf16[4,512,512]{2,1,0:T(8,128)(2,1)} %get-tuple-element.152.refs_3_, ...), custom_call_target="tpu_custom_call" | custom-call | flops 10000000000 | bytes 20000000 | tf_op jit(solution)/shard_map/second_grads/pallas_call | solution.py:682
  372.2 3.4 collective-permute-start.31
  384.4 2.9 collective-permute-start.34
  389.9 26.1 %conv_back.1 = (f32[1024,512]{1,0:T(8,128)}, f32[512,1024]{1,0:T(8,128)}, f32[15,512]{1,0:T(8,128)}, f32[1,512]{1,0:T(1,128)}, f32[1,512]{1,0:T(1,128)}) custom-call(f32[1024,512]{1,0:T(8,128)} %get-tuple-element.107.slope_ref, f32[1024,512]{1,0:T(8,128)} %get-tuple-element.108.dshift_ref, f32[1024,512]{1,0:T(8,128)} %get-tuple-element.96.depth_ref, ...), custom_call_target="tpu_custom_call" | custom-call | flops 6000000000 | bytes 20000000 | tf_op jit(solution)/shard_map/conv_back/pallas_call | solution.py:1357
  416.0 59.1 %attend_backward.1 = (f32[1024,512]{1,0:T(8,128)}, f32[512,512]{1,0:T(8,128)}, f32[512,512]{1,0:T(8,128)}, f32[512,512]{1,0:T(8,128)}, f32[512,512]{1,0:T(8,128)...) custom-call(bf16[8,1024,1024]{2,1,0:T(8,128)(2,1)} %get-tuple-element.1, ...), custom_call_target="tpu_custom_call" | custom-call | flops 40000000000 | bytes 40000000 | tf_op jit(solution)/shard_map/attend_backward/pallas_call | solution.py:327
  484.6 14.0 %first_down_grads.1 = (bf16[32,4,64,512]{3,2,1,0:T(8,128)(2,1)}, bf16[4,512,512]{2,1,0:T(8,128)(2,1)}, f32[1024,128]{1,0:T(8,128)}) custom-call(s32[4]{0:T(128)} %convert_element_type.332.refs_0_, f32[1024,512]{1,0:T(8,128)} %get-tuple-element.120.refs_1_.refs_14_, f32[1024,128]{1,0:T(8,128)} %copy-done.4, s32[1024,1]{1,0:T(8,128)} %copy-done.7, ...), custom_call_target="tpu_custom_call" | custom-call | flops 5000000000 | bytes 20000000 | tf_op jit(solution)/shard_map/first_down_grads/pallas_call | solution.py:682
  498.6 19.2 %first_up_grads.1 = (bf16[32,4,16,2048]{3,2,1,0:T(8,128)(2,1)}, bf16[4,512,2048]{2,1,0:T(8,128)(2,1)}) custom-call(s32[4]{0:T(128)} %convert_element_type.332.refs_0_, s32[32]{0:T(128)} %stack.256.refs_1_, bf16[4,4,64,512]{3,2,1,0:T(8,128)(2,1)} %copy-done.8, bf16[4,4,64,512]{3,2,1,0:T(8,128)(2,1)} %collective-permute-done.3.refs_3_, ...), custom_call_target="tpu_custom_call" | custom-call | flops 8999999488 | bytes 20000000 | tf_op jit(solution)/shard_map/first_up_grads/pallas_call | solution.py:682
  517.9 16.4 %first_leave.1 = (f32[1024,512]{1,0:T(8,128)}, f32[1,512]{1,0:T(1,128)}, f32[1,512]{1,0:T(1,128)}, f32[128,1024]{1,0:T(8,128)}) custom-call(s32[4]{0:T(128)} %convert_element_type.332.refs_0_, s32[32]{0:T(128)} %stack.257.refs_1_, bf16[4,4,16,2048]{3,2,1,0:T(8,128)(2,1)} %pad_maximum_fusion.1.refs_2_, ...), custom_call_target="tpu_custom_call" | custom-call | flops 5000000000 | bytes 20000000 | tf_op jit(solution)/shard_map/first_leave/pallas_call | solution.py:682
  542.1 4.5 collective-permute-start.36
  548.2 2.6 dynamic-slice_bitcast_fusion
  550.8 4.1 collective-permute-done.38
  555.0 6.8 constant_dynamic-slice_fusion.4
  564.8 4.7 collective-permute-done.40
  570.3 4.9 collective-permute-done.41
  577.3 3.4 collective-permute-start.59
  583.9 8.4 %collective-permute-done.57 = bf16[4,16,4096]{2,1,0:T(8,128)(2,1)S(1)} collective-permute-done((bf16[4,16,4096]{2,1,0:T(8,128)(2,1)}, bf16[4,16,4096]{2,1,0:T(8,128)(2,1)S(1)}, u32[]{:S(2)}, u32[]{:S(2)}) %collective-permute-start.57) | collective-permute-done | bytes 524320 | tf_op jit(solution)/shard_map/ppermute | solution.py:429
  592.3 8.6 %collective-permute-done.58 = bf16[4,16,4096]{2,1,0:T(8,128)(2,1)S(1)} collective-permute-done((bf16[4,16,4096]{2,1,0:T(8,128)(2,1)}, bf16[4,16,4096]{2,1,0:T(8,128)(2,1)S(1)}, u32[]{:S(2)}, u32[]{:S(2)}) %collective-permute-start.58) | collective-permute-done | bytes 524320 | tf_op jit(solution)/shard_map/ppermute | solution.py:429
  602.3 5.2 fusion
  607.8 4.1 fusion.1
  616.9 16.6 %collective-permute-done.50 = bf16[2,2,4,64,512]{4,3,2,1,0:T(8,128)(2,1)S(1)} collective-permute-done((bf16[2,2,4,64,512]{4,3,2,1,0:T(8,128)(2,1)S(1)}, bf16[2,2,4,64,512]{4,3,2,1,0:T(8,128)(2,1)S(1)}, u32[]{:S(2)}, u32[]{:S(2)}) %collective-permute-start.50) | collective-permute-done | bytes 1048608 | tf_op jit(solution)/shard_map/ppermute | solution.py:429
  633.9 4.4 collective-permute-done.43
  638.3 18.4 %collective-permute-done.44 = bf16[4,4,16,2048]{3,2,1,0:T(8,128)(2,1)S(1)} collective-permute-done((bf16[4,4,16,2048]{3,2,1,0:T(8,128)(2,1)S(1)}, bf16[4,4,16,2048]{3,2,1,0:T(8,128)(2,1)S(1)}, u32[]{:S(2)}, u32[]{:S(2)}) %collective-permute-start.44) | collective-permute-done | bytes 1048608 | tf_op jit(solution)/shard_map/ppermute | solution.py:429
  659.4 4.0 collective-permute-start.62
  663.5 3.7 collective-permute-done.46
  667.3 2.6 collective-permute-start.47
  674.7 3.7 collective-permute-done.47
  679.2 20.3 %collective-permute-done.52 = bf16[2,2,4,64,512]{4,3,2,1,0:T(8,128)(2,1)S(1)} collective-permute-done((bf16[2,2,4,64,512]{4,3,2,1,0:T(8,128)(2,1)S(1)}, bf16[2,2,4,64,512]{4,3,2,1,0:T(8,128)(2,1)S(1)}, u32[]{:S(2)}, u32[]{:S(2)}) %collective-permute-start.52) | collective-permute-done | bytes 1048608 | tf_op jit(solution)/shard_map/ppermute | solution.py:429
  706.4 3.4 collective-permute-done.54
  (364 shorter events, 147.9 us)
Async XLA Ops:
  7.2 186.2 %all-gather.6.cloned.1.call-start = ((), (), s32[]{:S(2)}) async-start(), calls=%async_computation.1 | async-start | bytes 4325376 | tf_op jit(solution)/shard_map/all_gather | solution.py:1379
  11.7 279.8 %all-gather.8.cloned.1.call-start = ((), (), s32[]{:S(2)}) async-start(), calls=%async_computation.3 | async-start | bytes 8650752 | tf_op jit(solution)/shard_map/all_gather | solution.py:523
  12.5 282.6 %all-gather.10.cloned.1.call-start = ((), (), s32[]{:S(2)}) async-start(), calls=%async_computation.4 | async-start | bytes 8650752 | tf_op jit(solution)/shard_map/all_gather | solution.py:523
  13.2 697.5 %reduce-scatter.2.cloned.1.call-start = ((), (), s32[]{:S(2)}) async-start(), calls=%async_computation.2 | async-start | bytes 17301504 | tf_op jit(solution)/shard_map/reduce_scatter | solution.py:1396
  13.2 19.6 %collective-permute-start = (bf16[1,4,64,512]{3,2,1,0:T(8,128)(2,1)}, bf16[1,4,64,512]{3,2,1,0:T(8,128)(2,1)S(1)}, u32[]{:S(2)}, u32[]{:S(2)}) collective-permute-start(bf16[1,4,64,512]{3,2,1,0:T(8,128)(2,1)} %bitcast.276), channel_id=1, source_target_pairs={{0,2},{1,3},{2,0},{3,1},{4,6},{5,7},{6,4},{7,5},{8,10},{9,11},{10,... | collective-permute-start | bytes 786440 | tf_op jit(solution)/shard_map/ppermute | solution.py:429
  16.2 16.6 %collective-permute-start.1 = (bf16[1,4,64,512]{3,2,1,0:T(8,128)(2,1)}, bf16[1,4,64,512]{3,2,1,0:T(8,128)(2,1)S(1)}, u32[]{:S(2)}, u32[]{:S(2)}) collective-permute-start(bf16[1,4,64,512]{3,2,1,0:T(8,128)(2,1)} %bitcast.277), channel_id=1, source_target_pairs={{0,4},{1,5},{2,6},{3,7},{4,0},{5,1},{6,2},{7,3},{8,12},{9,13},{10,... | collective-permute-start | bytes 786440 | tf_op jit(solution)/shard_map/ppermute | solution.py:429
  17.8 15.1 %collective-permute-start.2 = (bf16[1,4,64,512]{3,2,1,0:T(8,128)(2,1)}, bf16[1,4,64,512]{3,2,1,0:T(8,128)(2,1)S(1)}, u32[]{:S(2)}, u32[]{:S(2)}) collective-permute-start(bf16[1,4,64,512]{3,2,1,0:T(8,128)(2,1)} %bitcast.278), channel_id=1, source_target_pairs={{0,6},{1,7},{2,4},{3,5},{4,2},{5,3},{6,0},{7,1},{8,14},{9,15},{10,... | collective-permute-start | bytes 786440 | tf_op jit(solution)/shard_map/ppermute | solution.py:429
  17.8 17.8 %collective-permute-start.10 = (bf16[1,4,16,2048]{3,2,1,0:T(8,128)(2,1)}, bf16[1,4,16,2048]{3,2,1,0:T(8,128)(2,1)S(1)}, u32[]{:S(2)}, u32[]{:S(2)}) collective-permute-start(bf16[1,4,16,2048]{3,2,1,0:T(8,128)(2,1)} %bitcast.280), channel_id=1, source_target_pairs={{0,8},{1,9},{2,10},{3,11},{4,12},{5,13},{6,14},{7,15},{8,16},{9,17... | collective-permute-start | bytes 786440 | tf_op jit(solution)/shard_map/ppermute | solution.py:429
  34.0 44.1 %collective-permute-start.3 = (bf16[4,4,64,512]{3,2,1,0:T(8,128)(2,1)S(1)}, bf16[4,4,64,512]{3,2,1,0:T(8,128)(2,1)}, u32[]{:S(2)}, u32[]{:S(2)}) collective-permute-start(bf16[4,4,64,512]{3,2,1,0:T(8,128)(2,1)S(1)} %pad_maximum_fusion.refs_2_), channel_id=1, source_target_pairs={{0,8},{1,9},{2,10},{3,11},{4,12},{5,13},{6,14},{7,15},{8,16},{9,17... | collective-permute-start | bytes 3145736 | tf_op jit(solution)/shard_map/ppermute | solution.py:429
  35.6 42.4 %collective-permute-start.20 = (bf16[1,16,128]{2,1,0:T(8,128)(2,1)S(1)}, bf16[1,16,128]{2,1,0:T(8,128)(2,1)S(1)}, u32[]{:S(2)}, u32[]{:S(2)}) collective-permute-start(bf16[1,16,128]{2,1,0:T(8,128)(2,1)S(1)} %pad_bitcast_fusion), channel_id=1, source_target_pairs={{0,1},{1,0},{2,3},{3,2},{4,5},{5,4},{6,7},{7,6},{8,9},{9,8},{10,11... | collective-permute-start | bytes 12296 | tf_op jit(solution)/shard_map/ppermute | solution.py:447
  35.6 29.8 %collective-permute-start.11 = (bf16[1,4,16,2048]{3,2,1,0:T(8,128)(2,1)S(1)}, bf16[1,4,16,2048]{3,2,1,0:T(8,128)(2,1)S(1)}, u32[]{:S(2)}, u32[]{:S(2)}) collective-permute-start(bf16[1,4,16,2048]{3,2,1,0:T(8,128)(2,1)S(1)} %collective-permute-done.10), channel_id=1, source_target_pairs={{0,8},{1,9},{2,10},{3,11},{4,12},{5,13},{6,14},{7,15},{8,16},{9,17... | collective-permute-start | bytes 786440 | tf_op jit(solution)/shard_map/ppermute | solution.py:429
  65.5 8.4 %collective-permute-start.12 = (bf16[1,4,16,2048]{3,2,1,0:T(8,128)(2,1)S(1)}, bf16[1,4,16,2048]{3,2,1,0:T(8,128)(2,1)S(1)}, u32[]{:S(2)}, u32[]{:S(2)}) collective-permute-start(bf16[1,4,16,2048]{3,2,1,0:T(8,128)(2,1)S(1)} %collective-permute-done.11), channel_id=1, source_target_pairs={{0,8},{1,9},{2,10},{3,11},{4,12},{5,13},{6,14},{7,15},{8,16},{9,17... | collective-permute-start | bytes 786440 | tf_op jit(solution)/shard_map/ppermute | solution.py:429
  74.9 54.7 %collective-permute-start.13 = (bf16[4,4,16,2048]{3,2,1,0:T(8,128)(2,1)}, bf16[4,4,16,2048]{3,2,1,0:T(8,128)(2,1)}, u32[]{:S(2)}, u32[]{:S(2)}) collective-permute-start(bf16[4,4,16,2048]{3,2,1,0:T(8,128)(2,1)} %pad_maximum_fusion.1.refs_2_), channel_id=1, source_target_pairs={{0,2},{1,3},{2,0},{3,1},{4,6},{5,7},{6,4},{7,5},{8,10},{9,11},{10,... | collective-permute-start | bytes 3145736 | tf_op jit(solution)/shard_map/ppermute | solution.py:429
  76.2 54.0 %collective-permute-start.14 = (bf16[4,4,16,2048]{3,2,1,0:T(8,128)(2,1)}, bf16[4,4,16,2048]{3,2,1,0:T(8,128)(2,1)}, u32[]{:S(2)}, u32[]{:S(2)}) collective-permute-start(bf16[4,4,16,2048]{3,2,1,0:T(8,128)(2,1)} %pad_maximum_fusion.1.refs_2_), channel_id=1, source_target_pairs={{0,4},{1,5},{2,6},{3,7},{4,0},{5,1},{6,2},{7,3},{8,12},{9,13},{10,... | collective-permute-start | bytes 3145736 | tf_op jit(solution)/shard_map/ppermute | solution.py:429
  78.1 52.2 %collective-permute-start.4 = (bf16[4,4,64,512]{3,2,1,0:T(8,128)(2,1)}, bf16[4,4,64,512]{3,2,1,0:T(8,128)(2,1)}, u32[]{:S(2)}, u32[]{:S(2)}) collective-permute-start(bf16[4,4,64,512]{3,2,1,0:T(8,128)(2,1)} %collective-permute-done.3.refs_3_), channel_id=1, source_target_pairs={{0,8},{1,9},{2,10},{3,11},{4,12},{5,13},{6,14},{7,15},{8,16},{9,17... | collective-permute-start | bytes 3145736 | tf_op jit(solution)/shard_map/ppermute | solution.py:429
  78.1 27.5 %collective-permute-start.21 = (bf16[2,16,128]{2,1,0:T(8,128)(2,1)S(1)}, bf16[2,16,128]{2,1,0:T(8,128)(2,1)S(1)}, u32[]{:S(2)}, u32[]{:S(2)}) collective-permute-start(bf16[2,16,128]{2,1,0:T(8,128)(2,1)S(1)} %maximum_select_fusion.4), channel_id=1, source_target_pairs={{0,2},{1,3},{2,0},{3,1},{4,6},{5,7},{6,4},{7,5},{8,10},{9,11},{10,... | collective-permute-start | bytes 24584 | tf_op jit(solution)/shard_map/ppermute | solution.py:447
  109.3 15.1 %collective-permute-start.23 = (bf16[8,16,128]{2,1,0:T(8,128)(2,1)S(1)}, bf16[8,16,128]{2,1,0:T(8,128)(2,1)S(1)}, u32[]{:S(2)}, u32[]{:S(2)}) collective-permute-start(bf16[8,16,128]{2,1,0:T(8,128)(2,1)S(1)} %maximum_select_fusion.2), channel_id=1, source_target_pairs={{0,8},{1,9},{2,10},{3,11},{4,12},{5,13},{6,14},{7,15},{8,0},{9,1},... | collective-permute-start | bytes 98312 | tf_op jit(solution)/shard_map/ppermute | solution.py:447
  121.8 17.9 %collective-permute-start.15 = (bf16[4,4,16,2048]{3,2,1,0:T(8,128)(2,1)}, bf16[4,4,16,2048]{3,2,1,0:T(8,128)(2,1)}, u32[]{:S(2)}, u32[]{:S(2)}) collective-permute-start(bf16[4,4,16,2048]{3,2,1,0:T(8,128)(2,1)} %pad_maximum_fusion.1.refs_2_), channel_id=1, source_target_pairs={{0,6},{1,7},{2,4},{3,5},{4,2},{5,3},{6,0},{7,1},{8,14},{9,15},{10,... | collective-permute-start | bytes 3145736 | tf_op jit(solution)/shard_map/ppermute | solution.py:429
  129.7 15.7 %collective-permute-start.16 = (bf16[4,4,16,2048]{3,2,1,0:T(8,128)(2,1)}, bf16[4,4,16,2048]{3,2,1,0:T(8,128)(2,1)}, u32[]{:S(2)}, u32[]{:S(2)}) collective-permute-start(bf16[4,4,16,2048]{3,2,1,0:T(8,128)(2,1)} %pad_maximum_fusion.1.refs_2_), channel_id=1, source_target_pairs={{0,1},{1,0},{2,3},{3,2},{4,5},{5,4},{6,7},{7,6},{8,9},{9,8},{10,11... | collective-permute-start | bytes 3145736 | tf_op jit(solution)/shard_map/ppermute | solution.py:429
  129.7 16.3 %collective-permute-start.17 = (bf16[4,4,16,2048]{3,2,1,0:T(8,128)(2,1)}, bf16[4,4,16,2048]{3,2,1,0:T(8,128)(2,1)}, u32[]{:S(2)}, u32[]{:S(2)}) collective-permute-start(bf16[4,4,16,2048]{3,2,1,0:T(8,128)(2,1)} %collective-permute-done.13.refs_3_), channel_id=1, source_target_pairs={{0,1},{1,0},{2,3},{3,2},{4,5},{5,4},{6,7},{7,6},{8,9},{9,8},{10,11... | collective-permute-start | bytes 3145736 | tf_op jit(solution)/shard_map/ppermute | solution.py:429
  130.2 15.8 %collective-permute-start.18 = (bf16[4,4,16,2048]{3,2,1,0:T(8,128)(2,1)}, bf16[4,4,16,2048]{3,2,1,0:T(8,128)(2,1)}, u32[]{:S(2)}, u32[]{:S(2)}) collective-permute-start(bf16[4,4,16,2048]{3,2,1,0:T(8,128)(2,1)} %collective-permute-done.14.refs_4_), channel_id=1, source_target_pairs={{0,1},{1,0},{2,3},{3,2},{4,5},{5,4},{6,7},{7,6},{8,9},{9,8},{10,11... | collective-permute-start | bytes 3145736 | tf_op jit(solution)/shard_map/ppermute | solution.py:429
  130.3 31.3 %collective-permute-start.5 = (bf16[4,4,64,512]{3,2,1,0:T(8,128)(2,1)}, bf16[4,4,64,512]{3,2,1,0:T(8,128)(2,1)}, u32[]{:S(2)}, u32[]{:S(2)}) collective-permute-start(bf16[4,4,64,512]{3,2,1,0:T(8,128)(2,1)} %collective-permute-done.4.refs_4_), channel_id=1, source_target_pairs={{0,8},{1,9},{2,10},{3,11},{4,12},{5,13},{6,14},{7,15},{8,16},{9,17... | collective-permute-start | bytes 3145736 | tf_op jit(solution)/shard_map/ppermute | solution.py:429
  139.7 27.4 %collective-permute-start.19 = (bf16[4,4,16,2048]{3,2,1,0:T(8,128)(2,1)}, bf16[4,4,16,2048]{3,2,1,0:T(8,128)(2,1)}, u32[]{:S(2)}, u32[]{:S(2)}) collective-permute-start(bf16[4,4,16,2048]{3,2,1,0:T(8,128)(2,1)} %collective-permute-done.15.refs_5_), channel_id=1, source_target_pairs={{0,1},{1,0},{2,3},{3,2},{4,5},{5,4},{6,7},{7,6},{8,9},{9,8},{10,11... | collective-permute-start | bytes 3145736 | tf_op jit(solution)/shard_map/ppermute | solution.py:429
  145.4 33.5 %collective-permute-start.6 = (bf16[4,4,64,512]{3,2,1,0:T(8,128)(2,1)}, bf16[4,4,64,512]{3,2,1,0:T(8,128)(2,1)}, u32[]{:S(2)}, u32[]{:S(2)}) collective-permute-start(bf16[4,4,64,512]{3,2,1,0:T(8,128)(2,1)} %copy-done.8), channel_id=1, source_target_pairs={{0,1},{1,0},{2,3},{3,2},{4,5},{5,4},{6,7},{7,6},{8,9},{9,8},{10,11... | collective-permute-start | bytes 3145736 | tf_op jit(solution)/shard_map/ppermute | solution.py:429
  145.9 32.9 %collective-permute-start.7 = (bf16[4,4,64,512]{3,2,1,0:T(8,128)(2,1)}, bf16[4,4,64,512]{3,2,1,0:T(8,128)(2,1)}, u32[]{:S(2)}, u32[]{:S(2)}) collective-permute-start(bf16[4,4,64,512]{3,2,1,0:T(8,128)(2,1)} %collective-permute-done.3.refs_3_), channel_id=1, source_target_pairs={{0,1},{1,0},{2,3},{3,2},{4,5},{5,4},{6,7},{7,6},{8,9},{9,8},{10,11... | collective-permute-start | bytes 3145736 | tf_op jit(solution)/shard_map/ppermute | solution.py:429
  146.0 32.9 %collective-permute-start.8 = (bf16[4,4,64,512]{3,2,1,0:T(8,128)(2,1)}, bf16[4,4,64,512]{3,2,1,0:T(8,128)(2,1)}, u32[]{:S(2)}, u32[]{:S(2)}) collective-permute-start(bf16[4,4,64,512]{3,2,1,0:T(8,128)(2,1)} %collective-permute-done.4.refs_4_), channel_id=1, source_target_pairs={{0,1},{1,0},{2,3},{3,2},{4,5},{5,4},{6,7},{7,6},{8,9},{9,8},{10,11... | collective-permute-start | bytes 3145736 | tf_op jit(solution)/shard_map/ppermute | solution.py:429
  161.6 17.3 %collective-permute-start.9 = (bf16[4,4,64,512]{3,2,1,0:T(8,128)(2,1)}, bf16[4,4,64,512]{3,2,1,0:T(8,128)(2,1)}, u32[]{:S(2)}, u32[]{:S(2)}) collective-permute-start(bf16[4,4,64,512]{3,2,1,0:T(8,128)(2,1)} %collective-permute-done.5.refs_5_), channel_id=1, source_target_pairs={{0,1},{1,0},{2,3},{3,2},{4,5},{5,4},{6,7},{7,6},{8,9},{9,8},{10,11... | collective-permute-start | bytes 3145736 | tf_op jit(solution)/shard_map/ppermute | solution.py:429
  541.5 33.8 %collective-permute-start.56 = (bf16[4,2,2,16,4096]{4,3,0,2,1:T(8,128)(2,1)S(1)}, bf16[4,2,2,16,4096]{4,3,0,2,1:T(8,128)(2,1)S(1)}, u32[]{:S(2)}, u32[]{:S(2)}) collective-permute-start(bf16[4,2,2,16,4096]{4,3,0,2,1:T(8,128)(2,1)S(1)} %bitcast.258), channel_id=1, source_target_pairs={{0,1},{1,0},{2,3},{3,2},{4,5},{5,4},{6,7},{7,6},{8,9},{9,8},{10,11... | collective-permute-start | bytes 6291464 | tf_op jit(solution)/shard_map/ppermute | solution.py:429
  542.1 8.7 %collective-permute-start.36 = (f32[4,16,43]{2,1,0:T(8,128)S(1)}, f32[4,16,43]{2,1,0:T(8,128)S(1)}, u32[]{:S(2)}, u32[]{:S(2)}) collective-permute-start(f32[4,16,43]{2,1,0:T(8,128)S(1)} %get-tuple-element.275), channel_id=1, source_target_pairs={{0,2},{1,3},{2,0},{3,1},{4,6},{5,7},{6,4},{7,5},{8,10},{9,11},{10,... | collective-permute-start | bytes 33032 | tf_op jit(solution)/shard_map/ppermute | solution.py:429
  550.7 51.6 %collective-permute-start.49 = (bf16[4,2,2,4,64,512]{5,4,3,2,1,0:T(8,128)(2,1)}, bf16[4,2,2,4,64,512]{5,4,3,2,1,0:T(8,128)(2,1)}, u32[]{:S(2)}, u32[]{:S(2)}) collective-permute-start(bf16[4,2,2,4,64,512]{5,4,3,2,1,0:T(8,128)(2,1)} %dynamic-slice_bitcast_fusion), channel_id=1, source_target_pairs={{0,1},{1,0},{2,3},{3,2},{4,5},{5,4},{6,7},{7,6},{8,9},{9,8},{10,11... | collective-permute-start | bytes 12582920 | tf_op jit(solution)/shard_map/ppermute | solution.py:429
  554.9 9.1 %collective-permute-start.39 = (f32[16,43]{1,0:T(8,128)S(1)}, f32[16,43]{1,0:T(8,128)S(1)}, u32[]{:S(2)}, u32[]{:S(2)}) collective-permute-start(f32[16,43]{1,0:T(8,128)S(1)} %fusion.32), channel_id=1, source_target_pairs={{0,8},{1,9},{2,10},{3,11},{4,12},{5,13},{6,14},{7,15},{8,16},{9,17... | collective-permute-start | bytes 8264 | tf_op jit(solution)/shard_map/ppermute | solution.py:429
  564.0 43.7 %collective-permute-start.42 = (bf16[4,2,2,4,16,2048]{5,4,3,0,2,1:T(8,128)(2,1)}, bf16[4,2,2,4,16,2048]{5,4,3,0,2,1:T(8,128)(2,1)}, u32[]{:S(2)}, u32[]{:S(2)}) collective-permute-start(bf16[4,2,2,4,16,2048]{5,4,3,0,2,1:T(8,128)(2,1)} %bitcast.238), channel_id=1, source_target_pairs={{0,1},{1,0},{2,3},{3,2},{4,5},{5,4},{6,7},{7,6},{8,9},{9,8},{10,11... | collective-permute-start | bytes 12582920 | tf_op jit(solution)/shard_map/ppermute | solution.py:429
  577.2 15.1 %collective-permute-start.57 = (bf16[4,16,4096]{2,1,0:T(8,128)(2,1)}, bf16[4,16,4096]{2,1,0:T(8,128)(2,1)S(1)}, u32[]{:S(2)}, u32[]{:S(2)}) collective-permute-start(bf16[4,16,4096]{2,1,0:T(8,128)(2,1)} %get-tuple-element.260), channel_id=1, source_target_pairs={{0,2},{1,3},{2,0},{3,1},{4,6},{5,7},{6,4},{7,5},{8,10},{9,11},{10,... | collective-permute-start | bytes 1572872 | tf_op jit(solution)/shard_map/ppermute | solution.py:429
  577.2 23.7 %collective-permute-start.58 = (bf16[4,16,4096]{2,1,0:T(8,128)(2,1)}, bf16[4,16,4096]{2,1,0:T(8,128)(2,1)S(1)}, u32[]{:S(2)}, u32[]{:S(2)}) collective-permute-start(bf16[4,16,4096]{2,1,0:T(8,128)(2,1)} %get-tuple-element.262), channel_id=1, source_target_pairs={{0,4},{1,5},{2,6},{3,7},{4,0},{5,1},{6,2},{7,3},{8,12},{9,13},{10,... | collective-permute-start | bytes 1572872 | tf_op jit(solution)/shard_map/ppermute | solution.py:429
  577.3 23.7 %collective-permute-start.59 = (bf16[4,16,4096]{2,1,0:T(8,128)(2,1)}, bf16[4,16,4096]{2,1,0:T(8,128)(2,1)}, u32[]{:S(2)}, u32[]{:S(2)}) collective-permute-start(bf16[4,16,4096]{2,1,0:T(8,128)(2,1)} %get-tuple-element.261), channel_id=1, source_target_pairs={{0,6},{1,7},{2,4},{3,5},{4,2},{5,3},{6,0},{7,1},{8,14},{9,15},{10,... | collective-permute-start | bytes 1572872 | tf_op jit(solution)/shard_map/ppermute | solution.py:429
  602.2 13.5 %collective-permute-start.60 = (bf16[16,4096]{1,0:T(8,128)(2,1)S(1)}, bf16[16,4096]{1,0:T(8,128)(2,1)S(1)}, u32[]{:S(2)}, u32[]{:S(2)}) collective-permute-start(bf16[16,4096]{1,0:T(8,128)(2,1)S(1)} %dynamic-slice_bitcast_fusion.12), channel_id=1, source_target_pairs={{0,8},{1,9},{2,10},{3,11},{4,12},{5,13},{6,14},{7,15},{8,16},{9,17... | collective-permute-start | bytes 393224 | tf_op jit(solution)/shard_map/ppermute | solution.py:429
  607.7 25.8 %collective-permute-start.50 = (bf16[2,2,4,64,512]{4,3,2,1,0:T(8,128)(2,1)S(1)}, bf16[2,2,4,64,512]{4,3,2,1,0:T(8,128)(2,1)S(1)}, u32[]{:S(2)}, u32[]{:S(2)}) collective-permute-start(bf16[2,2,4,64,512]{4,3,2,1,0:T(8,128)(2,1)S(1)} %dynamic-slice_bitcast_fusion.1), channel_id=1, source_target_pairs={{0,8},{1,9},{2,10},{3,11},{4,12},{5,13},{6,14},{7,15},{8,16},{9,17... | collective-permute-start | bytes 3145736 | tf_op jit(solution)/shard_map/ppermute | solution.py:429
  612.1 26.2 %collective-permute-start.43 = (bf16[4,4,16,2048]{3,2,1,0:T(8,128)(2,1)S(1)}, bf16[4,4,16,2048]{3,2,1,0:T(8,128)(2,1)S(1)}, u32[]{:S(2)}, u32[]{:S(2)}) collective-permute-start(bf16[4,4,16,2048]{3,2,1,0:T(8,128)(2,1)S(1)} %get-tuple-element.254), channel_id=1, source_target_pairs={{0,2},{1,3},{2,0},{3,1},{4,6},{5,7},{6,4},{7,5},{8,10},{9,11},{10,... | collective-permute-start | bytes 3145736 | tf_op jit(solution)/shard_map/ppermute | solution.py:429
  613.9 42.7 %collective-permute-start.44 = (bf16[4,4,16,2048]{3,2,1,0:T(8,128)(2,1)S(1)}, bf16[4,4,16,2048]{3,2,1,0:T(8,128)(2,1)S(1)}, u32[]{:S(2)}, u32[]{:S(2)}) collective-permute-start(bf16[4,4,16,2048]{3,2,1,0:T(8,128)(2,1)S(1)} %get-tuple-element.256), channel_id=1, source_target_pairs={{0,4},{1,5},{2,6},{3,7},{4,0},{5,1},{6,2},{7,3},{8,12},{9,13},{10,... | collective-permute-start | bytes 3145736 | tf_op jit(solution)/shard_map/ppermute | solution.py:429
  614.2 44.0 %collective-permute-start.45 = (bf16[4,4,16,2048]{3,2,1,0:T(8,128)(2,1)S(1)}, bf16[4,4,16,2048]{3,2,1,0:T(8,128)(2,1)S(1)}, u32[]{:S(2)}, u32[]{:S(2)}) collective-permute-start(bf16[4,4,16,2048]{3,2,1,0:T(8,128)(2,1)S(1)} %get-tuple-element.255), channel_id=1, source_target_pairs={{0,6},{1,7},{2,4},{3,5},{4,2},{5,3},{6,0},{7,1},{8,14},{9,15},{10,... | collective-permute-start | bytes 3145736 | tf_op jit(solution)/shard_map/ppermute | solution.py:429
  615.7 43.7 %collective-permute-start.61 = (bf16[16,4096]{1,0:T(8,128)(2,1)S(1)}, bf16[16,4096]{1,0:T(8,128)(2,1)S(1)}, u32[]{:S(2)}, u32[]{:S(2)}) collective-permute-start(bf16[16,4096]{1,0:T(8,128)(2,1)S(1)} %fusion.22), channel_id=1, source_target_pairs={{0,8},{1,9},{2,10},{3,11},{4,12},{5,13},{6,14},{7,15},{8,16},{9,17... | collective-permute-start | bytes 393224 | tf_op jit(solution)/shard_map/ppermute | solution.py:429
  633.8 36.1 %collective-permute-start.51 = (bf16[2,2,4,64,512]{4,3,2,1,0:T(8,128)(2,1)S(1)}, bf16[2,2,4,64,512]{4,3,2,1,0:T(8,128)(2,1)S(1)}, u32[]{:S(2)}, u32[]{:S(2)}) collective-permute-start(bf16[2,2,4,64,512]{4,3,2,1,0:T(8,128)(2,1)S(1)} %fusion.5), channel_id=1, source_target_pairs={{0,8},{1,9},{2,10},{3,11},{4,12},{5,13},{6,14},{7,15},{8,16},{9,17... | collective-permute-start | bytes 3145736 | tf_op jit(solution)/shard_map/ppermute | solution.py:429
  659.0 8.2 %collective-permute-start.46 = (bf16[4,16,2048]{2,1,0:T(8,128)(2,1)S(1)}, bf16[4,16,2048]{2,1,0:T(8,128)(2,1)S(1)}, u32[]{:S(2)}, u32[]{:S(2)}) collective-permute-start(bf16[4,16,2048]{2,1,0:T(8,128)(2,1)S(1)} %dynamic-slice_bitcast_fusion.11), channel_id=1, source_target_pairs={{0,8},{1,9},{2,10},{3,11},{4,12},{5,13},{6,14},{7,15},{8,16},{9,17... | collective-permute-start | bytes 786440 | tf_op jit(solution)/shard_map/ppermute | solution.py:429
  659.4 13.3 %collective-permute-start.62 = (bf16[16,4096]{1,0:T(8,128)(2,1)S(1)}, bf16[16,4096]{1,0:T(8,128)(2,1)S(1)}, u32[]{:S(2)}, u32[]{:S(2)}) collective-permute-start(bf16[16,4096]{1,0:T(8,128)(2,1)S(1)} %fusion.23), channel_id=1, source_target_pairs={{0,8},{1,9},{2,10},{3,11},{4,12},{5,13},{6,14},{7,15},{8,16},{9,17... | collective-permute-start | bytes 393224 | tf_op jit(solution)/shard_map/ppermute | solution.py:429
  667.3 11.2 %collective-permute-start.47 = (bf16[4,16,2048]{2,1,0:T(8,128)(2,1)S(1)}, bf16[4,16,2048]{2,1,0:T(8,128)(2,1)S(1)}, u32[]{:S(2)}, u32[]{:S(2)}) collective-permute-start(bf16[4,16,2048]{2,1,0:T(8,128)(2,1)S(1)} %fusion.20), channel_id=1, source_target_pairs={{0,8},{1,9},{2,10},{3,11},{4,12},{5,13},{6,14},{7,15},{8,16},{9,17... | collective-permute-start | bytes 786440 | tf_op jit(solution)/shard_map/ppermute | solution.py:429
  670.2 29.3 %collective-permute-start.52 = (bf16[2,2,4,64,512]{4,3,2,1,0:T(8,128)(2,1)S(1)}, bf16[2,2,4,64,512]{4,3,2,1,0:T(8,128)(2,1)S(1)}, u32[]{:S(2)}, u32[]{:S(2)}) collective-permute-start(bf16[2,2,4,64,512]{4,3,2,1,0:T(8,128)(2,1)S(1)} %fusion.6), channel_id=1, source_target_pairs={{0,8},{1,9},{2,10},{3,11},{4,12},{5,13},{6,14},{7,15},{8,16},{9,17... | collective-permute-start | bytes 3145736 | tf_op jit(solution)/shard_map/ppermute | solution.py:429
  678.5 25.0 %collective-permute-start.48 = (bf16[4,16,2048]{2,1,0:T(8,128)(2,1)S(1)}, bf16[4,16,2048]{2,1,0:T(8,128)(2,1)S(1)}, u32[]{:S(2)}, u32[]{:S(2)}) collective-permute-start(bf16[4,16,2048]{2,1,0:T(8,128)(2,1)S(1)} %fusion.21), channel_id=1, source_target_pairs={{0,8},{1,9},{2,10},{3,11},{4,12},{5,13},{6,14},{7,15},{8,16},{9,17... | collective-permute-start | bytes 786440 | tf_op jit(solution)/shard_map/ppermute | solution.py:429
  700.6 9.2 %collective-permute-start.54 = (bf16[4,64,512]{2,1,0:T(8,128)(2,1)S(1)}, bf16[4,64,512]{2,1,0:T(8,128)(2,1)S(1)}, u32[]{:S(2)}, u32[]{:S(2)}) collective-permute-start(bf16[4,64,512]{2,1,0:T(8,128)(2,1)S(1)} %get-tuple-element.267), channel_id=1, source_target_pairs={{0,4},{1,5},{2,6},{3,7},{4,0},{5,1},{6,2},{7,3},{8,12},{9,13},{10,... | collective-permute-start | bytes 786440 | tf_op jit(solution)/shard_map/ppermute | solution.py:429
  (53 other events, 863.7 us)
Sparse Core Ops, SparseCore 0:
  11.8 105.6 all-gather.5
  120.3 95.5 all-gather.7
  218.9 76.1 all-gather.9
  370.4 184.6 reduce-scatter.1

commit v3 on v2

--- a/solution.py
+++ b/solution.py
@@ -60,6 +60,14 @@
     cosine = (cos_a * cos_b - sin_a * sin_b).reshape(length, width // 2)
     sine = (sin_a * cos_b + cos_a * sin_b).reshape(length, width // 2)
     return cosine, sine
+
+
+def halves_matrix(width):
+    row = lax.broadcasted_iota(jnp.int32, (width, width), 0)
+    column = lax.broadcasted_iota(jnp.int32, (width, width), 1)
+    half = width // 2
+    source = jnp.where(row < half, 2 * row, 2 * (row - half) + 1)
+    return (column == source).astype(jnp.float32).astype(jnp.bfloat16)
 
 
 def attend_forward_kernel(
@@ -85,6 +93,7 @@
     p_ref,
     ctx_ref,
     kt_ref,
+    sort_ref,
 ):
     length = resid_ref.shape[0]
     half = cos_ref.shape[1]
@@ -96,7 +105,9 @@
         unit, inverse = norm_parts(resid_ref[...])
         ha_ref[...] = (unit * gain_ref[...] + bias_ref[...]).astype(jnp.bfloat16)
         kt_ref[:, pair:] = tab_ref[...]
-
+        sort_ref[...] = halves_matrix(rel_ref.shape[0])
+
+    relative = mul(sort_ref[...], rel_ref[...]).astype(jnp.bfloat16)
     normed = ha_ref[...]
     query = mul(normed, pq_ref[...])
     keys = mul(normed, pk_ref[...]).astype(jnp.bfloat16)
@@ -115,7 +126,7 @@
             own = head_mask(rows, head)
             part_u = jnp.where(own, qu_ref[at, :], 0) * 0.125
             part_v = jnp.where(own, qv_ref[at, :], 0)
-            coef = mul(part_v, rel_ref[...], NT) * 0.125
+            coef = mul(part_v, relative, NT) * 0.125
             left, right = coef[:, :half], coef[:, half:]
             turned_a = (left * sine + right * cosine).astype(jnp.bfloat16)
             turned_b = (right * sine - left * cosine).astype(jnp.bfloat16)
@@ -135,7 +146,15 @@
     lax.fori_loop(0, length // rows, block, 0)
 
 
-def attend_backward_kernel(
+def attend_backward_kernel(resumed, ends, *refs):
+    operands = 18
+    if not resumed:
+        refs = refs[:operands] + (None,) + refs[operands:]
+    attend_backward_body(ends, *refs)
+
+
+def attend_backward_body(
+    ends,
     p_ref,
     tab_ref,
     cos_ref,
@@ -154,16 +173,14 @@
     pv_ref,
     rel_ref,
     gain_ref,
+    begin_ref,
     g1_ref,
     dao_ref,
     dpq_ref,
     dpk_ref,
     dpv_ref,
     drel_ref,
-    dcb_ref,
-    dpb_ref,
-    dgain_ref,
-    dbias_ref,
+    vec_ref,
     kt_ref,
     dout_ref,
     dctx_ref,
@@ -172,27 +189,30 @@
     dkt_ref,
     dvt_ref,
     drt_ref,
+    sort_ref,
 ):
     length = resid_ref.shape[0]
     half = cos_ref.shape[1]
     pair = 2 * HEAD_DIM
     rows = 256
     step = pl.program_id(0)
+    lanes = pl.ds(pl.multiple_of(step * pair, pair), pair)
 
     @pl.when(step == 0)
     def first():
         dout_ref[...] = slope_ref[...].astype(jnp.bfloat16)
         kt_ref[:, pair:] = tab_ref[...]
-        dn_ref[...] = jnp.zeros_like(dn_ref)
+        dn_ref[...] = jnp.zeros_like(dn_ref) if begin_ref is None else begin_ref[...]
+        vec_ref[...] = jnp.zeros_like(vec_ref)
+        sort_ref[...] = halves_matrix(rel_ref.shape[0])
 
     kt_ref[:, :pair] = k_ref[...]
-    dao_ref[...] = mul(ctx_ref[...], dout_ref[...], TN)
+    relative = mul(sort_ref[...], rel_ref[...]).astype(jnp.bfloat16)
+    dao_ref[...] = mul(ctx_ref[...], dout_ref[...], TN).astype(jnp.bfloat16)
     dctx_ref[...] = mul(dout_ref[...], ao_ref[...], NT).astype(jnp.bfloat16)
     dkt_ref[...] = jnp.zeros_like(dkt_ref)
     dvt_ref[...] = jnp.zeros_like(dvt_ref)
     drt_ref[...] = jnp.zeros_like(drt_ref)
-    dcb_ref[...] = jnp.zeros_like(dcb_ref)
-    dpb_ref[...] = jnp.zeros_like(dpb_ref)
 
     def block(index, carry):
         at = pl.ds(pl.multiple_of(index * rows, rows), rows)
@@ -221,35 +241,39 @@
                 ],
                 1,
             )
-            slope_v = jnp.where(own, mul(coef, rel_ref[...]), 0.0)
+            slope_v = jnp.where(own, mul(coef, relative), 0.0)
             drt_ref[...] += mul(jnp.where(own, qv_ref[at, :], 0), coef, TN)
             total = total + slope_u + slope_v
             sum_u = sum_u + jnp.sum(slope_u, 0, keepdims=True)
             sum_v = sum_v + jnp.sum(slope_v, 0, keepdims=True)
         dq_ref[at, :] = total
-        dcb_ref[...] += sum_u
-        dpb_ref[...] += sum_v
+        vec_ref[0:1, lanes] += sum_u
+        vec_ref[1:2, lanes] += sum_v
         return carry
 
     lax.fori_loop(0, length // rows, block, 0)
     low_q = dq_ref[...].astype(jnp.bfloat16)
     low_k = dkt_ref[...].T.astype(jnp.bfloat16)
     low_v = dvt_ref[...].T.astype(jnp.bfloat16)
-    drel_ref[...] = drt_ref[...].T
+    drel = drt_ref[...].T.astype(jnp.bfloat16)
+    drel_ref[...] = mul(sort_ref[...], drel, TN).astype(jnp.bfloat16)
     normed = ha_ref[...]
-    dpq_ref[...] = mul(normed, low_q, TN)
-    dpk_ref[...] = mul(normed, low_k, TN)
-    dpv_ref[...] = mul(normed, low_v, TN)
+    dpq_ref[...] = mul(normed, low_q, TN).astype(jnp.bfloat16)
+    dpk_ref[...] = mul(normed, low_k, TN).astype(jnp.bfloat16)
+    dpv_ref[...] = mul(normed, low_v, TN).astype(jnp.bfloat16)
     dn_ref[...] += (
         mul(low_q, pq_ref[...], NT) + mul(low_k, pk_ref[...], NT) + mul(low_v, pv_ref[...], NT)
     )
 
     @pl.when(step == pl.num_programs(0) - 1)
     def last():
+        slope = dn_ref[...]
+        if not ends:
+            g1_ref[...] = slope
+            return
         unit, inverse = norm_parts(resid_ref[...])
-        slope = dn_ref[...]
-        dgain_ref[...] = jnp.sum(slope * unit, 0, keepdims=True)
-        dbias_ref[...] = jnp.sum(slope, 0, keepdims=True)
+        vec_ref[2:3, :] = jnp.sum(slope * unit, 0, keepdims=True)
+        vec_ref[3:4, :] = jnp.sum(slope, 0, keepdims=True)
         g1_ref[...] = slope_ref[...] + norm_slope(unit, inverse, slope, gain_ref[...])
 
 
@@ -261,8 +285,8 @@
     return pl.BlockSpec((rows, width), lambda p: (0, p + shift))
 
 
-def attention_forward(resid, segments, weights, tables):
-    gain, bias, project_in, relative, content_bias, position_bias, attend_out = weights
+def attention_forward(first, count, resid, segments, segment_column, weights, tables):
+    gain, bias, packed, content_bias, position_bias = weights
     table, cosine, sine = tables
     length, width = resid.shape
     pair = 2 * HEAD_DIM
@@ -271,17 +295,17 @@
     shape = jax.ShapeDtypeStruct
     return pl.pallas_call(
         attend_forward_kernel,
-        grid=(pairs,),
+        grid=(count,),
         in_specs=[
             whole((length, width)),
-            whole((1, width)),
-            whole((1, width)),
-            columns(width, pair),
-            columns(width, pair, pairs),
-            columns(width, pair, 2 * pairs),
-            columns(width, pair),
-            columns(1, pair),
-            columns(1, pair),
+            pl.BlockSpec((None, 1, width), lambda p: (gain[1], 0, 0)),
+            pl.BlockSpec((None, 1, width), lambda p: (bias[1], 0, 0)),
+            columns(width, pair, first),
+            columns(width, pair, first + pairs),
+            columns(width, pair, first + 2 * pairs),
+            columns(width, pair, first + 3 * pairs),
+            pl.BlockSpec((None, 1, pair), lambda p: (content_bias[1], 0, p + first)),
+            pl.BlockSpec((None, 1, pair), lambda p: (position_bias[1], 0, p + first)),
             whole((1, length)),
             whole((length, 1)),
             whole((length, width)),
@@ -291,32 +315,33 @@
         out_specs=[whole((length, width))]
         + [columns(length, pair)] * 4
         + [pl.BlockSpec((2, length, length), lambda p: (p, 0, 0)), columns(length, pair)],
-        out_shape=[shape((length, width), low)] * 5
-        + [shape((HEADS, length, length), low), shape((length, width), low)],
-        scratch_shapes=[pltpu.VMEM((length, pair + width), low)],
+        out_shape=[shape((length, width), low)]
+        + [shape((length, count * pair), low)] * 4
+        + [shape((2 * count, length, length), low), shape((length, count * pair), low)],
+        scratch_shapes=[pltpu.VMEM((length, pair + width), low), pltpu.VMEM((width, width), low)],
         compiler_params=pltpu.CompilerParams(vmem_limit_bytes=56 * 1024 * 1024),
-        cost_estimate=pl.CostEstimate(flops=24 * 10**9, bytes_accessed=30 * 10**6, transcendentals=8 * 10**6),
+        cost_estimate=pl.CostEstimate(flops=count * 6 * 10**9, bytes_accessed=count * 8 * 10**6, transcendentals=count * 2 * 10**6),
         name="attend_forward",
     )(
         resid,
-        gain,
-        bias,
-        project_in,
-        project_in,
-        project_in,
-        relative,
-        content_bias,
-        position_bias,
+        gain[0],
+        bias[0],
+        packed,
+        packed,
+        packed,
+        packed,
+        content_bias[0],
+        position_bias[0],
         segments,
-        segments.reshape(length, 1),
+        segment_column,
         table,
         cosine,
         sine,
     )
 
 
-def attention_backward(resid, slope, weights, tables, kept):
-    gain, bias, project_in, relative, content_bias, position_bias, attend_out = weights
+def attention_backward(first, count, last, resid, slope, weights, tables, kept, partial):
+    gain, bias, packed, content_bias, position_bias = weights
     table, cosine, sine = tables
     normed, query_u, query_v, keys, values, chances, context = kept
     length, width = resid.shape
@@ -324,11 +349,12 @@
     pairs = HEADS // 2
     low, full = jnp.bfloat16, jnp.float32
     shape = jax.ShapeDtypeStruct
+    begin = [] if partial is None else [partial]
     return pl.pallas_call(
-        attend_backward_kernel,
-        grid=(pairs,),
+        functools.partial(attend_backward_kernel, bool(begin), last),
+        grid=(count,),
         in_specs=[
-            pl.BlockSpec((2, length, length), lambda p: (p, 0, 0)),
+            pl.BlockSpec((2, length, length), lambda p: (p + first, 0, 0)),
             whole((length, width)),
             whole((length, width // 2)),
             whole((length, width // 2)),
@@ -336,15 +362,16 @@
             whole((length, width)),
             whole((length, width)),
         ]
-        + [columns(length, pair)] * 5
+        + [columns(length, pair, first)] * 5
         + [
-            pl.BlockSpec((pair, width), lambda p: (p, 0)),
-            columns(width, pair),
-            columns(width, pair, pairs),
-            columns(width, pair, 2 * pairs),
-            columns(width, pair),
-            whole((1, width)),
-        ],
+            pl.BlockSpec((pair, width), lambda p: (p + first, pairs)),
+            columns(width, pair, first),
+            columns(width, pair, first + pairs),
+            columns(width, pair, first + 2 * pairs),
+            columns(width, pair, first + 3 * pairs),
+            pl.BlockSpec((None, 1, width), lambda p: (gain[1], 0, 0)),
+        ]
+        + [whole((length, width))] * len(begin),
         out_specs=[
             whole((length, width)),
             pl.BlockSpec((pair, width), lambda p: (p, 0)),
@@ -352,14 +379,11 @@
             columns(width, pair),
             columns(width, pair),
             columns(width, pair),
-            columns(1, pair),
-            columns(1, pair),
-            whole((1, width)),
-            whole((1, width)),
+            whole((8, width)),
         ],
-        out_shape=[shape((length, width), full)]
-        + [shape((width, width), full)] * 5
-        + [shape((1, width), full)] * 4,
+        out_shape=[shape((length, width), full), shape((count * pair, width), low)]
+        + [shape((width, count * pair), low)] * 4
+        + [shape((8, width), full)],
         scratch_shapes=[
             pltpu.VMEM((length, pair + width), low),
             pltpu.VMEM((length, width), low),
@@ -369,9 +393,12 @@
             pltpu.VMEM((pair, length), full),
             pltpu.VMEM((pair, length), full),
             pltpu.VMEM((pair, width), full),
+            pltpu.VMEM((width, width), low),
         ],
         compiler_params=pltpu.CompilerParams(vmem_limit_bytes=60 * 1024 * 1024),
-        cost_estimate=pl.CostEstimate(flops=40 * 10**9, bytes_accessed=40 * 10**6, transcendentals=0),
+        cost_estimate=pl.CostEstimate(
+            flops=count * 10**10, bytes_accessed=20 * 10**6, transcendentals=0
+        ),
         name="attend_backward",
     )(
         chances,
@@ -386,13 +413,17 @@
         keys,
         values,
         context,
-        attend_out,
-        project_in,
-        project_in,
-        project_in,
-        relative,
-        gain,
-    )
+        packed,
+        packed,
+        packed,
+        packed,
+        packed,
+        gain[0],
+        *begin,
+    )
+
+
+FAST = {"z": 4, "y": 2, "x": 2, "c": 2}
 
 
 def grid_of(count_dp, count_fsdp):
@@ -429,92 +460,134 @@
     return lax.ppermute(value, AXES, pairs)
 
 
-def total_of(value):
-    count = lax.axis_size(AXES)
-    bit = 1
-    while bit < count:
-        value = value + lax.ppermute(value, AXES, [(d, d ^ bit) for d in range(count)])
-        bit *= 2
-    return value
-
-
-def gather_small(value):
-    count = lax.axis_size(AXES)
-    index = lax.axis_index(AXES)
+PLANE = ((0, 1), (1, 0), (1, 1))
+
+
+def tie(*values):
+    return lax.optimization_barrier(values)
+
+
+def total_of(value, beside=None):
+    grid = sizes()
+    if grid != FAST:
+        done = beside(value) if beside else None
+        return lax.psum(value, AXES), done
+    value = value + move(value, grid, c=1)
+    moved = [move(value, grid, y=dy, x=dx) for dy, dx in PLANE]
+    done = None
+    if beside:
+        done = beside(value)
+        *moved, done = tie(*moved, done)
+    value = value + sum(moved)
+    return value + sum(move(value, grid, z=step) for step in range(1, grid["z"])), done
+
+
+class Chain:
+    def __init__(self, steps, grid):
+        self.steps, self.grid, self.value = steps, grid, None
+        self.start(next(steps))
+
+    def start(self, sends):
+        self.pending = [move(value, self.grid, **how) for value, how in sends]
+
+    def step(self, *held):
+        count = len(self.pending)
+        tied = tie(*self.pending, *held)
+        arrived, held = tied[:count], tied[count:]
+        try:
+            sends = self.steps.send(list(arrived))
+        except StopIteration as stop:
+            self.value, self.pending = stop.value, []
+            return held
+        count = len(sends)
+        tied = tie(*[value for value, _ in sends], *held)
+        self.start([(value, how) for value, (_, how) in zip(tied[:count], sends, strict=True)])
+        return tied[count:]
+
+    def finish(self):
+        while self.pending:
+            try:
+                self.start(self.steps.send(self.pending))
+            except StopIteration as stop:
+                self.value, self.pending = stop.value, []
+        return self.value
+
+
+class Still:
+    def __init__(self, value):
+        self.value, self.pending = value, []
+
+    def step(self, *held):
+        return held
+
+    def finish(self):
+        return self.value
+
+
+def advance(chains, *held):
+    pending = [value for chain in chains for value in chain.pending]
+    tied = list(tie(*pending, *held))
+    held = tied[len(pending) :]
+    sends = []
+    for chain in chains:
+        arrived = [tied.pop(0) for _ in chain.pending]
+        chain.pending = []
+        if not arrived:
+            sends.append([])
+            continue
+        try:
+            sends.append(chain.steps.send(arrived))
+        except StopIteration as stop:
+            chain.value = stop.value
+            sends.append([])
+    values = [value for part in sends for value, _ in part]
+    if not values:
+        return held
+    tied = list(tie(*values, *held))
+    held = tied[len(values) :]
+    for chain, part in zip(chains, sends, strict=True):
+        chain.pending = [move(tied.pop(0), chain.grid, **how) for _, how in part]
+    return held
+
+
+def gather_steps(value, depth_first):
     value = value[None]
-    bit = 1
-    while bit < count:
-        other = lax.ppermute(value, AXES, [(d, d ^ bit) for d in range(count)])
-        upper = (index // bit) % 2 == 1
-        value = jnp.where(
-            upper, jnp.concatenate([other, value], 0), jnp.concatenate([value, other], 0)
-        )
-        bit *= 2
-    return value
-
-
-PLANE = ((0, 1), (1, 0), (1, 1))
-
-
-def joined(pieces):
-    return (
-        jnp.concatenate([value for value, _ in pieces], 0),
-        [offset for _, offsets in pieces for offset in offsets],
-    )
-
-
-def along_depth(piece, grid):
-    value, offsets = piece
-    steps = [piece]
-    for step in range(1, grid["z"]):
-        value = move(value, grid, z=1)
-        steps.append((value, [dict(o, z=(o["z"] - step) % grid["z"]) for o in offsets]))
-    return steps
-
-
-def over_plane(piece, grid):
-    value, offsets = piece
-    return [piece] + [
-        (move(value, grid, y=dy, x=dx), [dict(o, y=o["y"] ^ dy, x=o["x"] ^ dx) for o in offsets])
-        for dy, dx in PLANE
-    ]
-
-
-def over_cores(pieces, grid):
-    return pieces + [
-        (move(value, grid, c=1), [dict(o, c=1 - o["c"]) for o in offsets])
-        for value, offsets in pieces
-    ]
-
-
-def gather_pieces(block, grid, depth_first):
-    piece = (block[None], [{"z": 0, "y": 0, "x": 0, "c": 0}])
+    plane = [{"y": dy, "x": dx} for dy, dx in PLANE]
     if depth_first:
-        pieces = over_plane(joined(along_depth(piece, grid)), grid)
+        column = [value] + (yield [(value, {"z": step}) for step in range(1, 4)])
+        value = jnp.concatenate(column, 0)
+        pieces = [value] + (yield [(value, how) for how in plane])
     else:
-        pieces = along_depth(joined(over_plane(piece, grid)), grid)
-    return over_cores(pieces, grid)
-
-
-def owners(pieces, grid):
+        chips = [value] + (yield [(value, how) for how in plane])
+        value = jnp.concatenate(chips, 0)
+        pieces = [value]
+        for _ in range(3):
+            (value,) = yield [(value, {"z": 1})]
+            pieces.append(value)
+    return pieces + (yield [(piece, {"c": 1}) for piece in pieces])
+
+
+def gathered_from(grid, depth_first):
     own = {axis: place(grid, axis) for axis in grid}
+    column = [{"z": -step} for step in range(4)]
+    plane = [{}] + [{"y": dy, "x": dx} for dy, dx in PLANE]
     found = []
-    for _, offsets in pieces:
-        for offset in offsets:
-            at = {axis: (own[axis] + offset[axis]) % grid[axis] for axis in grid}
-            found.append(number(grid, at))
+    for core in range(2):
+        for outer in plane if depth_first else column:
+            for inner in column if depth_first else plane:
+                at = {"c": core, **outer, **inner}
+                found.append(
+                    number(grid, {axis: (own[axis] + at.get(axis, 0)) % grid[axis] for axis in grid})
+                )
     return jnp.stack(found)
-
-
-FAST = {"z": 4, "y": 2, "x": 2, "c": 2}
 
 
 def gather_experts(value, depth_first):
     grid = sizes()
     if grid == FAST:
-        pieces = gather_pieces(value, grid, depth_first)
-        return [piece for piece, _ in pieces], owners(pieces, grid)
-    return gather_whole(value)
+        return Chain(gather_steps(value, depth_first), grid), gathered_from(grid, depth_first)
+    pieces, ids = gather_whole(value)
+    return Still(pieces), ids
 
 
 def gather_whole(value):
@@ -534,50 +607,316 @@
     return value.astype(jnp.float32)
 
 
-def sum_cores(value, grid, at):
-    own = place(grid, "c")
-    other = move(block_at(value, own + 1, at), grid, c=1)
-    return (wide(block_at(value, own, at)) + wide(other)).astype(value.dtype)
-
-
-def sum_plane(value, grid, at, dtype):
-    y, x = place(grid, "y"), place(grid, "x")
-
-    def block(dy, dx):
-        return block_at(block_at(value, y + dy, at), x + dx, at)
-
-    total = wide(block(0, 0))
-    for dy, dx in PLANE:
-        total = total + wide(move(block(dy, dx), grid, y=dy, x=dx))
-    return total.astype(dtype)
-
-
-def sum_depth(value, grid, dtype):
-    length = grid["z"]
-    own = place(grid, "z")
-    part = block_at(value, own + length - 1, 0)
-    for step in range(1, length):
-        total = wide(block_at(value, own + 2 * length - 1 - step, 0)) + wide(move(part, grid, z=1))
-        part = total.astype(dtype if step == length - 1 else value.dtype)
-    return part
-
-
-def scatter_blocks(value, depth_first):
+def scatter_steps(keep, send, depth_first, grid):
+    shape = (4, 2, 2) + keep.shape[1:]
+    low = jnp.bfloat16
+    z, y, x = (place(grid, axis) for axis in "zyx")
+    (other,) = yield [(send, {"c": 1})]
+    keep, other = keep.reshape(shape), other.reshape(shape)
+
+    def near(value, at, dy, dx):
+        return wide(block_at(block_at(value, y + dy, at), x + dx, at))
+
+    def below(value, step):
+        return wide(block_at(value, z + 4 - step, 0))
+
+    if depth_first:
+        part = (below(keep, 1) + below(other, 1)).astype(low)
+        for step in (2, 3, 0):
+            (part,) = yield [(part, {"z": 1})]
+            part = (wide(part) + below(keep, step) + below(other, step)).astype(low)
+        moved = yield [(near(part, 0, dy, dx).astype(low), {"y": dy, "x": dx}) for dy, dx in PLANE]
+        return near(part, 0, 0, 0) + sum(wide(value) for value in moved)
+    sends = [
+        ((near(keep, 1, dy, dx) + near(other, 1, dy, dx)).astype(low), {"y": dy, "x": dx})
+        for dy, dx in PLANE
+    ]
+    moved = yield sends
+    column = near(keep, 1, 0, 0) + near(other, 1, 0, 0) + sum(wide(value) for value in moved)
+    column = column.astype(low)
+    moved = yield [(block_at(column, z + step, 0), {"z": step}) for step in range(1, 4)]
+    return wide(block_at(column, z, 0)) + sum(wide(value) for value in moved)
+
+
+def scatter_parts(parts, depth_first):
+    grid = sizes()
+    if len(parts) == 2:
+        return Chain(scatter_steps(*parts, depth_first, grid), grid)
+    return Still(wide(scatter_rows(by_devices(parts[0]))))
+
+
+def scatter_rows(value):
+    return lax.psum_scatter(value, AXES, scatter_dimension=0, tiled=False)
+
+
+def halves(value):
     grid = sizes()
     if grid != FAST:
-        return wide(lax.psum_scatter(value, AXES, scatter_dimension=0, tiled=False))
-    value = value.reshape((4, 2, 2, 2) + value.shape[1:])
-    value = sum_cores(value, grid, 3)
-    if depth_first:
-        return sum_plane(sum_depth(value, grid, value.dtype), grid, 0, jnp.float32)
-    return sum_depth(sum_plane(value, grid, 1, value.dtype), grid, jnp.float32)
+        return [value]
+    value = value.reshape((16, 2) + value.shape[1:])
+    core = place(grid, "c")
+    return [block_at(value, core, 1), block_at(value, core + 1, 1)]
 
 
 def by_devices(value):
-    if value.shape[0] > 1:
+    if value.ndim < 4:
         return value
     devices = lax.axis_size(AXES)
     return value.reshape((EXPERTS, devices, -1, value.shape[3])).transpose(1, 0, 2, 3)
+
+
+def single(kernel, name, inputs, outputs, scratch, flops, size):
+    values, specs = [], []
+    for item in inputs:
+        if not isinstance(item, tuple):
+            value, block, index = item, item.shape, (0,) * item.ndim
+        elif len(item) == 2:
+            value, block, index = item[0], (None,) + item[0].shape[1:], (item[1], 0, 0)
+        else:
+            value, block, index = item
+        values.append(value)
+        specs.append(pl.BlockSpec(block, functools.partial(lambda index, step: index, index)))
+    return pl.pallas_call(
+        kernel,
+        grid=(1,),
+        in_specs=specs,
+        out_specs=[pl.BlockSpec(o.shape, lambda step: (0, 0)) for o in outputs],
+        out_shape=outputs,
+        scratch_shapes=scratch,
+        compiler_params=pltpu.CompilerParams(vmem_limit_bytes=60 * 1024 * 1024),
+        cost_estimate=pl.CostEstimate(flops=flops, bytes_accessed=size, transcendentals=10**6),
+        name=name,
+    )(*values)
+
+
+CHUNK = 64
+EDGE = 8
+
+
+def tap_masks(segments):
+    half = KERNEL // 2
+    segment = segments[0]
+    length = segment.shape[0]
+    padded = jnp.pad(segment, (half, half), constant_values=-1)
+    same = [padded[k : k + length] == segment for k in range(KERNEL)]
+    masks = jnp.stack(same, 1).astype(jnp.float32)
+    return jnp.pad(masks, ((0, 0), (0, 128 - KERNEL)))
+
+
+def conv_front_kernel(
+    resid_ref, ctx_ref, ao_ref, gain_ref, bias_ref, gated_ref, taps_ref, mask_ref,
+    out_ref, normed_ref, joined_ref, depth_ref, sums_ref,
+    pad_ref,
+):
+    length, width = resid_ref.shape
+    resid = resid_ref[...] + mul(ctx_ref[...], ao_ref[...])
+    out_ref[...] = resid
+    unit, inverse = norm_parts(resid)
+    normed = (unit * gain_ref[...] + bias_ref[...]).astype(jnp.bfloat16)
+    normed_ref[...] = normed
+    joined = mul(normed, gated_ref[...])
+    joined_ref[...] = joined
+    pad_ref[:EDGE, :] = jnp.zeros((EDGE, width), jnp.float32)
+    pad_ref[EDGE + length :, :] = jnp.zeros((EDGE, width), jnp.float32)
+    pad_ref[EDGE : EDGE + length, :] = joined[:, :width] * sigmoid(joined[:, width:])
+    sums_ref[...] = jnp.zeros_like(sums_ref)
+
+    def chunk(index, carry):
+        at = pl.ds(pl.multiple_of(index * CHUNK, CHUNK), CHUNK)
+        window = pad_ref[pl.ds(pl.multiple_of(index * CHUNK, CHUNK), CHUNK + 2 * EDGE), :]
+        masks = mask_ref[at, :]
+        total = jnp.zeros((CHUNK, width), jnp.float32)
+        for k in range(KERNEL):
+            total = total + window[k + 1 : k + 1 + CHUNK] * masks[:, k : k + 1] * taps_ref[k : k + 1, :]
+        depth_ref[at, :] = total
+        sums_ref[0:1, :] += jnp.sum(total, 0, keepdims=True)
+        sums_ref[1:2, :] += jnp.sum(total * total, 0, keepdims=True)
+        return carry
+
+    lax.fori_loop(0, length // CHUNK, chunk, 0)
+
+
+def conv_front(resid, context, attend_out, gain, bias, gated_in, taps, masks):
+    length, width = resid.shape
+    low, full = jnp.bfloat16, jnp.float32
+    shape = jax.ShapeDtypeStruct
+    return single(
+        conv_front_kernel,
+        "conv_front",
+        [resid, context, attend_out, gain, bias, gated_in, taps, masks],
+        [
+            shape((length, width), full),
+            shape((length, width), low),
+            shape((length, 2 * width), full),
+            shape((length, width), full),
+            shape((2, width), full),
+        ],
+        [pltpu.VMEM((length + 2 * EDGE, width), full)],
+        4 * 10**9,
+        16 * 10**6,
+    )
+
+
+def batch_stats(stats, frames):
+    average = stats[0:1, :] * (1.0 / frames)
+    spread = stats[1:2, :] * (1.0 / frames) - average * average
+    return average, lax.rsqrt(spread + eps)
+
+
+def conv_tail_kernel(
+    frames, depth_ref, stats_ref, bgain_ref, bbias_ref, point_ref, resid_ref,
+    embed_ref, router_ref, gain_ref, bias_ref,
+    out_ref, normed_ref, probs_ref,
+):
+    average, inverse = batch_stats(stats_ref[...], frames)
+    shifted = (depth_ref[...] - average) * inverse * bgain_ref[...] + bbias_ref[...]
+    tail = (shifted * sigmoid(shifted)).astype(jnp.bfloat16)
+    resid = resid_ref[...] + mul(tail, point_ref[...])
+    out_ref[...] = resid
+    unit, spread = norm_parts(resid)
+    normed = (unit * gain_ref[...] + bias_ref[...]).astype(jnp.bfloat16)
+    normed_ref[...] = normed
+    probs_ref[...] = route_probs(normed, embed_ref[...], router_ref)
+
+
+def conv_tail(frames, depth, stats, bgain, bbias, point_out, resid, embedding, router, gain, bias):
+    length, width = resid.shape
+    shape = jax.ShapeDtypeStruct
+    return single(
+        functools.partial(conv_tail_kernel, frames),
+        "conv_tail",
+        [depth, stats, bgain, bbias, point_out, resid, embedding, router, gain, bias],
+        [
+            shape((length, width), jnp.float32),
+            shape((length, width), jnp.bfloat16),
+            shape((length, 128), jnp.float32),
+        ],
+        [],
+        10**9,
+        8 * 10**6,
+    )
+
+
+def conv_turn_kernel(
+    frames, slope_ref, depth_ref, stats_ref, bgain_ref, bbias_ref, point_ref,
+    dshift_ref, dpoint_ref, sums_ref,
+):
+    average, inverse = batch_stats(stats_ref[...], frames)
+    centered = (depth_ref[...] - average) * inverse
+    shifted = centered * bgain_ref[...] + bbias_ref[...]
+    sigma = sigmoid(shifted)
+    low = slope_ref[...].astype(jnp.bfloat16)
+    dpoint_ref[...] = mul((shifted * sigma).astype(jnp.bfloat16), low, TN).astype(jnp.bfloat16)
+    dshift = mul(low, point_ref[...], NT) * (sigma * (1.0 + shifted * (1.0 - sigma)))
+    dshift_ref[...] = dshift
+    sums_ref[0:1, :] = jnp.sum(dshift * centered, 0, keepdims=True)
+    sums_ref[1:2, :] = jnp.sum(dshift, 0, keepdims=True)
+
+
+def conv_turn(frames, slope, depth, stats, bgain, bbias, point_out):
+    length, width = slope.shape
+    shape = jax.ShapeDtypeStruct
+    return single(
+        functools.partial(conv_turn_kernel, frames),
+        "conv_turn",
+        [slope, depth, stats, bgain, bbias, point_out],
+        [
+            shape((length, width), jnp.float32),
+            shape((width, width), jnp.bfloat16),
+            shape((2, width), jnp.float32),
+        ],
+        [],
+        10**9,
+        8 * 10**6,
+    )
+
+
+def conv_back_kernel(
+    frames, slope_ref, dshift_ref, depth_ref, stats_ref, sums_ref, bgain_ref, joined_ref, normed_ref,
+    resid_ref, gain_ref, gated_ref, taps_ref, mask_ref,
+    out_ref, dgated_ref, dtaps_ref, dgain_ref, dbias_ref,
+    pad_ref, dpad_ref, dtap_ref, dglu_ref,
+):
+    length, width = resid_ref.shape
+    average, inverse = batch_stats(stats_ref[...], frames)
+    bgain = bgain_ref[...]
+    sums = sums_ref[...] * (1.0 / frames) * bgain
+    centered = (depth_ref[...] - average) * inverse
+    edge = jnp.zeros((EDGE, width), jnp.float32)
+    left = joined_ref[:, :width]
+    sigma = sigmoid(joined_ref[:, width:])
+    for ref, value in (
+        (pad_ref, left * sigma),
+        (dpad_ref, inverse * (dshift_ref[...] * bgain - sums[1:2, :] - centered * sums[0:1, :])),
+    ):
+        ref[:EDGE, :] = edge
+        ref[EDGE + length :, :] = edge
+        ref[EDGE : EDGE + length, :] = value
+    dtap_ref[...] = jnp.zeros_like(dtap_ref)
+
+    def chunk(index, carry):
+        at = pl.ds(pl.multiple_of(index * CHUNK, CHUNK), CHUNK)
+        around = pl.ds(pl.multiple_of(index * CHUNK, CHUNK), CHUNK + 2 * EDGE)
+        window = pad_ref[around, :]
+        dwindow = dpad_ref[around, :]
+        masks = mask_ref[at, :]
+        middle = dwindow[EDGE : EDGE + CHUNK]
+        total = jnp.zeros((CHUNK, width), jnp.float32)
+        for k in range(KERNEL):
+            mask = masks[:, k : k + 1]
+            back = KERNEL - 1 - k
+            total = total + dwindow[k + 1 : k + 1 + CHUNK] * mask * taps_ref[back : back + 1, :]
+            term = window[k + 1 : k + 1 + CHUNK] * mask * middle
+            dtap_ref[8 * k : 8 * k + 8, :] += jnp.sum(term.reshape(CHUNK // 8, 8, width), 0)
+        dglu_ref[at, :] = total
+        return carry
+
+    lax.fori_loop(0, length // CHUNK, chunk, 0)
+    for k in range(KERNEL):
+        dtaps_ref[k : k + 1, :] = jnp.sum(dtap_ref[8 * k : 8 * k + 8, :], 0, keepdims=True)
+    dglu = dglu_ref[...]
+    low = jnp.concatenate(
+        [
+            (dglu * sigma).astype(jnp.bfloat16),
+            (dglu * left * sigma * (1.0 - sigma)).astype(jnp.bfloat16),
+        ],
+        1,
+    )
+    dgated_ref[...] = mul(normed_ref[...], low, TN).astype(jnp.bfloat16)
+    slope = mul(low, gated_ref[...], NT)
+    unit, spread = norm_parts(resid_ref[...])
+    dgain_ref[...] = jnp.sum(slope * unit, 0, keepdims=True)
+    dbias_ref[...] = jnp.sum(slope, 0, keepdims=True)
+    out_ref[...] = slope_ref[...] + norm_slope(unit, spread, slope, gain_ref[...])
+
+
+def conv_back(
+    frames, slope, dshift, depth, stats, sums, bgain, joined, normed, resid, gain, gated_in, taps, masks
+):
+    length, width = resid.shape
+    full = jnp.float32
+    shape = jax.ShapeDtypeStruct
+    padded = pltpu.VMEM((length + 2 * EDGE, width), full)
+    return single(
+        functools.partial(conv_back_kernel, frames),
+        "conv_back",
+        [slope, dshift, depth, stats, sums, bgain, joined, normed, resid, gain, gated_in, taps, masks],
+        [
+            shape((length, width), full),
+            shape((width, 2 * width), jnp.bfloat16),
+            shape((KERNEL, width), full),
+            shape((1, width), full),
+            shape((1, width), full),
+        ],
+        [
+            padded,
+            padded,
+            pltpu.VMEM((8 * KERNEL, width), full),
+            pltpu.VMEM((length, width), full),
+        ],
+        6 * 10**9,
+        20 * 10**6,
+    )
 
 
 ROWS = (256, 384, 512)
@@ -635,8 +974,8 @@
 
 
 class Weights:
-    def __init__(self, gathered):
-        self.arrays, self.ids = gathered
+    def __init__(self, pieces, ids):
+        self.arrays, self.ids = pieces, ids
         rows = sum(piece.shape[0] * piece.shape[2] for piece in self.arrays)
         self.shape = (rows, self.arrays[0].shape[3])
         self.rows = self.arrays[0].shape[2]
@@ -657,12 +996,16 @@
     return pl.BlockSpec((shape[0], 1) + shape[2:], lambda e, *_: (0, e, 0, 0))
 
 
-def grads_shape(weights):
+def grads_outputs(weights):
     count = weights.shape[0] // weights.rows
-    return (count, EXPERTS, weights.rows, weights.shape[1])
-
-
-def expert_call(kernel, name, counts, weights, inputs, outputs, scratch, flops):
+    if count == 1:
+        shapes = [(1, EXPERTS) + weights.shape]
+    else:
+        shapes = [(count // 2, EXPERTS, weights.rows, weights.shape[1])] * 2
+    return [(struct(shape, jnp.bfloat16), by_owner(shape)) for shape in shapes]
+
+
+def expert_call(kernel, name, counts, weights, inputs, outputs, scratch, flops, with_core=False):
     scalars = [counts] + [weight.ids for weight in weights]
     arrays = [piece for weight in weights for piece in weight.arrays]
     n_in, n_out = len(inputs), len(outputs)
@@ -677,7 +1020,10 @@
             own = pieces[: len(weight.arrays)]
             pieces = pieces[len(weight.arrays) :]
             assemble(own, ids[at], rest[at])
-        kernel(expert, count_ref[expert], *rest[: len(weights)], *operands, *results, *rest[len(weights) :])
+        kernel(
+            expert, count_ref[expert], *rest[: len(weights)], *operands, *results, *rest[len(weights) :],
+            **({"core": count_ref[EXPERTS]} if with_core else {}),
+        )
 
     return pl.pallas_call(
         body,
@@ -703,7 +1049,13 @@
 
 
 def whole_in(value):
+    if isinstance(value, tuple):
+        return row_in(*value)
     return (value, fixed(value.shape))
+
+
+def row_in(vectors, index):
+    return (vectors, pl.BlockSpec((None, 1, vectors.shape[2]), lambda e, *_: (index, 0, 0)))
 
 
 def whole_out(shape, dtype=jnp.float32):
@@ -883,31 +1235,37 @@
     return sigma * (1.0 + inner * (1.0 - sigma))
 
 
-def store_rows(ref, span, value):
-    owned = ref.shape[2]
-    count = span.stop - span.start
-    if owned > count:
-        ref[0, 0, span, :] = value
-    else:
-        ref[span.start // owned : span.stop // owned] = value.reshape((count // owned,) + ref.shape[1:])
-
-
-def down_grads(rows, inner_ref, dpicked, ddown_ref):
+def store_rows(refs, core, first, span, value):
+    rows = value.shape[0]
+    if len(refs) == 1:
+        refs[0][0, 0, first : first + rows, span] = value
+        return
+    owned = refs[0].shape[2]
+    value = value.reshape((rows // owned // 2, 2, 1, owned, value.shape[1]))
+    at = slice(first // owned // 2, (first + rows) // owned // 2)
+    for own in range(2):
+
+        @pl.when(core == own)
+        def store():
+            refs[0][at, :, :, span] = value[:, own]
+            refs[1][at, :, :, span] = value[:, 1 - own]
+
+
+def down_grads(rows, core, inner_ref, dpicked, ddown_refs):
     for span in spans(inner_ref.shape[2]):
         grads = mul(active_of(inner_ref[0, :rows, span]), dpicked, TN)
-        store_rows(ddown_ref, span, grads.astype(jnp.bfloat16))
-
-
-def up_grads(picked, dinner, span, dup_ref):
-    grads = mul(picked, dinner, TN).astype(jnp.bfloat16)
-    dup_ref[:, :, :, span] = grads.reshape(dup_ref.shape[:3] + (grads.shape[1],))
+        store_rows(ddown_refs, core, span.start, slice(None), grads.astype(jnp.bfloat16))
+
+
+def up_grads(core, picked, dinner, span, dup_refs):
+    store_rows(dup_refs, core, 0, span, mul(picked, dinner, TN).astype(jnp.bfloat16))
 
 
 def first_back_kernel(
-    expert, count, slope_ref, probs_ref, route_ref, branch_ref, posr_ref, inner_ref,
-    ddown_ref, dpicked_ref, dlogits_ref,
-    low_ref,
+    expert, count, slope_ref, probs_ref, route_ref, branch_ref, posr_ref, inner_ref, *rest, core
 ):
+    *ddown_refs, dpicked_ref, dlogits_ref, low_ref = rest
+
     @pl.when(expert == 0)
     def first():
         enter_slope(slope_ref, probs_ref, route_ref, branch_ref, low_ref, dlogits_ref)
@@ -916,31 +1274,29 @@
         hot = one_hot_rows(posr_ref[...], expert * CAPACITY, rows)
         dpicked = mul(hot, low_ref[...]).astype(jnp.bfloat16)
         dpicked_ref[0, :rows, :] = dpicked
-        down_grads(rows, inner_ref, dpicked, ddown_ref)
+        down_grads(rows, core, inner_ref, dpicked, ddown_refs)
 
     sized(count, run)
 
 
 def first_back_call(counts, pos_row, slope, probs, routes, branch, inner, down):
     length, width = slope.shape
-    shape = grads_shape(down)
     return expert_call(
         first_back_kernel,
         "first_down_grads",
         counts,
         [],
         [whole_in(v) for v in (slope, probs, routes, branch, pos_row)] + [expert_in(inner)],
-        [
-            (struct(shape, jnp.bfloat16), by_owner(shape)),
-            expert_out((CAPACITY, width)),
-            whole_out((length, 128)),
-        ],
+        grads_outputs(down) + [expert_out((CAPACITY, width)), whole_out((length, 128))],
         [pltpu.VMEM((length, width), jnp.bfloat16)],
         5 * 10**9,
-    )
-
-
-def first_middle_kernel(expert, count, down_ref, dpicked_ref, picked_ref, inner_ref, dup_ref, dinner_ref):
+        True,
+    )
+
+
+def first_middle_kernel(expert, count, down_ref, dpicked_ref, picked_ref, inner_ref, *rest, core):
+    *dup_refs, dinner_ref = rest
+
     def run(rows):
         dpicked = dpicked_ref[0, :rows, :]
         picked = picked_ref[0, :rows, :]
@@ -948,22 +1304,22 @@
             dactive = mul(dpicked, down_ref[span, :], NT)
             dinner = (dactive * slope_of(inner_ref[0, :rows, span])).astype(jnp.bfloat16)
             dinner_ref[0, :rows, span] = dinner
-            up_grads(picked, dinner, span, dup_ref)
+            up_grads(core, picked, dinner, span, dup_refs)
 
     sized(count, run)
 
 
 def first_middle_call(counts, dpicked, picked, inner, up, down):
-    shape = grads_shape(up)
     return expert_call(
         first_middle_kernel,
         "first_up_grads",
         counts,
         [down],
         [expert_in(v) for v in (dpicked, picked, inner)],
-        [(struct(shape, jnp.bfloat16), by_owner(shape)), expert_out(inner.shape[1:])],
+        grads_outputs(up) + [expert_out(inner.shape[1:])],
         [],
         9 * 10**9,
+        True,
     )
 
 
@@ -1128,259 +1484,30 @@
 
 def expert_enter(resid, embedding, router, gain, bias):
     length, width = resid.shape
-    return pl.pallas_call(
+    return single(
         enter_kernel,
-        out_shape=[
-            jax.ShapeDtypeStruct((length, width), jnp.bfloat16),
-            jax.ShapeDtypeStruct((length, 128), jnp.float32),
-        ],
-        compiler_params=pltpu.CompilerParams(vmem_limit_bytes=40 * 1024 * 1024),
-        cost_estimate=pl.CostEstimate(flops=10**9, bytes_accessed=4 * 10**6, transcendentals=10**5),
-        name="expert_enter",
-    )(resid, embedding, router, gain, bias)
-
-
-def places(routes):
+        "expert_enter",
+        [resid, embedding, router, gain, bias],
+        [struct((length, width), jnp.bfloat16), struct((length, 128))],
+        [],
+        10**9,
+        4 * 10**6,
+    )
+
+
+def places(routes, core):
     length = routes.shape[0]
     chosen = (routes == jnp.arange(EXPERTS, dtype=jnp.int32)[None, :]).astype(jnp.float32)
     row = lax.broadcasted_iota(jnp.int32, (length, length), 0)
     before = (lax.broadcasted_iota(jnp.int32, (length, length), 1) < row).astype(jnp.bfloat16)
     earlier = product(before, chosen.astype(jnp.bfloat16))
     slot = jnp.sum(earlier * chosen, 1).astype(jnp.int32) + routes[:, 0] * CAPACITY
-    counts = jnp.sum(chosen, 0).astype(jnp.int32)
+    counts = jnp.concatenate([jnp.sum(chosen, 0).astype(jnp.int32), core])
     return counts, slot[None, :], slot[:, None]
-
-
-CHUNK = 64
-EDGE = 8
-
-
-def tap_masks(segments):
-    half = KERNEL // 2
-    segment = segments[0]
-    length = segment.shape[0]
-    padded = jnp.pad(segment, (half, half), constant_values=-1)
-    same = [padded[k : k + length] == segment for k in range(KERNEL)]
-    masks = jnp.stack(same, 1).astype(jnp.float32)
-    return jnp.pad(masks, ((0, 0), (0, 128 - KERNEL)))
-
-
-def conv_front_kernel(
-    resid_ref, ctx_ref, ao_ref, gain_ref, bias_ref, gated_ref, taps_ref, mask_ref,
-    out_ref, normed_ref, joined_ref, depth_ref, sums_ref,
-    pad_ref,
-):
-    length, width = resid_ref.shape
-    resid = resid_ref[...] + mul(ctx_ref[...], ao_ref[...])
-    out_ref[...] = resid
-    unit, inverse = norm_parts(resid)
-    normed = (unit * gain_ref[...] + bias_ref[...]).astype(jnp.bfloat16)
-    normed_ref[...] = normed
-    joined = mul(normed, gated_ref[...])
-    joined_ref[...] = joined
-    pad_ref[:EDGE, :] = jnp.zeros((EDGE, width), jnp.float32)
-    pad_ref[EDGE + length :, :] = jnp.zeros((EDGE, width), jnp.float32)
-    pad_ref[EDGE : EDGE + length, :] = joined[:, :width] * sigmoid(joined[:, width:])
-    sums_ref[...] = jnp.zeros_like(sums_ref)
-
-    def chunk(index, carry):
-        at = pl.ds(pl.multiple_of(index * CHUNK, CHUNK), CHUNK)
-        window = pad_ref[pl.ds(pl.multiple_of(index * CHUNK, CHUNK), CHUNK + 2 * EDGE), :]
-        masks = mask_ref[at, :]
-        total = jnp.zeros((CHUNK, width), jnp.float32)
-        for k in range(KERNEL):
-            total = total + window[k + 1 : k + 1 + CHUNK] * masks[:, k : k + 1] * taps_ref[k : k + 1, :]
-        depth_ref[at, :] = total
-        sums_ref[0:1, :] += jnp.sum(total, 0, keepdims=True)
-        sums_ref[1:2, :] += jnp.sum(total * total, 0, keepdims=True)
-        return carry
-
-    lax.fori_loop(0, length // CHUNK, chunk, 0)
-
-
-def conv_front(resid, context, attend_out, gain, bias, gated_in, taps, masks):
-    length, width = resid.shape
-    low, full = jnp.bfloat16, jnp.float32
-    shape = jax.ShapeDtypeStruct
-    return pl.pallas_call(
-        conv_front_kernel,
-        out_shape=[
-            shape((length, width), full),
-            shape((length, width), low),
-            shape((length, 2 * width), full),
-            shape((length, width), full),
-            shape((2, width), full),
-        ],
-        scratch_shapes=[pltpu.VMEM((length + 2 * EDGE, width), full)],
-        compiler_params=pltpu.CompilerParams(vmem_limit_bytes=56 * 1024 * 1024),
-        cost_estimate=pl.CostEstimate(flops=4 * 10**9, bytes_accessed=16 * 10**6, transcendentals=10**6),
-        name="conv_front",
-    )(resid, context, attend_out, gain, bias, gated_in, taps, masks)
-
-
-def batch_stats(stats, frames):
-    average = stats[0:1, :] * (1.0 / frames)
-    spread = stats[1:2, :] * (1.0 / frames) - average * average
-    return average, lax.rsqrt(spread + eps)
-
-
-def conv_tail_kernel(
-    frames, depth_ref, stats_ref, bgain_ref, bbias_ref, point_ref, resid_ref,
-    embed_ref, router_ref, gain_ref, bias_ref,
-    out_ref, normed_ref, probs_ref,
-):
-    average, inverse = batch_stats(stats_ref[...], frames)
-    shifted = (depth_ref[...] - average) * inverse * bgain_ref[...] + bbias_ref[...]
-    tail = (shifted * sigmoid(shifted)).astype(jnp.bfloat16)
-    resid = resid_ref[...] + mul(tail, point_ref[...])
-    out_ref[...] = resid
-    unit, spread = norm_parts(resid)
-    normed = (unit * gain_ref[...] + bias_ref[...]).astype(jnp.bfloat16)
-    normed_ref[...] = normed
-    probs_ref[...] = route_probs(normed, embed_ref[...], router_ref)
-
-
-def conv_tail(frames, depth, stats, bgain, bbias, point_out, resid, embedding, router, gain, bias):
-    length, width = resid.shape
-    shape = jax.ShapeDtypeStruct
-    return pl.pallas_call(
-        functools.partial(conv_tail_kernel, frames),
-        out_shape=[
-            shape((length, width), jnp.float32),
-            shape((length, width), jnp.bfloat16),
-            shape((length, 128), jnp.float32),
-        ],
-        compiler_params=pltpu.CompilerParams(vmem_limit_bytes=56 * 1024 * 1024),
-        cost_estimate=pl.CostEstimate(flops=10**9, bytes_accessed=8 * 10**6, transcendentals=10**6),
-        name="conv_tail",
-    )(depth, stats, bgain, bbias, point_out, resid, embedding, router, gain, bias)
-
-
-def conv_turn_kernel(
-    frames, slope_ref, depth_ref, stats_ref, bgain_ref, bbias_ref, point_ref,
-    dshift_ref, dpoint_ref, sums_ref,
-):
-    average, inverse = batch_stats(stats_ref[...], frames)
-    centered = (depth_ref[...] - average) * inverse
-    shifted = centered * bgain_ref[...] + bbias_ref[...]
-    sigma = sigmoid(shifted)
-    low = slope_ref[...].astype(jnp.bfloat16)
-    dpoint_ref[...] = mul((shifted * sigma).astype(jnp.bfloat16), low, TN)
-    dshift = mul(low, point_ref[...], NT) * (sigma * (1.0 + shifted * (1.0 - sigma)))
-    dshift_ref[...] = dshift
-    sums_ref[0:1, :] = jnp.sum(dshift * centered, 0, keepdims=True)
-    sums_ref[1:2, :] = jnp.sum(dshift, 0, keepdims=True)
-
-
-def conv_turn(frames, slope, depth, stats, bgain, bbias, point_out):
-    length, width = slope.shape
-    shape = jax.ShapeDtypeStruct
-    return pl.pallas_call(
-        functools.partial(conv_turn_kernel, frames),
-        out_shape=[
-            shape((length, width), jnp.float32),
-            shape((width, width), jnp.float32),
-            shape((2, width), jnp.float32),
-        ],
-        compiler_params=pltpu.CompilerParams(vmem_limit_bytes=56 * 1024 * 1024),
-        cost_estimate=pl.CostEstimate(flops=10**9, bytes_accessed=8 * 10**6, transcendentals=10**6),
-        name="conv_turn",
-    )(slope, depth, stats, bgain, bbias, point_out)
-
-
-def conv_back_kernel(
-    frames, slope_ref, dshift_ref, depth_ref, stats_ref, sums_ref, bgain_ref, joined_ref, normed_ref,
-    resid_ref, gain_ref, gated_ref, taps_ref, mask_ref,
-    out_ref, dgated_ref, dtaps_ref, dgain_ref, dbias_ref,
-    pad_ref, dpad_ref, dtap_ref, dglu_ref,
-):
-    length, width = resid_ref.shape
-    average, inverse = batch_stats(stats_ref[...], frames)
-    bgain = bgain_ref[...]
-    sums = sums_ref[...] * (1.0 / frames) * bgain
-    centered = (depth_ref[...] - average) * inverse
-    edge = jnp.zeros((EDGE, width), jnp.float32)
-    left = joined_ref[:, :width]
-    sigma = sigmoid(joined_ref[:, width:])
-    for ref, value in (
-        (pad_ref, left * sigma),
-        (dpad_ref, inverse * (dshift_ref[...] * bgain - sums[1:2, :] - centered * sums[0:1, :])),
-    ):
-        ref[:EDGE, :] = edge
-        ref[EDGE + length :, :] = edge
-        ref[EDGE : EDGE + length, :] = value
-    dtap_ref[...] = jnp.zeros_like(dtap_ref)
-
-    def chunk(index, carry):
-        at = pl.ds(pl.multiple_of(index * CHUNK, CHUNK), CHUNK)
-        around = pl.ds(pl.multiple_of(index * CHUNK, CHUNK), CHUNK + 2 * EDGE)
-        window = pad_ref[around, :]
-        dwindow = dpad_ref[around, :]
-        masks = mask_ref[at, :]
-        middle = dwindow[EDGE : EDGE + CHUNK]
-        total = jnp.zeros((CHUNK, width), jnp.float32)
-        for k in range(KERNEL):
-            mask = masks[:, k : k + 1]
-            back = KERNEL - 1 - k
-            total = total + dwindow[k + 1 : k + 1 + CHUNK] * mask * taps_ref[back : back + 1, :]
-            term = window[k + 1 : k + 1 + CHUNK] * mask * middle
-            dtap_ref[8 * k : 8 * k + 8, :] += jnp.sum(term.reshape(CHUNK // 8, 8, width), 0)
-        dglu_ref[at, :] = total
-        return carry
-
-    lax.fori_loop(0, length // CHUNK, chunk, 0)
-    for k in range(KERNEL):
-        dtaps_ref[k : k + 1, :] = jnp.sum(dtap_ref[8 * k : 8 * k + 8, :], 0, keepdims=True)
-    dglu = dglu_ref[...]
-    low = jnp.concatenate(
-        [
-            (dglu * sigma).astype(jnp.bfloat16),
-            (dglu * left * sigma * (1.0 - sigma)).astype(jnp.bfloat16),
-        ],
-        1,
-    )
-    dgated_ref[...] = mul(normed_ref[...], low, TN)
-    slope = mul(low, gated_ref[...], NT)
-    unit, spread = norm_parts(resid_ref[...])
-    dgain_ref[...] = jnp.sum(slope * unit, 0, keepdims=True)
-    dbias_ref[...] = jnp.sum(slope, 0, keepdims=True)
-    out_ref[...] = slope_ref[...] + norm_slope(unit, spread, slope, gain_ref[...])
-
-
-def conv_back(
-    frames, slope, dshift, depth, stats, sums, bgain, joined, normed, resid, gain, gated_in, taps, masks
-):
-    length, width = resid.shape
-    full = jnp.float32
-    shape = jax.ShapeDtypeStruct
-    padded = pltpu.VMEM((length + 2 * EDGE, width), full)
-    return pl.pallas_call(
-        functools.partial(conv_back_kernel, frames),
-        out_shape=[
-            shape((length, width), full),
-            shape((width, 2 * width), full),
-            shape((KERNEL, width), full),
-            shape((1, width), full),
-            shape((1, width), full),
-        ],
-        scratch_shapes=[
-            padded,
-            padded,
-            pltpu.VMEM((8 * KERNEL, width), full),
-            pltpu.VMEM((length, width), full),
-        ],
-        compiler_params=pltpu.CompilerParams(vmem_limit_bytes=60 * 1024 * 1024),
-        cost_estimate=pl.CostEstimate(flops=6 * 10**9, bytes_accessed=20 * 10**6, transcendentals=10**6),
-        name="conv_back",
-    )(slope, dshift, depth, stats, sums, bgain, joined, normed, resid, gain, gated_in, taps, masks)
 
 
 def gather_rows(value):
     return lax.all_gather(value, AXES, axis=0, tiled=True)
-
-
-def scatter_small(value):
-    return scatter_blocks(value.reshape((lax.axis_size(AXES), -1) + value.shape[1:]), False)
 
 
 def gathered_count(devices):
@@ -1392,23 +1519,11 @@
         up = by_devices(value[:, :, :width])
         down = value[0, :, width:].reshape(EXPERTS, width, -1, width).transpose(0, 2, 1, 3)
         down = by_devices(down.reshape(1, EXPERTS, -1, width))
-        return [wide(lax.psum_scatter(part, AXES, scatter_dimension=0)) for part in (up, down)]
-    total = wide(lax.psum_scatter(value, AXES, scatter_dimension=0, tiled=False))
+        return [wide(scatter_rows(part)) for part in (up, down)]
+    total = wide(scatter_rows(value))
     owned = width // devices
     down = total[:, owned:].reshape(EXPERTS, owned, -1, width).transpose(0, 2, 1, 3)
     return [total[:, :owned], down.reshape(EXPERTS, -1, width)]
-
-
-def router_columns(router):
-    count = router.shape[0] // 2
-    return router.reshape(2, count, EXPERTS).transpose(1, 0, 2).reshape(count, 2 * EXPERTS)
-
-
-def router_rows(packed, devices):
-    count = packed.shape[0] // devices
-    return (
-        packed.reshape(devices, count, 2, EXPERTS).transpose(0, 2, 1, 3).reshape(-1, EXPERTS)
-    )
 
 
 def on_device(
@@ -1445,11 +1560,18 @@
     final_gain,
     final_bias,
 ):
-    segment = segments[0]
     devices = lax.axis_size(AXES)
     length, width = inputs.shape
     frames = length * devices
-    vectors = jnp.stack(
+    core = jnp.reshape(place(sizes(), "c"), (1,))
+
+    first_up_chain, up_ids = gather_experts(first_up, True)
+    first_down_chain, down_ids = gather_experts(first_down, False)
+    n_vec = 14
+    taps_at = n_vec * first_gain.shape[0]
+    routers_at = taps_at + depth_kernel.size
+    n_router = first_router.size
+    small = jnp.concatenate(
         [
             first_gain,
             first_bias,
@@ -1465,81 +1587,72 @@
             batch_bias,
             final_gain,
             final_bias,
-        ],
-        1,
-    )
-    n_vec = vectors.shape[1]
-    small = jnp.concatenate(
-        [
-            vectors,
-            depth_kernel.T,
-            router_columns(first_router),
-            router_columns(second_router),
-        ],
-        1,
-    )
-    n_small = small.shape[1]
-    small = jnp.pad(small, ((0, 0), (0, 128 - n_small)))
-    first_ups = Weights(gather_experts(first_up, True))
-    first_downs = Weights(gather_experts(first_down, False))
-    small = gather_small(small).reshape(width, 128)[:, :n_small]
+            depth_kernel.reshape(-1),
+            first_router.reshape(-1),
+            second_router.reshape(-1),
+        ]
+    )
+    own = project_in.shape[0]
+    small = jnp.pad(small, (0, -small.size % (128 * own))).reshape(own, -1)
     packed = gather_rows(
-        jnp.concatenate([project_in, relative_weight, attend_out, gated_in, point_out], 1)
-    )
-    rows = small[:, : n_vec + KERNEL].T
-    col = n_vec + KERNEL
-    first_router_full = router_rows(small[:, col : col + 2 * EXPERTS], devices)
-    second_router_full = router_rows(small[:, col + 2 * EXPERTS : col + 4 * EXPERTS], devices)
-    at = 0
-    project_full = packed[:, at : at + 3 * width]
-    at = at + 3 * width
-    relative_full = packed[:, at : at + width]
-    at = at + width
-    attend_out_full = packed[:, at : at + width]
-    at = at + width
-    gated_full = packed[:, at : at + 2 * width]
-    at = at + 2 * width
-    point_full = packed[:, at : at + width]
-    relative_full = relative_full.reshape(width // 2, 2, width).transpose(1, 0, 2).reshape(width, width)
-    floats = rows.astype(jnp.float32)
+        jnp.concatenate([project_in, relative_weight, attend_out, point_out, gated_in, small], 1)
+    )
+    small = packed[:, 8 * width :].reshape(devices, -1)
+    second_ups = Weights(*gather_whole(second_up))
+    second_downs = Weights(*gather_whole(second_down))
+
+    first_places = places(routes_first, core)
+    second_places = places(routes_second, core)
+    masks = tap_masks(segments)
+    segment_column = segments.reshape(length, 1)
+    cosine, sine = angles(length, width)
+    table = jnp.concatenate([cosine, sine], 1).astype(jnp.bfloat16)
+    masks, table, cosine, sine = advance(
+        [first_up_chain, first_down_chain], masks, table, cosine, sine
+    )
+    pos_row, pos_col = first_down_chain.step(first_places[1], first_places[2])
+    tables = (table, cosine, sine)
+    counts = first_places[0]
+
+    floats = small[:, :taps_at].reshape(devices, n_vec, -1).transpose(1, 0, 2)
+    floats = floats.reshape(n_vec, 1, width).astype(jnp.float32)
+    taps = small[:, taps_at:routers_at].reshape(devices, KERNEL, -1).transpose(1, 0, 2)
+    taps = taps.reshape(KERNEL, width).astype(jnp.float32)
+
+    def router_wide(start):
+        router = small[:, start : start + n_router].reshape(2 * width, EXPERTS)
+        return jnp.pad(router, ((0, 0), (0, 128 - EXPERTS)))
+
+    first_router_full = router_wide(routers_at)
+    second_router_full = router_wide(routers_at + n_router)
 
     def vec(index):
-        return floats[index : index + 1]
-
-    def router_wide(router):
-        return jnp.pad(router, ((0, 0), (0, 128 - EXPERTS)))
-
-    first_router_full = router_wide(first_router_full)
-    second_router_full = router_wide(second_router_full)
-    taps = floats[n_vec : n_vec + KERNEL]
-    masks = tap_masks(segments)
-    first_places = places(routes_first)
-    second_places = places(routes_second)
-    second_ups = Weights(gather_whole(second_up))
-    second_downs = Weights(gather_whole(second_down))
-    attend_full = (
-        vec(4),
-        vec(5),
-        project_full,
-        relative_full,
-        vec(6),
-        vec(7),
-        attend_out_full,
-    )
-    cosine, sine = angles(length, width)
-    tables = (jnp.concatenate([cosine, sine], 1).astype(jnp.bfloat16), cosine, sine)
+        return (floats, index)
 
     first_normed, first_probs = expert_enter(inputs, embedding, first_router_full, vec(0), vec(1))
-    counts, pos_row, pos_col = first_places
+    first_normed, first_probs, floats, taps, second_router_full = first_up_chain.step(
+        first_normed, first_probs, floats, taps, second_router_full
+    )
+    first_ups = Weights(first_up_chain.finish(), up_ids)
+
+    attend_full = (vec(4), vec(5), packed, vec(6), vec(7))
+    attend_out_full = (packed, (width, width), (0, 4))
+    point_full = (packed, (width, width), (0, 5))
+    gated_full = (packed, (width, 2 * width), (0, 3))
+
     first_picked, first_inner = first_up_call(counts, pos_row, first_normed, first_ups)
+    first_downs = Weights(first_down_chain.finish(), down_ids)
     first_resid, first_branch = first_down_call(
         counts, pos_col, first_inner, inputs, first_probs, routes_first, first_downs
     )
-    attend_kept = attention_forward(first_resid, segments, attend_full, tables)
+    pairs = HEADS // 2
+    kept = attention_forward(
+        0, pairs, first_resid, segments, segment_column, attend_full, tables
+    )
     attend_resid, conv_normed, joined, depth, stats = conv_front(
-        first_resid, attend_kept[6], attend_out_full, vec(8), vec(9), gated_full, taps, masks
-    )
-    stats = total_of(stats)
+        first_resid, kept[6], attend_out_full, vec(8), vec(9), gated_full, taps, masks
+    )
+    stats, _ = total_of(stats)
     conv_resid, second_normed, second_probs = conv_tail(
         frames, depth, stats, vec(10), vec(11), point_full, attend_resid,
         embedding, second_router_full, vec(2), vec(3),
@@ -1561,38 +1674,37 @@
         second_router_full, conv_resid, second_normed, embedding, vec(2), second_ups, second_downs,
     )
     dshift, dpoint, sums = conv_turn(frames, slope, depth, stats, vec(10), vec(11), point_full)
-    sums, dpicked = lax.optimization_barrier((sums, dpicked))
-    second_large = scatter_second(
-        second_grads_call(
-            second_places[0], second_picked, second_inner, dpicked, dinner, gathered_count(devices)
-        ),
-        devices,
-        width,
-    )
-    sums = total_of(sums)
+
+    def deferred(sums):
+        held, _ = tie(dpicked, sums)
+        return second_grads_call(
+            second_places[0], second_picked, second_inner, held, dinner, gathered_count(devices)
+        )
+
+    sums, second_large = total_of(sums, deferred)
+    second_large = scatter_second(second_large, devices, width)
     slope, dgated, dtaps, dgain_depth, dbias_depth = conv_back(
         frames, slope, dshift, depth, stats, sums, vec(10), joined, conv_normed,
         attend_resid, vec(8), gated_full, taps, masks,
     )
-    slope, dao, dpq, dpk, dpv, drel, dcb, dpb, dgain_attend, dbias_attend = attention_backward(
-        first_resid, slope, attend_full, tables, attend_kept
-    )
-    drel = drel.reshape(2, width // 2, width).transpose(1, 0, 2).reshape(width, width)
-    matrices = scatter_small(
-        jnp.concatenate([dpq, dpk, dpv, drel, dao, dgated, dpoint], 1).astype(jnp.bfloat16)
-    )
-    first_ddown, dpicked, dlogits = first_back_call(
+    slope, dao, dpq, dpk, dpv, drel, attend_vec = attention_backward(
+        0, pairs, True, first_resid, slope, attend_full, tables, kept, None
+    )
+    *first_ddown, first_dpicked, dlogits = first_back_call(
         counts, pos_row, slope, first_probs, routes_first, first_branch, first_inner, first_downs
     )
-    first_down_grad = scatter_blocks(by_devices(first_ddown), True)
-    first_dup, dinner = first_middle_call(
-        counts, dpicked, first_picked, first_inner, first_ups, first_downs
-    )
-    first_up_grad = scatter_blocks(by_devices(first_dup), False)
+    first_ddown = scatter_parts(first_ddown, True)
+    *first_dup, first_dinner = first_middle_call(
+        counts, first_dpicked, first_picked, first_inner, first_ups, first_downs
+    )
+    first_dup = scatter_parts(first_dup, False)
+    (first_dinner,) = first_ddown.step(first_dinner)
     slope, dgain_first, dbias_first, drouter_first = first_leave_call(
-        counts, pos_col, dinner, dlogits, first_router_full, slope, inputs, first_normed, embedding,
+        counts, pos_col, first_dinner, dlogits, first_router_full, slope, inputs, first_normed, embedding,
         vec(0), first_ups,
     )
+    (slope,) = advance([first_ddown], slope)
+    (slope,) = advance([first_dup], slope)
 
     def columns_of(grad):
         return (
@@ -1602,33 +1714,41 @@
             .reshape(width, 2 * EXPERTS)
         )
 
-    small_grad = scatter_small(
-        jnp.concatenate(
-            [
-                jnp.concatenate(
-                    [
-                        dgain_first,
-                        dbias_first,
-                        dgain_second,
-                        dbias_second,
-                        dgain_attend,
-                        dbias_attend,
-                        dcb,
-                        dpb,
-                        dgain_depth,
-                        dbias_depth,
-                        final_gain_grad,
-                        final_bias_grad,
-                        dtaps,
-                    ],
-                    0,
-                ).T,
-                columns_of(drouter_first),
-                columns_of(drouter_second),
-            ],
-            1,
-        )
-    )
+    small_grad = jnp.concatenate(
+        [
+            jnp.concatenate(
+                [
+                    dgain_first,
+                    dbias_first,
+                    dgain_second,
+                    dbias_second,
+                    attend_vec[2:4],
+                    attend_vec[0:2],
+                    dgain_depth,
+                    dbias_depth,
+                    final_gain_grad,
+                    final_bias_grad,
+                    dtaps,
+                ],
+                0,
+            ).T,
+            columns_of(drouter_first),
+            columns_of(drouter_second),
+        ],
+        1,
+    )
+    n_small = small_grad.shape[1]
+    small_grad = jnp.pad(small_grad, ((0, 0), (0, -n_small % 128))).astype(jnp.bfloat16)
+    matrices = jnp.concatenate([dpq, dpk, dpv, drel, dao, dgated, dpoint, small_grad], 1)
+    matrices = matrices.reshape((devices, -1) + matrices.shape[1:])
+    matrices = scatter_parts(halves(matrices), False)
+    (slope,) = advance([first_ddown], slope)
+    (slope,) = advance([first_dup, matrices], slope)
+    (slope,) = advance([first_ddown, matrices], slope)
+    first_up_grad = first_dup.finish()
+    first_down_grad = first_ddown.finish()
+    matrices = matrices.finish()
+    small_grad = matrices[:, 8 * width : 8 * width + n_small]
     own = small_grad.shape[0]
     start = own * lax.axis_index(AXES)
     own_sums = lax.dynamic_slice_in_dim(sums, start, own, 1)
@@ -1661,7 +1781,7 @@
         small_grad[:, 12 : 12 + KERNEL].T,
         own_sums[0],
         own_sums[1],
-        matrices[:, 7 * width :],
+        matrices[:, 7 * width : 8 * width],
         vector(2),
         vector(3),
         router_of(12 + KERNEL + 2 * EXPERTS),

time: 727 us -> 696 us (0.957)
  waiting for transfers between devices: 213 us -> 193 us
  local copies, waits for them, and re-layouts: 67.8 us -> 53.7 us
  Pallas kernels: 306 us -> 315 us
    ppermute x15 -> x0, waiting for transfers between devices: 48.9 us -> none  [the longest x5 30.6 us: gather_small(): other = lax.ppermute(value, AXES, [(d, d ^ bit) for d in range(count)])]
    ppermute x15 -> x0, starting transfers between devices: 29 us -> none  [the longest x5 16.9 us: gather_small(): other = lax.ppermute(value, AXES, [(d, d ^ bit) for d in range(count)])]
    ppermute x48 -> x55, starting transfers between devices: 46.4 us -> 69.4 us  [move(): return lax.ppermute(value, AXES, pairs)]
    ppermute x48 -> x55, waiting for transfers between devices: 159 us -> 179 us  [move(): return lax.ppermute(value, AXES, pairs)]
    another operation x16 -> x2, local copies, waits for them, and re-layouts: 11.7 us -> 1.37 us  [gathered_from(): return jnp.stack(found)]
    convert_element_type x15 -> x12, other arithmetic: 14.4 us -> 24.4 us  [the longest x3 8.87 us: scatter_steps(): part = (wide(part) + below(keep, step) + below(other, step)).astype(low)]
    another operation x9 -> x12, other arithmetic: 11.1 us -> 1.51 us
    all_gather x2, waiting for transfers between devices: 3.51 us -> 12.9 us  [gather_whole(): blocks = lax.all_gather(value, AXES, axis=0, tiled=False)]
  transfers between devices with their start and end apart: 67 -> 59, of which waited for: 31 -> 22; matrix products, arithmetic and copies ran while one was open for 14% -> 10% of each run, Pallas kernels for 32% -> 38%
where the time goes in v3:
time: 696 us; the launch traced here: 688 us
  Pallas kernels  315 us (45%)
  waiting for transfers between devices  193 us (28%)
  starting transfers between devices  69.6 us (10%)
  local copies, waits for them, and re-layouts  53.7 us (8%)
  other arithmetic  40.2 us (6%)
  between operations  15.2 us (2%)
    ppermute x55, waiting for transfers between devices, move(): return lax.ppermute(value, AXES, pairs)  179 us
    pallas_call x8, Pallas kernels, expert_call(): pl.pallas_call(body, grid_spec=pltpu.PrefetchScalarGridSpec(num_scalar_pr...  149 us
    ppermute x55, starting transfers between devices, move(): return lax.ppermute(value, AXES, pairs)  69.4 us
    pallas_call x1, Pallas kernels, attention_backward(): pl.pallas_call(functools.partial(attend_backward_kernel, bool(begin), las...  60.2 us
    pallas_call x5, Pallas kernels, single(): pl.pallas_call(kernel, grid=(1,), in_specs=specs, out_specs=[pl.BlockSpec...  58.5 us
    pallas_call x1, Pallas kernels, attention_forward(): pl.pallas_call(attend_forward_kernel, grid=(count,), in_specs=[whole((len...  47.7 us
    unnamed x80, local copies, waits for them, and re-layouts  16.9 us
  transfers between devices with their start and end apart: 59, of which 22 were waited for; matrix products, arithmetic and copies ran while one was open for 10% of the time, Pallas kernels for 38%

profile of v3, /device:TPU:0, one launch (start us, length us, event | category | flops | bytes accessed | tf_op | source)
XLA Modules:
  0.0 687.9 jit_solution(8522756280852018471)
XLA Ops:
  13.5 9.4 %concatenate.38 = bf16[720]{0:T(1024)(128)(2,1)S(1)} concatenate(bf16[16]{0:T(256)(128)(2,1)} %param.38, bf16[16]{0:T(256)(128)(2,1)} %param.39, bf16[16]{0:T(256)(128)(2,1)} %param.57, bf16[16]{0:T(256)(128)(2,1)} %param.58, bf16[16]{0:T(256)(128)(2,1)} %param.43, bf16[16]{0:T(256)(128)(2,1)} %param.44, bf16[16]{0:T(256)(128)(2,1)} %param.47, bf16[16]{0:T(256)(128)(2,1)} %param.48, ...), dimensions={0} | concatenate | bytes 2880 | tf_op jit(solution)/shard_map/concatenate | solution.py:1574
  25.2 3.1 collective-permute-start
  28.3 2.6 collective-permute-start.1
  42.4 7.5 %collective-permute-done.1 = bf16[1,4,16,2048]{3,2,1,0:T(8,128)(2,1)S(1)} collective-permute-done((bf16[1,4,16,2048]{3,2,1,0:T(8,128)(2,1)}, bf16[1,4,16,2048]{3,2,1,0:T(8,128)(2,1)S(1)}, u32[]{:S(2)}, u32[]{:S(2)}) %collective-permute-start.1) | collective-permute-done | bytes 262176 | tf_op jit(solution)/shard_map/ppermute | solution.py:460
  50.6 7.1 %collective-permute-start.6 = (bf16[4,4,64,512]{3,2,1,0:T(8,128)(2,1)S(1)}, bf16[4,4,64,512]{3,2,1,0:T(8,128)(2,1)}, u32[]{:S(2)}, u32[]{:S(2)}) collective-permute-start(bf16[4,4,64,512]{3,2,1,0:T(8,128)(2,1)S(1)} %pad_maximum_fusion.1.refs_2_), channel_id=1, source_target_pairs={{0,8},{1,9},{2,10},{3,11},{4,12},{5,13},{6,14},{7,15},{8,16},{9,17... | collective-permute-start | bytes 3145736 | tf_op jit(solution)/shard_map/ppermute | solution.py:460
  60.2 26.6 %collective-permute-done.6.refs_3_ = bf16[4,4,64,512]{3,2,1,0:T(8,128)(2,1)} collective-permute-done((bf16[4,4,64,512]{3,2,1,0:T(8,128)(2,1)S(1)}, bf16[4,4,64,512]{3,2,1,0:T(8,128)(2,1)}, u32[]{:S(2)}, u32[]{:S(2)}) %collective-permute-start.6) | collective-permute-done | bytes 1048608 | tf_op jit(solution)/shard_map/ppermute | solution.py:460
  92.0 31.9 %collective-permute-done.7.refs_4_ = bf16[4,4,64,512]{3,2,1,0:T(8,128)(2,1)} collective-permute-done((bf16[4,4,64,512]{3,2,1,0:T(8,128)(2,1)}, bf16[4,4,64,512]{3,2,1,0:T(8,128)(2,1)}, u32[]{:S(2)}, u32[]{:S(2)}) %collective-permute-start.7) | collective-permute-done | bytes 1048608 | tf_op jit(solution)/shard_map/ppermute | solution.py:460
  130.4 3.8 expert_enter.1
  134.2 10.4 %collective-permute-done.14.refs_4_ = bf16[4,4,16,2048]{3,2,1,0:T(8,128)(2,1)} collective-permute-done((bf16[4,4,16,2048]{3,2,1,0:T(8,128)(2,1)S(1)}, bf16[4,4,16,2048]{3,2,1,0:T(8,128)(2,1)}, u32[]{:S(2)}, u32[]{:S(2)}) %collective-permute-start.14) | collective-permute-done | bytes 1048608 | tf_op jit(solution)/shard_map/ppermute | solution.py:460
  146.6 7.3 %collective-permute-done.8.refs_5_ = bf16[4,4,64,512]{3,2,1,0:T(8,128)(2,1)} collective-permute-done((bf16[4,4,64,512]{3,2,1,0:T(8,128)(2,1)}, bf16[4,4,64,512]{3,2,1,0:T(8,128)(2,1)}, u32[]{:S(2)}, u32[]{:S(2)}) %collective-permute-start.8) | collective-permute-done | bytes 1048608 | tf_op jit(solution)/shard_map/ppermute | solution.py:460
  160.7 11.8 %first_up.1 = (bf16[4,512,512]{2,1,0:T(8,128)(2,1)}, bf16[4,512,2048]{2,1,0:T(8,128)(2,1)}) custom-call(s32[5]{0:T(128)} %pad_add_fusion.1.refs_0_, s32[32]{0:T(128)} %stack.231.refs_1_, bf16[4,4,16,2048]{3,2,1,0:T(8,128)(2,1)} %copy-done.5, bf16[4,4,16,2048]{3,2,1,0:T(8,128)(2,1)} %collective-permute-done.13.refs_3_, ...), custom_call_target="tpu_custom_call" | custom-call | flops 5000000000 | bytes 20000000 | tf_op jit(solution)/shard_map/first_up/pallas_call | solution.py:1028
  173.4 14.2 %first_down.1 = (f32[1024,512]{1,0:T(8,128)}, f32[1024,512]{1,0:T(8,128)}) custom-call(s32[5]{0:T(128)} %pad_add_fusion.1.refs_0_, s32[32]{0:T(128)} %stack.214.refs_1_, bf16[4,4,64,512]{3,2,1,0:T(8,128)(2,1)} %copy-done.2, bf16[4,4,64,512]{3,2,1,0:T(8,128)(2,1)} %collective-permute-done.6.refs_3_, bf16[4,4,64,512]{3,2,1,0:T(8,128)(2,1)} %collective-permute-done.7.refs_4_, ...), custom_call_target="tpu_custom_call" | custom-call | flops 5000000000 | bytes 20000000 | tf_op jit(solution)/shard_map/first_down/pallas_call | solution.py:1028
  187.6 47.7 %attend_forward.1 = (bf16[1024,512]{1,0:T(8,128)(2,1)}, bf16[1024,512]{1,0:T(8,128)(2,1)}, bf16[1024,512]{1,0:T(8,128)(2,1)}, bf16[1024,512]{1,0:T(8,128)(2,1)},...) custom-call(f32[1024,512]{1,0:T(8,128)} %get-tuple-element.209.resid_ref.refs_4_, ...), custom_call_target="tpu_custom_call" | custom-call | flops 24000000000 | bytes 32000000 | tf_op jit(solution)/shard_map/attend_forward/pallas_call | solution.py:296
  235.3 16.8 %conv_front.1 = (f32[1024,512]{1,0:T(8,128)}, bf16[1024,512]{1,0:T(8,128)(2,1)}, f32[1024,1024]{1,0:T(8,128)}, f32[1024,512]{1,0:T(8,128)}, f32[2,512]{1,0:T(2,128)}) custom-call(f32[1024,512]{1,0:T(8,128)} %get-tuple-element.209.resid_ref.refs_4_, bf16[1024,512]{1,0:T(8,128)(2,1)} %get-tuple-element.214.ctx_ref.refs_11_, ...), custom_call_target="tpu_custom_call" | custom-call | flops 4000000000 | bytes 16000000 | tf_op jit(solution)/shard_map/conv_front/pallas_call | solution.py:679
  259.4 2.9 collective-permute-done.23
  262.3 3.7 collective-permute-start.26
  268.9 6.1 conv_tail.1
  275.1 12.9 %all-gather.10.cloned.1.call-done = bf16[128,64,512]{2,1,0:T(8,128)(2,1)} async-done(((bf16[4,64,512]{2,1,0:T(8,128)(2,1)}), bf16[128,64,512]{2,1,0:T(8,128)(2,1)}) %all-gather.10.cloned.1.call-update) | async-done | bytes 8388624 | tf_op jit(solution)/shard_map/all_gather | solution.py:596
  288.5 23.6 %second_forward.1 = (bf16[4,512,512]{2,1,0:T(8,128)(2,1)}, bf16[4,512,2048]{2,1,0:T(8,128)(2,1)}, f32[1024,512]{1,0:T(8,128)}, bf16[1024,512]{1,0:T(8,128)(2,1)}...) custom-call(s32[5]{0:T(128)} %pad_add_fusion.refs_0_, s32[32]{0:T(128)} %iota.66.refs_1_.refs_2_, ...), custom_call_target="tpu_custom_call" | custom-call | flops 10000000000 | bytes 20000000 | tf_op jit(solution)/shard_map/second_forward/pallas_call | solution.py:1028
  312.6 27.1 %second_back.1 = (f32[1024,512]{1,0:T(8,128)}, f32[1,512]{1,0:T(1,128)}, f32[1,512]{1,0:T(1,128)}, f32[128,1024]{1,0:T(8,128)}, bf16[4,512,512]{2,1,0:T(8,128)(2,1)}, /*index=5*/bf16[4,512,2048]{2,1,0:T(8,128)(2,1)}) custom-call(s32[5]{0:T(128)} %pad_add_fusion.refs_0_, s32[32]{0:T(128)} %iota.72.refs_1_.refs_2_, s32[32]{0:T(128)} %iota.72.refs_1_.refs_2_, ...), custom_call_target="tpu_custom_call" | custom-call | flops 10000000000 | bytes 20000000 | tf_op jit(solution)/shard_map/second_back/pallas_call | solution.py:1028
  339.8 5.7 conv_turn.1
  347.5 2.6 collective-permute-start.28
  351.6 16.2 %second_grads.1 = bf16[32,4,32,2048]{3,2,1,0:T(8,128)(2,1)} custom-call(s32[5]{0:T(128)} %pad_add_fusion.refs_0_, bf16[4,512,512]{2,1,0:T(8,128)(2,1)} %get-tuple-element.232.refs_1_, bf16[4,512,2048]{2,1,0:T(8,128)(2,1)} %get-tuple-element.228.refs_11_.refs_2_, bf16[4,512,512]{2,1,0:T(8,128)(2,1)} %get-tuple-element.234.refs_3_, ...), custom_call_target="tpu_custom_call" | custom-call | flops 10000000000 | bytes 20000000 | tf_op jit(solution)/shard_map/second_grads/pallas_call | solution.py:1028
  367.8 2.7 collective-permute-start.31
  371.5 2.1 collective-permute-start.33
  375.7 26.1 %conv_back.1 = (f32[1024,512]{1,0:T(8,128)}, bf16[512,1024]{1,0:T(8,128)(2,1)}, f32[15,512]{1,0:T(8,128)}, f32[1,512]{1,0:T(1,128)}, f32[1,512]{1,0:T(1,128)}) custom-call(f32[1024,512]{1,0:T(8,128)} %get-tuple-element.229.slope_ref, f32[1024,512]{1,0:T(8,128)} %get-tuple-element.230.dshift_ref, f32[1024,512]{1,0:T(8,128)} %get-tuple-element.217.depth_ref, ...), custom_call_target="tpu_custom_call" | custom-call | flops 6000000000 | bytes 20000000 | tf_op jit(solution)/shard_map/conv_back/pallas_call | solution.py:679
  401.8 60.2 %attend_backward.1 = (f32[1024,512]{1,0:T(8,128)}, bf16[512,512]{1,0:T(8,128)(2,1)}, bf16[512,512]{1,0:T(8,128)(2,1)}, bf16[512,512]{1,0:T(8,128)(2,1)}, bf16[51...) custom-call(bf16[8,1024,1024]{2,1,0:T(8,128)(2,1)} %get-tuple-element.225.refs_0_, ...), custom_call_target="tpu_custom_call" | custom-call | flops 40000000000 | bytes 20000000 | tf_op jit(solution)/shard_map/attend_backward/pallas_call | solution.py:353
  461.9 17.4 %first_down_grads.1 = (bf16[16,4,64,512]{3,2,1,0:T(8,128)(2,1)}, bf16[16,4,64,512]{3,2,1,0:T(8,128)(2,1)}, bf16[4,512,512]{2,1,0:T(8,128)(2,1)}, f32[1024,128]{1,0:T(8,128)}) custom-call(s32[5]{0:T(128)} %pad_add_fusion.1.refs_0_, f32[1024,512]{1,0:T(8,128)} %get-tuple-element.247.refs_1_.refs_14_, f32[1024,128]{1,0:T(8,128)} %get-tuple-element.208.refs_13_.refs_2_, ...), custom_call_target="tpu_custom_call" | custom-call | flops 5000000000 | bytes 20000000 | tf_op jit(solution)/shard_map/first_down_grads/pallas_call | solution.py:1028
  479.5 21.4 %first_up_grads.1 = (bf16[16,4,16,2048]{3,2,1,0:T(8,128)(2,1)}, bf16[16,4,16,2048]{3,2,1,0:T(8,128)(2,1)}, bf16[4,512,2048]{2,1,0:T(8,128)(2,1)}) custom-call(s32[5]{0:T(128)} %pad_add_fusion.1.refs_0_, s32[32]{0:T(128)} %stack.214.refs_1_, bf16[4,4,64,512]{3,2,1,0:T(8,128)(2,1)} %copy-done.2, bf16[4,4,64,512]{3,2,1,0:T(8,128)(2,1)} %collective-permute-done.6.refs_3_, ...), custom_call_target="tpu_custom_call" | custom-call | flops 8999999488 | bytes 20000000 | tf_op jit(solution)/shard_map/first_up_grads/pallas_call | solution.py:1028
  509.1 2.9 fusion.11
  512.0 17.2 %first_leave.1 = (f32[1024,512]{1,0:T(8,128)}, f32[1,512]{1,0:T(1,128)}, f32[1,512]{1,0:T(1,128)}, f32[128,1024]{1,0:T(8,128)}) custom-call(s32[5]{0:T(128)} %pad_add_fusion.1.refs_0_, s32[32]{0:T(128)} %stack.231.refs_1_, bf16[4,4,16,2048]{3,2,1,0:T(8,128)(2,1)} %copy-done.5, bf16[4,4,16,2048]{3,2,1,0:T(8,128)(2,1)} %collective-permute-done.13.refs_3_, ...), custom_call_target="tpu_custom_call" | custom-call | flops 5000000000 | bytes 20000000 | tf_op jit(solution)/shard_map/first_leave/pallas_call | solution.py:1028
  533.4 4.0 constant_dynamic-slice_fusion
  537.3 28.7 %collective-permute-done.35 = bf16[2,2,4,64,512]{4,3,2,1,0:T(8,128)(2,1)S(1)} collective-permute-done((bf16[2,2,4,64,512]{4,3,2,1,0:T(8,128)(2,1)}, bf16[2,2,4,64,512]{4,3,2,1,0:T(8,128)(2,1)S(1)}, u32[]{:S(2)}, u32[]{:S(2)}) %collective-permute-start.35) | collective-permute-done | bytes 1048608 | tf_op jit(solution)/shard_map/ppermute | solution.py:460
  566.0 3.1 fusion.4
  569.2 4.6 fusion.14
  574.9 2.3 collective-permute-start.41
  577.2 18.8 %collective-permute-done.36 = bf16[2,2,4,64,512]{4,3,2,1,0:T(8,128)(2,1)} collective-permute-done((bf16[2,2,4,64,512]{4,3,2,1,0:T(8,128)(2,1)}, bf16[2,2,4,64,512]{4,3,2,1,0:T(8,128)(2,1)}, u32[]{:S(2)}, u32[]{:S(2)}) %collective-permute-start.36) | collective-permute-done | bytes 1048608 | tf_op jit(solution)/shard_map/ppermute | solution.py:460
  596.0 3.3 fusion.3
  600.1 21.1 %collective-permute-done.40 = bf16[4,4,16,2048]{3,2,1,0:T(8,128)(2,1)} collective-permute-done((bf16[4,4,16,2048]{3,2,1,0:T(8,128)(2,1)}, bf16[4,4,16,2048]{3,2,1,0:T(8,128)(2,1)}, u32[]{:S(2)}, u32[]{:S(2)}) %collective-permute-start.40) | collective-permute-done | bytes 1048608 | tf_op jit(solution)/shard_map/ppermute | solution.py:460
  621.3 3.4 fusion.5
  625.5 2.8 fusion.17
  634.6 9.2 %collective-permute-done.43 = bf16[4,16,4224]{2,1,0:T(8,128)(2,1)} collective-permute-done((bf16[4,16,4224]{2,1,0:T(8,128)(2,1)}, bf16[4,16,4224]{2,1,0:T(8,128)(2,1)}, u32[]{:S(2)}, u32[]{:S(2)}) %collective-permute-start.43) | collective-permute-done | bytes 540704 | tf_op jit(solution)/shard_map/ppermute | solution.py:460
  643.8 3.0 collective-permute-start.50
  646.8 5.7 collective-permute-done.44
  652.5 3.2 collective-permute-start.51
  657.7 2.4 fusion.2
  660.2 3.2 collective-permute-start.47
  666.4 2.4 collective-permute-start.53
  (301 shorter events, 100.4 us)
Async XLA Ops:
  7.2 117.3 %all-gather.6.cloned.1.call-start = ((), (), s32[]{:S(2)}) async-start(), calls=%async_computation.1 | async-start | bytes 4460544 | tf_op jit(solution)/shard_map/all_gather | solution.py:1510
  23.7 251.4 %all-gather.8.cloned.1.call-start = ((), (), s32[]{:S(2)}) async-start(), calls=%async_computation.3 | async-start | bytes 8650752 | tf_op jit(solution)/shard_map/all_gather | solution.py:596
  24.4 263.6 %all-gather.10.cloned.1.call-start = ((), (), s32[]{:S(2)}) async-start(), calls=%async_computation.4 | async-start | bytes 8650752 | tf_op jit(solution)/shard_map/all_gather | solution.py:596
  25.1 652.4 %reduce-scatter.2.cloned.1.call-start = ((), (), s32[]{:S(2)}) async-start(), calls=%async_computation.2 | async-start | bytes 17301504 | tf_op jit(solution)/shard_map/reduce_scatter | solution.py:649
  25.2 12.8 %collective-permute-start = (bf16[1,4,16,2048]{3,2,1,0:T(8,128)(2,1)}, bf16[1,4,16,2048]{3,2,1,0:T(8,128)(2,1)S(1)}, u32[]{:S(2)}, u32[]{:S(2)}) collective-permute-start(bf16[1,4,16,2048]{3,2,1,0:T(8,128)(2,1)} %bitcast.219), channel_id=1, source_target_pairs={{0,8},{1,9},{2,10},{3,11},{4,12},{5,13},{6,14},{7,15},{8,16},{9,17... | collective-permute-start | bytes 786440 | tf_op jit(solution)/shard_map/ppermute | solution.py:460
  28.3 21.7 %collective-permute-start.1 = (bf16[1,4,16,2048]{3,2,1,0:T(8,128)(2,1)}, bf16[1,4,16,2048]{3,2,1,0:T(8,128)(2,1)S(1)}, u32[]{:S(2)}, u32[]{:S(2)}) collective-permute-start(bf16[1,4,16,2048]{3,2,1,0:T(8,128)(2,1)} %bitcast.220), channel_id=1, source_target_pairs={{0,16},{1,17},{2,18},{3,19},{4,20},{5,21},{6,22},{7,23},{8,24},{9,... | collective-permute-start | bytes 786440 | tf_op jit(solution)/shard_map/ppermute | solution.py:460
  30.9 19.4 %collective-permute-start.2 = (bf16[1,4,16,2048]{3,2,1,0:T(8,128)(2,1)}, bf16[1,4,16,2048]{3,2,1,0:T(8,128)(2,1)S(1)}, u32[]{:S(2)}, u32[]{:S(2)}) collective-permute-start(bf16[1,4,16,2048]{3,2,1,0:T(8,128)(2,1)} %bitcast.221), channel_id=1, source_target_pairs={{0,24},{1,25},{2,26},{3,27},{4,28},{5,29},{6,30},{7,31},{8,0},{9,1... | collective-permute-start | bytes 786440 | tf_op jit(solution)/shard_map/ppermute | solution.py:460
  32.2 18.1 %collective-permute-start.3 = (bf16[1,4,64,512]{3,2,1,0:T(8,128)(2,1)}, bf16[1,4,64,512]{3,2,1,0:T(8,128)(2,1)S(1)}, u32[]{:S(2)}, u32[]{:S(2)}) collective-permute-start(bf16[1,4,64,512]{3,2,1,0:T(8,128)(2,1)} %bitcast.215), channel_id=1, source_target_pairs={{0,2},{1,3},{2,0},{3,1},{4,6},{5,7},{6,4},{7,5},{8,10},{9,11},{10,... | collective-permute-start | bytes 786440 | tf_op jit(solution)/shard_map/ppermute | solution.py:460
  33.7 16.6 %collective-permute-start.4 = (bf16[1,4,64,512]{3,2,1,0:T(8,128)(2,1)}, bf16[1,4,64,512]{3,2,1,0:T(8,128)(2,1)S(1)}, u32[]{:S(2)}, u32[]{:S(2)}) collective-permute-start(bf16[1,4,64,512]{3,2,1,0:T(8,128)(2,1)} %bitcast.216), channel_id=1, source_target_pairs={{0,4},{1,5},{2,6},{3,7},{4,0},{5,1},{6,2},{7,3},{8,12},{9,13},{10,... | collective-permute-start | bytes 786440 | tf_op jit(solution)/shard_map/ppermute | solution.py:460
  39.0 11.3 %collective-permute-start.5 = (bf16[1,4,64,512]{3,2,1,0:T(8,128)(2,1)S(1)}, bf16[1,4,64,512]{3,2,1,0:T(8,128)(2,1)S(1)}, u32[]{:S(2)}, u32[]{:S(2)}) collective-permute-start(bf16[1,4,64,512]{3,2,1,0:T(8,128)(2,1)S(1)} %bitcast.217), channel_id=1, source_target_pairs={{0,6},{1,7},{2,4},{3,5},{4,2},{5,3},{6,0},{7,1},{8,14},{9,15},{10,... | collective-permute-start | bytes 786440 | tf_op jit(solution)/shard_map/ppermute | solution.py:460
  50.6 36.1 %collective-permute-start.6 = (bf16[4,4,64,512]{3,2,1,0:T(8,128)(2,1)S(1)}, bf16[4,4,64,512]{3,2,1,0:T(8,128)(2,1)}, u32[]{:S(2)}, u32[]{:S(2)}) collective-permute-start(bf16[4,4,64,512]{3,2,1,0:T(8,128)(2,1)S(1)} %pad_maximum_fusion.1.refs_2_), channel_id=1, source_target_pairs={{0,8},{1,9},{2,10},{3,11},{4,12},{5,13},{6,14},{7,15},{8,16},{9,17... | collective-permute-start | bytes 3145736 | tf_op jit(solution)/shard_map/ppermute | solution.py:460
  86.8 37.1 %collective-permute-start.7 = (bf16[4,4,64,512]{3,2,1,0:T(8,128)(2,1)}, bf16[4,4,64,512]{3,2,1,0:T(8,128)(2,1)}, u32[]{:S(2)}, u32[]{:S(2)}) collective-permute-start(bf16[4,4,64,512]{3,2,1,0:T(8,128)(2,1)} %collective-permute-done.6.refs_3_), channel_id=1, source_target_pairs={{0,8},{1,9},{2,10},{3,11},{4,12},{5,13},{6,14},{7,15},{8,16},{9,17... | collective-permute-start | bytes 3145736 | tf_op jit(solution)/shard_map/ppermute | solution.py:460
  88.5 45.7 %collective-permute-start.13 = (bf16[4,4,16,2048]{3,2,1,0:T(8,128)(2,1)S(1)}, bf16[4,4,16,2048]{3,2,1,0:T(8,128)(2,1)}, u32[]{:S(2)}, u32[]{:S(2)}) collective-permute-start(bf16[4,4,16,2048]{3,2,1,0:T(8,128)(2,1)S(1)} %pad_maximum_fusion.2.refs_2_), channel_id=1, source_target_pairs={{0,2},{1,3},{2,0},{3,1},{4,6},{5,7},{6,4},{7,5},{8,10},{9,11},{10,... | collective-permute-start | bytes 3145736 | tf_op jit(solution)/shard_map/ppermute | solution.py:460
  90.0 54.6 %collective-permute-start.14 = (bf16[4,4,16,2048]{3,2,1,0:T(8,128)(2,1)S(1)}, bf16[4,4,16,2048]{3,2,1,0:T(8,128)(2,1)}, u32[]{:S(2)}, u32[]{:S(2)}) collective-permute-start(bf16[4,4,16,2048]{3,2,1,0:T(8,128)(2,1)S(1)} %pad_maximum_fusion.2.refs_2_), channel_id=1, source_target_pairs={{0,4},{1,5},{2,6},{3,7},{4,0},{5,1},{6,2},{7,3},{8,12},{9,13},{10,... | collective-permute-start | bytes 3145736 | tf_op jit(solution)/shard_map/ppermute | solution.py:460
  91.5 54.0 %collective-permute-start.15 = (bf16[4,4,16,2048]{3,2,1,0:T(8,128)(2,1)S(1)}, bf16[4,4,16,2048]{3,2,1,0:T(8,128)(2,1)}, u32[]{:S(2)}, u32[]{:S(2)}) collective-permute-start(bf16[4,4,16,2048]{3,2,1,0:T(8,128)(2,1)S(1)} %pad_maximum_fusion.2.refs_2_), channel_id=1, source_target_pairs={{0,6},{1,7},{2,4},{3,5},{4,2},{5,3},{6,0},{7,1},{8,14},{9,15},{10,... | collective-permute-start | bytes 3145736 | tf_op jit(solution)/shard_map/ppermute | solution.py:460
  123.9 30.0 %collective-permute-start.8 = (bf16[4,4,64,512]{3,2,1,0:T(8,128)(2,1)}, bf16[4,4,64,512]{3,2,1,0:T(8,128)(2,1)}, u32[]{:S(2)}, u32[]{:S(2)}) collective-permute-start(bf16[4,4,64,512]{3,2,1,0:T(8,128)(2,1)} %collective-permute-done.7.refs_4_), channel_id=1, source_target_pairs={{0,8},{1,9},{2,10},{3,11},{4,12},{5,13},{6,14},{7,15},{8,16},{9,17... | collective-permute-start | bytes 3145736 | tf_op jit(solution)/shard_map/ppermute | solution.py:460
  145.5 8.4 %collective-permute-start.16 = (bf16[4,4,16,2048]{3,2,1,0:T(8,128)(2,1)S(1)}, bf16[4,4,16,2048]{3,2,1,0:T(8,128)(2,1)S(1)}, u32[]{:S(2)}, u32[]{:S(2)}) collective-permute-start(bf16[4,4,16,2048]{3,2,1,0:T(8,128)(2,1)S(1)} %pad_maximum_fusion.2.refs_2_), channel_id=1, source_target_pairs={{0,1},{1,0},{2,3},{3,2},{4,5},{5,4},{6,7},{7,6},{8,9},{9,8},{10,11... | collective-permute-start | bytes 3145736 | tf_op jit(solution)/shard_map/ppermute | solution.py:460
  145.5 9.9 %collective-permute-start.17 = (bf16[4,4,16,2048]{3,2,1,0:T(8,128)(2,1)}, bf16[4,4,16,2048]{3,2,1,0:T(8,128)(2,1)}, u32[]{:S(2)}, u32[]{:S(2)}) collective-permute-start(bf16[4,4,16,2048]{3,2,1,0:T(8,128)(2,1)} %collective-permute-done.13.refs_3_), channel_id=1, source_target_pairs={{0,1},{1,0},{2,3},{3,2},{4,5},{5,4},{6,7},{7,6},{8,9},{9,8},{10,11... | collective-permute-start | bytes 3145736 | tf_op jit(solution)/shard_map/ppermute | solution.py:460
  146.1 9.4 %collective-permute-start.18 = (bf16[4,4,16,2048]{3,2,1,0:T(8,128)(2,1)}, bf16[4,4,16,2048]{3,2,1,0:T(8,128)(2,1)}, u32[]{:S(2)}, u32[]{:S(2)}) collective-permute-start(bf16[4,4,16,2048]{3,2,1,0:T(8,128)(2,1)} %collective-permute-done.14.refs_4_), channel_id=1, source_target_pairs={{0,1},{1,0},{2,3},{3,2},{4,5},{5,4},{6,7},{7,6},{8,9},{9,8},{10,11... | collective-permute-start | bytes 3145736 | tf_op jit(solution)/shard_map/ppermute | solution.py:460
  146.1 14.6 %collective-permute-start.19 = (bf16[4,4,16,2048]{3,2,1,0:T(8,128)(2,1)}, bf16[4,4,16,2048]{3,2,1,0:T(8,128)(2,1)}, u32[]{:S(2)}, u32[]{:S(2)}) collective-permute-start(bf16[4,4,16,2048]{3,2,1,0:T(8,128)(2,1)} %collective-permute-done.15.refs_5_), channel_id=1, source_target_pairs={{0,1},{1,0},{2,3},{3,2},{4,5},{5,4},{6,7},{7,6},{8,9},{9,8},{10,11... | collective-permute-start | bytes 3145736 | tf_op jit(solution)/shard_map/ppermute | solution.py:460
  153.9 18.5 %collective-permute-start.9 = (bf16[4,4,64,512]{3,2,1,0:T(8,128)(2,1)S(1)}, bf16[4,4,64,512]{3,2,1,0:T(8,128)(2,1)}, u32[]{:S(2)}, u32[]{:S(2)}) collective-permute-start(bf16[4,4,64,512]{3,2,1,0:T(8,128)(2,1)S(1)} %pad_maximum_fusion.1.refs_2_), channel_id=1, source_target_pairs={{0,1},{1,0},{2,3},{3,2},{4,5},{5,4},{6,7},{7,6},{8,9},{9,8},{10,11... | collective-permute-start | bytes 3145736 | tf_op jit(solution)/shard_map/ppermute | solution.py:460
  154.9 17.5 %collective-permute-start.10 = (bf16[4,4,64,512]{3,2,1,0:T(8,128)(2,1)}, bf16[4,4,64,512]{3,2,1,0:T(8,128)(2,1)S(1)}, u32[]{:S(2)}, u32[]{:S(2)}) collective-permute-start(bf16[4,4,64,512]{3,2,1,0:T(8,128)(2,1)} %collective-permute-done.6.refs_3_), channel_id=1, source_target_pairs={{0,1},{1,0},{2,3},{3,2},{4,5},{5,4},{6,7},{7,6},{8,9},{9,8},{10,11... | collective-permute-start | bytes 3145736 | tf_op jit(solution)/shard_map/ppermute | solution.py:460
  155.4 17.0 %collective-permute-start.11 = (bf16[4,4,64,512]{3,2,1,0:T(8,128)(2,1)}, bf16[4,4,64,512]{3,2,1,0:T(8,128)(2,1)}, u32[]{:S(2)}, u32[]{:S(2)}) collective-permute-start(bf16[4,4,64,512]{3,2,1,0:T(8,128)(2,1)} %collective-permute-done.7.refs_4_), channel_id=1, source_target_pairs={{0,1},{1,0},{2,3},{3,2},{4,5},{5,4},{6,7},{7,6},{8,9},{9,8},{10,11... | collective-permute-start | bytes 3145736 | tf_op jit(solution)/shard_map/ppermute | solution.py:460
  155.4 17.0 %collective-permute-start.12 = (bf16[4,4,64,512]{3,2,1,0:T(8,128)(2,1)}, bf16[4,4,64,512]{3,2,1,0:T(8,128)(2,1)}, u32[]{:S(2)}, u32[]{:S(2)}) collective-permute-start(bf16[4,4,64,512]{3,2,1,0:T(8,128)(2,1)} %collective-permute-done.8.refs_5_), channel_id=1, source_target_pairs={{0,1},{1,0},{2,3},{3,2},{4,5},{5,4},{6,7},{7,6},{8,9},{9,8},{10,11... | collective-permute-start | bytes 3145736 | tf_op jit(solution)/shard_map/ppermute | solution.py:460
  347.5 20.2 %collective-permute-start.28 = (f32[2,512]{1,0:T(2,128)S(1)}, f32[2,512]{1,0:T(2,128)S(1)}, u32[]{:S(2)}, u32[]{:S(2)}) collective-permute-start(f32[2,512]{1,0:T(2,128)S(1)} %add.1386), channel_id=1, source_target_pairs={{0,2},{1,3},{2,0},{3,1},{4,6},{5,7},{6,4},{7,5},{8,10},{9,11},{10,... | collective-permute-start | bytes 12296 | tf_op jit(solution)/shard_map/ppermute | solution.py:460
  350.1 17.7 %collective-permute-start.29 = (f32[2,512]{1,0:T(2,128)S(1)}, f32[2,512]{1,0:T(2,128)S(1)}, u32[]{:S(2)}, u32[]{:S(2)}) collective-permute-start(f32[2,512]{1,0:T(2,128)S(1)} %add.1386), channel_id=1, source_target_pairs={{0,4},{1,5},{2,6},{3,7},{4,0},{5,1},{6,2},{7,3},{8,12},{9,13},{10,... | collective-permute-start | bytes 12296 | tf_op jit(solution)/shard_map/ppermute | solution.py:460
  350.1 17.7 %collective-permute-start.30 = (f32[2,512]{1,0:T(2,128)S(1)}, f32[2,512]{1,0:T(2,128)S(1)}, u32[]{:S(2)}, u32[]{:S(2)}) collective-permute-start(f32[2,512]{1,0:T(2,128)S(1)} %add.1386), channel_id=1, source_target_pairs={{0,6},{1,7},{2,4},{3,5},{4,2},{5,3},{6,0},{7,1},{8,14},{9,15},{10,... | collective-permute-start | bytes 12296 | tf_op jit(solution)/shard_map/ppermute | solution.py:460
  479.3 29.7 %collective-permute-start.34 = (bf16[16,4,64,512]{3,2,1,0:T(8,128)(2,1)}, bf16[16,4,64,512]{3,2,1,0:T(8,128)(2,1)}, u32[]{:S(2)}, u32[]{:S(2)}) collective-permute-start(bf16[16,4,64,512]{3,2,1,0:T(8,128)(2,1)} %get-tuple-element.250), channel_id=1, source_target_pairs={{0,1},{1,0},{2,3},{3,2},{4,5},{5,4},{6,7},{7,6},{8,9},{9,8},{10,11... | collective-permute-start | bytes 12582920 | tf_op jit(solution)/shard_map/ppermute | solution.py:460
  501.0 68.2 %collective-permute-start.37 = (bf16[16,4,16,2048]{3,2,1,0:T(8,128)(2,1)}, bf16[16,4,16,2048]{3,2,1,0:T(8,128)(2,1)}, u32[]{:S(2)}, u32[]{:S(2)}) collective-permute-start(bf16[16,4,16,2048]{3,2,1,0:T(8,128)(2,1)} %get-tuple-element.264), channel_id=1, source_target_pairs={{0,1},{1,0},{2,3},{3,2},{4,5},{5,4},{6,7},{7,6},{8,9},{9,8},{10,11... | collective-permute-start | bytes 12582920 | tf_op jit(solution)/shard_map/ppermute | solution.py:460
  532.0 34.0 %collective-permute-start.35 = (bf16[2,2,4,64,512]{4,3,2,1,0:T(8,128)(2,1)}, bf16[2,2,4,64,512]{4,3,2,1,0:T(8,128)(2,1)S(1)}, u32[]{:S(2)}, u32[]{:S(2)}) collective-permute-start(bf16[2,2,4,64,512]{4,3,2,1,0:T(8,128)(2,1)} %fusion.11), channel_id=1, source_target_pairs={{0,8},{1,9},{2,10},{3,11},{4,12},{5,13},{6,14},{7,15},{8,16},{9,17... | collective-permute-start | bytes 3145736 | tf_op jit(solution)/shard_map/ppermute | solution.py:460
  537.3 83.9 %collective-permute-start.42 = (bf16[16,16,4224]{2,1,0:T(8,128)(2,1)}, bf16[16,16,4224]{2,1,0:T(8,128)(2,1)}, u32[]{:S(2)}, u32[]{:S(2)}) collective-permute-start(bf16[16,16,4224]{2,1,0:T(8,128)(2,1)} %get-tuple-element.451), channel_id=1, source_target_pairs={{0,1},{1,0},{2,3},{3,2},{4,5},{5,4},{6,7},{7,6},{8,9},{9,8},{10,11... | collective-permute-start | bytes 6488072 | tf_op jit(solution)/shard_map/ppermute | solution.py:460
  569.1 26.9 %collective-permute-start.36 = (bf16[2,2,4,64,512]{4,3,2,1,0:T(8,128)(2,1)}, bf16[2,2,4,64,512]{4,3,2,1,0:T(8,128)(2,1)}, u32[]{:S(2)}, u32[]{:S(2)}) collective-permute-start(bf16[2,2,4,64,512]{4,3,2,1,0:T(8,128)(2,1)} %fusion.4), channel_id=1, source_target_pairs={{0,8},{1,9},{2,10},{3,11},{4,12},{5,13},{6,14},{7,15},{8,16},{9,17... | collective-permute-start | bytes 3145736 | tf_op jit(solution)/shard_map/ppermute | solution.py:460
  573.7 26.4 %collective-permute-start.39 = (bf16[4,4,16,2048]{3,2,1,0:T(8,128)(2,1)}, bf16[4,4,16,2048]{3,2,1,0:T(8,128)(2,1)}, u32[]{:S(2)}, u32[]{:S(2)}) collective-permute-start(bf16[4,4,16,2048]{3,2,1,0:T(8,128)(2,1)} %get-tuple-element.272), channel_id=1, source_target_pairs={{0,2},{1,3},{2,0},{3,1},{4,6},{5,7},{6,4},{7,5},{8,10},{9,11},{10,... | collective-permute-start | bytes 3145736 | tf_op jit(solution)/shard_map/ppermute | solution.py:460
  573.7 47.5 %collective-permute-start.40 = (bf16[4,4,16,2048]{3,2,1,0:T(8,128)(2,1)}, bf16[4,4,16,2048]{3,2,1,0:T(8,128)(2,1)}, u32[]{:S(2)}, u32[]{:S(2)}) collective-permute-start(bf16[4,4,16,2048]{3,2,1,0:T(8,128)(2,1)} %get-tuple-element.273), channel_id=1, source_target_pairs={{0,4},{1,5},{2,6},{3,7},{4,0},{5,1},{6,2},{7,3},{8,12},{9,13},{10,... | collective-permute-start | bytes 3145736 | tf_op jit(solution)/shard_map/ppermute | solution.py:460
  574.9 46.3 %collective-permute-start.41 = (bf16[4,4,16,2048]{3,2,1,0:T(8,128)(2,1)S(1)}, bf16[4,4,16,2048]{3,2,1,0:T(8,128)(2,1)}, u32[]{:S(2)}, u32[]{:S(2)}) collective-permute-start(bf16[4,4,16,2048]{3,2,1,0:T(8,128)(2,1)S(1)} %get-tuple-element.274), channel_id=1, source_target_pairs={{0,6},{1,7},{2,4},{3,5},{4,2},{5,3},{6,0},{7,1},{8,14},{9,15},{10,... | collective-permute-start | bytes 3145736 | tf_op jit(solution)/shard_map/ppermute | solution.py:460
  599.4 56.4 %collective-permute-start.38 = (bf16[2,2,4,64,512]{4,3,2,1,0:T(8,128)(2,1)}, bf16[2,2,4,64,512]{4,3,2,1,0:T(8,128)(2,1)}, u32[]{:S(2)}, u32[]{:S(2)}) collective-permute-start(bf16[2,2,4,64,512]{4,3,2,1,0:T(8,128)(2,1)} %fusion.3), channel_id=1, source_target_pairs={{0,8},{1,9},{2,10},{3,11},{4,12},{5,13},{6,14},{7,15},{8,16},{9,17... | collective-permute-start | bytes 3145736 | tf_op jit(solution)/shard_map/ppermute | solution.py:460
  628.3 15.5 %collective-permute-start.43 = (bf16[4,16,4224]{2,1,0:T(8,128)(2,1)}, bf16[4,16,4224]{2,1,0:T(8,128)(2,1)}, u32[]{:S(2)}, u32[]{:S(2)}) collective-permute-start(bf16[4,16,4224]{2,1,0:T(8,128)(2,1)} %get-tuple-element.300), channel_id=1, source_target_pairs={{0,2},{1,3},{2,0},{3,1},{4,6},{5,7},{6,4},{7,5},{8,10},{9,11},{10,... | collective-permute-start | bytes 1622024 | tf_op jit(solution)/shard_map/ppermute | solution.py:460
  630.0 22.5 %collective-permute-start.44 = (bf16[4,16,4224]{2,1,0:T(8,128)(2,1)}, bf16[4,16,4224]{2,1,0:T(8,128)(2,1)}, u32[]{:S(2)}, u32[]{:S(2)}) collective-permute-start(bf16[4,16,4224]{2,1,0:T(8,128)(2,1)} %get-tuple-element.301), channel_id=1, source_target_pairs={{0,4},{1,5},{2,6},{3,7},{4,0},{5,1},{6,2},{7,3},{8,12},{9,13},{10,... | collective-permute-start | bytes 1622024 | tf_op jit(solution)/shard_map/ppermute | solution.py:460
  630.3 25.4 %collective-permute-start.45 = (bf16[4,16,4224]{2,1,0:T(8,128)(2,1)}, bf16[4,16,4224]{2,1,0:T(8,128)(2,1)}, u32[]{:S(2)}, u32[]{:S(2)}) collective-permute-start(bf16[4,16,4224]{2,1,0:T(8,128)(2,1)} %get-tuple-element.302), channel_id=1, source_target_pairs={{0,6},{1,7},{2,4},{3,5},{4,2},{5,3},{6,0},{7,1},{8,14},{9,15},{10,... | collective-permute-start | bytes 1622024 | tf_op jit(solution)/shard_map/ppermute | solution.py:460
  633.1 30.4 %collective-permute-start.49 = (bf16[4,16,2048]{2,1,0:T(8,128)(2,1)}, bf16[4,16,2048]{2,1,0:T(8,128)(2,1)S(1)}, u32[]{:S(2)}, u32[]{:S(2)}) collective-permute-start(bf16[4,16,2048]{2,1,0:T(8,128)(2,1)} %get-tuple-element.313), channel_id=1, source_target_pairs={{0,8},{1,9},{2,10},{3,11},{4,12},{5,13},{6,14},{7,15},{8,16},{9,17... | collective-permute-start | bytes 786440 | tf_op jit(solution)/shard_map/ppermute | solution.py:460
  643.8 20.5 %collective-permute-start.50 = (bf16[4,16,2048]{2,1,0:T(8,128)(2,1)}, bf16[4,16,2048]{2,1,0:T(8,128)(2,1)S(1)}, u32[]{:S(2)}, u32[]{:S(2)}) collective-permute-start(bf16[4,16,2048]{2,1,0:T(8,128)(2,1)} %get-tuple-element.314), channel_id=1, source_target_pairs={{0,16},{1,17},{2,18},{3,19},{4,20},{5,21},{6,22},{7,23},{8,24},{9,... | collective-permute-start | bytes 786440 | tf_op jit(solution)/shard_map/ppermute | solution.py:460
  652.5 11.8 %collective-permute-start.51 = (bf16[4,16,2048]{2,1,0:T(8,128)(2,1)S(1)}, bf16[4,16,2048]{2,1,0:T(8,128)(2,1)S(1)}, u32[]{:S(2)}, u32[]{:S(2)}) collective-permute-start(bf16[4,16,2048]{2,1,0:T(8,128)(2,1)S(1)} %get-tuple-element.315), channel_id=1, source_target_pairs={{0,24},{1,25},{2,26},{3,27},{4,28},{5,29},{6,30},{7,31},{8,0},{9,1... | collective-permute-start | bytes 786440 | tf_op jit(solution)/shard_map/ppermute | solution.py:460
  660.1 8.7 %collective-permute-start.46 = (bf16[16,4224]{1,0:T(8,128)(2,1)S(1)}, bf16[16,4224]{1,0:T(8,128)(2,1)S(1)}, u32[]{:S(2)}, u32[]{:S(2)}) collective-permute-start(bf16[16,4224]{1,0:T(8,128)(2,1)S(1)} %get-tuple-element.310), channel_id=1, source_target_pairs={{0,8},{1,9},{2,10},{3,11},{4,12},{5,13},{6,14},{7,15},{8,16},{9,17... | collective-permute-start | bytes 405512 | tf_op jit(solution)/shard_map/ppermute | solution.py:460
  660.2 11.2 %collective-permute-start.47 = (bf16[16,4224]{1,0:T(8,128)(2,1)S(1)}, bf16[16,4224]{1,0:T(8,128)(2,1)S(1)}, u32[]{:S(2)}, u32[]{:S(2)}) collective-permute-start(bf16[16,4224]{1,0:T(8,128)(2,1)S(1)} %get-tuple-element.311), channel_id=1, source_target_pairs={{0,16},{1,17},{2,18},{3,19},{4,20},{5,21},{6,22},{7,23},{8,24},{9,... | collective-permute-start | bytes 405512 | tf_op jit(solution)/shard_map/ppermute | solution.py:460
  663.4 8.0 %collective-permute-start.48 = (bf16[16,4224]{1,0:T(8,128)(2,1)S(1)}, bf16[16,4224]{1,0:T(8,128)(2,1)S(1)}, u32[]{:S(2)}, u32[]{:S(2)}) collective-permute-start(bf16[16,4224]{1,0:T(8,128)(2,1)S(1)} %get-tuple-element.312), channel_id=1, source_target_pairs={{0,24},{1,25},{2,26},{3,27},{4,28},{5,29},{6,30},{7,31},{8,0},{9,1... | collective-permute-start | bytes 405512 | tf_op jit(solution)/shard_map/ppermute | solution.py:460
  665.3 11.3 %collective-permute-start.52 = (bf16[4,64,512]{2,1,0:T(8,128)(2,1)S(1)}, bf16[4,64,512]{2,1,0:T(8,128)(2,1)S(1)}, u32[]{:S(2)}, u32[]{:S(2)}) collective-permute-start(bf16[4,64,512]{2,1,0:T(8,128)(2,1)S(1)} %get-tuple-element.316), channel_id=1, source_target_pairs={{0,2},{1,3},{2,0},{3,1},{4,6},{5,7},{6,4},{7,5},{8,10},{9,11},{10,... | collective-permute-start | bytes 786440 | tf_op jit(solution)/shard_map/ppermute | solution.py:460
  666.4 10.3 %collective-permute-start.53 = (bf16[4,64,512]{2,1,0:T(8,128)(2,1)S(1)}, bf16[4,64,512]{2,1,0:T(8,128)(2,1)S(1)}, u32[]{:S(2)}, u32[]{:S(2)}) collective-permute-start(bf16[4,64,512]{2,1,0:T(8,128)(2,1)S(1)} %get-tuple-element.317), channel_id=1, source_target_pairs={{0,4},{1,5},{2,6},{3,7},{4,0},{5,1},{6,2},{7,3},{8,12},{9,13},{10,... | collective-permute-start | bytes 786440 | tf_op jit(solution)/shard_map/ppermute | solution.py:460
  668.8 7.8 %collective-permute-start.54 = (bf16[4,64,512]{2,1,0:T(8,128)(2,1)S(1)}, bf16[4,64,512]{2,1,0:T(8,128)(2,1)S(1)}, u32[]{:S(2)}, u32[]{:S(2)}) collective-permute-start(bf16[4,64,512]{2,1,0:T(8,128)(2,1)S(1)} %get-tuple-element.318), channel_id=1, source_target_pairs={{0,6},{1,7},{2,4},{3,5},{4,2},{5,3},{6,0},{7,1},{8,14},{9,15},{10,... | collective-permute-start | bytes 786440 | tf_op jit(solution)/shard_map/ppermute | solution.py:460
  (41 other events, 739.5 us)
Sparse Core Ops, SparseCore 0:
  23.8 99.0 all-gather.5
  125.8 83.5 all-gather.7
  212.2 75.7 all-gather.9
  367.9 192.8 reduce-scatter.1

commit v4 on v3

--- a/solution.py
+++ b/solution.py
@@ -71,6 +71,7 @@
 
 
 def attend_forward_kernel(
+    windows_ref,
     resid_ref,
     gain_ref,
     bias_ref,
@@ -117,9 +118,10 @@
     qu_ref[...] = (query + cb_ref[...]).astype(jnp.bfloat16)
     qv_ref[...] = (query + pb_ref[...]).astype(jnp.bfloat16)
 
-    def block(index, carry):
+    def windowed(index, size):
+        keys = pl.ds(pl.multiple_of(windows_ref[index], 128), size)
         at = pl.ds(pl.multiple_of(index * rows, rows), rows)
-        same = segc_ref[at, :] == segr_ref[...]
+        same = segc_ref[at, :] == segr_ref[:, keys]
         cosine, sine = cos_ref[at, :], sin_ref[at, :]
         contexts = []
         for head in range(2):
@@ -131,30 +133,36 @@
             turned_a = (left * sine + right * cosine).astype(jnp.bfloat16)
             turned_b = (right * sine - left * cosine).astype(jnp.bfloat16)
             scores = mul(
-                jnp.concatenate([part_u.astype(jnp.bfloat16), turned_a, turned_b], 1), kt_ref[...], NT
+                jnp.concatenate([part_u.astype(jnp.bfloat16), turned_a, turned_b], 1), kt_ref[keys, :], NT
             )
             scores = jnp.where(same, scores, blocked)
             peak = jnp.max(scores, -1, keepdims=True)
             raised = jnp.exp(scores - peak)
             summed = jnp.sum(raised, -1, keepdims=True)
             chances = (raised * (1.0 / summed)).astype(jnp.bfloat16)
-            p_ref[head, at, :] = chances
-            contexts.append(mul(chances, v_ref[...]))
+            p_ref[head, at, keys] = chances
+            contexts.append(mul(chances, v_ref[keys, :]))
         ctx_ref[at, :] = jnp.where(head_mask(rows, 0), contexts[0], contexts[1]).astype(jnp.bfloat16)
+
+    def block(index, carry):
+        count = windows_ref[length // rows + index]
+        for size in WINDOWS:
+            pl.when(count == size)(functools.partial(windowed, index, size))
         return carry
 
     lax.fori_loop(0, length // rows, block, 0)
 
 
-def attend_backward_kernel(resumed, ends, *refs):
+def attend_backward_kernel(resumed, ends, windows_ref, *refs):
     operands = 18
     if not resumed:
         refs = refs[:operands] + (None,) + refs[operands:]
-    attend_backward_body(ends, *refs)
+    attend_backward_body(ends, windows_ref, *refs)
 
 
 def attend_backward_body(
     ends,
+    windows_ref,
     p_ref,
     tab_ref,
     cos_ref,
@@ -214,7 +222,8 @@
     dvt_ref[...] = jnp.zeros_like(dvt_ref)
     drt_ref[...] = jnp.zeros_like(drt_ref)
 
-    def block(index, carry):
+    def windowed(index, size):
+        keys = pl.ds(pl.multiple_of(windows_ref[index], 128), size)
         at = pl.ds(pl.multiple_of(index * rows, rows), rows)
         cosine, sine = cos_ref[at, :], sin_ref[at, :]
         total = jnp.zeros((rows, pair), jnp.float32)
@@ -223,15 +232,15 @@
         for head in range(2):
             own = head_mask(rows, head)
             part = jnp.where(own, dctx_ref[at, :], 0)
-            low = p_ref[head, at, :]
+            low = p_ref[head, at, keys]
             chances = low.astype(jnp.float32)
-            raw = mul(part, v_ref[...], NT)
+            raw = mul(part, v_ref[keys, :], NT)
             weighted = chances * raw
             delta = jnp.sum(weighted, -1, keepdims=True)
             slope = ((weighted - chances * delta) * 0.125).astype(jnp.bfloat16)
-            dvt_ref[...] += mul(part, low, TN)
-            dkt_ref[...] += mul(jnp.where(own, qu_ref[at, :], 0), slope, TN)
-            wide = mul(slope, kt_ref[...])
+            dvt_ref[:, keys] += mul(part, low, TN)
+            dkt_ref[:, keys] += mul(jnp.where(own, qu_ref[at, :], 0), slope, TN)
+            wide = mul(slope, kt_ref[keys, :])
             slope_u = jnp.where(own, wide[:, :pair], 0.0)
             first, second = wide[:, pair : pair + half], wide[:, pair + half :]
             coef = jnp.concatenate(
@@ -249,6 +258,11 @@
         dq_ref[at, :] = total
         vec_ref[0:1, lanes] += sum_u
         vec_ref[1:2, lanes] += sum_v
+
+    def block(index, carry):
+        count = windows_ref[length // rows + index]
+        for size in WINDOWS:
+            pl.when(count == size)(functools.partial(windowed, index, size))
         return carry
 
     lax.fori_loop(0, length // rows, block, 0)
@@ -278,14 +292,30 @@
 
 
 def whole(shape):
-    return pl.BlockSpec(shape, lambda p: (0,) * len(shape))
+    return pl.BlockSpec(shape, lambda p, *_: (0,) * len(shape))
 
 
 def columns(rows, width, shift=0):
-    return pl.BlockSpec((rows, width), lambda p: (0, p + shift))
-
-
-def attention_forward(first, count, resid, segments, segment_column, weights, tables):
+    return pl.BlockSpec((rows, width), lambda p, *_: (0, p + shift))
+
+
+ROW_BLOCK = 256
+WINDOWS = (512, 640, 768, 1024)
+
+
+def key_windows(segment):
+    length = segment.shape[0]
+    firsts = segment[::ROW_BLOCK]
+    lasts = segment[ROW_BLOCK - 1 :: ROW_BLOCK]
+    start = jnp.sum(segment[None, :] < firsts[:, None], 1).astype(jnp.int32) // 128 * 128
+    need = jnp.sum(segment[None, :] <= lasts[:, None], 1).astype(jnp.int32) - start
+    count = jnp.full_like(need, length)
+    for size in WINDOWS[::-1]:
+        count = jnp.where(need <= size, size, count)
+    return jnp.concatenate([jnp.minimum(start, length - count), count])
+
+
+def attention_forward(first, count, resid, segments, segment_column, weights, tables, windows):
     gain, bias, packed, content_bias, position_bias = weights
     table, cosine, sine = tables
     length, width = resid.shape
@@ -295,17 +325,19 @@
     shape = jax.ShapeDtypeStruct
     return pl.pallas_call(
         attend_forward_kernel,
-        grid=(count,),
-        in_specs=[
+        grid_spec=pltpu.PrefetchScalarGridSpec(
+            num_scalar_prefetch=1,
+            grid=(count,),
+            in_specs=[
             whole((length, width)),
-            pl.BlockSpec((None, 1, width), lambda p: (gain[1], 0, 0)),
-            pl.BlockSpec((None, 1, width), lambda p: (bias[1], 0, 0)),
+            pl.BlockSpec((None, 1, width), lambda p, *_: (gain[1], 0, 0)),
+            pl.BlockSpec((None, 1, width), lambda p, *_: (bias[1], 0, 0)),
             columns(width, pair, first),
             columns(width, pair, first + pairs),
             columns(width, pair, first + 2 * pairs),
             columns(width, pair, first + 3 * pairs),
-            pl.BlockSpec((None, 1, pair), lambda p: (content_bias[1], 0, p + first)),
-            pl.BlockSpec((None, 1, pair), lambda p: (position_bias[1], 0, p + first)),
+            pl.BlockSpec((None, 1, pair), lambda p, *_: (content_bias[1], 0, p + first)),
+            pl.BlockSpec((None, 1, pair), lambda p, *_: (position_bias[1], 0, p + first)),
             whole((1, length)),
             whole((length, 1)),
             whole((length, width)),
@@ -314,15 +346,17 @@
         ],
         out_specs=[whole((length, width))]
         + [columns(length, pair)] * 4
-        + [pl.BlockSpec((2, length, length), lambda p: (p, 0, 0)), columns(length, pair)],
+        + [pl.BlockSpec((2, length, length), lambda p, *_: (p, 0, 0)), columns(length, pair)],
+        scratch_shapes=[pltpu.VMEM((length, pair + width), low), pltpu.VMEM((width, width), low)],
+        ),
         out_shape=[shape((length, width), low)]
         + [shape((length, count * pair), low)] * 4
         + [shape((2 * count, length, length), low), shape((length, count * pair), low)],
-        scratch_shapes=[pltpu.VMEM((length, pair + width), low), pltpu.VMEM((width, width), low)],
         compiler_params=pltpu.CompilerParams(vmem_limit_bytes=56 * 1024 * 1024),
         cost_estimate=pl.CostEstimate(flops=count * 6 * 10**9, bytes_accessed=count * 8 * 10**6, transcendentals=count * 2 * 10**6),
         name="attend_forward",
     )(
+        windows,
         resid,
         gain[0],
         bias[0],
@@ -340,7 +374,7 @@
     )
 
 
-def attention_backward(first, count, last, resid, slope, weights, tables, kept, partial):
+def attention_backward(first, count, last, resid, slope, weights, tables, kept, partial, windows):
     gain, bias, packed, content_bias, position_bias = weights
     table, cosine, sine = tables
     normed, query_u, query_v, keys, values, chances, context = kept
@@ -352,9 +386,11 @@
     begin = [] if partial is None else [partial]
     return pl.pallas_call(
         functools.partial(attend_backward_kernel, bool(begin), last),
-        grid=(count,),
-        in_specs=[
-            pl.BlockSpec((2, length, length), lambda p: (p + first, 0, 0)),
+        grid_spec=pltpu.PrefetchScalarGridSpec(
+            num_scalar_prefetch=1,
+            grid=(count,),
+            in_specs=[
+            pl.BlockSpec((2, length, length), lambda p, *_: (p + first, 0, 0)),
             whole((length, width)),
             whole((length, width // 2)),
             whole((length, width // 2)),
@@ -364,26 +400,23 @@
         ]
         + [columns(length, pair, first)] * 5
         + [
-            pl.BlockSpec((pair, width), lambda p: (p + first, pairs)),
+            pl.BlockSpec((pair, width), lambda p, *_: (p + first, pairs)),
             columns(width, pair, first),
             columns(width, pair, first + pairs),
             columns(width, pair, first + 2 * pairs),
             columns(width, pair, first + 3 * pairs),
-            pl.BlockSpec((None, 1, width), lambda p: (gain[1], 0, 0)),
+            pl.BlockSpec((None, 1, width), lambda p, *_: (gain[1], 0, 0)),
         ]
         + [whole((length, width))] * len(begin),
         out_specs=[
             whole((length, width)),
-            pl.BlockSpec((pair, width), lambda p: (p, 0)),
+            pl.BlockSpec((pair, width), lambda p, *_: (p, 0)),
             columns(width, pair),
             columns(width, pair),
             columns(width, pair),
             columns(width, pair),
             whole((8, width)),
         ],
-        out_shape=[shape((length, width), full), shape((count * pair, width), low)]
-        + [shape((width, count * pair), low)] * 4
-        + [shape((8, width), full)],
         scratch_shapes=[
             pltpu.VMEM((length, pair + width), low),
             pltpu.VMEM((length, width), low),
@@ -395,12 +428,17 @@
             pltpu.VMEM((pair, width), full),
             pltpu.VMEM((width, width), low),
         ],
+        ),
+        out_shape=[shape((length, width), full), shape((count * pair, width), low)]
+        + [shape((width, count * pair), low)] * 4
+        + [shape((8, width), full)],
         compiler_params=pltpu.CompilerParams(vmem_limit_bytes=60 * 1024 * 1024),
         cost_estimate=pl.CostEstimate(
             flops=count * 10**10, bytes_accessed=20 * 10**6, transcendentals=0
         ),
         name="attend_backward",
     )(
+        windows,
         chances,
         table,
         cosine,
@@ -597,6 +635,11 @@
         return [blocks], jnp.arange(blocks.shape[0], dtype=jnp.int32)
     blocks = lax.all_gather(value, AXES, axis=1, tiled=True)
     return [blocks[None]], jnp.zeros((1,), jnp.int32)
+
+
+def gather_both(value):
+    (blocks,), ids = gather_whole(value)
+    return blocks, ids
 
 
 def block_at(value, index, at):
@@ -980,8 +1023,42 @@
         self.shape = (rows, self.arrays[0].shape[3])
         self.rows = self.arrays[0].shape[2]
 
+        self.scratch = [pltpu.VMEM(self.shape, jnp.bfloat16)]
+
     def specs(self):
         return [by_owner(piece.shape) for piece in self.arrays]
+
+    def assemble(self, refs, ids_ref, whole_refs):
+        assemble(refs, ids_ref, whole_refs[0])
+
+
+class Both:
+    def __init__(self, array, ids, width):
+        self.arrays, self.ids = [array], ids
+        devices, _, rows, hidden = array.shape
+        self.rows, self.across = rows // 2, hidden // width
+        self.shape = (devices * self.rows, hidden)
+        down = (devices * self.rows * self.across, width)
+        self.scratch = [pltpu.VMEM(self.shape, jnp.bfloat16), pltpu.VMEM(down, jnp.bfloat16)]
+
+    def specs(self):
+        return [by_owner(self.arrays[0].shape)]
+
+    def assemble(self, refs, ids_ref, whole_refs):
+        (ref,), (up_ref, down_ref) = refs, whole_refs
+        rows, width = self.rows, down_ref.shape[1]
+        for block in range(ref.shape[0]):
+            up_ref[block * rows : (block + 1) * rows, :] = ref[block, 0, :rows, :]
+            for at in range(self.across):
+                start = (block * self.across + at) * rows
+                down_ref[start : start + rows, :] = ref[block, 0, rows:, at * width : (at + 1) * width]
+
+
+def side_by_side(up, down):
+    experts, rows, hidden = up.shape
+    width = down.shape[2]
+    down = down.reshape(experts, hidden // width, rows, width).transpose(0, 2, 1, 3)
+    return jnp.concatenate([up, down.reshape(experts, rows, hidden)], 1)
 
 
 def fixed(shape):
@@ -1016,12 +1093,14 @@
         pieces, refs = refs[: len(arrays)], refs[len(arrays) :]
         operands, results, rest = refs[:n_in], refs[n_in : n_in + n_out], refs[n_in + n_out :]
         expert = pl.program_id(0)
+        n_whole = 0
         for at, weight in enumerate(weights):
             own = pieces[: len(weight.arrays)]
             pieces = pieces[len(weight.arrays) :]
-            assemble(own, ids[at], rest[at])
+            weight.assemble(own, ids[at], rest[n_whole : n_whole + len(weight.scratch)])
+            n_whole += len(weight.scratch)
         kernel(
-            expert, count_ref[expert], *rest[: len(weights)], *operands, *results, *rest[len(weights) :],
+            expert, count_ref[expert], *rest[:n_whole], *operands, *results, *rest[n_whole:],
             **({"core": count_ref[EXPERTS]} if with_core else {}),
         )
 
@@ -1033,7 +1112,7 @@
             in_specs=[spec for weight in weights for spec in weight.specs()]
             + [spec for _, spec in inputs],
             out_specs=[spec for _, spec in outputs],
-            scratch_shapes=[pltpu.VMEM(weight.shape, jnp.bfloat16) for weight in weights] + scratch,
+            scratch_shapes=[whole for weight in weights for whole in weight.scratch] + scratch,
         ),
         out_shape=[shape for shape, _ in outputs],
         compiler_params=pltpu.CompilerParams(vmem_limit_bytes=60 * 1024 * 1024),
@@ -1179,17 +1258,17 @@
         g4_ref[...] = norm_slope(unit, inverse, cot, gain)
 
 
-def second_forward_call(counts, pos_row, pos_col, normed, resid, probs, routes, cot, gain, bias, up, down):
+def second_forward_call(counts, pos_row, pos_col, normed, resid, probs, routes, cot, gain, bias, weights):
     length, width = normed.shape
     return expert_call(
         second_forward_kernel,
         "second_forward",
         counts,
-        [up, down],
+        weights,
         [whole_in(v) for v in (normed, pos_row, pos_col, resid, probs, routes, cot, gain, bias)],
         [
             expert_out((CAPACITY, width)),
-            expert_out((CAPACITY, up.shape[1])),
+            expert_out((CAPACITY, weights[0].shape[1])),
             whole_out((length, width)),
             whole_out((length, width), jnp.bfloat16),
             whole_out((length, width)),
@@ -1407,14 +1486,14 @@
 
 
 def second_back_call(
-    counts, pos_row, pos_col, slope, probs, routes, branch, inner, router, resid, normed, embedding, gain, up, down
+    counts, pos_row, pos_col, slope, probs, routes, branch, inner, router, resid, normed, embedding, gain, weights
 ):
     length, width = slope.shape
     return expert_call(
         second_back_kernel,
         "second_back",
         counts,
-        [up, down],
+        weights,
         [whole_in(v) for v in (slope, probs, routes, branch, pos_row, pos_col)]
         + [expert_in(inner)]
         + [whole_in(v) for v in (router, resid, normed, embedding, gain)],
@@ -1508,6 +1587,22 @@
 
 def gather_rows(value):
     return lax.all_gather(value, AXES, axis=0, tiled=True)
+
+
+SMALL = 32
+ROUTERS = 64
+
+
+def small_rows(vectors, taps, first_router, second_router):
+    row = lax.broadcasted_iota(jnp.int32, (SMALL, vectors[0].shape[0]), 0)
+    total = jnp.pad(taps, ((len(vectors), SMALL - len(vectors) - taps.shape[0]), (0, 0)))
+    for at, vector in enumerate(vectors):
+        total = jnp.where(row == at, vector[None, :], total)
+    total = jnp.pad(total, ((0, 0), (0, 128 - total.shape[1])))
+    for at, router in ((ROUTERS, first_router), (ROUTERS + EXPERTS, second_router)):
+        below, behind = SMALL - router.shape[0], 128 - at - EXPERTS
+        total = total + jnp.pad(router, ((0, below), (at, behind)))
+    return total
 
 
 def gathered_count(devices):
@@ -1567,39 +1662,31 @@
 
     first_up_chain, up_ids = gather_experts(first_up, True)
     first_down_chain, down_ids = gather_experts(first_down, False)
-    n_vec = 14
-    taps_at = n_vec * first_gain.shape[0]
-    routers_at = taps_at + depth_kernel.size
-    n_router = first_router.size
-    small = jnp.concatenate(
-        [
-            first_gain,
-            first_bias,
-            second_gain,
-            second_bias,
-            attend_gain,
-            attend_bias,
-            content_bias,
-            position_bias,
-            depth_gain,
-            depth_bias,
-            batch_gain,
-            batch_bias,
-            final_gain,
-            final_bias,
-            depth_kernel.reshape(-1),
-            first_router.reshape(-1),
-            second_router.reshape(-1),
-        ]
-    )
+    vectors = [
+        first_gain,
+        first_bias,
+        second_gain,
+        second_bias,
+        attend_gain,
+        attend_bias,
+        content_bias,
+        position_bias,
+        depth_gain,
+        depth_bias,
+        batch_gain,
+        batch_bias,
+        final_gain,
+        final_bias,
+    ]
     own = project_in.shape[0]
-    small = jnp.pad(small, (0, -small.size % (128 * own))).reshape(own, -1)
+    small = small_rows(vectors, depth_kernel, first_router, second_router)
+    small = jnp.concatenate([small[start : start + own] for start in range(0, SMALL, own)], 1)
     packed = gather_rows(
         jnp.concatenate([project_in, relative_weight, attend_out, point_out, gated_in, small], 1)
     )
-    small = packed[:, 8 * width :].reshape(devices, -1)
-    second_ups = Weights(*gather_whole(second_up))
-    second_downs = Weights(*gather_whole(second_down))
+    second = [second_up, second_down]
+    if sizes() == FAST:
+        second = [side_by_side(second_up, second_down)]
 
     first_places = places(routes_first, core)
     second_places = places(routes_second, core)
@@ -1614,17 +1701,20 @@
     tables = (table, cosine, sine)
     counts = first_places[0]
 
-    floats = small[:, :taps_at].reshape(devices, n_vec, -1).transpose(1, 0, 2)
-    floats = floats.reshape(n_vec, 1, width).astype(jnp.float32)
-    taps = small[:, taps_at:routers_at].reshape(devices, KERNEL, -1).transpose(1, 0, 2)
+    packed, *second = first_down_chain.step(packed, *second)
+    small = packed[:, 8 * width :].reshape(devices, own, SMALL // own, 128)
+    small = small.transpose(0, 2, 1, 3).reshape(devices, SMALL, 128)
+    n_vec = len(vectors)
+    floats = small[:, :n_vec, :own].transpose(1, 0, 2).reshape(n_vec, 1, width).astype(jnp.float32)
+    taps = small[:, n_vec : n_vec + KERNEL, :own].transpose(1, 0, 2)
     taps = taps.reshape(KERNEL, width).astype(jnp.float32)
 
-    def router_wide(start):
-        router = small[:, start : start + n_router].reshape(2 * width, EXPERTS)
+    def router_wide(at):
+        router = small[:, : 2 * own, at : at + EXPERTS].reshape(2 * width, EXPERTS)
         return jnp.pad(router, ((0, 0), (0, 128 - EXPERTS)))
 
-    first_router_full = router_wide(routers_at)
-    second_router_full = router_wide(routers_at + n_router)
+    first_router_full = router_wide(ROUTERS)
+    second_router_full = router_wide(ROUTERS + EXPERTS)
 
     def vec(index):
         return (floats, index)
@@ -1635,11 +1725,17 @@
     )
     first_ups = Weights(first_up_chain.finish(), up_ids)
 
+    windows = key_windows(segments[0])
     attend_full = (vec(4), vec(5), packed, vec(6), vec(7))
     attend_out_full = (packed, (width, width), (0, 4))
     point_full = (packed, (width, width), (0, 5))
     gated_full = (packed, (width, 2 * width), (0, 3))
 
+    first_normed, *second = first_down_chain.step(first_normed, *second)
+    if sizes() == FAST:
+        second_weights = [Both(*gather_both(second[0]), width)]
+    else:
+        second_weights = [Weights(*gather_whole(value)) for value in second]
     first_picked, first_inner = first_up_call(counts, pos_row, first_normed, first_ups)
     first_downs = Weights(first_down_chain.finish(), down_ids)
     first_resid, first_branch = first_down_call(
@@ -1647,7 +1743,7 @@
     )
     pairs = HEADS // 2
     kept = attention_forward(
-        0, pairs, first_resid, segments, segment_column, attend_full, tables
+        0, pairs, first_resid, segments, segment_column, attend_full, tables, windows
     )
     attend_resid, conv_normed, joined, depth, stats = conv_front(
         first_resid, kept[6], attend_out_full, vec(8), vec(9), gated_full, taps, masks
@@ -1667,11 +1763,11 @@
         final_bias_grad,
     ) = second_forward_call(
         *second_places, second_normed, conv_resid, second_probs, routes_second,
-        cotangent, vec(12), vec(13), second_ups, second_downs,
+        cotangent, vec(12), vec(13), second_weights,
     )
     slope, dgain_second, dbias_second, drouter_second, dpicked, dinner = second_back_call(
         *second_places, slope, second_probs, routes_second, second_branch, second_inner,
-        second_router_full, conv_resid, second_normed, embedding, vec(2), second_ups, second_downs,
+        second_router_full, conv_resid, second_normed, embedding, vec(2), second_weights,
     )
     dshift, dpoint, sums = conv_turn(frames, slope, depth, stats, vec(10), vec(11), point_full)
 
@@ -1688,7 +1784,7 @@
         attend_resid, vec(8), gated_full, taps, masks,
     )
     slope, dao, dpq, dpk, dpv, drel, attend_vec = attention_backward(
-        0, pairs, True, first_resid, slope, attend_full, tables, kept, None
+        0, pairs, True, first_resid, slope, attend_full, tables, kept, None, windows
     )
     *first_ddown, first_dpicked, dlogits = first_back_call(
         counts, pos_row, slope, first_probs, routes_first, first_branch, first_inner, first_downs
@@ -1703,8 +1799,10 @@
         counts, pos_col, first_dinner, dlogits, first_router_full, slope, inputs, first_normed, embedding,
         vec(0), first_ups,
     )
-    (slope,) = advance([first_ddown], slope)
-    (slope,) = advance([first_dup], slope)
+    slope, dgain_first, dbias_first, drouter_first, *matrices = advance(
+        [first_ddown, first_dup], slope, dgain_first, dbias_first, drouter_first,
+        dpq, dpk, dpv, drel, dao, dgated, dpoint,
+    )
 
     def columns_of(grad):
         return (
@@ -1739,12 +1837,13 @@
     )
     n_small = small_grad.shape[1]
     small_grad = jnp.pad(small_grad, ((0, 0), (0, -n_small % 128))).astype(jnp.bfloat16)
-    matrices = jnp.concatenate([dpq, dpk, dpv, drel, dao, dgated, dpoint, small_grad], 1)
+    matrices = jnp.concatenate([*matrices, small_grad], 1)
     matrices = matrices.reshape((devices, -1) + matrices.shape[1:])
     matrices = scatter_parts(halves(matrices), False)
     (slope,) = advance([first_ddown], slope)
     (slope,) = advance([first_dup, matrices], slope)
-    (slope,) = advance([first_ddown, matrices], slope)
+    (slope,) = advance([first_ddown], slope)
+    (slope,) = advance([matrices], slope)
     first_up_grad = first_dup.finish()
     first_down_grad = first_ddown.finish()
     matrices = matrices.finish()

time: 696 us -> 658 us (0.945)
  local copies, waits for them, and re-layouts: 53.7 us -> 33.1 us
  Pallas kernels: 315 us -> 305 us
    all_gather x2 -> x1, waiting for transfers between devices: 12.9 us -> 0.01 us  [gather_whole(): blocks = lax.all_gather(value, AXES, axis=0, tiled=False)]
    ppermute x55, waiting for transfers between devices: 179 us -> 191 us  [move(): return lax.ppermute(value, AXES, pairs)]
    concatenate x2 -> x1, local copies, waits for them, and re-layouts: 10.1 us -> 0.05 us  [on_device(): matrices = jnp.concatenate([*matrices, small_grad], 1)]
    unnamed x80 -> x83, local copies, waits for them, and re-layouts: 16.9 us -> 10.9 us
  transfers between devices with their start and end apart: 59 -> 58, of which waited for: 22 -> 23; matrix products, arithmetic and copies ran while one was open for 10% -> 9% of each run, Pallas kernels for 38% -> 38%
where the time goes in v4:
time: 658 us; the launch traced here: 652 us
  Pallas kernels  305 us (46%)
  waiting for transfers between devices  191 us (29%)
  starting transfers between devices  66.7 us (10%)
  other arithmetic  39.8 us (6%)
  local copies, waits for them, and re-layouts  33.1 us (5%)
  between operations  15.3 us (2%)
    ppermute x55, waiting for transfers between devices, move(): return lax.ppermute(value, AXES, pairs)  191 us
    pallas_call x8, Pallas kernels, expert_call(): pl.pallas_call(body, grid_spec=pltpu.PrefetchScalarGridSpec(num_scalar_pr...  146 us
    ppermute x55, starting transfers between devices, move(): return lax.ppermute(value, AXES, pairs)  66.1 us
    pallas_call x5, Pallas kernels, single(): pl.pallas_call(kernel, grid=(1,), in_specs=specs, out_specs=[pl.BlockSpec...  58.1 us
    pallas_call x1, Pallas kernels, attention_backward(): pl.pallas_call(functools.partial(attend_backward_kernel, bool(begin), las...  55.3 us
    pallas_call x1, Pallas kernels, attention_forward(): pl.pallas_call(attend_forward_kernel, grid_spec=pltpu.PrefetchScalarGridS...  45.7 us
  transfers between devices with their start and end apart: 58, of which 23 were waited for; matrix products, arithmetic and copies ran while one was open for 9% of the time, Pallas kernels for 38%

profile of v4, /device:TPU:0, one launch (start us, length us, event | category | flops | bytes accessed | tf_op | source)
XLA Modules:
  0.0 651.7 jit_solution(4949704760542519841)
XLA Ops:
  14.4 3.1 collective-permute-start
  17.5 2.6 collective-permute-start.1
  31.6 7.7 %collective-permute-done.1 = bf16[1,4,16,2048]{3,2,1,0:T(8,128)(2,1)S(1)} collective-permute-done((bf16[1,4,16,2048]{3,2,1,0:T(8,128)(2,1)}, bf16[1,4,16,2048]{3,2,1,0:T(8,128)(2,1)S(1)}, u32[]{:S(2)}, u32[]{:S(2)}) %collective-permute-start.1) | collective-permute-done | bytes 262176 | tf_op jit(solution)/shard_map/ppermute | solution.py:498
  39.7 7.2 %collective-permute-start.6 = (bf16[4,4,64,512]{3,2,1,0:T(8,128)(2,1)S(1)}, bf16[4,4,64,512]{3,2,1,0:T(8,128)(2,1)}, u32[]{:S(2)}, u32[]{:S(2)}) collective-permute-start(bf16[4,4,64,512]{3,2,1,0:T(8,128)(2,1)S(1)} %pad_maximum_fusion.1.refs_2_), channel_id=1, source_target_pairs={{0,8},{1,9},{2,10},{3,11},{4,12},{5,13},{6,14},{7,15},{8,16},{9,17... | collective-permute-start | bytes 3145736 | tf_op jit(solution)/shard_map/ppermute | solution.py:498
  49.3 26.9 %collective-permute-done.6.refs_3_ = bf16[4,4,64,512]{3,2,1,0:T(8,128)(2,1)} collective-permute-done((bf16[4,4,64,512]{3,2,1,0:T(8,128)(2,1)S(1)}, bf16[4,4,64,512]{3,2,1,0:T(8,128)(2,1)}, u32[]{:S(2)}, u32[]{:S(2)}) %collective-permute-start.6) | collective-permute-done | bytes 1048608 | tf_op jit(solution)/shard_map/ppermute | solution.py:498
  76.2 1.7 collective-permute-start.7
  81.9 1.8 pad_maximum_fusion.3
  83.7 30.2 %collective-permute-done.7.refs_4_ = bf16[4,4,64,512]{3,2,1,0:T(8,128)(2,1)} collective-permute-done((bf16[4,4,64,512]{3,2,1,0:T(8,128)(2,1)}, bf16[4,4,64,512]{3,2,1,0:T(8,128)(2,1)}, u32[]{:S(2)}, u32[]{:S(2)}) %collective-permute-start.7) | collective-permute-done | bytes 1048608 | tf_op jit(solution)/shard_map/ppermute | solution.py:498
  119.3 3.7 expert_enter.1
  123.0 11.0 %collective-permute-done.10.refs_4_ = bf16[4,4,16,2048]{3,2,1,0:T(8,128)(2,1)} collective-permute-done((bf16[4,4,16,2048]{3,2,1,0:T(8,128)(2,1)S(1)}, bf16[4,4,16,2048]{3,2,1,0:T(8,128)(2,1)}, u32[]{:S(2)}, u32[]{:S(2)}) %collective-permute-start.10) | collective-permute-done | bytes 1048608 | tf_op jit(solution)/shard_map/ppermute | solution.py:498
  134.1 6.4 collective-permute-done.8.refs_5_
  146.5 3.6 collective-permute-done.18.refs_8_
  155.3 11.1 %first_up.1 = (bf16[4,512,512]{2,1,0:T(8,128)(2,1)}, bf16[4,512,2048]{2,1,0:T(8,128)(2,1)}) custom-call(s32[5]{0:T(128)} %pad_add_fusion.2.refs_0_, s32[32]{0:T(128)} %stack.231.refs_1_, bf16[4,4,16,2048]{3,2,1,0:T(8,128)(2,1)} %copy-done.5, bf16[4,4,16,2048]{3,2,1,0:T(8,128)(2,1)} %collective-permute-done.9.refs_3_, ...), custom_call_target="tpu_custom_call" | custom-call | flops 5000000000 | bytes 20000000 | tf_op jit(solution)/shard_map/first_up/pallas_call | solution.py:1107
  167.4 13.6 %first_down.1 = (f32[1024,512]{1,0:T(8,128)}, f32[1024,512]{1,0:T(8,128)}) custom-call(s32[5]{0:T(128)} %pad_add_fusion.2.refs_0_, s32[32]{0:T(128)} %stack.230.refs_1_, bf16[4,4,64,512]{3,2,1,0:T(8,128)(2,1)} %copy-done.2, bf16[4,4,64,512]{3,2,1,0:T(8,128)(2,1)} %collective-permute-done.6.refs_3_, bf16[4,4,64,512]{3,2,1,0:T(8,128)(2,1)} %collective-permute-done.7.refs_4_, ...), custom_call_target="tpu_custom_call" | custom-call | flops 5000000000 | bytes 20000000 | tf_op jit(solution)/shard_map/first_down/pallas_call | solution.py:1107
  181.0 45.7 %attend_forward.1 = (bf16[1024,512]{1,0:T(8,128)(2,1)}, bf16[1024,512]{1,0:T(8,128)(2,1)}, bf16[1024,512]{1,0:T(8,128)(2,1)}, bf16[1024,512]{1,0:T(8,128)(2,1)},...) custom-call(s32[8]{0:T(128)} %pad_add_fusion.3.windows_ref, ...), custom_call_target="tpu_custom_call" | custom-call | flops 24000000000 | bytes 32000000 | tf_op jit(solution)/shard_map/attend_forward/pallas_call | solution.py:326
  226.7 16.7 %conv_front.1 = (f32[1024,512]{1,0:T(8,128)}, bf16[1024,512]{1,0:T(8,128)(2,1)}, f32[1024,1024]{1,0:T(8,128)}, f32[1024,512]{1,0:T(8,128)}, f32[2,512]{1,0:T(2,128)}) custom-call(f32[1024,512]{1,0:T(8,128)} %get-tuple-element.255.resid_ref.refs_4_, bf16[1024,512]{1,0:T(8,128)(2,1)} %get-tuple-element.260.ctx_ref.refs_11_, ...), custom_call_target="tpu_custom_call" | custom-call | flops 4000000000 | bytes 16000000 | tf_op jit(solution)/shard_map/conv_front/pallas_call | solution.py:722
  247.2 1.8 collective-permute-start.22
  254.6 2.8 collective-permute-done.24
  258.2 6.1 conv_tail.1
  264.8 23.5 %second_forward.1 = (bf16[4,512,512]{2,1,0:T(8,128)(2,1)}, bf16[4,512,2048]{2,1,0:T(8,128)(2,1)}, f32[1024,512]{1,0:T(8,128)}, bf16[1024,512]{1,0:T(8,128)(2,1)}...) custom-call(s32[5]{0:T(128)} %pad_add_fusion.1.refs_0_, s32[32]{0:T(128)} %iota.119.refs_1_, ...), custom_call_target="tpu_custom_call" | custom-call | flops 10000000000 | bytes 20000000 | tf_op jit(solution)/shard_map/second_forward/pallas_call | solution.py:1107
  288.8 27.4 %second_back.1 = (f32[1024,512]{1,0:T(8,128)}, f32[1,512]{1,0:T(1,128)}, f32[1,512]{1,0:T(1,128)}, f32[128,1024]{1,0:T(8,128)}, bf16[4,512,512]{2,1,0:T(8,128)(2,1)}, /*index=5*/bf16[4,512,2048]{2,1,0:T(8,128)(2,1)}) custom-call(s32[5]{0:T(128)} %pad_add_fusion.1.refs_0_, s32[32]{0:T(128)} %iota.153.refs_1_, bf16[32,4,32,2048]{3,2,1,0:T(8,128)(2,1)} %bitcast.253, ...), custom_call_target="tpu_custom_call" | custom-call | flops 10000000000 | bytes 20000000 | tf_op jit(solution)/shard_map/second_back/pallas_call | solution.py:1107
  316.3 5.7 conv_turn.1
  324.0 3.6 collective-permute-start.28
  329.1 16.2 %second_grads.1 = bf16[32,4,32,2048]{3,2,1,0:T(8,128)(2,1)} custom-call(s32[5]{0:T(128)} %pad_add_fusion.1.refs_0_, bf16[4,512,512]{2,1,0:T(8,128)(2,1)} %get-tuple-element.278.refs_1_, bf16[4,512,2048]{2,1,0:T(8,128)(2,1)} %get-tuple-element.274.refs_9_.refs_2_, bf16[4,512,512]{2,1,0:T(8,128)(2,1)} %get-tuple-element.280.refs_3_, ...), custom_call_target="tpu_custom_call" | custom-call | flops 10000000000 | bytes 20000000 | tf_op jit(solution)/shard_map/second_grads/pallas_call | solution.py:1107
  345.3 4.3 collective-permute-start.33
  351.0 4.2 collective-permute-done.31
  355.8 25.9 %conv_back.1 = (f32[1024,512]{1,0:T(8,128)}, bf16[512,1024]{1,0:T(8,128)(2,1)}, f32[15,512]{1,0:T(8,128)}, f32[1,512]{1,0:T(1,128)}, f32[1,512]{1,0:T(1,128)}) custom-call(f32[1024,512]{1,0:T(8,128)} %get-tuple-element.275.slope_ref, f32[1024,512]{1,0:T(8,128)} %get-tuple-element.276.dshift_ref, f32[1024,512]{1,0:T(8,128)} %get-tuple-element.263.depth_ref, ...), custom_call_target="tpu_custom_call" | custom-call | flops 6000000000 | bytes 20000000 | tf_op jit(solution)/shard_map/conv_back/pallas_call | solution.py:722
  381.7 55.3 %attend_backward.1 = (f32[1024,512]{1,0:T(8,128)}, bf16[512,512]{1,0:T(8,128)(2,1)}, bf16[512,512]{1,0:T(8,128)(2,1)}, bf16[512,512]{1,0:T(8,128)(2,1)}, bf16[51...) custom-call(s32[8]{0:T(128)} %pad_add_fusion.3.windows_ref, ...), custom_call_target="tpu_custom_call" | custom-call | flops 40000000000 | bytes 20000000 | tf_op jit(solution)/shard_map/attend_backward/pallas_call | solution.py:387
  436.9 17.2 %first_down_grads.1 = (bf16[16,4,64,512]{3,2,1,0:T(8,128)(2,1)}, bf16[16,4,64,512]{3,2,1,0:T(8,128)(2,1)}, bf16[4,512,512]{2,1,0:T(8,128)(2,1)}, f32[1024,128]{1,0:T(8,128)}) custom-call(s32[5]{0:T(128)} %pad_add_fusion.2.refs_0_, f32[1024,512]{1,0:T(8,128)} %get-tuple-element.293.refs_1_.refs_14_, f32[1024,128]{1,0:T(8,128)} %get-tuple-element.254.refs_13_.refs_2_, ...), custom_call_target="tpu_custom_call" | custom-call | flops 5000000000 | bytes 20000000 | tf_op jit(solution)/shard_map/first_down_grads/pallas_call | solution.py:1107
  454.2 20.6 %first_up_grads.1 = (bf16[16,4,16,2048]{3,2,1,0:T(8,128)(2,1)}, bf16[16,4,16,2048]{3,2,1,0:T(8,128)(2,1)}, bf16[4,512,2048]{2,1,0:T(8,128)(2,1)}) custom-call(s32[5]{0:T(128)} %pad_add_fusion.2.refs_0_, s32[32]{0:T(128)} %stack.230.refs_1_, bf16[4,4,64,512]{3,2,1,0:T(8,128)(2,1)} %copy-done.2, bf16[4,4,64,512]{3,2,1,0:T(8,128)(2,1)} %collective-permute-done.6.refs_3_, ...), custom_call_target="tpu_custom_call" | custom-call | flops 8999999488 | bytes 20000000 | tf_op jit(solution)/shard_map/first_up_grads/pallas_call | solution.py:1107
  475.0 1.9 fusion.11
  478.3 16.5 %first_leave.1 = (f32[1024,512]{1,0:T(8,128)}, f32[1,512]{1,0:T(1,128)}, f32[1,512]{1,0:T(1,128)}, f32[128,1024]{1,0:T(8,128)}) custom-call(s32[5]{0:T(128)} %pad_add_fusion.2.refs_0_, s32[32]{0:T(128)} %stack.231.refs_1_, bf16[4,4,16,2048]{3,2,1,0:T(8,128)(2,1)} %copy-done.5, bf16[4,4,16,2048]{3,2,1,0:T(8,128)(2,1)} %collective-permute-done.9.refs_3_, ...), custom_call_target="tpu_custom_call" | custom-call | flops 5000000000 | bytes 20000000 | tf_op jit(solution)/shard_map/first_leave/pallas_call | solution.py:1107
  494.8 18.8 %collective-permute-done.35 = bf16[2,2,4,64,512]{4,3,2,1,0:T(8,128)(2,1)S(1)} collective-permute-done((bf16[2,2,4,64,512]{4,3,2,1,0:T(8,128)(2,1)S(1)}, bf16[2,2,4,64,512]{4,3,2,1,0:T(8,128)(2,1)S(1)}, u32[]{:S(2)}, u32[]{:S(2)}) %collective-permute-start.35) | collective-permute-done | bytes 1048608 | tf_op jit(solution)/shard_map/ppermute | solution.py:498
  513.6 3.2 fusion.4
  516.8 4.7 fusion.14
  526.4 2.5 collective-permute-start.38
  531.1 23.4 %collective-permute-done.41 = bf16[2,2,4,64,512]{4,3,2,1,0:T(8,128)(2,1)} collective-permute-done((bf16[2,2,4,64,512]{4,3,2,1,0:T(8,128)(2,1)}, bf16[2,2,4,64,512]{4,3,2,1,0:T(8,128)(2,1)}, u32[]{:S(2)}, u32[]{:S(2)}) %collective-permute-start.41) | collective-permute-done | bytes 1048608 | tf_op jit(solution)/shard_map/ppermute | solution.py:498
  554.6 2.3 fusion.3
  556.9 2.8 collective-permute-start.45
  559.7 22.9 %collective-permute-done.39 = bf16[4,4,16,2048]{3,2,1,0:T(8,128)(2,1)} collective-permute-done((bf16[4,4,16,2048]{3,2,1,0:T(8,128)(2,1)S(1)}, bf16[4,4,16,2048]{3,2,1,0:T(8,128)(2,1)}, u32[]{:S(2)}, u32[]{:S(2)}) %collective-permute-start.39) | collective-permute-done | bytes 1048608 | tf_op jit(solution)/shard_map/ppermute | solution.py:498
  582.6 3.5 fusion.5
  588.9 2.1 collective-permute-start.43
  591.0 2.1 collective-permute-start.51
  594.2 2.0 fusion.2
  596.2 3.7 collective-permute-done.51
  600.7 15.6 %collective-permute-done.50 = bf16[4,16,2048]{2,1,0:T(8,128)(2,1)S(1)} collective-permute-done((bf16[4,16,2048]{2,1,0:T(8,128)(2,1)S(1)}, bf16[4,16,2048]{2,1,0:T(8,128)(2,1)S(1)}, u32[]{:S(2)}, u32[]{:S(2)}) %collective-permute-start.50) | collective-permute-done | bytes 262176 | tf_op jit(solution)/shard_map/ppermute | solution.py:498
  624.0 5.1 collective-permute-start.47
  630.9 5.5 collective-permute-done.47
  (312 shorter events, 90.3 us)
Async XLA Ops:
  7.2 106.7 %all-gather.4.cloned.1.call-start = ((), (), s32[]{:S(2)}) async-start(), calls=%async_computation.1 | async-start | bytes 4595712 | tf_op jit(solution)/shard_map/all_gather | solution.py:1589
  14.3 249.9 %all-gather.6.cloned.1.call-start = ((), (), s32[]{:S(2)}) async-start(), calls=%async_computation.3 | async-start | bytes 17301504 | tf_op jit(solution)/shard_map/all_gather | solution.py:634
  14.4 12.8 %collective-permute-start = (bf16[1,4,16,2048]{3,2,1,0:T(8,128)(2,1)}, bf16[1,4,16,2048]{3,2,1,0:T(8,128)(2,1)S(1)}, u32[]{:S(2)}, u32[]{:S(2)}) collective-permute-start(bf16[1,4,16,2048]{3,2,1,0:T(8,128)(2,1)} %bitcast.230), channel_id=1, source_target_pairs={{0,8},{1,9},{2,10},{3,11},{4,12},{5,13},{6,14},{7,15},{8,16},{9,17... | collective-permute-start | bytes 786440 | tf_op jit(solution)/shard_map/ppermute | solution.py:498
  17.5 21.8 %collective-permute-start.1 = (bf16[1,4,16,2048]{3,2,1,0:T(8,128)(2,1)}, bf16[1,4,16,2048]{3,2,1,0:T(8,128)(2,1)S(1)}, u32[]{:S(2)}, u32[]{:S(2)}) collective-permute-start(bf16[1,4,16,2048]{3,2,1,0:T(8,128)(2,1)} %bitcast.231), channel_id=1, source_target_pairs={{0,16},{1,17},{2,18},{3,19},{4,20},{5,21},{6,22},{7,23},{8,24},{9,... | collective-permute-start | bytes 786440 | tf_op jit(solution)/shard_map/ppermute | solution.py:498
  20.1 19.3 %collective-permute-start.2 = (bf16[1,4,16,2048]{3,2,1,0:T(8,128)(2,1)}, bf16[1,4,16,2048]{3,2,1,0:T(8,128)(2,1)S(1)}, u32[]{:S(2)}, u32[]{:S(2)}) collective-permute-start(bf16[1,4,16,2048]{3,2,1,0:T(8,128)(2,1)} %bitcast.232), channel_id=1, source_target_pairs={{0,24},{1,25},{2,26},{3,27},{4,28},{5,29},{6,30},{7,31},{8,0},{9,1... | collective-permute-start | bytes 786440 | tf_op jit(solution)/shard_map/ppermute | solution.py:498
  21.4 17.9 %collective-permute-start.3 = (bf16[1,4,64,512]{3,2,1,0:T(8,128)(2,1)}, bf16[1,4,64,512]{3,2,1,0:T(8,128)(2,1)S(1)}, u32[]{:S(2)}, u32[]{:S(2)}) collective-permute-start(bf16[1,4,64,512]{3,2,1,0:T(8,128)(2,1)} %bitcast.226), channel_id=1, source_target_pairs={{0,2},{1,3},{2,0},{3,1},{4,6},{5,7},{6,4},{7,5},{8,10},{9,11},{10,... | collective-permute-start | bytes 786440 | tf_op jit(solution)/shard_map/ppermute | solution.py:498
  22.9 16.4 %collective-permute-start.4 = (bf16[1,4,64,512]{3,2,1,0:T(8,128)(2,1)}, bf16[1,4,64,512]{3,2,1,0:T(8,128)(2,1)S(1)}, u32[]{:S(2)}, u32[]{:S(2)}) collective-permute-start(bf16[1,4,64,512]{3,2,1,0:T(8,128)(2,1)} %bitcast.227), channel_id=1, source_target_pairs={{0,4},{1,5},{2,6},{3,7},{4,0},{5,1},{6,2},{7,3},{8,12},{9,13},{10,... | collective-permute-start | bytes 786440 | tf_op jit(solution)/shard_map/ppermute | solution.py:498
  28.2 11.1 %collective-permute-start.5 = (bf16[1,4,64,512]{3,2,1,0:T(8,128)(2,1)S(1)}, bf16[1,4,64,512]{3,2,1,0:T(8,128)(2,1)S(1)}, u32[]{:S(2)}, u32[]{:S(2)}) collective-permute-start(bf16[1,4,64,512]{3,2,1,0:T(8,128)(2,1)S(1)} %bitcast.228), channel_id=1, source_target_pairs={{0,6},{1,7},{2,4},{3,5},{4,2},{5,3},{6,0},{7,1},{8,14},{9,15},{10,... | collective-permute-start | bytes 786440 | tf_op jit(solution)/shard_map/ppermute | solution.py:498
  39.7 36.5 %collective-permute-start.6 = (bf16[4,4,64,512]{3,2,1,0:T(8,128)(2,1)S(1)}, bf16[4,4,64,512]{3,2,1,0:T(8,128)(2,1)}, u32[]{:S(2)}, u32[]{:S(2)}) collective-permute-start(bf16[4,4,64,512]{3,2,1,0:T(8,128)(2,1)S(1)} %pad_maximum_fusion.1.refs_2_), channel_id=1, source_target_pairs={{0,8},{1,9},{2,10},{3,11},{4,12},{5,13},{6,14},{7,15},{8,16},{9,17... | collective-permute-start | bytes 3145736 | tf_op jit(solution)/shard_map/ppermute | solution.py:498
  76.2 37.7 %collective-permute-start.7 = (bf16[4,4,64,512]{3,2,1,0:T(8,128)(2,1)}, bf16[4,4,64,512]{3,2,1,0:T(8,128)(2,1)}, u32[]{:S(2)}, u32[]{:S(2)}) collective-permute-start(bf16[4,4,64,512]{3,2,1,0:T(8,128)(2,1)} %collective-permute-done.6.refs_3_), channel_id=1, source_target_pairs={{0,8},{1,9},{2,10},{3,11},{4,12},{5,13},{6,14},{7,15},{8,16},{9,17... | collective-permute-start | bytes 3145736 | tf_op jit(solution)/shard_map/ppermute | solution.py:498
  78.3 44.7 %collective-permute-start.9 = (bf16[4,4,16,2048]{3,2,1,0:T(8,128)(2,1)S(1)}, bf16[4,4,16,2048]{3,2,1,0:T(8,128)(2,1)}, u32[]{:S(2)}, u32[]{:S(2)}) collective-permute-start(bf16[4,4,16,2048]{3,2,1,0:T(8,128)(2,1)S(1)} %pad_maximum_fusion.2.refs_2_), channel_id=1, source_target_pairs={{0,2},{1,3},{2,0},{3,1},{4,6},{5,7},{6,4},{7,5},{8,10},{9,11},{10,... | collective-permute-start | bytes 3145736 | tf_op jit(solution)/shard_map/ppermute | solution.py:498
  79.9 54.2 %collective-permute-start.10 = (bf16[4,4,16,2048]{3,2,1,0:T(8,128)(2,1)S(1)}, bf16[4,4,16,2048]{3,2,1,0:T(8,128)(2,1)}, u32[]{:S(2)}, u32[]{:S(2)}) collective-permute-start(bf16[4,4,16,2048]{3,2,1,0:T(8,128)(2,1)S(1)} %pad_maximum_fusion.2.refs_2_), channel_id=1, source_target_pairs={{0,4},{1,5},{2,6},{3,7},{4,0},{5,1},{6,2},{7,3},{8,12},{9,13},{10,... | collective-permute-start | bytes 3145736 | tf_op jit(solution)/shard_map/ppermute | solution.py:498
  81.4 52.6 %collective-permute-start.11 = (bf16[4,4,16,2048]{3,2,1,0:T(8,128)(2,1)S(1)}, bf16[4,4,16,2048]{3,2,1,0:T(8,128)(2,1)}, u32[]{:S(2)}, u32[]{:S(2)}) collective-permute-start(bf16[4,4,16,2048]{3,2,1,0:T(8,128)(2,1)S(1)} %pad_maximum_fusion.2.refs_2_), channel_id=1, source_target_pairs={{0,6},{1,7},{2,4},{3,5},{4,2},{5,3},{6,0},{7,1},{8,14},{9,15},{10,... | collective-permute-start | bytes 3145736 | tf_op jit(solution)/shard_map/ppermute | solution.py:498
  113.9 26.5 %collective-permute-start.8 = (bf16[4,4,64,512]{3,2,1,0:T(8,128)(2,1)}, bf16[4,4,64,512]{3,2,1,0:T(8,128)(2,1)}, u32[]{:S(2)}, u32[]{:S(2)}) collective-permute-start(bf16[4,4,64,512]{3,2,1,0:T(8,128)(2,1)} %collective-permute-done.7.refs_4_), channel_id=1, source_target_pairs={{0,8},{1,9},{2,10},{3,11},{4,12},{5,13},{6,14},{7,15},{8,16},{9,17... | collective-permute-start | bytes 3145736 | tf_op jit(solution)/shard_map/ppermute | solution.py:498
  140.5 501.1 %reduce-scatter.2.cloned.1.call-start = ((), (), s32[]{:S(2)}) async-start(), calls=%async_computation.2 | async-start | bytes 17301504 | tf_op jit(solution)/shard_map/reduce_scatter | solution.py:692
  141.6 8.5 %collective-permute-start.18 = (bf16[4,4,16,2048]{3,2,1,0:T(8,128)(2,1)}, bf16[4,4,16,2048]{3,2,1,0:T(8,128)(2,1)}, u32[]{:S(2)}, u32[]{:S(2)}) collective-permute-start(bf16[4,4,16,2048]{3,2,1,0:T(8,128)(2,1)} %collective-permute-done.10.refs_4_), channel_id=1, source_target_pairs={{0,1},{1,0},{2,3},{3,2},{4,5},{5,4},{6,7},{7,6},{8,9},{9,8},{10,11... | collective-permute-start | bytes 3145736 | tf_op jit(solution)/shard_map/ppermute | solution.py:498
  141.7 13.6 %collective-permute-start.19 = (bf16[4,4,16,2048]{3,2,1,0:T(8,128)(2,1)}, bf16[4,4,16,2048]{3,2,1,0:T(8,128)(2,1)}, u32[]{:S(2)}, u32[]{:S(2)}) collective-permute-start(bf16[4,4,16,2048]{3,2,1,0:T(8,128)(2,1)} %collective-permute-done.11.refs_5_), channel_id=1, source_target_pairs={{0,1},{1,0},{2,3},{3,2},{4,5},{5,4},{6,7},{7,6},{8,9},{9,8},{10,11... | collective-permute-start | bytes 3145736 | tf_op jit(solution)/shard_map/ppermute | solution.py:498
  142.7 23.7 %collective-permute-start.12 = (bf16[4,4,64,512]{3,2,1,0:T(8,128)(2,1)S(1)}, bf16[4,4,64,512]{3,2,1,0:T(8,128)(2,1)}, u32[]{:S(2)}, u32[]{:S(2)}) collective-permute-start(bf16[4,4,64,512]{3,2,1,0:T(8,128)(2,1)S(1)} %pad_maximum_fusion.1.refs_2_), channel_id=1, source_target_pairs={{0,1},{1,0},{2,3},{3,2},{4,5},{5,4},{6,7},{7,6},{8,9},{9,8},{10,11... | collective-permute-start | bytes 3145736 | tf_op jit(solution)/shard_map/ppermute | solution.py:498
  144.6 21.8 %collective-permute-start.13 = (bf16[4,4,64,512]{3,2,1,0:T(8,128)(2,1)}, bf16[4,4,64,512]{3,2,1,0:T(8,128)(2,1)S(1)}, u32[]{:S(2)}, u32[]{:S(2)}) collective-permute-start(bf16[4,4,64,512]{3,2,1,0:T(8,128)(2,1)} %collective-permute-done.6.refs_3_), channel_id=1, source_target_pairs={{0,1},{1,0},{2,3},{3,2},{4,5},{5,4},{6,7},{7,6},{8,9},{9,8},{10,11... | collective-permute-start | bytes 3145736 | tf_op jit(solution)/shard_map/ppermute | solution.py:498
  146.4 20.0 %collective-permute-start.14 = (bf16[4,4,64,512]{3,2,1,0:T(8,128)(2,1)}, bf16[4,4,64,512]{3,2,1,0:T(8,128)(2,1)}, u32[]{:S(2)}, u32[]{:S(2)}) collective-permute-start(bf16[4,4,64,512]{3,2,1,0:T(8,128)(2,1)} %collective-permute-done.7.refs_4_), channel_id=1, source_target_pairs={{0,1},{1,0},{2,3},{3,2},{4,5},{5,4},{6,7},{7,6},{8,9},{9,8},{10,11... | collective-permute-start | bytes 3145736 | tf_op jit(solution)/shard_map/ppermute | solution.py:498
  150.1 16.4 %collective-permute-start.15 = (bf16[4,4,64,512]{3,2,1,0:T(8,128)(2,1)}, bf16[4,4,64,512]{3,2,1,0:T(8,128)(2,1)}, u32[]{:S(2)}, u32[]{:S(2)}) collective-permute-start(bf16[4,4,64,512]{3,2,1,0:T(8,128)(2,1)} %collective-permute-done.8.refs_5_), channel_id=1, source_target_pairs={{0,1},{1,0},{2,3},{3,2},{4,5},{5,4},{6,7},{7,6},{8,9},{9,8},{10,11... | collective-permute-start | bytes 3145736 | tf_op jit(solution)/shard_map/ppermute | solution.py:498
  251.8 5.6 collective-permute-start.24
  324.0 21.2 %collective-permute-start.28 = (f32[2,512]{1,0:T(2,128)S(1)}, f32[2,512]{1,0:T(2,128)S(1)}, u32[]{:S(2)}, u32[]{:S(2)}) collective-permute-start(f32[2,512]{1,0:T(2,128)S(1)} %add.1401), channel_id=1, source_target_pairs={{0,2},{1,3},{2,0},{3,1},{4,6},{5,7},{6,4},{7,5},{8,10},{9,11},{10,... | collective-permute-start | bytes 12296 | tf_op jit(solution)/shard_map/ppermute | solution.py:498
  327.6 17.7 %collective-permute-start.29 = (f32[2,512]{1,0:T(2,128)S(1)}, f32[2,512]{1,0:T(2,128)S(1)}, u32[]{:S(2)}, u32[]{:S(2)}) collective-permute-start(f32[2,512]{1,0:T(2,128)S(1)} %add.1401), channel_id=1, source_target_pairs={{0,4},{1,5},{2,6},{3,7},{4,0},{5,1},{6,2},{7,3},{8,12},{9,13},{10,... | collective-permute-start | bytes 12296 | tf_op jit(solution)/shard_map/ppermute | solution.py:498
  327.6 17.7 %collective-permute-start.30 = (f32[2,512]{1,0:T(2,128)S(1)}, f32[2,512]{1,0:T(2,128)S(1)}, u32[]{:S(2)}, u32[]{:S(2)}) collective-permute-start(f32[2,512]{1,0:T(2,128)S(1)} %add.1401), channel_id=1, source_target_pairs={{0,6},{1,7},{2,4},{3,5},{4,2},{5,3},{6,0},{7,1},{8,14},{9,15},{10,... | collective-permute-start | bytes 12296 | tf_op jit(solution)/shard_map/ppermute | solution.py:498
  345.3 5.7 collective-permute-start.33
  349.7 5.5 collective-permute-start.31
  454.1 20.8 %collective-permute-start.34 = (bf16[16,4,64,512]{3,2,1,0:T(8,128)(2,1)}, bf16[16,4,64,512]{3,2,1,0:T(8,128)(2,1)}, u32[]{:S(2)}, u32[]{:S(2)}) collective-permute-start(bf16[16,4,64,512]{3,2,1,0:T(8,128)(2,1)} %get-tuple-element.296), channel_id=1, source_target_pairs={{0,1},{1,0},{2,3},{3,2},{4,5},{5,4},{6,7},{7,6},{8,9},{9,8},{10,11... | collective-permute-start | bytes 12582920 | tf_op jit(solution)/shard_map/ppermute | solution.py:498
  474.9 19.9 %collective-permute-start.36 = (bf16[16,4,16,2048]{3,2,1,0:T(8,128)(2,1)}, bf16[16,4,16,2048]{3,2,1,0:T(8,128)(2,1)}, u32[]{:S(2)}, u32[]{:S(2)}) collective-permute-start(bf16[16,4,16,2048]{3,2,1,0:T(8,128)(2,1)} %get-tuple-element.303), channel_id=1, source_target_pairs={{0,1},{1,0},{2,3},{3,2},{4,5},{5,4},{6,7},{7,6},{8,9},{9,8},{10,11... | collective-permute-start | bytes 12582920 | tf_op jit(solution)/shard_map/ppermute | solution.py:498
  476.9 36.7 %collective-permute-start.35 = (bf16[2,2,4,64,512]{4,3,2,1,0:T(8,128)(2,1)S(1)}, bf16[2,2,4,64,512]{4,3,2,1,0:T(8,128)(2,1)S(1)}, u32[]{:S(2)}, u32[]{:S(2)}) collective-permute-start(bf16[2,2,4,64,512]{4,3,2,1,0:T(8,128)(2,1)S(1)} %fusion.11), channel_id=1, source_target_pairs={{0,8},{1,9},{2,10},{3,11},{4,12},{5,13},{6,14},{7,15},{8,16},{9,17... | collective-permute-start | bytes 3145736 | tf_op jit(solution)/shard_map/ppermute | solution.py:498
  526.4 56.2 %collective-permute-start.40 = (bf16[16,16,4224]{2,1,0:T(8,128)(2,1)}, bf16[16,16,4224]{2,1,0:T(8,128)(2,1)}, u32[]{:S(2)}, u32[]{:S(2)}) collective-permute-start(bf16[16,16,4224]{2,1,0:T(8,128)(2,1)} %get-tuple-element.548), channel_id=1, source_target_pairs={{0,1},{1,0},{2,3},{3,2},{4,5},{5,4},{6,7},{7,6},{8,9},{9,8},{10,11... | collective-permute-start | bytes 6488072 | tf_op jit(solution)/shard_map/ppermute | solution.py:498
  526.4 28.2 %collective-permute-start.41 = (bf16[2,2,4,64,512]{4,3,2,1,0:T(8,128)(2,1)}, bf16[2,2,4,64,512]{4,3,2,1,0:T(8,128)(2,1)}, u32[]{:S(2)}, u32[]{:S(2)}) collective-permute-start(bf16[2,2,4,64,512]{4,3,2,1,0:T(8,128)(2,1)} %fusion.4), channel_id=1, source_target_pairs={{0,8},{1,9},{2,10},{3,11},{4,12},{5,13},{6,14},{7,15},{8,16},{9,17... | collective-permute-start | bytes 3145736 | tf_op jit(solution)/shard_map/ppermute | solution.py:498
  526.4 33.3 %collective-permute-start.37 = (bf16[4,4,16,2048]{3,2,1,0:T(8,128)(2,1)}, bf16[4,4,16,2048]{3,2,1,0:T(8,128)(2,1)}, u32[]{:S(2)}, u32[]{:S(2)}) collective-permute-start(bf16[4,4,16,2048]{3,2,1,0:T(8,128)(2,1)} %get-tuple-element.350), channel_id=1, source_target_pairs={{0,2},{1,3},{2,0},{3,1},{4,6},{5,7},{6,4},{7,5},{8,10},{9,11},{10,... | collective-permute-start | bytes 3145736 | tf_op jit(solution)/shard_map/ppermute | solution.py:498
  526.4 33.3 %collective-permute-start.38 = (bf16[4,4,16,2048]{3,2,1,0:T(8,128)(2,1)}, bf16[4,4,16,2048]{3,2,1,0:T(8,128)(2,1)}, u32[]{:S(2)}, u32[]{:S(2)}) collective-permute-start(bf16[4,4,16,2048]{3,2,1,0:T(8,128)(2,1)} %get-tuple-element.351), channel_id=1, source_target_pairs={{0,4},{1,5},{2,6},{3,7},{4,0},{5,1},{6,2},{7,3},{8,12},{9,13},{10,... | collective-permute-start | bytes 3145736 | tf_op jit(solution)/shard_map/ppermute | solution.py:498
  528.8 53.7 %collective-permute-start.39 = (bf16[4,4,16,2048]{3,2,1,0:T(8,128)(2,1)S(1)}, bf16[4,4,16,2048]{3,2,1,0:T(8,128)(2,1)}, u32[]{:S(2)}, u32[]{:S(2)}) collective-permute-start(bf16[4,4,16,2048]{3,2,1,0:T(8,128)(2,1)S(1)} %get-tuple-element.352), channel_id=1, source_target_pairs={{0,6},{1,7},{2,4},{3,5},{4,2},{5,3},{6,0},{7,1},{8,14},{9,15},{10,... | collective-permute-start | bytes 3145736 | tf_op jit(solution)/shard_map/ppermute | solution.py:498
  556.9 34.1 %collective-permute-start.45 = (bf16[2,2,4,64,512]{4,3,2,1,0:T(8,128)(2,1)S(1)}, bf16[2,2,4,64,512]{4,3,2,1,0:T(8,128)(2,1)S(1)}, u32[]{:S(2)}, u32[]{:S(2)}) collective-permute-start(bf16[2,2,4,64,512]{4,3,2,1,0:T(8,128)(2,1)S(1)} %fusion.3), channel_id=1, source_target_pairs={{0,8},{1,9},{2,10},{3,11},{4,12},{5,13},{6,14},{7,15},{8,16},{9,17... | collective-permute-start | bytes 3145736 | tf_op jit(solution)/shard_map/ppermute | solution.py:498
  588.8 30.3 %collective-permute-start.42 = (bf16[4,16,4224]{2,1,0:T(8,128)(2,1)S(1)}, bf16[4,16,4224]{2,1,0:T(8,128)(2,1)S(1)}, u32[]{:S(2)}, u32[]{:S(2)}) collective-permute-start(bf16[4,16,4224]{2,1,0:T(8,128)(2,1)S(1)} %get-tuple-element.363), channel_id=1, source_target_pairs={{0,2},{1,3},{2,0},{3,1},{4,6},{5,7},{6,4},{7,5},{8,10},{9,11},{10,... | collective-permute-start | bytes 1622024 | tf_op jit(solution)/shard_map/ppermute | solution.py:498
  588.9 31.9 %collective-permute-start.43 = (bf16[4,16,4224]{2,1,0:T(8,128)(2,1)S(1)}, bf16[4,16,4224]{2,1,0:T(8,128)(2,1)S(1)}, u32[]{:S(2)}, u32[]{:S(2)}) collective-permute-start(bf16[4,16,4224]{2,1,0:T(8,128)(2,1)S(1)} %get-tuple-element.364), channel_id=1, source_target_pairs={{0,4},{1,5},{2,6},{3,7},{4,0},{5,1},{6,2},{7,3},{8,12},{9,13},{10,... | collective-permute-start | bytes 1622024 | tf_op jit(solution)/shard_map/ppermute | solution.py:498
  591.0 9.0 %collective-permute-start.51 = (bf16[4,16,2048]{2,1,0:T(8,128)(2,1)S(1)}, bf16[4,16,2048]{2,1,0:T(8,128)(2,1)S(1)}, u32[]{:S(2)}, u32[]{:S(2)}) collective-permute-start(bf16[4,16,2048]{2,1,0:T(8,128)(2,1)S(1)} %get-tuple-element.381), channel_id=1, source_target_pairs={{0,24},{1,25},{2,26},{3,27},{4,28},{5,29},{6,30},{7,31},{8,0},{9,1... | collective-permute-start | bytes 786440 | tf_op jit(solution)/shard_map/ppermute | solution.py:498
  593.1 23.2 %collective-permute-start.50 = (bf16[4,16,2048]{2,1,0:T(8,128)(2,1)S(1)}, bf16[4,16,2048]{2,1,0:T(8,128)(2,1)S(1)}, u32[]{:S(2)}, u32[]{:S(2)}) collective-permute-start(bf16[4,16,2048]{2,1,0:T(8,128)(2,1)S(1)} %get-tuple-element.380), channel_id=1, source_target_pairs={{0,16},{1,17},{2,18},{3,19},{4,20},{5,21},{6,22},{7,23},{8,24},{9,... | collective-permute-start | bytes 786440 | tf_op jit(solution)/shard_map/ppermute | solution.py:498
  593.9 23.9 %collective-permute-start.49 = (bf16[4,16,2048]{2,1,0:T(8,128)(2,1)S(1)}, bf16[4,16,2048]{2,1,0:T(8,128)(2,1)S(1)}, u32[]{:S(2)}, u32[]{:S(2)}) collective-permute-start(bf16[4,16,2048]{2,1,0:T(8,128)(2,1)S(1)} %get-tuple-element.379), channel_id=1, source_target_pairs={{0,8},{1,9},{2,10},{3,11},{4,12},{5,13},{6,14},{7,15},{8,16},{9,17... | collective-permute-start | bytes 786440 | tf_op jit(solution)/shard_map/ppermute | solution.py:498
  599.9 20.8 %collective-permute-start.44 = (bf16[4,16,4224]{2,1,0:T(8,128)(2,1)S(1)}, bf16[4,16,4224]{2,1,0:T(8,128)(2,1)S(1)}, u32[]{:S(2)}, u32[]{:S(2)}) collective-permute-start(bf16[4,16,4224]{2,1,0:T(8,128)(2,1)S(1)} %fusion.17), channel_id=1, source_target_pairs={{0,6},{1,7},{2,4},{3,5},{4,2},{5,3},{6,0},{7,1},{8,14},{9,15},{10,... | collective-permute-start | bytes 1622024 | tf_op jit(solution)/shard_map/ppermute | solution.py:498
  616.4 12.7 %collective-permute-start.54 = (bf16[4,64,512]{2,1,0:T(8,128)(2,1)S(1)}, bf16[4,64,512]{2,1,0:T(8,128)(2,1)S(1)}, u32[]{:S(2)}, u32[]{:S(2)}) collective-permute-start(bf16[4,64,512]{2,1,0:T(8,128)(2,1)S(1)} %get-tuple-element.384), channel_id=1, source_target_pairs={{0,6},{1,7},{2,4},{3,5},{4,2},{5,3},{6,0},{7,1},{8,14},{9,15},{10,... | collective-permute-start | bytes 786440 | tf_op jit(solution)/shard_map/ppermute | solution.py:498
  617.8 12.2 %collective-permute-start.53 = (bf16[4,64,512]{2,1,0:T(8,128)(2,1)S(1)}, bf16[4,64,512]{2,1,0:T(8,128)(2,1)S(1)}, u32[]{:S(2)}, u32[]{:S(2)}) collective-permute-start(bf16[4,64,512]{2,1,0:T(8,128)(2,1)S(1)} %get-tuple-element.383), channel_id=1, source_target_pairs={{0,4},{1,5},{2,6},{3,7},{4,0},{5,1},{6,2},{7,3},{8,12},{9,13},{10,... | collective-permute-start | bytes 786440 | tf_op jit(solution)/shard_map/ppermute | solution.py:498
  619.1 10.9 %collective-permute-start.52 = (bf16[4,64,512]{2,1,0:T(8,128)(2,1)S(1)}, bf16[4,64,512]{2,1,0:T(8,128)(2,1)S(1)}, u32[]{:S(2)}, u32[]{:S(2)}) collective-permute-start(bf16[4,64,512]{2,1,0:T(8,128)(2,1)S(1)} %get-tuple-element.382), channel_id=1, source_target_pairs={{0,2},{1,3},{2,0},{3,1},{4,6},{5,7},{6,4},{7,5},{8,10},{9,11},{10,... | collective-permute-start | bytes 786440 | tf_op jit(solution)/shard_map/ppermute | solution.py:498
  622.2 8.6 %collective-permute-start.48 = (bf16[16,4224]{1,0:T(8,128)(2,1)S(1)}, bf16[16,4224]{1,0:T(8,128)(2,1)S(1)}, u32[]{:S(2)}, u32[]{:S(2)}) collective-permute-start(bf16[16,4224]{1,0:T(8,128)(2,1)S(1)} %get-tuple-element.378), channel_id=1, source_target_pairs={{0,24},{1,25},{2,26},{3,27},{4,28},{5,29},{6,30},{7,31},{8,0},{9,1... | collective-permute-start | bytes 405512 | tf_op jit(solution)/shard_map/ppermute | solution.py:498
  624.0 12.4 %collective-permute-start.47 = (bf16[16,4224]{1,0:T(8,128)(2,1)S(1)}, bf16[16,4224]{1,0:T(8,128)(2,1)S(1)}, u32[]{:S(2)}, u32[]{:S(2)}) collective-permute-start(bf16[16,4224]{1,0:T(8,128)(2,1)S(1)} %get-tuple-element.377), channel_id=1, source_target_pairs={{0,16},{1,17},{2,18},{3,19},{4,20},{5,21},{6,22},{7,23},{8,24},{9,... | collective-permute-start | bytes 405512 | tf_op jit(solution)/shard_map/ppermute | solution.py:498
  629.0 7.3 %collective-permute-start.46 = (bf16[16,4224]{1,0:T(8,128)(2,1)S(1)}, bf16[16,4224]{1,0:T(8,128)(2,1)S(1)}, u32[]{:S(2)}, u32[]{:S(2)}) collective-permute-start(bf16[16,4224]{1,0:T(8,128)(2,1)S(1)} %get-tuple-element.376), channel_id=1, source_target_pairs={{0,8},{1,9},{2,10},{3,11},{4,12},{5,13},{6,14},{7,15},{8,16},{9,17... | collective-permute-start | bytes 405512 | tf_op jit(solution)/shard_map/ppermute | solution.py:498
  (42 other events, 547.8 us)
Sparse Core Ops, SparseCore 0:
  14.5 98.4 all-gather.3
  140.6 112.1 all-gather.5
  345.5 199.4 reduce-scatter.1

commit v5 on v4

--- a/solution.py
+++ b/solution.py
@@ -1723,7 +1723,6 @@
     first_normed, first_probs, floats, taps, second_router_full = first_up_chain.step(
         first_normed, first_probs, floats, taps, second_router_full
     )
-    first_ups = Weights(first_up_chain.finish(), up_ids)
 
     windows = key_windows(segments[0])
     attend_full = (vec(4), vec(5), packed, vec(6), vec(7))
@@ -1731,7 +1730,8 @@
     point_full = (packed, (width, width), (0, 5))
     gated_full = (packed, (width, 2 * width), (0, 3))
 
-    first_normed, *second = first_down_chain.step(first_normed, *second)
+    first_normed, *second = advance([first_down_chain, first_up_chain], first_normed, *second)
+    first_ups = Weights(first_up_chain.finish(), up_ids)
     if sizes() == FAST:
         second_weights = [Both(*gather_both(second[0]), width)]
     else:

time: 658 us -> 653 us (level)
  waiting for transfers between devices: 191 us -> 182 us
    ppermute x55, waiting for transfers between devices: 191 us -> 182 us  [move(): return lax.ppermute(value, AXES, pairs)]
    unnamed x83 -> x89, local copies, waits for them, and re-layouts: 10.9 us -> 13.9 us
where the time goes in v5:
time: 653 us; the launch traced here: 646 us
  Pallas kernels  302 us (46%)
  waiting for transfers between devices  182 us (28%)
  starting transfers between devices  69.8 us (11%)
  other arithmetic  39.7 us (6%)
  local copies, waits for them, and re-layouts  36.1 us (6%)
  between operations  15.2 us (2%)
    ppermute x55, waiting for transfers between devices, move(): return lax.ppermute(value, AXES, pairs)  182 us
    pallas_call x8, Pallas kernels, expert_call(): pl.pallas_call(body, grid_spec=pltpu.PrefetchScalarGridSpec(num_scalar_pr...  145 us
    ppermute x55, starting transfers between devices, move(): return lax.ppermute(value, AXES, pairs)  69.2 us
    pallas_call x5, Pallas kernels, single(): pl.pallas_call(kernel, grid=(1,), in_specs=specs, out_specs=[pl.BlockSpec...  58.1 us
    pallas_call x1, Pallas kernels, attention_backward(): pl.pallas_call(functools.partial(attend_backward_kernel, bool(begin), las...  54 us
    pallas_call x1, Pallas kernels, attention_forward(): pl.pallas_call(attend_forward_kernel, grid_spec=pltpu.PrefetchScalarGridS...  45 us
    unnamed x89, local copies, waits for them, and re-layouts  13.9 us
  transfers between devices with their start and end apart: 58, of which 23 were waited for; matrix products, arithmetic and copies ran while one was open for 9% of the time, Pallas kernels for 38%

profile of v5, /device:TPU:0, one launch (start us, length us, event | category | flops | bytes accessed | tf_op | source)
XLA Modules:
  0.0 645.9 jit_solution(7934256610645564200)
XLA Ops:
  14.4 3.1 collective-permute-start
  17.5 2.6 collective-permute-start.1
  31.6 7.7 %collective-permute-done.1 = bf16[1,4,16,2048]{3,2,1,0:T(8,128)(2,1)S(1)} collective-permute-done((bf16[1,4,16,2048]{3,2,1,0:T(8,128)(2,1)}, bf16[1,4,16,2048]{3,2,1,0:T(8,128)(2,1)S(1)}, u32[]{:S(2)}, u32[]{:S(2)}) %collective-permute-start.1) | collective-permute-done | bytes 262176 | tf_op jit(solution)/shard_map/ppermute | solution.py:498
  39.7 7.2 %collective-permute-start.6 = (bf16[4,4,64,512]{3,2,1,0:T(8,128)(2,1)S(1)}, bf16[4,4,64,512]{3,2,1,0:T(8,128)(2,1)}, u32[]{:S(2)}, u32[]{:S(2)}) collective-permute-start(bf16[4,4,64,512]{3,2,1,0:T(8,128)(2,1)S(1)} %pad_maximum_fusion.1.refs_2_), channel_id=1, source_target_pairs={{0,8},{1,9},{2,10},{3,11},{4,12},{5,13},{6,14},{7,15},{8,16},{9,17... | collective-permute-start | bytes 3145736 | tf_op jit(solution)/shard_map/ppermute | solution.py:498
  49.3 26.9 %collective-permute-done.6.refs_3_ = bf16[4,4,64,512]{3,2,1,0:T(8,128)(2,1)} collective-permute-done((bf16[4,4,64,512]{3,2,1,0:T(8,128)(2,1)S(1)}, bf16[4,4,64,512]{3,2,1,0:T(8,128)(2,1)}, u32[]{:S(2)}, u32[]{:S(2)}) %collective-permute-start.6) | collective-permute-done | bytes 1048608 | tf_op jit(solution)/shard_map/ppermute | solution.py:498
  83.6 30.3 %collective-permute-done.7.refs_4_ = bf16[4,4,64,512]{3,2,1,0:T(8,128)(2,1)} collective-permute-done((bf16[4,4,64,512]{3,2,1,0:T(8,128)(2,1)}, bf16[4,4,64,512]{3,2,1,0:T(8,128)(2,1)}, u32[]{:S(2)}, u32[]{:S(2)}) %collective-permute-start.7) | collective-permute-done | bytes 1048608 | tf_op jit(solution)/shard_map/ppermute | solution.py:498
  119.3 3.7 expert_enter.1
  123.0 10.6 %collective-permute-done.10.refs_4_ = bf16[4,4,16,2048]{3,2,1,0:T(8,128)(2,1)} collective-permute-done((bf16[4,4,16,2048]{3,2,1,0:T(8,128)(2,1)S(1)}, bf16[4,4,16,2048]{3,2,1,0:T(8,128)(2,1)}, u32[]{:S(2)}, u32[]{:S(2)}) %collective-permute-start.10) | collective-permute-done | bytes 1048608 | tf_op jit(solution)/shard_map/ppermute | solution.py:498
  134.6 5.8 collective-permute-done.8.refs_5_
  150.8 11.2 %first_up.1 = (bf16[4,512,512]{2,1,0:T(8,128)(2,1)}, bf16[4,512,2048]{2,1,0:T(8,128)(2,1)}) custom-call(s32[5]{0:T(128)} %pad_add_fusion.2.refs_0_, s32[32]{0:T(128)} %stack.231.refs_1_, bf16[4,4,16,2048]{3,2,1,0:T(8,128)(2,1)} %copy-done.5, bf16[4,4,16,2048]{3,2,1,0:T(8,128)(2,1)} %collective-permute-done.9.refs_3_, ...), custom_call_target="tpu_custom_call" | custom-call | flops 5000000000 | bytes 20000000 | tf_op jit(solution)/shard_map/first_up/pallas_call | solution.py:1107
  163.0 13.7 %first_down.1 = (f32[1024,512]{1,0:T(8,128)}, f32[1024,512]{1,0:T(8,128)}) custom-call(s32[5]{0:T(128)} %pad_add_fusion.2.refs_0_, s32[32]{0:T(128)} %stack.230.refs_1_, bf16[4,4,64,512]{3,2,1,0:T(8,128)(2,1)} %copy-done.2, bf16[4,4,64,512]{3,2,1,0:T(8,128)(2,1)} %collective-permute-done.6.refs_3_, bf16[4,4,64,512]{3,2,1,0:T(8,128)(2,1)} %collective-permute-done.7.refs_4_, ...), custom_call_target="tpu_custom_call" | custom-call | flops 5000000000 | bytes 20000000 | tf_op jit(solution)/shard_map/first_down/pallas_call | solution.py:1107
  176.6 45.0 %attend_forward.1 = (bf16[1024,512]{1,0:T(8,128)(2,1)}, bf16[1024,512]{1,0:T(8,128)(2,1)}, bf16[1024,512]{1,0:T(8,128)(2,1)}, bf16[1024,512]{1,0:T(8,128)(2,1)},...) custom-call(s32[8]{0:T(128)} %pad_add_fusion.3.windows_ref, ...), custom_call_target="tpu_custom_call" | custom-call | flops 24000000000 | bytes 32000000 | tf_op jit(solution)/shard_map/attend_forward/pallas_call | solution.py:326
  221.6 16.7 %conv_front.1 = (f32[1024,512]{1,0:T(8,128)}, bf16[1024,512]{1,0:T(8,128)(2,1)}, f32[1024,1024]{1,0:T(8,128)}, f32[1024,512]{1,0:T(8,128)}, f32[2,512]{1,0:T(2,128)}) custom-call(f32[1024,512]{1,0:T(8,128)} %get-tuple-element.263.resid_ref.refs_4_, bf16[1024,512]{1,0:T(8,128)(2,1)} %get-tuple-element.268.ctx_ref.refs_11_, ...), custom_call_target="tpu_custom_call" | custom-call | flops 4000000000 | bytes 16000000 | tf_op jit(solution)/shard_map/conv_front/pallas_call | solution.py:722
  240.5 2.5 collective-permute-start.23
  248.0 2.2 collective-permute-start.24
  251.6 2.1 collective-permute-done.24
  255.4 6.1 conv_tail.1
  262.0 23.1 %second_forward.1 = (bf16[4,512,512]{2,1,0:T(8,128)(2,1)}, bf16[4,512,2048]{2,1,0:T(8,128)(2,1)}, f32[1024,512]{1,0:T(8,128)}, bf16[1024,512]{1,0:T(8,128)(2,1)}...) custom-call(s32[5]{0:T(128)} %pad_add_fusion.1.refs_0_, s32[32]{0:T(128)} %iota.119.refs_1_, ...), custom_call_target="tpu_custom_call" | custom-call | flops 10000000000 | bytes 20000000 | tf_op jit(solution)/shard_map/second_forward/pallas_call | solution.py:1107
  285.6 27.2 %second_back.1 = (f32[1024,512]{1,0:T(8,128)}, f32[1,512]{1,0:T(1,128)}, f32[1,512]{1,0:T(1,128)}, f32[128,1024]{1,0:T(8,128)}, bf16[4,512,512]{2,1,0:T(8,128)(2,1)}, /*index=5*/bf16[4,512,2048]{2,1,0:T(8,128)(2,1)}) custom-call(s32[5]{0:T(128)} %pad_add_fusion.1.refs_0_, s32[32]{0:T(128)} %iota.153.refs_1_, bf16[32,4,32,2048]{3,2,1,0:T(8,128)(2,1)} %bitcast.253, ...), custom_call_target="tpu_custom_call" | custom-call | flops 10000000000 | bytes 20000000 | tf_op jit(solution)/shard_map/second_back/pallas_call | solution.py:1107
  312.9 5.7 conv_turn.1
  320.7 2.3 collective-permute-start.28
  324.4 16.1 %second_grads.1 = bf16[32,4,32,2048]{3,2,1,0:T(8,128)(2,1)} custom-call(s32[5]{0:T(128)} %pad_add_fusion.1.refs_0_, bf16[4,512,512]{2,1,0:T(8,128)(2,1)} %get-tuple-element.286.refs_1_, bf16[4,512,2048]{2,1,0:T(8,128)(2,1)} %get-tuple-element.282.refs_9_.refs_2_, bf16[4,512,512]{2,1,0:T(8,128)(2,1)} %get-tuple-element.288.refs_3_, ...), custom_call_target="tpu_custom_call" | custom-call | flops 10000000000 | bytes 20000000 | tf_op jit(solution)/shard_map/second_grads/pallas_call | solution.py:1107
  340.5 4.1 collective-permute-start.33
  346.0 4.2 collective-permute-done.31
  350.7 25.8 %conv_back.1 = (f32[1024,512]{1,0:T(8,128)}, bf16[512,1024]{1,0:T(8,128)(2,1)}, f32[15,512]{1,0:T(8,128)}, f32[1,512]{1,0:T(1,128)}, f32[1,512]{1,0:T(1,128)}) custom-call(f32[1024,512]{1,0:T(8,128)} %get-tuple-element.283.slope_ref, f32[1024,512]{1,0:T(8,128)} %get-tuple-element.284.dshift_ref, f32[1024,512]{1,0:T(8,128)} %get-tuple-element.271.depth_ref, ...), custom_call_target="tpu_custom_call" | custom-call | flops 6000000000 | bytes 20000000 | tf_op jit(solution)/shard_map/conv_back/pallas_call | solution.py:722
  376.6 54.0 %attend_backward.1 = (f32[1024,512]{1,0:T(8,128)}, bf16[512,512]{1,0:T(8,128)(2,1)}, bf16[512,512]{1,0:T(8,128)(2,1)}, bf16[512,512]{1,0:T(8,128)(2,1)}, bf16[51...) custom-call(s32[8]{0:T(128)} %pad_add_fusion.3.windows_ref, ...), custom_call_target="tpu_custom_call" | custom-call | flops 40000000000 | bytes 20000000 | tf_op jit(solution)/shard_map/attend_backward/pallas_call | solution.py:387
  430.6 16.8 %first_down_grads.1 = (bf16[16,4,64,512]{3,2,1,0:T(8,128)(2,1)}, bf16[16,4,64,512]{3,2,1,0:T(8,128)(2,1)}, bf16[4,512,512]{2,1,0:T(8,128)(2,1)}, f32[1024,128]{1,0:T(8,128)}) custom-call(s32[5]{0:T(128)} %pad_add_fusion.2.refs_0_, f32[1024,512]{1,0:T(8,128)} %get-tuple-element.301.refs_1_.refs_14_, f32[1024,128]{1,0:T(8,128)} %get-tuple-element.262.refs_13_.refs_2_, ...), custom_call_target="tpu_custom_call" | custom-call | flops 5000000000 | bytes 20000000 | tf_op jit(solution)/shard_map/first_down_grads/pallas_call | solution.py:1107
  447.5 20.5 %first_up_grads.1 = (bf16[16,4,16,2048]{3,2,1,0:T(8,128)(2,1)}, bf16[16,4,16,2048]{3,2,1,0:T(8,128)(2,1)}, bf16[4,512,2048]{2,1,0:T(8,128)(2,1)}) custom-call(s32[5]{0:T(128)} %pad_add_fusion.2.refs_0_, s32[32]{0:T(128)} %stack.230.refs_1_, bf16[4,4,64,512]{3,2,1,0:T(8,128)(2,1)} %copy-done.2, bf16[4,4,64,512]{3,2,1,0:T(8,128)(2,1)} %collective-permute-done.6.refs_3_, ...), custom_call_target="tpu_custom_call" | custom-call | flops 8999999488 | bytes 20000000 | tf_op jit(solution)/shard_map/first_up_grads/pallas_call | solution.py:1107
  468.5 1.9 fusion.11
  470.4 1.9 collective-permute-start.35
  473.5 16.6 %first_leave.1 = (f32[1024,512]{1,0:T(8,128)}, f32[1,512]{1,0:T(1,128)}, f32[1,512]{1,0:T(1,128)}, f32[128,1024]{1,0:T(8,128)}) custom-call(s32[5]{0:T(128)} %pad_add_fusion.2.refs_0_, s32[32]{0:T(128)} %stack.231.refs_1_, bf16[4,4,16,2048]{3,2,1,0:T(8,128)(2,1)} %copy-done.5, bf16[4,4,16,2048]{3,2,1,0:T(8,128)(2,1)} %collective-permute-done.9.refs_3_, ...), custom_call_target="tpu_custom_call" | custom-call | flops 5000000000 | bytes 20000000 | tf_op jit(solution)/shard_map/first_leave/pallas_call | solution.py:1107
  490.1 19.1 %collective-permute-done.35 = bf16[2,2,4,64,512]{4,3,2,1,0:T(8,128)(2,1)S(1)} collective-permute-done((bf16[2,2,4,64,512]{4,3,2,1,0:T(8,128)(2,1)S(1)}, bf16[2,2,4,64,512]{4,3,2,1,0:T(8,128)(2,1)S(1)}, u32[]{:S(2)}, u32[]{:S(2)}) %collective-permute-start.35) | collective-permute-done | bytes 1048608 | tf_op jit(solution)/shard_map/ppermute | solution.py:498
  509.2 3.2 fusion.4
  512.5 4.7 fusion.14
  522.0 2.2 collective-permute-start.38
  526.8 23.8 %collective-permute-done.41 = bf16[2,2,4,64,512]{4,3,2,1,0:T(8,128)(2,1)} collective-permute-done((bf16[2,2,4,64,512]{4,3,2,1,0:T(8,128)(2,1)}, bf16[2,2,4,64,512]{4,3,2,1,0:T(8,128)(2,1)}, u32[]{:S(2)}, u32[]{:S(2)}) %collective-permute-start.41) | collective-permute-done | bytes 1048608 | tf_op jit(solution)/shard_map/ppermute | solution.py:498
  550.6 2.3 fusion.3
  553.0 2.8 collective-permute-start.45
  555.8 21.8 %collective-permute-done.39 = bf16[4,4,16,2048]{3,2,1,0:T(8,128)(2,1)} collective-permute-done((bf16[4,4,16,2048]{3,2,1,0:T(8,128)(2,1)S(1)}, bf16[4,4,16,2048]{3,2,1,0:T(8,128)(2,1)}, u32[]{:S(2)}, u32[]{:S(2)}) %collective-permute-start.39) | collective-permute-done | bytes 1048608 | tf_op jit(solution)/shard_map/ppermute | solution.py:498
  577.6 3.5 fusion.5
  584.0 2.2 collective-permute-start.43
  588.6 2.0 collective-permute-start.49
  590.6 2.0 fusion.2
  592.7 2.2 collective-permute-done.51
  594.9 1.9 collective-permute-start.44
  596.9 14.4 %collective-permute-done.50 = bf16[4,16,2048]{2,1,0:T(8,128)(2,1)S(1)} collective-permute-done((bf16[4,16,2048]{2,1,0:T(8,128)(2,1)S(1)}, bf16[4,16,2048]{2,1,0:T(8,128)(2,1)S(1)}, u32[]{:S(2)}, u32[]{:S(2)}) %collective-permute-start.50) | collective-permute-done | bytes 262176 | tf_op jit(solution)/shard_map/ppermute | solution.py:498
  618.7 4.2 collective-permute-start.47
  625.8 4.7 collective-permute-done.47
  (318 shorter events, 96.0 us)
Async XLA Ops:
  7.2 106.7 %all-gather.4.cloned.1.call-start = ((), (), s32[]{:S(2)}) async-start(), calls=%async_computation.1 | async-start | bytes 4595712 | tf_op jit(solution)/shard_map/all_gather | solution.py:1589
  14.3 247.1 %all-gather.6.cloned.1.call-start = ((), (), s32[]{:S(2)}) async-start(), calls=%async_computation.3 | async-start | bytes 17301504 | tf_op jit(solution)/shard_map/all_gather | solution.py:634
  14.4 12.8 %collective-permute-start = (bf16[1,4,16,2048]{3,2,1,0:T(8,128)(2,1)}, bf16[1,4,16,2048]{3,2,1,0:T(8,128)(2,1)S(1)}, u32[]{:S(2)}, u32[]{:S(2)}) collective-permute-start(bf16[1,4,16,2048]{3,2,1,0:T(8,128)(2,1)} %bitcast.230), channel_id=1, source_target_pairs={{0,8},{1,9},{2,10},{3,11},{4,12},{5,13},{6,14},{7,15},{8,16},{9,17... | collective-permute-start | bytes 786440 | tf_op jit(solution)/shard_map/ppermute | solution.py:498
  17.5 21.8 %collective-permute-start.1 = (bf16[1,4,16,2048]{3,2,1,0:T(8,128)(2,1)}, bf16[1,4,16,2048]{3,2,1,0:T(8,128)(2,1)S(1)}, u32[]{:S(2)}, u32[]{:S(2)}) collective-permute-start(bf16[1,4,16,2048]{3,2,1,0:T(8,128)(2,1)} %bitcast.231), channel_id=1, source_target_pairs={{0,16},{1,17},{2,18},{3,19},{4,20},{5,21},{6,22},{7,23},{8,24},{9,... | collective-permute-start | bytes 786440 | tf_op jit(solution)/shard_map/ppermute | solution.py:498
  20.1 19.3 %collective-permute-start.2 = (bf16[1,4,16,2048]{3,2,1,0:T(8,128)(2,1)}, bf16[1,4,16,2048]{3,2,1,0:T(8,128)(2,1)S(1)}, u32[]{:S(2)}, u32[]{:S(2)}) collective-permute-start(bf16[1,4,16,2048]{3,2,1,0:T(8,128)(2,1)} %bitcast.232), channel_id=1, source_target_pairs={{0,24},{1,25},{2,26},{3,27},{4,28},{5,29},{6,30},{7,31},{8,0},{9,1... | collective-permute-start | bytes 786440 | tf_op jit(solution)/shard_map/ppermute | solution.py:498
  21.4 17.9 %collective-permute-start.3 = (bf16[1,4,64,512]{3,2,1,0:T(8,128)(2,1)}, bf16[1,4,64,512]{3,2,1,0:T(8,128)(2,1)S(1)}, u32[]{:S(2)}, u32[]{:S(2)}) collective-permute-start(bf16[1,4,64,512]{3,2,1,0:T(8,128)(2,1)} %bitcast.226), channel_id=1, source_target_pairs={{0,2},{1,3},{2,0},{3,1},{4,6},{5,7},{6,4},{7,5},{8,10},{9,11},{10,... | collective-permute-start | bytes 786440 | tf_op jit(solution)/shard_map/ppermute | solution.py:498
  22.9 16.4 %collective-permute-start.4 = (bf16[1,4,64,512]{3,2,1,0:T(8,128)(2,1)}, bf16[1,4,64,512]{3,2,1,0:T(8,128)(2,1)S(1)}, u32[]{:S(2)}, u32[]{:S(2)}) collective-permute-start(bf16[1,4,64,512]{3,2,1,0:T(8,128)(2,1)} %bitcast.227), channel_id=1, source_target_pairs={{0,4},{1,5},{2,6},{3,7},{4,0},{5,1},{6,2},{7,3},{8,12},{9,13},{10,... | collective-permute-start | bytes 786440 | tf_op jit(solution)/shard_map/ppermute | solution.py:498
  28.2 11.1 %collective-permute-start.5 = (bf16[1,4,64,512]{3,2,1,0:T(8,128)(2,1)S(1)}, bf16[1,4,64,512]{3,2,1,0:T(8,128)(2,1)S(1)}, u32[]{:S(2)}, u32[]{:S(2)}) collective-permute-start(bf16[1,4,64,512]{3,2,1,0:T(8,128)(2,1)S(1)} %bitcast.228), channel_id=1, source_target_pairs={{0,6},{1,7},{2,4},{3,5},{4,2},{5,3},{6,0},{7,1},{8,14},{9,15},{10,... | collective-permute-start | bytes 786440 | tf_op jit(solution)/shard_map/ppermute | solution.py:498
  39.7 36.5 %collective-permute-start.6 = (bf16[4,4,64,512]{3,2,1,0:T(8,128)(2,1)S(1)}, bf16[4,4,64,512]{3,2,1,0:T(8,128)(2,1)}, u32[]{:S(2)}, u32[]{:S(2)}) collective-permute-start(bf16[4,4,64,512]{3,2,1,0:T(8,128)(2,1)S(1)} %pad_maximum_fusion.1.refs_2_), channel_id=1, source_target_pairs={{0,8},{1,9},{2,10},{3,11},{4,12},{5,13},{6,14},{7,15},{8,16},{9,17... | collective-permute-start | bytes 3145736 | tf_op jit(solution)/shard_map/ppermute | solution.py:498
  76.2 37.7 %collective-permute-start.7 = (bf16[4,4,64,512]{3,2,1,0:T(8,128)(2,1)}, bf16[4,4,64,512]{3,2,1,0:T(8,128)(2,1)}, u32[]{:S(2)}, u32[]{:S(2)}) collective-permute-start(bf16[4,4,64,512]{3,2,1,0:T(8,128)(2,1)} %collective-permute-done.6.refs_3_), channel_id=1, source_target_pairs={{0,8},{1,9},{2,10},{3,11},{4,12},{5,13},{6,14},{7,15},{8,16},{9,17... | collective-permute-start | bytes 3145736 | tf_op jit(solution)/shard_map/ppermute | solution.py:498
  77.9 45.1 %collective-permute-start.9 = (bf16[4,4,16,2048]{3,2,1,0:T(8,128)(2,1)S(1)}, bf16[4,4,16,2048]{3,2,1,0:T(8,128)(2,1)}, u32[]{:S(2)}, u32[]{:S(2)}) collective-permute-start(bf16[4,4,16,2048]{3,2,1,0:T(8,128)(2,1)S(1)} %pad_maximum_fusion.2.refs_2_), channel_id=1, source_target_pairs={{0,2},{1,3},{2,0},{3,1},{4,6},{5,7},{6,4},{7,5},{8,10},{9,11},{10,... | collective-permute-start | bytes 3145736 | tf_op jit(solution)/shard_map/ppermute | solution.py:498
  79.4 54.2 %collective-permute-start.10 = (bf16[4,4,16,2048]{3,2,1,0:T(8,128)(2,1)S(1)}, bf16[4,4,16,2048]{3,2,1,0:T(8,128)(2,1)}, u32[]{:S(2)}, u32[]{:S(2)}) collective-permute-start(bf16[4,4,16,2048]{3,2,1,0:T(8,128)(2,1)S(1)} %pad_maximum_fusion.2.refs_2_), channel_id=1, source_target_pairs={{0,4},{1,5},{2,6},{3,7},{4,0},{5,1},{6,2},{7,3},{8,12},{9,13},{10,... | collective-permute-start | bytes 3145736 | tf_op jit(solution)/shard_map/ppermute | solution.py:498
  81.0 52.6 %collective-permute-start.11 = (bf16[4,4,16,2048]{3,2,1,0:T(8,128)(2,1)S(1)}, bf16[4,4,16,2048]{3,2,1,0:T(8,128)(2,1)}, u32[]{:S(2)}, u32[]{:S(2)}) collective-permute-start(bf16[4,4,16,2048]{3,2,1,0:T(8,128)(2,1)S(1)} %pad_maximum_fusion.2.refs_2_), channel_id=1, source_target_pairs={{0,6},{1,7},{2,4},{3,5},{4,2},{5,3},{6,0},{7,1},{8,14},{9,15},{10,... | collective-permute-start | bytes 3145736 | tf_op jit(solution)/shard_map/ppermute | solution.py:498
  113.9 26.5 %collective-permute-start.8 = (bf16[4,4,64,512]{3,2,1,0:T(8,128)(2,1)}, bf16[4,4,64,512]{3,2,1,0:T(8,128)(2,1)}, u32[]{:S(2)}, u32[]{:S(2)}) collective-permute-start(bf16[4,4,64,512]{3,2,1,0:T(8,128)(2,1)} %collective-permute-done.7.refs_4_), channel_id=1, source_target_pairs={{0,8},{1,9},{2,10},{3,11},{4,12},{5,13},{6,14},{7,15},{8,16},{9,17... | collective-permute-start | bytes 3145736 | tf_op jit(solution)/shard_map/ppermute | solution.py:498
  133.6 6.8 %collective-permute-start.12 = (bf16[4,4,16,2048]{3,2,1,0:T(8,128)(2,1)S(1)}, bf16[4,4,16,2048]{3,2,1,0:T(8,128)(2,1)S(1)}, u32[]{:S(2)}, u32[]{:S(2)}) collective-permute-start(bf16[4,4,16,2048]{3,2,1,0:T(8,128)(2,1)S(1)} %pad_maximum_fusion.2.refs_2_), channel_id=1, source_target_pairs={{0,1},{1,0},{2,3},{3,2},{4,5},{5,4},{6,7},{7,6},{8,9},{9,8},{10,11... | collective-permute-start | bytes 3145736 | tf_op jit(solution)/shard_map/ppermute | solution.py:498
  133.6 7.8 %collective-permute-start.13 = (bf16[4,4,16,2048]{3,2,1,0:T(8,128)(2,1)}, bf16[4,4,16,2048]{3,2,1,0:T(8,128)(2,1)S(1)}, u32[]{:S(2)}, u32[]{:S(2)}) collective-permute-start(bf16[4,4,16,2048]{3,2,1,0:T(8,128)(2,1)} %collective-permute-done.9.refs_3_), channel_id=1, source_target_pairs={{0,1},{1,0},{2,3},{3,2},{4,5},{5,4},{6,7},{7,6},{8,9},{9,8},{10,11... | collective-permute-start | bytes 3145736 | tf_op jit(solution)/shard_map/ppermute | solution.py:498
  134.1 8.3 %collective-permute-start.14 = (bf16[4,4,16,2048]{3,2,1,0:T(8,128)(2,1)}, bf16[4,4,16,2048]{3,2,1,0:T(8,128)(2,1)S(1)}, u32[]{:S(2)}, u32[]{:S(2)}) collective-permute-start(bf16[4,4,16,2048]{3,2,1,0:T(8,128)(2,1)} %collective-permute-done.10.refs_4_), channel_id=1, source_target_pairs={{0,1},{1,0},{2,3},{3,2},{4,5},{5,4},{6,7},{7,6},{8,9},{9,8},{10,11... | collective-permute-start | bytes 3145736 | tf_op jit(solution)/shard_map/ppermute | solution.py:498
  134.2 9.3 %collective-permute-start.15 = (bf16[4,4,16,2048]{3,2,1,0:T(8,128)(2,1)}, bf16[4,4,16,2048]{3,2,1,0:T(8,128)(2,1)}, u32[]{:S(2)}, u32[]{:S(2)}) collective-permute-start(bf16[4,4,16,2048]{3,2,1,0:T(8,128)(2,1)} %collective-permute-done.11.refs_5_), channel_id=1, source_target_pairs={{0,1},{1,0},{2,3},{3,2},{4,5},{5,4},{6,7},{7,6},{8,9},{9,8},{10,11... | collective-permute-start | bytes 3145736 | tf_op jit(solution)/shard_map/ppermute | solution.py:498
  143.5 492.3 %reduce-scatter.2.cloned.1.call-start = ((), (), s32[]{:S(2)}) async-start(), calls=%async_computation.2 | async-start | bytes 17301504 | tf_op jit(solution)/shard_map/reduce_scatter | solution.py:692
  144.7 17.3 %collective-permute-start.16 = (bf16[4,4,64,512]{3,2,1,0:T(8,128)(2,1)S(1)}, bf16[4,4,64,512]{3,2,1,0:T(8,128)(2,1)S(1)}, u32[]{:S(2)}, u32[]{:S(2)}) collective-permute-start(bf16[4,4,64,512]{3,2,1,0:T(8,128)(2,1)S(1)} %pad_maximum_fusion.1.refs_2_), channel_id=1, source_target_pairs={{0,1},{1,0},{2,3},{3,2},{4,5},{5,4},{6,7},{7,6},{8,9},{9,8},{10,11... | collective-permute-start | bytes 3145736 | tf_op jit(solution)/shard_map/ppermute | solution.py:498
  144.8 17.2 %collective-permute-start.17 = (bf16[4,4,64,512]{3,2,1,0:T(8,128)(2,1)}, bf16[4,4,64,512]{3,2,1,0:T(8,128)(2,1)}, u32[]{:S(2)}, u32[]{:S(2)}) collective-permute-start(bf16[4,4,64,512]{3,2,1,0:T(8,128)(2,1)} %collective-permute-done.6.refs_3_), channel_id=1, source_target_pairs={{0,1},{1,0},{2,3},{3,2},{4,5},{5,4},{6,7},{7,6},{8,9},{9,8},{10,11... | collective-permute-start | bytes 3145736 | tf_op jit(solution)/shard_map/ppermute | solution.py:498
  145.3 16.7 %collective-permute-start.18 = (bf16[4,4,64,512]{3,2,1,0:T(8,128)(2,1)}, bf16[4,4,64,512]{3,2,1,0:T(8,128)(2,1)}, u32[]{:S(2)}, u32[]{:S(2)}) collective-permute-start(bf16[4,4,64,512]{3,2,1,0:T(8,128)(2,1)} %collective-permute-done.7.refs_4_), channel_id=1, source_target_pairs={{0,1},{1,0},{2,3},{3,2},{4,5},{5,4},{6,7},{7,6},{8,9},{9,8},{10,11... | collective-permute-start | bytes 3145736 | tf_op jit(solution)/shard_map/ppermute | solution.py:498
  145.3 16.7 %collective-permute-start.19 = (bf16[4,4,64,512]{3,2,1,0:T(8,128)(2,1)}, bf16[4,4,64,512]{3,2,1,0:T(8,128)(2,1)}, u32[]{:S(2)}, u32[]{:S(2)}) collective-permute-start(bf16[4,4,64,512]{3,2,1,0:T(8,128)(2,1)} %collective-permute-done.8.refs_5_), channel_id=1, source_target_pairs={{0,1},{1,0},{2,3},{3,2},{4,5},{5,4},{6,7},{7,6},{8,9},{9,8},{10,11... | collective-permute-start | bytes 3145736 | tf_op jit(solution)/shard_map/ppermute | solution.py:498
  248.0 5.7 collective-permute-start.24
  320.7 19.8 %collective-permute-start.28 = (f32[2,512]{1,0:T(2,128)S(1)}, f32[2,512]{1,0:T(2,128)S(1)}, u32[]{:S(2)}, u32[]{:S(2)}) collective-permute-start(f32[2,512]{1,0:T(2,128)S(1)} %add.1401), channel_id=1, source_target_pairs={{0,2},{1,3},{2,0},{3,1},{4,6},{5,7},{6,4},{7,5},{8,10},{9,11},{10,... | collective-permute-start | bytes 12296 | tf_op jit(solution)/shard_map/ppermute | solution.py:498
  322.9 17.5 %collective-permute-start.29 = (f32[2,512]{1,0:T(2,128)S(1)}, f32[2,512]{1,0:T(2,128)S(1)}, u32[]{:S(2)}, u32[]{:S(2)}) collective-permute-start(f32[2,512]{1,0:T(2,128)S(1)} %add.1401), channel_id=1, source_target_pairs={{0,4},{1,5},{2,6},{3,7},{4,0},{5,1},{6,2},{7,3},{8,12},{9,13},{10,... | collective-permute-start | bytes 12296 | tf_op jit(solution)/shard_map/ppermute | solution.py:498
  324.3 16.2 %collective-permute-start.30 = (f32[2,512]{1,0:T(2,128)S(1)}, f32[2,512]{1,0:T(2,128)S(1)}, u32[]{:S(2)}, u32[]{:S(2)}) collective-permute-start(f32[2,512]{1,0:T(2,128)S(1)} %add.1401), channel_id=1, source_target_pairs={{0,6},{1,7},{2,4},{3,5},{4,2},{5,3},{6,0},{7,1},{8,14},{9,15},{10,... | collective-permute-start | bytes 12296 | tf_op jit(solution)/shard_map/ppermute | solution.py:498
  447.4 21.0 %collective-permute-start.34 = (bf16[16,4,64,512]{3,2,1,0:T(8,128)(2,1)}, bf16[16,4,64,512]{3,2,1,0:T(8,128)(2,1)}, u32[]{:S(2)}, u32[]{:S(2)}) collective-permute-start(bf16[16,4,64,512]{3,2,1,0:T(8,128)(2,1)} %get-tuple-element.304), channel_id=1, source_target_pairs={{0,1},{1,0},{2,3},{3,2},{4,5},{5,4},{6,7},{7,6},{8,9},{9,8},{10,11... | collective-permute-start | bytes 12582920 | tf_op jit(solution)/shard_map/ppermute | solution.py:498
  468.1 22.0 %collective-permute-start.36 = (bf16[16,4,16,2048]{3,2,1,0:T(8,128)(2,1)}, bf16[16,4,16,2048]{3,2,1,0:T(8,128)(2,1)}, u32[]{:S(2)}, u32[]{:S(2)}) collective-permute-start(bf16[16,4,16,2048]{3,2,1,0:T(8,128)(2,1)} %get-tuple-element.311), channel_id=1, source_target_pairs={{0,1},{1,0},{2,3},{3,2},{4,5},{5,4},{6,7},{7,6},{8,9},{9,8},{10,11... | collective-permute-start | bytes 12582920 | tf_op jit(solution)/shard_map/ppermute | solution.py:498
  470.4 38.9 %collective-permute-start.35 = (bf16[2,2,4,64,512]{4,3,2,1,0:T(8,128)(2,1)S(1)}, bf16[2,2,4,64,512]{4,3,2,1,0:T(8,128)(2,1)S(1)}, u32[]{:S(2)}, u32[]{:S(2)}) collective-permute-start(bf16[2,2,4,64,512]{4,3,2,1,0:T(8,128)(2,1)S(1)} %fusion.11), channel_id=1, source_target_pairs={{0,8},{1,9},{2,10},{3,11},{4,12},{5,13},{6,14},{7,15},{8,16},{9,17... | collective-permute-start | bytes 3145736 | tf_op jit(solution)/shard_map/ppermute | solution.py:498
  522.0 55.6 %collective-permute-start.40 = (bf16[16,16,4224]{2,1,0:T(8,128)(2,1)}, bf16[16,16,4224]{2,1,0:T(8,128)(2,1)}, u32[]{:S(2)}, u32[]{:S(2)}) collective-permute-start(bf16[16,16,4224]{2,1,0:T(8,128)(2,1)} %get-tuple-element.556), channel_id=1, source_target_pairs={{0,1},{1,0},{2,3},{3,2},{4,5},{5,4},{6,7},{7,6},{8,9},{9,8},{10,11... | collective-permute-start | bytes 6488072 | tf_op jit(solution)/shard_map/ppermute | solution.py:498
  522.0 28.6 %collective-permute-start.41 = (bf16[2,2,4,64,512]{4,3,2,1,0:T(8,128)(2,1)}, bf16[2,2,4,64,512]{4,3,2,1,0:T(8,128)(2,1)}, u32[]{:S(2)}, u32[]{:S(2)}) collective-permute-start(bf16[2,2,4,64,512]{4,3,2,1,0:T(8,128)(2,1)} %fusion.4), channel_id=1, source_target_pairs={{0,8},{1,9},{2,10},{3,11},{4,12},{5,13},{6,14},{7,15},{8,16},{9,17... | collective-permute-start | bytes 3145736 | tf_op jit(solution)/shard_map/ppermute | solution.py:498
  522.0 33.7 %collective-permute-start.37 = (bf16[4,4,16,2048]{3,2,1,0:T(8,128)(2,1)}, bf16[4,4,16,2048]{3,2,1,0:T(8,128)(2,1)}, u32[]{:S(2)}, u32[]{:S(2)}) collective-permute-start(bf16[4,4,16,2048]{3,2,1,0:T(8,128)(2,1)} %get-tuple-element.358), channel_id=1, source_target_pairs={{0,2},{1,3},{2,0},{3,1},{4,6},{5,7},{6,4},{7,5},{8,10},{9,11},{10,... | collective-permute-start | bytes 3145736 | tf_op jit(solution)/shard_map/ppermute | solution.py:498
  522.0 33.7 %collective-permute-start.38 = (bf16[4,4,16,2048]{3,2,1,0:T(8,128)(2,1)}, bf16[4,4,16,2048]{3,2,1,0:T(8,128)(2,1)}, u32[]{:S(2)}, u32[]{:S(2)}) collective-permute-start(bf16[4,4,16,2048]{3,2,1,0:T(8,128)(2,1)} %get-tuple-element.359), channel_id=1, source_target_pairs={{0,4},{1,5},{2,6},{3,7},{4,0},{5,1},{6,2},{7,3},{8,12},{9,13},{10,... | collective-permute-start | bytes 3145736 | tf_op jit(solution)/shard_map/ppermute | solution.py:498
  524.2 53.4 %collective-permute-start.39 = (bf16[4,4,16,2048]{3,2,1,0:T(8,128)(2,1)S(1)}, bf16[4,4,16,2048]{3,2,1,0:T(8,128)(2,1)}, u32[]{:S(2)}, u32[]{:S(2)}) collective-permute-start(bf16[4,4,16,2048]{3,2,1,0:T(8,128)(2,1)S(1)} %get-tuple-element.360), channel_id=1, source_target_pairs={{0,6},{1,7},{2,4},{3,5},{4,2},{5,3},{6,0},{7,1},{8,14},{9,15},{10,... | collective-permute-start | bytes 3145736 | tf_op jit(solution)/shard_map/ppermute | solution.py:498
  553.0 33.2 %collective-permute-start.45 = (bf16[2,2,4,64,512]{4,3,2,1,0:T(8,128)(2,1)S(1)}, bf16[2,2,4,64,512]{4,3,2,1,0:T(8,128)(2,1)S(1)}, u32[]{:S(2)}, u32[]{:S(2)}) collective-permute-start(bf16[2,2,4,64,512]{4,3,2,1,0:T(8,128)(2,1)S(1)} %fusion.3), channel_id=1, source_target_pairs={{0,8},{1,9},{2,10},{3,11},{4,12},{5,13},{6,14},{7,15},{8,16},{9,17... | collective-permute-start | bytes 3145736 | tf_op jit(solution)/shard_map/ppermute | solution.py:498
  583.9 31.2 %collective-permute-start.42 = (bf16[4,16,4224]{2,1,0:T(8,128)(2,1)S(1)}, bf16[4,16,4224]{2,1,0:T(8,128)(2,1)S(1)}, u32[]{:S(2)}, u32[]{:S(2)}) collective-permute-start(bf16[4,16,4224]{2,1,0:T(8,128)(2,1)S(1)} %get-tuple-element.371), channel_id=1, source_target_pairs={{0,2},{1,3},{2,0},{3,1},{4,6},{5,7},{6,4},{7,5},{8,10},{9,11},{10,... | collective-permute-start | bytes 1622024 | tf_op jit(solution)/shard_map/ppermute | solution.py:498
  584.0 31.7 %collective-permute-start.43 = (bf16[4,16,4224]{2,1,0:T(8,128)(2,1)S(1)}, bf16[4,16,4224]{2,1,0:T(8,128)(2,1)S(1)}, u32[]{:S(2)}, u32[]{:S(2)}) collective-permute-start(bf16[4,16,4224]{2,1,0:T(8,128)(2,1)S(1)} %get-tuple-element.372), channel_id=1, source_target_pairs={{0,4},{1,5},{2,6},{3,7},{4,0},{5,1},{6,2},{7,3},{8,12},{9,13},{10,... | collective-permute-start | bytes 1622024 | tf_op jit(solution)/shard_map/ppermute | solution.py:498
  586.2 8.7 %collective-permute-start.51 = (bf16[4,16,2048]{2,1,0:T(8,128)(2,1)S(1)}, bf16[4,16,2048]{2,1,0:T(8,128)(2,1)S(1)}, u32[]{:S(2)}, u32[]{:S(2)}) collective-permute-start(bf16[4,16,2048]{2,1,0:T(8,128)(2,1)S(1)} %get-tuple-element.389), channel_id=1, source_target_pairs={{0,24},{1,25},{2,26},{3,27},{4,28},{5,29},{6,30},{7,31},{8,0},{9,1... | collective-permute-start | bytes 786440 | tf_op jit(solution)/shard_map/ppermute | solution.py:498
  588.0 23.3 %collective-permute-start.50 = (bf16[4,16,2048]{2,1,0:T(8,128)(2,1)S(1)}, bf16[4,16,2048]{2,1,0:T(8,128)(2,1)S(1)}, u32[]{:S(2)}, u32[]{:S(2)}) collective-permute-start(bf16[4,16,2048]{2,1,0:T(8,128)(2,1)S(1)} %get-tuple-element.388), channel_id=1, source_target_pairs={{0,16},{1,17},{2,18},{3,19},{4,20},{5,21},{6,22},{7,23},{8,24},{9,... | collective-permute-start | bytes 786440 | tf_op jit(solution)/shard_map/ppermute | solution.py:498
  588.6 24.0 %collective-permute-start.49 = (bf16[4,16,2048]{2,1,0:T(8,128)(2,1)S(1)}, bf16[4,16,2048]{2,1,0:T(8,128)(2,1)S(1)}, u32[]{:S(2)}, u32[]{:S(2)}) collective-permute-start(bf16[4,16,2048]{2,1,0:T(8,128)(2,1)S(1)} %get-tuple-element.387), channel_id=1, source_target_pairs={{0,8},{1,9},{2,10},{3,11},{4,12},{5,13},{6,14},{7,15},{8,16},{9,17... | collective-permute-start | bytes 786440 | tf_op jit(solution)/shard_map/ppermute | solution.py:498
  594.9 20.8 %collective-permute-start.44 = (bf16[4,16,4224]{2,1,0:T(8,128)(2,1)S(1)}, bf16[4,16,4224]{2,1,0:T(8,128)(2,1)S(1)}, u32[]{:S(2)}, u32[]{:S(2)}) collective-permute-start(bf16[4,16,4224]{2,1,0:T(8,128)(2,1)S(1)} %fusion.17), channel_id=1, source_target_pairs={{0,6},{1,7},{2,4},{3,5},{4,2},{5,3},{6,0},{7,1},{8,14},{9,15},{10,... | collective-permute-start | bytes 1622024 | tf_op jit(solution)/shard_map/ppermute | solution.py:498
  611.3 11.5 %collective-permute-start.54 = (bf16[4,64,512]{2,1,0:T(8,128)(2,1)S(1)}, bf16[4,64,512]{2,1,0:T(8,128)(2,1)S(1)}, u32[]{:S(2)}, u32[]{:S(2)}) collective-permute-start(bf16[4,64,512]{2,1,0:T(8,128)(2,1)S(1)} %get-tuple-element.392), channel_id=1, source_target_pairs={{0,6},{1,7},{2,4},{3,5},{4,2},{5,3},{6,0},{7,1},{8,14},{9,15},{10,... | collective-permute-start | bytes 786440 | tf_op jit(solution)/shard_map/ppermute | solution.py:498
  612.6 12.1 %collective-permute-start.53 = (bf16[4,64,512]{2,1,0:T(8,128)(2,1)S(1)}, bf16[4,64,512]{2,1,0:T(8,128)(2,1)S(1)}, u32[]{:S(2)}, u32[]{:S(2)}) collective-permute-start(bf16[4,64,512]{2,1,0:T(8,128)(2,1)S(1)} %get-tuple-element.391), channel_id=1, source_target_pairs={{0,4},{1,5},{2,6},{3,7},{4,0},{5,1},{6,2},{7,3},{8,12},{9,13},{10,... | collective-permute-start | bytes 786440 | tf_op jit(solution)/shard_map/ppermute | solution.py:498
  615.1 9.7 %collective-permute-start.52 = (bf16[4,64,512]{2,1,0:T(8,128)(2,1)S(1)}, bf16[4,64,512]{2,1,0:T(8,128)(2,1)S(1)}, u32[]{:S(2)}, u32[]{:S(2)}) collective-permute-start(bf16[4,64,512]{2,1,0:T(8,128)(2,1)S(1)} %get-tuple-element.390), channel_id=1, source_target_pairs={{0,2},{1,3},{2,0},{3,1},{4,6},{5,7},{6,4},{7,5},{8,10},{9,11},{10,... | collective-permute-start | bytes 786440 | tf_op jit(solution)/shard_map/ppermute | solution.py:498
  617.2 8.6 %collective-permute-start.48 = (bf16[16,4224]{1,0:T(8,128)(2,1)S(1)}, bf16[16,4224]{1,0:T(8,128)(2,1)S(1)}, u32[]{:S(2)}, u32[]{:S(2)}) collective-permute-start(bf16[16,4224]{1,0:T(8,128)(2,1)S(1)} %get-tuple-element.386), channel_id=1, source_target_pairs={{0,24},{1,25},{2,26},{3,27},{4,28},{5,29},{6,30},{7,31},{8,0},{9,1... | collective-permute-start | bytes 405512 | tf_op jit(solution)/shard_map/ppermute | solution.py:498
  618.7 11.9 %collective-permute-start.47 = (bf16[16,4224]{1,0:T(8,128)(2,1)S(1)}, bf16[16,4224]{1,0:T(8,128)(2,1)S(1)}, u32[]{:S(2)}, u32[]{:S(2)}) collective-permute-start(bf16[16,4224]{1,0:T(8,128)(2,1)S(1)} %get-tuple-element.385), channel_id=1, source_target_pairs={{0,16},{1,17},{2,18},{3,19},{4,20},{5,21},{6,22},{7,23},{8,24},{9,... | collective-permute-start | bytes 405512 | tf_op jit(solution)/shard_map/ppermute | solution.py:498
  622.8 7.7 %collective-permute-start.46 = (bf16[16,4224]{1,0:T(8,128)(2,1)S(1)}, bf16[16,4224]{1,0:T(8,128)(2,1)S(1)}, u32[]{:S(2)}, u32[]{:S(2)}) collective-permute-start(bf16[16,4224]{1,0:T(8,128)(2,1)S(1)} %get-tuple-element.384), channel_id=1, source_target_pairs={{0,8},{1,9},{2,10},{3,11},{4,12},{5,13},{6,14},{7,15},{8,16},{9,17... | collective-permute-start | bytes 405512 | tf_op jit(solution)/shard_map/ppermute | solution.py:498
  (45 other events, 567.9 us)
Sparse Core Ops, SparseCore 0:
  14.5 98.4 all-gather.3
  143.6 112.3 all-gather.5
  340.6 199.7 reduce-scatter.1
